TPU v7x, 512 devices: a whole 4x8x8 slice. The times are simulated.
512 devices in a mesh: tile: 64 (over z_hi, y, core), head: 8 (over x, z_lo).
Axes of the slice: x: 4, y: 8, z: 8 (z_hi: 4, z_lo: 2; z = z_hi * 2 + z_lo), core: 2. Of those that a mesh axis runs over, the one named last changes fastest.
Arguments:
- queries: bfloat16 [16384, 3072], P('tile', 'head'), may hold values from -32 to 32, as said below
- key_rows: bfloat16 [16384, 3072], P('tile', 'head'), may hold values from -32 to 32, as said below
- value_rows: bfloat16 [16384, 3072], P('tile', 'head'), may hold values from -18 to 18
- windows: int32 [64, 3], P('tile'), may hold values from 0 to 1
- residual: bfloat16 [16384, 3072], P('tile', 'head'), may hold values from -6 to 6
- out_weight: bfloat16 [3072, 3072], P('head'), may hold values from -0.109375 to 0.109375
- gate_scale: float32 [3072], P('head'), may hold values from 1 to 4
Outputs:
- layer_out: bfloat16 [16384, 3072], P('tile', 'head')
Inputs may be any that keep to these rules, and one draw needn't show every extreme that they name: `queries`: queries per head. `key_rows`: keys per head.
All inputs are finite; a program needn't handle non-finite values.
Results may differ from a plain program's by a relative error of at most 0.017.
Values may be sent and summed in bfloat16 or wider, within the bound.
No kernel may reach another device: no remote copies, remote signals or barrier semaphores. Data moves between devices by JAX's collectives and lax.ppermute only.
A program may use at most 64 MiB of HBM per device.

v0:
```python
import jax
import jax.numpy as jnp
from jax import lax
from jax.sharding import PartitionSpec as P

HD = 128
HEIGHT_TILES = 4


OFFSETS = [(-1, -1), (-1, 0), (-1, 1), (0, -1), (0, 0), (0, 1), (1, -1), (1, 0), (1, 1)]


def passed_along(block, axis, distance):
    devices = range(lax.axis_size(axis))
    route = [(i - distance, i) for i in devices if i - distance in devices]
    return lax.ppermute(block, axis, route)


def gather_blocks(key_rows, value_rows):
    blocks = {(0, 0): (key_rows, value_rows)}
    for step_time, step_height in OFFSETS:
        if step_time != 0 or step_height != 0:
            blocks[step_time, step_height] = passed_along(
                (key_rows, value_rows), "tile", -(step_time * HEIGHT_TILES + step_height)
            )
    key_stack = jnp.concatenate([blocks[offset][0] for offset in OFFSETS], axis=0)
    value_stack = jnp.concatenate([blocks[offset][1] for offset in OFFSETS], axis=0)
    return (key_stack, value_stack)


def build_mask(windows, tile_len):
    width_tiles = windows.shape[0]
    place = lax.axis_index("tile")
    time_tiles = lax.axis_size("tile") // HEIGHT_TILES
    time_pos = place // HEIGHT_TILES
    height_pos = place % HEIGHT_TILES
    step_time = jnp.array([offset[0] for offset in OFFSETS], jnp.int32)
    step_height = jnp.array([offset[1] for offset in OFFSETS], jnp.int32)
    inside = (time_pos + step_time >= 0) & (time_pos + step_time < time_tiles)
    inside = inside & (height_pos + step_height >= 0) & (height_pos + step_height < HEIGHT_TILES)
    tile_range = jnp.arange(width_tiles, dtype=jnp.int32)
    width_gap = jnp.abs(tile_range[None, :] - tile_range[:, None])
    allowed = inside[None, :, None]
    allowed = allowed & (jnp.abs(step_time)[None, :, None] <= windows[:, 0][:, None, None])
    allowed = allowed & (jnp.abs(step_height)[None, :, None] <= windows[:, 1][:, None, None])
    allowed = allowed & (width_gap[:, None, :] <= windows[:, 2][:, None, None])
    flat = allowed.reshape(width_tiles, 9 * width_tiles)
    return jnp.repeat(jnp.repeat(flat, tile_len, axis=0), tile_len, axis=1)


def attend(queries, key_stack, value_stack, token_mask):
    head_count = queries.shape[1] // HD
    scale = HD ** (-0.5)
    outputs = []
    for head_index in range(head_count):
        low = head_index * HD
        scores = (
            jnp.einsum(
                "qd,kd->qk",
                queries[:, low : low + HD],
                key_stack[:, low : low + HD],
                preferred_element_type=jnp.float32,
            )
            * scale
        )
        scores = jnp.where(token_mask, scores, -1e30)
        largest = jnp.max(scores, axis=1, keepdims=True)
        weights = jnp.where(token_mask, jnp.exp(scores - largest), 0.0)
        row_total = jnp.sum(weights, axis=1, keepdims=True)
        head_mix = jnp.dot(
            weights.astype(jnp.bfloat16),
            value_stack[:, low : low + HD],
            preferred_element_type=jnp.float32,
        )
        outputs.append((head_mix / row_total).astype(jnp.bfloat16))
    return jnp.concatenate(outputs, axis=1)


def shards(queries, key_rows, value_rows, windows, residual, out_weight, gate_scale):
    tile_len = queries.shape[0] // windows.shape[0]
    key_stack, value_stack = gather_blocks(key_rows, value_rows)
    token_mask = build_mask(windows, tile_len)
    attention = attend(queries, key_stack, value_stack, token_mask)
    partial_term = jnp.dot(attention, out_weight, preferred_element_type=jnp.float32)
    projected = lax.psum_scatter(
        partial_term.astype(jnp.bfloat16), "head", scatter_dimension=1, tiled=True
    ).astype(jnp.float32)
    return (residual.astype(jnp.float32) + gate_scale * projected).astype(jnp.bfloat16)


def solution(mesh):
    return jax.shard_map(
        shards,
        mesh=mesh,
        in_specs=(
            P("tile", "head"),
            P("tile", "head"),
            P("tile", "head"),
            P("tile", None),
            P("tile", "head"),
            P("head", None),
            P("head"),
        ),
        out_specs=P("tile", "head"),
        check_vma=False,
    )
```

profile of v0, /device:TPU:1, one launch (start us, length us, event | category | flops | bytes accessed | tf_op | source)
XLA Modules:
  0.0 194.9 jit_solution(5580703667807250933)
XLA Ops:
  6.5 1.6 collective-permute-start.6
  8.1 1.3 collective-permute-start.5
  9.4 8.8 %collective-permute-start.4 = (bf16[256,384]{1,0:T(8,128)(2,1)}, bf16[256,384]{1,0:T(8,128)(2,1)S(1)}, u32[]{:S(2)}, u32[]{:S(2)}) collective-permute-start(bf16[256,384]{1,0:T(8,128)(2,1)} %param.10), channel_id=1, source_target_pairs={{8,0},{16,8},{24,16},{32,24},{40,32},{48,40},{56,48},{64,56},{72,6... | collective-permute-start | bytes 589832 | tf_op jit(solution)/shard_map/ppermute | solution.py:16
  18.2 5.8 %collective-permute-start.1 = (bf16[256,384]{1,0:T(8,128)(2,1)}, bf16[256,384]{1,0:T(8,128)(2,1)S(1)}, u32[]{:S(2)}, u32[]{:S(2)}) collective-permute-start(bf16[256,384]{1,0:T(8,128)(2,1)} %param.10), channel_id=1, source_target_pairs={{0,32},{8,40},{16,48},{24,56},{32,64},{40,72},{48,80},{56,88},{64,... | collective-permute-start | bytes 589832 | tf_op jit(solution)/shard_map/ppermute | solution.py:16
  24.0 2.5 %collective-permute-start = (bf16[256,384]{1,0:T(8,128)(2,1)}, bf16[256,384]{1,0:T(8,128)(2,1)}, u32[]{:S(2)}, u32[]{:S(2)}) collective-permute-start(bf16[256,384]{1,0:T(8,128)(2,1)} %param.10), channel_id=1, source_target_pairs={{0,40},{8,48},{16,56},{24,64},{32,72},{40,80},{48,88},{56,96},{64,... | collective-permute-start | bytes 589832 | tf_op jit(solution)/shard_map/ppermute | solution.py:16
  26.5 1.4 fusion.60
  28.6 2.0 %and_and_fusion = pred[9]{0:T(512)(128)(4,1)S(1)} fusion(s32[9]{0:T(128)} %constant.55, s32[9]{0:T(128)} %constant.54, pred[]{:T(512)} %bitcast.2, s32[9]{0:T(128)} %constant.52.clone, s32[9]{0:T(128)} %constant.51.clone, s32[]{:T(128)} %bitcast.1, s32[]{:T(128)} %bitcast, s32[]{:T(128)S(6)} %select_n.34, s32[]{:T(128)S(6)} %select_n.33), kind=kLoop, calls=%fused_computation.67 | loop fusion | flops 126 | bytes 170 | tf_op jit(solution)/shard_map/and | solution.py:46
  30.6 9.7 %collective-permute-done = bf16[256,384]{1,0:T(8,128)(2,1)} collective-permute-done((bf16[256,384]{1,0:T(8,128)(2,1)}, bf16[256,384]{1,0:T(8,128)(2,1)}, u32[]{:S(2)}, u32[]{:S(2)}) %collective-permute-start) | collective-permute-done | bytes 196640 | tf_op jit(solution)/shard_map/ppermute | solution.py:16
  40.4 4.8 %collective-permute-start.2 = (bf16[256,384]{1,0:T(8,128)(2,1)}, bf16[256,384]{1,0:T(8,128)(2,1)S(1)}, u32[]{:S(2)}, u32[]{:S(2)}) collective-permute-start(bf16[256,384]{1,0:T(8,128)(2,1)} %param.10), channel_id=1, source_target_pairs={{0,24},{8,32},{16,40},{24,48},{32,56},{40,64},{48,72},{56,80},{64,... | collective-permute-start | bytes 589832 | tf_op jit(solution)/shard_map/ppermute | solution.py:16
  45.2 0.9 constant_dynamic-update-slice_fusion.8
  46.2 3.8 %collective-permute-start.3 = (bf16[256,384]{1,0:T(8,128)(2,1)}, bf16[256,384]{1,0:T(8,128)(2,1)S(1)}, u32[]{:S(2)}, u32[]{:S(2)}) collective-permute-start(bf16[256,384]{1,0:T(8,128)(2,1)} %param.10), channel_id=1, source_target_pairs={{0,8},{8,16},{16,24},{24,32},{32,40},{40,48},{48,56},{56,64},{64,7... | collective-permute-start | bytes 589832 | tf_op jit(solution)/shard_map/ppermute | solution.py:16
  50.2 1.3 collective-permute-start.7
  51.6 1.3 collective-permute-done.3
  52.9 1.3 collective-permute-start.14
  54.3 1.3 collective-permute-start.13
  55.7 1.9 collective-permute-start.12
  57.7 8.5 %collective-permute-start.9 = (bf16[256,384]{1,0:T(8,128)(2,1)S(1)}, bf16[256,384]{1,0:T(8,128)(2,1)S(1)}, u32[]{:S(2)}, u32[]{:S(2)}) collective-permute-start(bf16[256,384]{1,0:T(8,128)(2,1)S(1)} %copy-done.2), channel_id=1, source_target_pairs={{0,32},{8,40},{16,48},{24,56},{32,64},{40,72},{48,80},{56,88},{64,... | collective-permute-start | bytes 589832 | tf_op jit(solution)/shard_map/ppermute | solution.py:16
  66.2 1.6 collective-permute-done.7
  67.8 6.0 %collective-permute-start.8 = (bf16[256,384]{1,0:T(8,128)(2,1)S(1)}, bf16[256,384]{1,0:T(8,128)(2,1)S(1)}, u32[]{:S(2)}, u32[]{:S(2)}) collective-permute-start(bf16[256,384]{1,0:T(8,128)(2,1)S(1)} %copy-done.2), channel_id=1, source_target_pairs={{0,40},{8,48},{16,56},{24,64},{32,72},{40,80},{48,88},{56,96},{64,... | collective-permute-start | bytes 589832 | tf_op jit(solution)/shard_map/ppermute | solution.py:16
  75.8 1.8 fusion.3
  77.6 4.7 %collective-permute-done.8 = bf16[256,384]{1,0:T(8,128)(2,1)S(1)} collective-permute-done((bf16[256,384]{1,0:T(8,128)(2,1)S(1)}, bf16[256,384]{1,0:T(8,128)(2,1)S(1)}, u32[]{:S(2)}, u32[]{:S(2)}) %collective-permute-start.8) | collective-permute-done | bytes 196640 | tf_op jit(solution)/shard_map/ppermute | solution.py:16
  82.3 9.3 %collective-permute-start.10 = (bf16[256,384]{1,0:T(8,128)(2,1)S(1)}, bf16[256,384]{1,0:T(8,128)(2,1)S(1)}, u32[]{:S(2)}, u32[]{:S(2)}) collective-permute-start(bf16[256,384]{1,0:T(8,128)(2,1)S(1)} %copy-done.2), channel_id=1, source_target_pairs={{0,24},{8,32},{16,40},{24,48},{32,56},{40,64},{48,72},{56,80},{64,... | collective-permute-start | bytes 589832 | tf_op jit(solution)/shard_map/ppermute | solution.py:16
  91.6 1.9 collective-permute-start.11
  93.6 2.5 %collective-permute-done.10 = bf16[256,384]{1,0:T(8,128)(2,1)S(1)} collective-permute-done((bf16[256,384]{1,0:T(8,128)(2,1)S(1)}, bf16[256,384]{1,0:T(8,128)(2,1)S(1)}, u32[]{:S(2)}, u32[]{:S(2)}) %collective-permute-start.10) | collective-permute-done | bytes 196640 | tf_op jit(solution)/shard_map/ppermute | solution.py:16
  96.1 1.3 collective-permute-start.15
  98.4 12.3 %collective-permute-done.15 = bf16[256,384]{1,0:T(8,128)(2,1)S(1)} collective-permute-done((bf16[256,384]{1,0:T(8,128)(2,1)S(1)}, bf16[256,384]{1,0:T(8,128)(2,1)S(1)}, u32[]{:S(2)}, u32[]{:S(2)}) %collective-permute-start.15) | collective-permute-done | bytes 196640 | tf_op jit(solution)/shard_map/ppermute | solution.py:16
  111.7 0.9 fusion.36
  112.6 0.9 fusion.39
  113.6 2.1 %convolution_convert_fusion = bf16[256,3072]{1,0:T(8,128)(2,1)} fusion(bf16[384,3072]{1,0:T(8,128)(2,1)S(1)} %copy-done, bf16[256,128]{1,0:T(8,128)(2,1)S(1)} %fusion.33, bf16[256,128]{1,0:T(8,128)(2,1)S(1)} %fusion.36, bf16[256,128]{1,0:T(8,128)(2,1)S(1)} %fusion.39), kind=kOutput, calls=%fused_computation.6 | convolution fusion | flops 605356032 | bytes 4128768 | tf_op jit(solution)/shard_map/dot_general | solution.py:84
  115.7 2.6 %copy.10 = bf16[256,3072]{0,1:T(8,128)(2,1)} copy(bf16[256,3072]{1,0:T(8,128)(2,1)} %convolution_convert_fusion) | data formatting | bytes 3145728
  118.3 67.9 %reduce-scatter.4.cloned.1.call-done = bf16[384,256]{1,0:T(8,128)(2,1)} async-done(((bf16[3072,256]{1,0:T(8,128)(2,1)}), bf16[384,256]{1,0:T(8,128)(2,1)}) %reduce-scatter.4.cloned.1.call-update) | async-done | bytes 196624
  186.2 1.1 copy.11
  (48 shorter events, 5.2 us)
Async XLA Ops:
  6.5 107.0 %copy-start = (bf16[384,3072]{1,0:T(8,128)(2,1)S(1)}, bf16[384,3072]{1,0:T(8,128)(2,1)}, u32[]{:S(2)}) copy-start(bf16[384,3072]{1,0:T(8,128)(2,1)} %param.14) | copy-start | bytes 7077892
  6.5 47.7 %copy-start.1 = (bf16[256,384]{1,0:T(8,128)(2,1)S(1)}, bf16[256,384]{1,0:T(8,128)(2,1)}, u32[]{:S(2)}) copy-start(bf16[256,384]{1,0:T(8,128)(2,1)} %param.10) | copy-start | bytes 589828
  6.5 47.8 %copy-start.2 = (bf16[256,384]{1,0:T(8,128)(2,1)S(1)}, bf16[256,384]{1,0:T(8,128)(2,1)}, u32[]{:S(2)}) copy-start(bf16[256,384]{1,0:T(8,128)(2,1)} %param.11) | copy-start | bytes 589828
  6.5 179.7 %reduce-scatter.4.cloned.1.call-start = ((), (), s32[]{:S(2)}) async-start(), calls=%async_computation.1 | async-start | bytes 1769472
  6.5 51.1 %collective-permute-start.6 = (bf16[256,384]{1,0:T(8,128)(2,1)}, bf16[256,384]{1,0:T(8,128)(2,1)S(1)}, u32[]{:S(2)}, u32[]{:S(2)}) collective-permute-start(bf16[256,384]{1,0:T(8,128)(2,1)} %param.10), channel_id=1, source_target_pairs={{32,0},{40,8},{48,16},{56,24},{64,32},{72,40},{80,48},{88,56},{96,... | collective-permute-start | bytes 589832 | tf_op jit(solution)/shard_map/ppermute | solution.py:16
  8.1 47.6 %collective-permute-start.5 = (bf16[256,384]{1,0:T(8,128)(2,1)}, bf16[256,384]{1,0:T(8,128)(2,1)S(1)}, u32[]{:S(2)}, u32[]{:S(2)}) collective-permute-start(bf16[256,384]{1,0:T(8,128)(2,1)} %param.10), channel_id=1, source_target_pairs={{24,0},{32,8},{40,16},{48,24},{56,32},{64,40},{72,48},{80,56},{88,... | collective-permute-start | bytes 589832 | tf_op jit(solution)/shard_map/ppermute | solution.py:16
  9.4 44.9 %collective-permute-start.4 = (bf16[256,384]{1,0:T(8,128)(2,1)}, bf16[256,384]{1,0:T(8,128)(2,1)S(1)}, u32[]{:S(2)}, u32[]{:S(2)}) collective-permute-start(bf16[256,384]{1,0:T(8,128)(2,1)} %param.10), channel_id=1, source_target_pairs={{8,0},{16,8},{24,16},{32,24},{40,32},{48,40},{56,48},{64,56},{72,6... | collective-permute-start | bytes 589832 | tf_op jit(solution)/shard_map/ppermute | solution.py:16
  18.2 28.0 %collective-permute-start.1 = (bf16[256,384]{1,0:T(8,128)(2,1)}, bf16[256,384]{1,0:T(8,128)(2,1)S(1)}, u32[]{:S(2)}, u32[]{:S(2)}) collective-permute-start(bf16[256,384]{1,0:T(8,128)(2,1)} %param.10), channel_id=1, source_target_pairs={{0,32},{8,40},{16,48},{24,56},{32,64},{40,72},{48,80},{56,88},{64,... | collective-permute-start | bytes 589832 | tf_op jit(solution)/shard_map/ppermute | solution.py:16
  24.0 16.4 %collective-permute-start = (bf16[256,384]{1,0:T(8,128)(2,1)}, bf16[256,384]{1,0:T(8,128)(2,1)}, u32[]{:S(2)}, u32[]{:S(2)}) collective-permute-start(bf16[256,384]{1,0:T(8,128)(2,1)} %param.10), channel_id=1, source_target_pairs={{0,40},{8,48},{16,56},{24,64},{32,72},{40,80},{48,88},{56,96},{64,... | collective-permute-start | bytes 589832 | tf_op jit(solution)/shard_map/ppermute | solution.py:16
  30.6 43.3 %copy-start.5 = (bf16[256,384]{1,0:T(8,128)(2,1)S(1)}, bf16[256,384]{1,0:T(8,128)(2,1)}, u32[]{:S(2)}) copy-start(bf16[256,384]{1,0:T(8,128)(2,1)} %param.9) | copy-start | bytes 589828
  40.4 9.9 %collective-permute-start.2 = (bf16[256,384]{1,0:T(8,128)(2,1)}, bf16[256,384]{1,0:T(8,128)(2,1)S(1)}, u32[]{:S(2)}, u32[]{:S(2)}) collective-permute-start(bf16[256,384]{1,0:T(8,128)(2,1)} %param.10), channel_id=1, source_target_pairs={{0,24},{8,32},{16,40},{24,48},{32,56},{40,64},{48,72},{56,80},{64,... | collective-permute-start | bytes 589832 | tf_op jit(solution)/shard_map/ppermute | solution.py:16
  46.2 6.7 %collective-permute-start.3 = (bf16[256,384]{1,0:T(8,128)(2,1)}, bf16[256,384]{1,0:T(8,128)(2,1)S(1)}, u32[]{:S(2)}, u32[]{:S(2)}) collective-permute-start(bf16[256,384]{1,0:T(8,128)(2,1)} %param.10), channel_id=1, source_target_pairs={{0,8},{8,16},{16,24},{24,32},{32,40},{40,48},{48,56},{56,64},{64,7... | collective-permute-start | bytes 589832 | tf_op jit(solution)/shard_map/ppermute | solution.py:16
  50.2 17.6 %collective-permute-start.7 = (bf16[256,384]{1,0:T(8,128)(2,1)}, bf16[256,384]{1,0:T(8,128)(2,1)S(1)}, u32[]{:S(2)}, u32[]{:S(2)}) collective-permute-start(bf16[256,384]{1,0:T(8,128)(2,1)} %param.10), channel_id=1, source_target_pairs={{40,0},{48,8},{56,16},{64,24},{72,32},{80,40},{88,48},{96,56},{104... | collective-permute-start | bytes 589832 | tf_op jit(solution)/shard_map/ppermute | solution.py:16
  52.9 45.5 %collective-permute-start.14 = (bf16[256,384]{1,0:T(8,128)(2,1)}, bf16[256,384]{1,0:T(8,128)(2,1)S(1)}, u32[]{:S(2)}, u32[]{:S(2)}) collective-permute-start(bf16[256,384]{1,0:T(8,128)(2,1)} %param.11), channel_id=1, source_target_pairs={{32,0},{40,8},{48,16},{56,24},{64,32},{72,40},{80,48},{88,56},{96,... | collective-permute-start | bytes 589832 | tf_op jit(solution)/shard_map/ppermute | solution.py:16
  54.3 44.0 %collective-permute-start.13 = (bf16[256,384]{1,0:T(8,128)(2,1)S(1)}, bf16[256,384]{1,0:T(8,128)(2,1)S(1)}, u32[]{:S(2)}, u32[]{:S(2)}) collective-permute-start(bf16[256,384]{1,0:T(8,128)(2,1)S(1)} %copy-done.2), channel_id=1, source_target_pairs={{24,0},{32,8},{40,16},{48,24},{56,32},{64,40},{72,48},{80,56},{88,... | collective-permute-start | bytes 589832 | tf_op jit(solution)/shard_map/ppermute | solution.py:16
  55.7 42.6 %collective-permute-start.12 = (bf16[256,384]{1,0:T(8,128)(2,1)S(1)}, bf16[256,384]{1,0:T(8,128)(2,1)S(1)}, u32[]{:S(2)}, u32[]{:S(2)}) collective-permute-start(bf16[256,384]{1,0:T(8,128)(2,1)S(1)} %copy-done.2), channel_id=1, source_target_pairs={{8,0},{16,8},{24,16},{32,24},{40,32},{48,40},{56,48},{64,56},{72,6... | collective-permute-start | bytes 589832 | tf_op jit(solution)/shard_map/ppermute | solution.py:16
  57.7 34.0 %collective-permute-start.9 = (bf16[256,384]{1,0:T(8,128)(2,1)S(1)}, bf16[256,384]{1,0:T(8,128)(2,1)S(1)}, u32[]{:S(2)}, u32[]{:S(2)}) collective-permute-start(bf16[256,384]{1,0:T(8,128)(2,1)S(1)} %copy-done.2), channel_id=1, source_target_pairs={{0,32},{8,40},{16,48},{24,56},{32,64},{40,72},{48,80},{56,88},{64,... | collective-permute-start | bytes 589832 | tf_op jit(solution)/shard_map/ppermute | solution.py:16
  67.8 14.4 %collective-permute-start.8 = (bf16[256,384]{1,0:T(8,128)(2,1)S(1)}, bf16[256,384]{1,0:T(8,128)(2,1)S(1)}, u32[]{:S(2)}, u32[]{:S(2)}) collective-permute-start(bf16[256,384]{1,0:T(8,128)(2,1)S(1)} %copy-done.2), channel_id=1, source_target_pairs={{0,40},{8,48},{16,56},{24,64},{32,72},{40,80},{48,88},{56,96},{64,... | collective-permute-start | bytes 589832 | tf_op jit(solution)/shard_map/ppermute | solution.py:16
  82.3 13.8 %collective-permute-start.10 = (bf16[256,384]{1,0:T(8,128)(2,1)S(1)}, bf16[256,384]{1,0:T(8,128)(2,1)S(1)}, u32[]{:S(2)}, u32[]{:S(2)}) collective-permute-start(bf16[256,384]{1,0:T(8,128)(2,1)S(1)} %copy-done.2), channel_id=1, source_target_pairs={{0,24},{8,32},{16,40},{24,48},{32,56},{40,64},{48,72},{56,80},{64,... | collective-permute-start | bytes 589832 | tf_op jit(solution)/shard_map/ppermute | solution.py:16
  91.6 6.6 %collective-permute-start.11 = (bf16[256,384]{1,0:T(8,128)(2,1)S(1)}, bf16[256,384]{1,0:T(8,128)(2,1)S(1)}, u32[]{:S(2)}, u32[]{:S(2)}) collective-permute-start(bf16[256,384]{1,0:T(8,128)(2,1)S(1)} %copy-done.2), channel_id=1, source_target_pairs={{0,8},{8,16},{16,24},{24,32},{32,40},{40,48},{48,56},{56,64},{64,7... | collective-permute-start | bytes 589832 | tf_op jit(solution)/shard_map/ppermute | solution.py:16
  96.1 14.6 %collective-permute-start.15 = (bf16[256,384]{1,0:T(8,128)(2,1)S(1)}, bf16[256,384]{1,0:T(8,128)(2,1)S(1)}, u32[]{:S(2)}, u32[]{:S(2)}) collective-permute-start(bf16[256,384]{1,0:T(8,128)(2,1)S(1)} %copy-done.2), channel_id=1, source_target_pairs={{40,0},{48,8},{56,16},{64,24},{72,32},{80,40},{88,48},{96,56},{104... | collective-permute-start | bytes 589832 | tf_op jit(solution)/shard_map/ppermute | solution.py:16
  118.3 69.0 %copy-start.3 = (bf16[256,384]{1,0:T(8,128)(2,1)S(1)}, bf16[256,384]{1,0:T(8,128)(2,1)}, u32[]{:S(2)}) copy-start(bf16[256,384]{1,0:T(8,128)(2,1)} %param.13) | copy-start | bytes 589828
  118.3 69.0 %copy-start.4 = (f32[384]{0:T(512)S(1)}, f32[384]{0:T(512)}, u32[]{:S(2)}) copy-start(f32[384]{0:T(512)} %param.15) | copy-start | bytes 4612
Sparse Core Ops, SparseCore 0:
  118.5 67.6 reduce-scatter.3
where the time goes:
time: 198 us; the launch traced here: 195 us
  waiting for transfers between devices  101 us (51%)
  starting transfers between devices  61.5 us (31%)
  between operations  14.4 us (7%)
  matrix products  6.81 us (3%)
  local copies, waits for them, and re-layouts  6.69 us (3%)
  other arithmetic  4.54 us (2%)
    unnamed x2, waiting for transfers between devices  67.9 us
    ppermute x16, starting transfers between devices, passed_along(): return lax.ppermute(block, axis, route)  61.5 us
    ppermute x16, waiting for transfers between devices, passed_along(): return lax.ppermute(block, axis, route)  33.1 us
    unnamed x30, local copies, waits for them, and re-layouts  5.15 us
  transfers between devices with their start and end apart: 17, of which 9 were waited for; matrix products, arithmetic and copies ran while one was open for 4% of the time, Pallas kernels for 0%

commit v1 on v0

v1 whole, which is shorter than its diff:
```python
import functools

import jax
import jax.numpy as jnp
from jax import lax
from jax.experimental import pallas as pl
from jax.experimental.pallas import tpu as pltpu
from jax.sharding import PartitionSpec as P

HD = 128
HEIGHT_TILES = 4
SIDE = 16
LOG2E = 1.4426950408889634
MASKED = -1e30
MESH_AXES = ("tile", "head")
VMEM = pltpu.VMEM
SMEM = pltpu.SMEM


def params(megabytes):
    return pltpu.CompilerParams(vmem_limit_bytes=megabytes * 1024 * 1024)


def swap_times(block, first_time):
    tiles = lax.axis_size("tile")
    times = tiles // HEIGHT_TILES
    route = []
    for time in range(first_time, times - 1, 2):
        for height in range(HEIGHT_TILES):
            low, high = time * HEIGHT_TILES + height, (time + 1) * HEIGHT_TILES + height
            route += [(low, high), (high, low)]
    return lax.ppermute(block, "tile", route)


def to_height(block, step):
    tiles = lax.axis_size("tile")
    route = [(i, i + step) for i in range(tiles) if 0 <= i % HEIGHT_TILES + step < HEIGHT_TILES]
    return lax.ppermute(block, "tile", route)


def pack_kernel(windows_ref, q_ref, out_ref):
    rows = q_ref.shape[0]
    out_ref[:rows] = q_ref[...]
    extent = windows_ref[0, 0].astype(jnp.float32)
    out_ref[rows:] = jnp.full((SIDE, q_ref.shape[1]), extent, jnp.float32).astype(out_ref.dtype)


def pack_queries(windows, queries):
    rows, width = queries.shape
    return pl.pallas_call(
        pack_kernel,
        out_shape=jax.ShapeDtypeStruct((rows + SIDE, width), queries.dtype),
        in_specs=[pl.BlockSpec(memory_space=SMEM), pl.BlockSpec(memory_space=VMEM)],
        out_specs=pl.BlockSpec(memory_space=VMEM),
        name="pack_queries",
    )(windows, queries)


def column(values, index):
    return values[:, index : index + 1]


def scores_kernel(windows_ref, q_ref, above_ref, below_ref, k0_ref, k1_ref, k2_ref, probs_ref, stats_ref):
    rows = q_ref.shape[0]
    time = lax.axis_index("tile") // HEIGHT_TILES
    times = lax.axis_size("tile") // HEIGHT_TILES
    has_first = jnp.where((time > 0) & (time < times - 1), 0.0, MASKED)
    own = jnp.where(windows_ref[0, 0] >= 1, 0.0, MASKED)
    sides = [own] + [
        jnp.where(jnp.max(ref[rows:].astype(jnp.float32)) > 0.5, 0.0, MASKED) for ref in (above_ref, below_ref)
    ]
    keys = [k0_ref[...], k1_ref[...], k2_ref[...]]
    scale = HD**-0.5 * LOG2E
    lane = lax.broadcasted_iota(jnp.int32, (rows, HD), 1)
    stats = jnp.zeros((rows, HD), jnp.float32)
    for place, ref in enumerate((q_ref, above_ref, below_ref)):
        block = ref[:rows]
        parts = []
        for key, bias in zip(keys, (None, sides[place] + has_first, sides[place])):
            part = lax.dot_general(block, key, (((1,), (1,)), ((), ())), preferred_element_type=jnp.float32) * scale
            parts.append(part if bias is None else part + bias)
        largest = jnp.max(jnp.maximum(jnp.maximum(parts[0], parts[1]), parts[2]), axis=1, keepdims=True)
        weights = [jnp.exp2(part - largest) for part in parts]
        total = jnp.sum(weights[0] + weights[1] + weights[2], axis=1, keepdims=True)
        for index, weight in enumerate(weights):
            probs_ref[place, :, index * rows : (index + 1) * rows] = weight.astype(probs_ref.dtype)
        stats = jnp.where(lane == 2 * place, largest, stats)
        stats = jnp.where(lane == 2 * place + 1, total, stats)
    stats_ref[0] = stats


def scores(windows, queries, above, below, key_rows, keys_first, keys_second):
    rows, width = queries.shape
    heads = width // HD
    own = pl.BlockSpec((rows, HD), lambda head: (0, head))
    sent = pl.BlockSpec((rows + SIDE, HD), lambda head: (0, head))
    return pl.pallas_call(
        scores_kernel,
        grid=(heads,),
        out_shape=(
            jax.ShapeDtypeStruct((3 * heads, rows, 3 * rows), jnp.bfloat16),
            jax.ShapeDtypeStruct((heads, rows, HD), jnp.float32),
        ),
        in_specs=[pl.BlockSpec(memory_space=SMEM), own, sent, sent, own, own, own],
        out_specs=(
            pl.BlockSpec((3, rows, 3 * rows), lambda head: (head, 0, 0)),
            pl.BlockSpec((1, rows, HD), lambda head: (head, 0, 0)),
        ),
        compiler_params=params(24),
        cost_estimate=pl.CostEstimate(flops=2 * 9 * heads * rows * rows * HD, bytes_accessed=6_000_000, transcendentals=9 * heads * rows * rows),
        name="scores",
    )(windows, queries, above, below, key_rows, keys_first, keys_second)


def split_float(value):
    high = value.astype(jnp.bfloat16).astype(jnp.float32)
    rest = value - high
    middle = rest.astype(jnp.bfloat16).astype(jnp.float32)
    return high, middle, (rest - middle).astype(jnp.bfloat16).astype(jnp.float32)


def mix_kernel(probs_ref, stats_ref, v0_ref, v1_ref, v2_ref, own_ref, above_ref, below_ref):
    rows = v0_ref.shape[0]
    stats = stats_ref[0]
    lane = lax.broadcasted_iota(jnp.int32, (rows, HD), 1)
    for place, ref in enumerate((own_ref, above_ref, below_ref)):
        mix = jnp.zeros((rows, HD), jnp.float32)
        for index, value_ref in enumerate((v0_ref, v1_ref, v2_ref)):
            mix += jnp.dot(
                probs_ref[place, :, index * rows : (index + 1) * rows],
                value_ref[...],
                preferred_element_type=jnp.float32,
            )
        if place == 0:
            ref[...] = mix
            continue
        total = column(stats, 2 * place + 1)
        ref[:rows] = (mix / total).astype(ref.dtype)
        side = jnp.zeros((rows, HD), jnp.float32)
        pieces = split_float(column(stats, 2 * place)) + split_float(total)
        for index, piece in enumerate(pieces):
            side = jnp.where(lane == index, piece, side)
        side = jnp.transpose(side)
        ref[rows : rows + 8] = side[:8, :HD].astype(ref.dtype)
        ref[rows + 8 :] = side[:8, HD:].astype(ref.dtype)


def mix(probs, stats, value_rows, values_first, values_second):
    rows, width = value_rows.shape
    heads = width // HD
    own = pl.BlockSpec((rows, HD), lambda head: (0, head))
    sent = pl.BlockSpec((rows + SIDE, HD), lambda head: (0, head))
    return pl.pallas_call(
        mix_kernel,
        grid=(heads,),
        out_shape=(
            jax.ShapeDtypeStruct((rows, width), jnp.float32),
            jax.ShapeDtypeStruct((rows + SIDE, width), jnp.bfloat16),
            jax.ShapeDtypeStruct((rows + SIDE, width), jnp.bfloat16),
        ),
        in_specs=[
            pl.BlockSpec((3, rows, 3 * rows), lambda head: (head, 0, 0)),
            pl.BlockSpec((1, rows, HD), lambda head: (head, 0, 0)),
            own,
            own,
            own,
        ],
        out_specs=(own, sent, sent),
        compiler_params=params(24),
        cost_estimate=pl.CostEstimate(flops=2 * 9 * heads * rows * rows * HD, bytes_accessed=6_000_000, transcendentals=0),
        name="mix",
    )(probs, stats, value_rows, values_first, values_second)


def project_kernel(windows_ref, own_ref, stats_ref, above_ref, below_ref, weight_ref, out_ref, attention_ref):
    rows, width = own_ref.shape

    @pl.when(pl.program_id(0) == 0)
    def merge():
        height = lax.axis_index("tile") % HEIGHT_TILES
        wide = windows_ref[0, 1] >= 1
        valid = (wide & (height > 0), wide & (height < HEIGHT_TILES - 1))
        for head in range(width // HD):
            low = head * HD
            stats = stats_ref[head]
            largest, total = [column(stats, 0)], [column(stats, 1)]
            for ref, flag in zip((above_ref, below_ref), valid):
                side = ref[rows:, low : low + HD].astype(jnp.float32)
                side = jnp.concatenate([jnp.transpose(side[:8]), jnp.transpose(side[8:])], axis=0)
                peak = column(side, 0) + column(side, 1) + column(side, 2)
                count = column(side, 3) + column(side, 4) + column(side, 5)
                largest.append(jnp.where(flag, peak, MASKED))
                total.append(jnp.where(flag, count, 0.0))
            peak = jnp.maximum(jnp.maximum(largest[0], largest[1]), largest[2])
            shrink = jnp.exp2(largest[0] - peak)
            shares = [total[i] * jnp.exp2(largest[i] - peak) for i in (1, 2)]
            merged = own_ref[:, low : low + HD] * shrink
            for share, ref in zip(shares, (above_ref, below_ref)):
                merged += ref[:rows, low : low + HD].astype(jnp.float32) * share
            merged = merged / (total[0] * shrink + shares[0] + shares[1])
            attention_ref[:, low : low + HD] = merged.astype(jnp.bfloat16)

    out_ref[0] = jnp.dot(attention_ref[...], weight_ref[...], preferred_element_type=jnp.float32).astype(out_ref.dtype)


def project(windows, own, stats, above, below, out_weight):
    rows, width = own.shape
    features = out_weight.shape[1]
    groups = features // width
    whole = lambda shape: pl.BlockSpec(shape, lambda group: (0,) * len(shape))
    return pl.pallas_call(
        project_kernel,
        grid=(groups,),
        out_shape=jax.ShapeDtypeStruct((groups, rows, width), jnp.bfloat16),
        in_specs=[
            pl.BlockSpec(memory_space=SMEM),
            whole(own.shape),
            whole(stats.shape),
            whole(above.shape),
            whole(below.shape),
            pl.BlockSpec((width, width), lambda group: (0, group)),
        ],
        out_specs=pl.BlockSpec((1, rows, width), lambda group: (group, 0, 0)),
        scratch_shapes=[pltpu.VMEM((rows, width), jnp.bfloat16)],
        compiler_params=params(24),
        cost_estimate=pl.CostEstimate(flops=2 * rows * width * features, bytes_accessed=5_000_000, transcendentals=0),
        name="project",
    )(windows, own, stats, above, below, out_weight)


def finish_kernel(terms_ref, residual_ref, gate_ref, out_ref):
    total = jnp.sum(terms_ref[...].astype(jnp.float32), axis=0)
    out_ref[...] = (residual_ref[...].astype(jnp.float32) + gate_ref[...] * total).astype(out_ref.dtype)


def finish(terms, residual, gate_scale):
    groups, rows, width = terms.shape
    steps = 2
    part = rows // steps
    return pl.pallas_call(
        finish_kernel,
        grid=(steps,),
        out_shape=jax.ShapeDtypeStruct((rows, width), residual.dtype),
        in_specs=[
            pl.BlockSpec((groups, part, width), lambda step: (0, step, 0)),
            pl.BlockSpec((part, width), lambda step: (step, 0)),
            pl.BlockSpec((1, width), lambda step: (0, 0)),
        ],
        out_specs=pl.BlockSpec((part, width), lambda step: (step, 0)),
        compiler_params=params(24),
        cost_estimate=pl.CostEstimate(flops=10 * groups * rows * width, bytes_accessed=2_000_000, transcendentals=0),
        name="finish",
    )(terms, residual, gate_scale.reshape(1, width))


def shards(queries, key_rows, value_rows, windows, residual, out_weight, gate_scale):
    keys_first, keys_second = swap_times(key_rows, 1), swap_times(key_rows, 0)
    values_first, values_second = swap_times(value_rows, 1), swap_times(value_rows, 0)
    packed = pack_queries(windows, queries)
    from_above, from_below = to_height(packed, 1), to_height(packed, -1)
    probs, stats = scores(windows, queries, from_above, from_below, key_rows, keys_first, keys_second)
    own, for_above, for_below = mix(probs, stats, value_rows, values_first, values_second)
    terms = project(windows, own, stats, to_height(for_below, 1), to_height(for_above, -1), out_weight)
    terms = lax.all_to_all(terms, "head", 0, 0)
    return finish(terms, residual, gate_scale)


def solution(mesh):
    return jax.shard_map(
        shards,
        mesh=mesh,
        in_specs=(
            P("tile", "head"),
            P("tile", "head"),
            P("tile", "head"),
            P("tile", None),
            P("tile", "head"),
            P("head", None),
            P("head"),
        ),
        out_specs=P("tile", "head"),
        check_vma=False,
    )
```

time: 198 us -> 80.9 us (0.41)
  the two profiles are of different devices: /device:TPU:1 before, /device:TPU:385 now
where the time goes in v1:
time: 80.9 us; the launch traced here: 80.5 us
  waiting for transfers between devices  34.8 us (43%)
  starting transfers between devices  28.8 us (36%)
  Pallas kernels  14.3 us (18%)
  local copies, waits for them, and re-layouts  2.53 us (3%)
    all_to_all x1, waiting for transfers between devices, shards(): terms = lax.all_to_all(terms, 'head', 0, 0)  19 us
    ppermute x4, starting transfers between devices, swap_times(): return lax.ppermute(block, 'tile', route)  14.6 us
    ppermute x4, waiting for transfers between devices, swap_times(): return lax.ppermute(block, 'tile', route)  11 us
    ppermute x4, starting transfers between devices, to_height(): return lax.ppermute(block, 'tile', route)  9.39 us
    pallas_call x1, Pallas kernels, project(): pl.pallas_call(project_kernel, grid=(groups,), out_shape=jax.ShapeDtypeSt...  6.73 us
    all_to_all x1, starting transfers between devices, shards(): terms = lax.all_to_all(terms, 'head', 0, 0)  4.82 us
    ppermute x4, waiting for transfers between devices, to_height(): return lax.ppermute(block, 'tile', route)  4.7 us
    pallas_call x1, Pallas kernels, scores(): pl.pallas_call(scores_kernel, grid=(heads,), out_shape=(jax.ShapeDtypeStr...  3.17 us
  transfers between devices with their start and end apart: 9, of which 5 were waited for; matrix products, arithmetic and copies ran while one was open for 0% of the time, Pallas kernels for 6%

profile of v1, /device:TPU:385, one launch (start us, length us, event | category | flops | bytes accessed | tf_op | source)
XLA Modules:
  0.0 80.5 jit_solution(8902553582976657676)
XLA Ops:
  0.0 0.0 copy-start.1
  0.0 6.0 %collective-permute-start.2 = (bf16[256,384]{1,0:T(8,128)(2,1)}, bf16[256,384]{1,0:T(8,128)(2,1)S(1)}, u32[]{:S(2)}, u32[]{:S(2)}) collective-permute-start(bf16[256,384]{1,0:T(8,128)(2,1)} %k0_ref.1), channel_id=1, source_target_pairs={{32,64},{64,32},{40,72},{72,40},{48,80},{80,48},{56,88},{88,56},{9... | collective-permute-start | bytes 589832 | tf_op jit(solution)/shard_map/ppermute | solution.py:32
  6.0 1.6 %pack_queries.1 = bf16[272,384]{1,0:T(8,128)(2,1)} custom-call(s32[1,3]{1,0:T(1,128)} %windows_ref.5, bf16[256,384]{1,0:T(8,128)(2,1)} %q_ref.3), custom_call_target="tpu_custom_call" | custom-call | tf_op jit(solution)/shard_map/pack_queries/pallas_call | solution.py:50
  7.6 3.1 %collective-permute-start = (bf16[272,384]{1,0:T(8,128)(2,1)}, bf16[272,384]{1,0:T(8,128)(2,1)S(1)}, u32[]{:S(2)}, u32[]{:S(2)}) collective-permute-start(bf16[272,384]{1,0:T(8,128)(2,1)} %pack_queries.1), channel_id=1, source_target_pairs={{0,8},{8,16},{16,24},{32,40},{40,48},{48,56},{64,72},{72,80},{80,8... | collective-permute-start | bytes 626696 | tf_op jit(solution)/shard_map/ppermute | solution.py:38
  10.8 1.9 %collective-permute-start.1 = (bf16[272,384]{1,0:T(8,128)(2,1)}, bf16[272,384]{1,0:T(8,128)(2,1)S(1)}, u32[]{:S(2)}, u32[]{:S(2)}) collective-permute-start(bf16[272,384]{1,0:T(8,128)(2,1)} %pack_queries.1), channel_id=1, source_target_pairs={{8,0},{16,8},{24,16},{40,32},{48,40},{56,48},{72,64},{80,72},{88,8... | collective-permute-start | bytes 626696 | tf_op jit(solution)/shard_map/ppermute | solution.py:38
  12.7 3.8 %collective-permute-start.3 = (bf16[256,384]{1,0:T(8,128)(2,1)}, bf16[256,384]{1,0:T(8,128)(2,1)S(1)}, u32[]{:S(2)}, u32[]{:S(2)}) collective-permute-start(bf16[256,384]{1,0:T(8,128)(2,1)} %k0_ref.1), channel_id=1, source_target_pairs={{0,32},{32,0},{8,40},{40,8},{16,48},{48,16},{24,56},{56,24},{64,96... | collective-permute-start | bytes 589832 | tf_op jit(solution)/shard_map/ppermute | solution.py:32
  16.5 2.8 %collective-permute-start.4 = (bf16[256,384]{1,0:T(8,128)(2,1)}, bf16[256,384]{1,0:T(8,128)(2,1)S(1)}, u32[]{:S(2)}, u32[]{:S(2)}) collective-permute-start(bf16[256,384]{1,0:T(8,128)(2,1)} %v0_ref.1), channel_id=1, source_target_pairs={{32,64},{64,32},{40,72},{72,40},{48,80},{80,48},{56,88},{88,56},{9... | collective-permute-start | bytes 589832 | tf_op jit(solution)/shard_map/ppermute | solution.py:32
  19.4 0.0 collective-permute-done.2.k1_ref
  19.4 1.9 %collective-permute-start.5 = (bf16[256,384]{1,0:T(8,128)(2,1)}, bf16[256,384]{1,0:T(8,128)(2,1)S(1)}, u32[]{:S(2)}, u32[]{:S(2)}) collective-permute-start(bf16[256,384]{1,0:T(8,128)(2,1)} %v0_ref.1), channel_id=1, source_target_pairs={{0,32},{32,0},{8,40},{40,8},{16,48},{48,16},{24,56},{56,24},{64,96... | collective-permute-start | bytes 589832 | tf_op jit(solution)/shard_map/ppermute | solution.py:32
  21.3 7.3 %collective-permute-done.3.k2_ref = bf16[256,384]{1,0:T(8,128)(2,1)S(1)} collective-permute-done((bf16[256,384]{1,0:T(8,128)(2,1)}, bf16[256,384]{1,0:T(8,128)(2,1)S(1)}, u32[]{:S(2)}, u32[]{:S(2)}) %collective-permute-start.3) | collective-permute-done | bytes 196640 | tf_op jit(solution)/shard_map/ppermute | solution.py:32
  28.7 0.0 collective-permute-done.above_ref
  28.7 0.0 collective-permute-done.1.below_ref
  28.7 0.9 %copy-done.2 = bf16[256,384]{1,0:T(8,128)(2,1)S(1)} copy-done((bf16[256,384]{1,0:T(8,128)(2,1)S(1)}, bf16[256,384]{1,0:T(8,128)(2,1)}, u32[]{:S(2)}) %copy-start.2) | copy-done | bytes 196632
  29.6 0.7 copy-done.4
  30.3 0.9 %copy-done.5 = bf16[256,384]{1,0:T(8,128)(2,1)S(1)} copy-done((bf16[256,384]{1,0:T(8,128)(2,1)S(1)}, bf16[256,384]{1,0:T(8,128)(2,1)}, u32[]{:S(2)}) %copy-start.5) | copy-done | bytes 196632
  31.2 3.2 %scores.1 = (bf16[9,256,768]{2,1,0:T(8,128)(2,1)S(1)}, f32[3,256,128]{2,1,0:T(8,128)S(1)}) custom-call(s32[1,3]{1,0:T(1,128)S(1)} %copy-done.4, bf16[256,384]{1,0:T(8,128)(2,1)S(1)} %copy-done.2, bf16[272,384]{1,0:T(8,128)(2,1)S(1)} %collective-permute-done.above_ref, bf16[272,384]{1,0:T(8,128)(2,1)S(1)} %collective-permute-done.1.below_ref, ...), custom_call_target="tpu_custom_call" | custom-call | flops 452984832 | bytes 6000000 | tf_op jit(solution)/shard_map/scores/pallas_call | solution.py:97
  34.4 0.0 copy-start
  34.4 3.7 %collective-permute-done.4.v1_ref = bf16[256,384]{1,0:T(8,128)(2,1)S(1)} collective-permute-done((bf16[256,384]{1,0:T(8,128)(2,1)}, bf16[256,384]{1,0:T(8,128)(2,1)S(1)}, u32[]{:S(2)}, u32[]{:S(2)}) %collective-permute-start.4) | collective-permute-done | bytes 196640 | tf_op jit(solution)/shard_map/ppermute | solution.py:32
  38.0 0.0 collective-permute-done.5.v2_ref
  38.0 0.0 copy-done.1
  38.1 1.7 %mix.1 = (f32[256,384]{1,0:T(8,128)S(1)}, bf16[272,384]{1,0:T(8,128)(2,1)S(1)}, bf16[272,384]{1,0:T(8,128)(2,1)S(1)}) custom-call(bf16[9,256,768]{2,1,0:T(8,128)(2,1)S(1)} %get-tuple-element.10.probs_ref, f32[3,256,128]{2,1,0:T(8,128)S(1)} %get-tuple-element.11.stats_ref, bf16[256,384]{1,0:T(8,128)(2,1)S(1)} %copy-done.1, ...), custom_call_target="tpu_custom_call" | custom-call | flops 452984832 | bytes 6000000 | tf_op jit(solution)/shard_map/mix/pallas_call | solution.py:153
  39.7 1.9 %collective-permute-start.6 = (bf16[272,384]{1,0:T(8,128)(2,1)S(1)}, bf16[272,384]{1,0:T(8,128)(2,1)S(1)}, u32[]{:S(2)}, u32[]{:S(2)}) collective-permute-start(bf16[272,384]{1,0:T(8,128)(2,1)S(1)} %get-tuple-element.13), channel_id=1, source_target_pairs={{0,8},{8,16},{16,24},{32,40},{40,48},{48,56},{64,72},{72,80},{80,8... | collective-permute-start | bytes 626696 | tf_op jit(solution)/shard_map/ppermute | solution.py:38
  41.7 2.4 %collective-permute-start.7 = (bf16[272,384]{1,0:T(8,128)(2,1)S(1)}, bf16[272,384]{1,0:T(8,128)(2,1)S(1)}, u32[]{:S(2)}, u32[]{:S(2)}) collective-permute-start(bf16[272,384]{1,0:T(8,128)(2,1)S(1)} %get-tuple-element.14), channel_id=1, source_target_pairs={{8,0},{16,8},{24,16},{40,32},{48,40},{56,48},{72,64},{80,72},{88,8... | collective-permute-start | bytes 626696 | tf_op jit(solution)/shard_map/ppermute | solution.py:38
  44.1 0.3 collective-permute-done.6.above_ref
  44.4 4.4 %collective-permute-done.7.below_ref = bf16[272,384]{1,0:T(8,128)(2,1)S(1)} collective-permute-done((bf16[272,384]{1,0:T(8,128)(2,1)S(1)}, bf16[272,384]{1,0:T(8,128)(2,1)S(1)}, u32[]{:S(2)}, u32[]{:S(2)}) %collective-permute-start.7) | collective-permute-done | bytes 208928 | tf_op jit(solution)/shard_map/ppermute | solution.py:38
  48.8 0.0 copy-done
  48.8 6.7 %project.1 = bf16[8,256,384]{2,1,0:T(8,128)(2,1)} custom-call(s32[1,3]{1,0:T(1,128)S(1)} %copy-done.4, f32[256,384]{1,0:T(8,128)S(1)} %get-tuple-element.12.own_ref, f32[3,256,128]{2,1,0:T(8,128)S(1)} %get-tuple-element.11.stats_ref, bf16[272,384]{1,0:T(8,128)(2,1)S(1)} %collective-permute-done.6.above_ref, ...), custom_call_target="tpu_custom_call" | custom-call | flops 603979776 | bytes 5000000 | tf_op jit(solution)/shard_map/project/pallas_call | solution.py:211
  55.5 4.8 %all-to-all-start = ((bf16[8,256,384]{2,1,0:T(8,128)(2,1)}), bf16[8,256,384]{2,1,0:T(8,128)(2,1)S(1)}, u32[]{:S(2)}, u32[]{:S(2)}) async-start(bf16[8,256,384]{2,1,0:T(8,128)(2,1)} %project.1), calls=%async_computation | async-start | bytes 3145728 | tf_op jit(solution)/shard_map/all_to_all | solution.py:264
  60.3 0.0 copy-done.6
  60.4 19.0 %all-to-all-done.terms_ref = bf16[8,256,384]{2,1,0:T(8,128)(2,1)S(1)} async-done(((bf16[8,256,384]{2,1,0:T(8,128)(2,1)}), bf16[8,256,384]{2,1,0:T(8,128)(2,1)S(1)}, u32[]{:S(2)}, u32[]{:S(2)}) %all-to-all-start) | async-done | bytes 1572896 | tf_op jit(solution)/shard_map/all_to_all | solution.py:264
  79.4 0.0 copy-done.3
  79.4 1.1 %finish.1 = bf16[256,384]{1,0:T(8,128)(2,1)} custom-call(bf16[8,256,384]{2,1,0:T(8,128)(2,1)S(1)} %all-to-all-done.terms_ref, bf16[256,384]{1,0:T(8,128)(2,1)S(1)} %copy-done.3, f32[1,384]{1,0:T(1,128)S(1)} %reshape.3.gate_ref), custom_call_target="tpu_custom_call" | custom-call | flops 7864320 | bytes 2000000 | tf_op jit(solution)/shard_map/finish/pallas_call | solution.py:240
  (6 shorter events, 0.0 us)
Async XLA Ops:
  0.0 38.0 %copy-start.1 = (bf16[256,384]{1,0:T(8,128)(2,1)S(1)}, bf16[256,384]{1,0:T(8,128)(2,1)}, u32[]{:S(2)}) copy-start(bf16[256,384]{1,0:T(8,128)(2,1)} %v0_ref.1) | copy-start | bytes 589828
  0.0 19.4 %collective-permute-start.2 = (bf16[256,384]{1,0:T(8,128)(2,1)}, bf16[256,384]{1,0:T(8,128)(2,1)S(1)}, u32[]{:S(2)}, u32[]{:S(2)}) collective-permute-start(bf16[256,384]{1,0:T(8,128)(2,1)} %k0_ref.1), channel_id=1, source_target_pairs={{32,64},{64,32},{40,72},{72,40},{48,80},{80,48},{56,88},{88,56},{9... | collective-permute-start | bytes 589832 | tf_op jit(solution)/shard_map/ppermute | solution.py:32
  7.6 21.0 %collective-permute-start = (bf16[272,384]{1,0:T(8,128)(2,1)}, bf16[272,384]{1,0:T(8,128)(2,1)S(1)}, u32[]{:S(2)}, u32[]{:S(2)}) collective-permute-start(bf16[272,384]{1,0:T(8,128)(2,1)} %pack_queries.1), channel_id=1, source_target_pairs={{0,8},{8,16},{16,24},{32,40},{40,48},{48,56},{64,72},{72,80},{80,8... | collective-permute-start | bytes 626696 | tf_op jit(solution)/shard_map/ppermute | solution.py:38
  10.8 17.9 %collective-permute-start.1 = (bf16[272,384]{1,0:T(8,128)(2,1)}, bf16[272,384]{1,0:T(8,128)(2,1)S(1)}, u32[]{:S(2)}, u32[]{:S(2)}) collective-permute-start(bf16[272,384]{1,0:T(8,128)(2,1)} %pack_queries.1), channel_id=1, source_target_pairs={{8,0},{16,8},{24,16},{40,32},{48,40},{56,48},{72,64},{80,72},{88,8... | collective-permute-start | bytes 626696 | tf_op jit(solution)/shard_map/ppermute | solution.py:38
  12.7 16.0 %collective-permute-start.3 = (bf16[256,384]{1,0:T(8,128)(2,1)}, bf16[256,384]{1,0:T(8,128)(2,1)S(1)}, u32[]{:S(2)}, u32[]{:S(2)}) collective-permute-start(bf16[256,384]{1,0:T(8,128)(2,1)} %k0_ref.1), channel_id=1, source_target_pairs={{0,32},{32,0},{8,40},{40,8},{16,48},{48,16},{24,56},{56,24},{64,96... | collective-permute-start | bytes 589832 | tf_op jit(solution)/shard_map/ppermute | solution.py:32
  16.5 21.5 %collective-permute-start.4 = (bf16[256,384]{1,0:T(8,128)(2,1)}, bf16[256,384]{1,0:T(8,128)(2,1)S(1)}, u32[]{:S(2)}, u32[]{:S(2)}) collective-permute-start(bf16[256,384]{1,0:T(8,128)(2,1)} %v0_ref.1), channel_id=1, source_target_pairs={{32,64},{64,32},{40,72},{72,40},{48,80},{80,48},{56,88},{88,56},{9... | collective-permute-start | bytes 589832 | tf_op jit(solution)/shard_map/ppermute | solution.py:32
  19.4 18.7 %collective-permute-start.5 = (bf16[256,384]{1,0:T(8,128)(2,1)}, bf16[256,384]{1,0:T(8,128)(2,1)S(1)}, u32[]{:S(2)}, u32[]{:S(2)}) collective-permute-start(bf16[256,384]{1,0:T(8,128)(2,1)} %v0_ref.1), channel_id=1, source_target_pairs={{0,32},{32,0},{8,40},{40,8},{16,48},{48,16},{24,56},{56,24},{64,96... | collective-permute-start | bytes 589832 | tf_op jit(solution)/shard_map/ppermute | solution.py:32
  28.7 0.9 %copy-start.2 = (bf16[256,384]{1,0:T(8,128)(2,1)S(1)}, bf16[256,384]{1,0:T(8,128)(2,1)}, u32[]{:S(2)}) copy-start(bf16[256,384]{1,0:T(8,128)(2,1)} %q_ref.3) | copy-start | bytes 589828
  29.6 0.7 copy-start.4
  30.3 0.9 %copy-start.5 = (bf16[256,384]{1,0:T(8,128)(2,1)S(1)}, bf16[256,384]{1,0:T(8,128)(2,1)}, u32[]{:S(2)}) copy-start(bf16[256,384]{1,0:T(8,128)(2,1)} %k0_ref.1) | copy-start | bytes 589828
  34.4 14.4 %copy-start = (bf16[384,3072]{1,0:T(8,128)(2,1)S(1)}, bf16[384,3072]{1,0:T(8,128)(2,1)}, u32[]{:S(2)}) copy-start(bf16[384,3072]{1,0:T(8,128)(2,1)} %weight_ref.1) | copy-start | bytes 7077892
  39.7 4.7 %collective-permute-start.6 = (bf16[272,384]{1,0:T(8,128)(2,1)S(1)}, bf16[272,384]{1,0:T(8,128)(2,1)S(1)}, u32[]{:S(2)}, u32[]{:S(2)}) collective-permute-start(bf16[272,384]{1,0:T(8,128)(2,1)S(1)} %get-tuple-element.13), channel_id=1, source_target_pairs={{0,8},{8,16},{16,24},{32,40},{40,48},{48,56},{64,72},{72,80},{80,8... | collective-permute-start | bytes 626696 | tf_op jit(solution)/shard_map/ppermute | solution.py:38
  41.7 7.1 %collective-permute-start.7 = (bf16[272,384]{1,0:T(8,128)(2,1)S(1)}, bf16[272,384]{1,0:T(8,128)(2,1)S(1)}, u32[]{:S(2)}, u32[]{:S(2)}) collective-permute-start(bf16[272,384]{1,0:T(8,128)(2,1)S(1)} %get-tuple-element.14), channel_id=1, source_target_pairs={{8,0},{16,8},{24,16},{40,32},{48,40},{56,48},{72,64},{80,72},{88,8... | collective-permute-start | bytes 626696 | tf_op jit(solution)/shard_map/ppermute | solution.py:38
  55.5 4.8 %copy-start.6 = (f32[384]{0:T(512)S(1)}, f32[384]{0:T(512)}, u32[]{:S(2)}) copy-start(f32[384]{0:T(512)} %param.13) | copy-start | bytes 4612
  55.5 23.9 %copy-start.3 = (bf16[256,384]{1,0:T(8,128)(2,1)S(1)}, bf16[256,384]{1,0:T(8,128)(2,1)}, u32[]{:S(2)}) copy-start(bf16[256,384]{1,0:T(8,128)(2,1)} %residual_ref.1) | copy-start | bytes 589828
  55.5 23.9 %all-to-all-start = ((bf16[8,256,384]{2,1,0:T(8,128)(2,1)}), bf16[8,256,384]{2,1,0:T(8,128)(2,1)S(1)}, u32[]{:S(2)}, u32[]{:S(2)}) async-start(bf16[8,256,384]{2,1,0:T(8,128)(2,1)} %project.1), calls=%async_computation | async-start | bytes 3145728 | tf_op jit(solution)/shard_map/all_to_all | solution.py:264

commit v2 on v1

v2 whole, which is shorter than its diff:
```python
import functools

import jax
import jax.numpy as jnp
from jax import lax
from jax.experimental import pallas as pl
from jax.experimental.pallas import tpu as pltpu
from jax.sharding import PartitionSpec as P

HD = 128
HEIGHT_TILES = 4
SIDE = 16
LOG2E = 1.4426950408889634
MASKED = -1e30
MESH_AXES = ("tile", "head")
VMEM = pltpu.VMEM
SMEM = pltpu.SMEM


def params(megabytes):
    return pltpu.CompilerParams(vmem_limit_bytes=megabytes * 1024 * 1024)


def places():
    tiles = lax.axis_size("tile")
    return [(tile, *divmod(tile, HEIGHT_TILES), tiles // HEIGHT_TILES) for tile in range(tiles)]


def time_partner(time, height, later):
    odd = (height < HEIGHT_TILES // 2) != later
    return time + 1 if time % 2 == int(odd) else time - 1


def swap_times(block, later):
    route = []
    for tile, time, height, times in places():
        partner = time_partner(time, height, later)
        if 0 <= partner < times:
            route.append((tile, partner * HEIGHT_TILES + height))
    return lax.ppermute(block, "tile", route)


def swap_pair(block):
    return lax.ppermute(block, "tile", [(tile, tile ^ 1) for tile, *_ in places()])


def swap_middle(block):
    route = [(tile, tile + (1 if height == 1 else -1)) for tile, _, height, _ in places() if height in (1, 2)]
    return lax.ppermute(block, "tile", route)


def pack_kernel(windows_ref, q_ref, k_ref, packed_ref, key_ref):
    rows = q_ref.shape[0]
    packed_ref[:rows] = q_ref[...]
    extent = windows_ref[0, 0].astype(jnp.float32)
    packed_ref[rows:] = jnp.full((SIDE, q_ref.shape[1]), extent, jnp.float32).astype(packed_ref.dtype)
    key_ref[...] = k_ref[...]


def pack_queries(windows, queries, key_rows):
    rows, width = queries.shape
    whole = pl.BlockSpec(memory_space=VMEM)
    return pl.pallas_call(
        pack_kernel,
        out_shape=(
            jax.ShapeDtypeStruct((rows + SIDE, width), queries.dtype),
            jax.ShapeDtypeStruct((rows, width), queries.dtype),
        ),
        in_specs=[pl.BlockSpec(memory_space=SMEM), whole, whole],
        out_specs=(whole, whole),
        name="pack_queries",
    )(windows, queries, key_rows)


def column(values, index):
    return values[:, index : index + 1]


def scores_kernel(q_ref, pair_ref, middle_ref, k0_ref, k1_ref, k2_ref, probs_ref, stats_ref):
    rows = k0_ref.shape[0]
    tile = lax.axis_index("tile")
    time, height = tile // HEIGHT_TILES, tile % HEIGHT_TILES
    times = lax.axis_size("tile") // HEIGHT_TILES
    inner = (time > 0) & (time < times - 1)
    lower = height < HEIGHT_TILES // 2
    keys = [k0_ref[...], k1_ref[...], k2_ref[...]]
    scale = HD**-0.5 * LOG2E
    lane = lax.broadcasted_iota(jnp.int32, (rows, HD), 1)
    stats = jnp.zeros((rows, HD), jnp.float32)
    for place, ref in enumerate((q_ref, pair_ref, middle_ref)):
        wide = jnp.max(ref[rows:].astype(jnp.float32)) > 0.5
        biases = (0.0, jnp.where(wide & (inner | ~lower), 0.0, MASKED), jnp.where(wide & (inner | lower), 0.0, MASKED))
        block = ref[:rows]
        parts = [
            lax.dot_general(block, key, (((1,), (1,)), ((), ())), preferred_element_type=jnp.float32) for key in keys
        ]
        peaks = [jnp.max(part, axis=1, keepdims=True) * scale + bias for part, bias in zip(parts, biases)]
        largest = jnp.maximum(jnp.maximum(peaks[0], peaks[1]), peaks[2])
        weights = [jnp.exp2(part * scale + (bias - largest)) for part, bias in zip(parts, biases)]
        total = jnp.sum(weights[0] + weights[1] + weights[2], axis=1, keepdims=True)
        for index, weight in enumerate(weights):
            probs_ref[place, :, index * rows : (index + 1) * rows] = weight.astype(probs_ref.dtype)
        stats = jnp.where(lane == 2 * place, largest, stats)
        stats = jnp.where(lane == 2 * place + 1, total, stats)
    stats_ref[0] = stats


def scores(queries, from_pair, from_middle, key_rows, keys_first, keys_second):
    rows, width = key_rows.shape
    heads = width // HD
    own = pl.BlockSpec((rows, HD), lambda head: (0, head))
    sent = pl.BlockSpec((rows + SIDE, HD), lambda head: (0, head))
    return pl.pallas_call(
        scores_kernel,
        grid=(heads,),
        out_shape=(
            jax.ShapeDtypeStruct((3 * heads, rows, 3 * rows), jnp.bfloat16),
            jax.ShapeDtypeStruct((heads, rows, HD), jnp.float32),
        ),
        in_specs=[sent, sent, sent, own, own, own],
        out_specs=(
            pl.BlockSpec((3, rows, 3 * rows), lambda head: (head, 0, 0)),
            pl.BlockSpec((1, rows, HD), lambda head: (head, 0, 0)),
        ),
        compiler_params=params(24),
        cost_estimate=pl.CostEstimate(flops=2 * 9 * heads * rows * rows * HD, bytes_accessed=6_000_000, transcendentals=9 * heads * rows * rows),
        name="scores",
    )(queries, from_pair, from_middle, key_rows, keys_first, keys_second)


def split_float(value):
    high = value.astype(jnp.bfloat16).astype(jnp.float32)
    rest = value - high
    middle = rest.astype(jnp.bfloat16).astype(jnp.float32)
    return high, middle, (rest - middle).astype(jnp.bfloat16).astype(jnp.float32)


def mix_kernel(probs_ref, stats_ref, v0_ref, v1_ref, v2_ref, own_ref, own_stats_ref, pair_ref, middle_ref):
    rows = v0_ref.shape[0]
    stats = jnp.transpose(stats_ref[0])[:8]
    own_stats_ref[0] = stats
    line = lax.broadcasted_iota(jnp.int32, (8, rows), 0)
    for place, ref in enumerate((own_ref, pair_ref, middle_ref)):
        mix = jnp.zeros((rows, HD), jnp.float32)
        for index, value_ref in enumerate((v0_ref, v1_ref, v2_ref)):
            mix += jnp.dot(
                probs_ref[place, :, index * rows : (index + 1) * rows],
                value_ref[...],
                preferred_element_type=jnp.float32,
            )
        if place == 0:
            ref[...] = mix
            continue
        ref[:rows] = mix.astype(ref.dtype)
        side = jnp.zeros((8, rows), jnp.float32)
        pieces = split_float(stats[2 * place : 2 * place + 1]) + split_float(stats[2 * place + 1 : 2 * place + 2])
        for index, piece in enumerate(pieces):
            side = jnp.where(line == index, piece, side)
        ref[rows:] = jnp.concatenate([side[:, :HD], side[:, HD:]], axis=0).astype(ref.dtype)


def mix(probs, stats, value_rows, values_first, values_second):
    rows, width = value_rows.shape
    heads = width // HD
    own = pl.BlockSpec((rows, HD), lambda head: (0, head))
    sent = pl.BlockSpec((rows + SIDE, HD), lambda head: (0, head))
    return pl.pallas_call(
        mix_kernel,
        grid=(heads,),
        out_shape=(
            jax.ShapeDtypeStruct((rows, width), jnp.float32),
            jax.ShapeDtypeStruct((heads, 8, rows), jnp.float32),
            jax.ShapeDtypeStruct((rows + SIDE, width), jnp.bfloat16),
            jax.ShapeDtypeStruct((rows + SIDE, width), jnp.bfloat16),
        ),
        in_specs=[
            pl.BlockSpec((3, rows, 3 * rows), lambda head: (head, 0, 0)),
            pl.BlockSpec((1, rows, HD), lambda head: (head, 0, 0)),
            own,
            own,
            own,
        ],
        out_specs=(own, pl.BlockSpec((1, 8, rows), lambda head: (head, 0, 0)), sent, sent),
        compiler_params=params(24),
        cost_estimate=pl.CostEstimate(flops=2 * 9 * heads * rows * rows * HD, bytes_accessed=6_000_000, transcendentals=0),
        name="mix",
    )(probs, stats, value_rows, values_first, values_second)


def merge_shares(windows_ref, stats_ref, pair_ref, middle_ref, rows, heads):
    height = lax.axis_index("tile") % HEIGHT_TILES
    wide = windows_ref[0, 1] >= 1
    valid = (wide, wide & (height > 0) & (height < HEIGHT_TILES - 1))
    line = lax.broadcasted_iota(jnp.int32, (16, rows), 0)
    shares = jnp.zeros((16, rows), jnp.float32)
    for head in range(heads):
        low = head * HD
        stats = stats_ref[head]
        largest, total = [stats[0:1]], [stats[1:2]]
        for ref, flag in zip((pair_ref, middle_ref), valid):
            side = ref[rows:, low : low + HD].astype(jnp.float32)
            side = jnp.concatenate([side[:8], side[8:]], axis=1)
            largest.append(jnp.where(flag, side[0:1] + side[1:2] + side[2:3], MASKED))
            total.append(jnp.where(flag, side[3:4] + side[4:5] + side[5:6], 0.0))
        peak = jnp.maximum(jnp.maximum(largest[0], largest[1]), largest[2])
        factors = [jnp.exp2(value - peak) for value in largest]
        whole = total[0] * factors[0] + total[1] * factors[1] + total[2] * factors[2]
        for index, factor in enumerate(factors):
            shares = jnp.where(line == 3 * head + index, factor / whole, shares)
    return jnp.transpose(shares)


def project_kernel(windows_ref, own_ref, stats_ref, pair_ref, middle_ref, weight_ref, out_ref):
    rows, width = own_ref.shape
    heads = width // HD
    shares = merge_shares(windows_ref, stats_ref, pair_ref, middle_ref, rows, heads)
    merged = []
    for head in range(heads):
        low = head * HD
        value = own_ref[:, low : low + HD] * column(shares, 3 * head)
        for index, ref in enumerate((pair_ref, middle_ref)):
            value += ref[:rows, low : low + HD].astype(jnp.float32) * column(shares, 3 * head + 1 + index)
        merged.append(value.astype(jnp.bfloat16))
    attention = jnp.concatenate(merged, axis=1)
    for group in range(out_ref.shape[0]):
        out_ref[group] = jnp.dot(
            attention, weight_ref[:, group * width : (group + 1) * width], preferred_element_type=jnp.float32
        ).astype(out_ref.dtype)


def project(windows, own, stats, pair, middle, out_weight):
    rows, width = own.shape
    features = out_weight.shape[1]
    whole = pl.BlockSpec(memory_space=VMEM)
    return pl.pallas_call(
        project_kernel,
        out_shape=jax.ShapeDtypeStruct((features // width, rows, width), jnp.bfloat16),
        in_specs=[pl.BlockSpec(memory_space=SMEM)] + [whole] * 5,
        out_specs=whole,
        compiler_params=params(24),
        cost_estimate=pl.CostEstimate(flops=2 * rows * width * features, bytes_accessed=5_000_000, transcendentals=0),
        name="project",
    )(windows, own, stats, pair, middle, out_weight)


def finish_kernel(terms_ref, residual_ref, gate_ref, out_ref):
    total = jnp.sum(terms_ref[...].astype(jnp.float32), axis=0)
    out_ref[...] = (residual_ref[...].astype(jnp.float32) + gate_ref[...] * total).astype(out_ref.dtype)


def finish(terms, residual, gate_scale):
    groups, rows, width = terms.shape
    steps = 2
    part = rows // steps
    return pl.pallas_call(
        finish_kernel,
        grid=(steps,),
        out_shape=jax.ShapeDtypeStruct((rows, width), residual.dtype),
        in_specs=[
            pl.BlockSpec((groups, part, width), lambda step: (0, step, 0)),
            pl.BlockSpec((part, width), lambda step: (step, 0)),
            pl.BlockSpec((1, width), lambda step: (0, 0)),
        ],
        out_specs=pl.BlockSpec((part, width), lambda step: (step, 0)),
        compiler_params=params(24),
        cost_estimate=pl.CostEstimate(flops=10 * groups * rows * width, bytes_accessed=2_000_000, transcendentals=0),
        name="finish",
    )(terms, residual, gate_scale.reshape(1, width))


def shards(queries, key_rows, value_rows, windows, residual, out_weight, gate_scale):
    keys_first, keys_second = swap_times(key_rows, False), swap_times(key_rows, True)
    values_first, values_second = swap_times(value_rows, False), swap_times(value_rows, True)
    packed, keys = pack_queries(windows, queries, key_rows)
    probs, stats = scores(packed, swap_pair(packed), swap_middle(packed), keys, keys_first, keys_second)
    own, stats, for_pair, for_middle = mix(probs, stats, value_rows, values_first, values_second)
    terms = project(windows, own, stats, swap_pair(for_pair), swap_middle(for_middle), out_weight)
    terms = lax.all_to_all(terms, "head", 0, 0)
    return finish(terms, residual, gate_scale)


def solution(mesh):
    return jax.shard_map(
        shards,
        mesh=mesh,
        in_specs=(
            P("tile", "head"),
            P("tile", "head"),
            P("tile", "head"),
            P("tile", None),
            P("tile", "head"),
            P("head", None),
            P("head"),
        ),
        out_specs=P("tile", "head"),
        check_vma=False,
    )
```

time: 80.9 us -> 76.5 us (0.946)
  the two profiles are of different devices: /device:TPU:385 before, /device:TPU:184 now
where the time goes in v2:
time: 76.5 us; the launch traced here: 76.1 us
  starting transfers between devices  35.8 us (47%)
  waiting for transfers between devices  27.3 us (36%)
  Pallas kernels  11 us (14%)
  local copies, waits for them, and re-layouts  1.88 us (2%)
    ppermute x4, starting transfers between devices, swap_times(): return lax.ppermute(block, 'tile', route)  17.1 us
    all_to_all x1, waiting for transfers between devices, shards(): terms = lax.all_to_all(terms, 'head', 0, 0)  16 us
    ppermute x2, starting transfers between devices, swap_middle(): return lax.ppermute(block, 'tile', route)  7.85 us
    all_to_all x1, starting transfers between devices, shards(): terms = lax.all_to_all(terms, 'head', 0, 0)  7.04 us
    ppermute x4, waiting for transfers between devices, swap_times(): return lax.ppermute(block, 'tile', route)  6.07 us
    ppermute x2, waiting for transfers between devices, swap_middle(): return lax.ppermute(block, 'tile', route)  5.18 us
    ppermute x2, starting transfers between devices, swap_pair(): lax.ppermute(block, 'tile', [(tile, tile ^ 1) for tile, *_ in places()])  3.83 us
    pallas_call x1, Pallas kernels, project(): pl.pallas_call(project_kernel, out_shape=jax.ShapeDtypeStruct((features /...  3.45 us
  transfers between devices with their start and end apart: 9, of which 4 were waited for; matrix products, arithmetic and copies ran while one was open for 0% of the time, Pallas kernels for 6%

profile of v2, /device:TPU:184, one launch (start us, length us, event | category | flops | bytes accessed | tf_op | source)
XLA Modules:
  0.0 76.1 jit_solution(6160626274234825624)
XLA Ops:
  0.0 4.2 %collective-permute-start.2 = (bf16[256,384]{1,0:T(8,128)(2,1)}, bf16[256,384]{1,0:T(8,128)(2,1)S(1)}, u32[]{:S(2)}, u32[]{:S(2)}) collective-permute-start(bf16[256,384]{1,0:T(8,128)(2,1)} %k_ref.1), channel_id=1, source_target_pairs={{16,48},{24,56},{32,64},{40,72},{48,16},{56,24},{64,32},{72,40},{8... | collective-permute-start | bytes 589832 | tf_op jit(solution)/shard_map/ppermute | solution.py:40
  4.2 1.8 %pack_queries.1 = (bf16[272,384]{1,0:T(8,128)(2,1)}, bf16[256,384]{1,0:T(8,128)(2,1)}) custom-call(s32[1,3]{1,0:T(1,128)} %windows_ref.3, bf16[256,384]{1,0:T(8,128)(2,1)} %q_ref.1, bf16[256,384]{1,0:T(8,128)(2,1)} %k_ref.1), custom_call_target="tpu_custom_call" | custom-call | tf_op jit(solution)/shard_map/pack_queries/pallas_call | solution.py:63
  6.0 1.9 %collective-permute-start = (bf16[272,384]{1,0:T(8,128)(2,1)}, bf16[272,384]{1,0:T(8,128)(2,1)S(1)}, u32[]{:S(2)}, u32[]{:S(2)}) collective-permute-start(bf16[272,384]{1,0:T(8,128)(2,1)} %get-tuple-element.13.q_ref), channel_id=1, source_target_pairs={{0,8},{8,0},{16,24},{24,16},{32,40},{40,32},{48,56},{56,48},{64,72... | collective-permute-start | bytes 626696 | tf_op jit(solution)/shard_map/ppermute | solution.py:44
  7.9 5.9 %collective-permute-start.1 = (bf16[272,384]{1,0:T(8,128)(2,1)}, bf16[272,384]{1,0:T(8,128)(2,1)S(1)}, u32[]{:S(2)}, u32[]{:S(2)}) collective-permute-start(bf16[272,384]{1,0:T(8,128)(2,1)} %get-tuple-element.13.q_ref), channel_id=1, source_target_pairs={{8,16},{16,8},{40,48},{48,40},{72,80},{80,72},{104,112},{112,104},... | collective-permute-start | bytes 626696 | tf_op jit(solution)/shard_map/ppermute | solution.py:49
  13.8 4.3 %collective-permute-start.3 = (bf16[256,384]{1,0:T(8,128)(2,1)}, bf16[256,384]{1,0:T(8,128)(2,1)S(1)}, u32[]{:S(2)}, u32[]{:S(2)}) collective-permute-start(bf16[256,384]{1,0:T(8,128)(2,1)} %k_ref.1), channel_id=1, source_target_pairs={{0,32},{8,40},{32,0},{40,8},{48,80},{56,88},{64,96},{72,104},{80,4... | collective-permute-start | bytes 589832 | tf_op jit(solution)/shard_map/ppermute | solution.py:40
  18.2 1.9 %collective-permute-start.4 = (bf16[256,384]{1,0:T(8,128)(2,1)}, bf16[256,384]{1,0:T(8,128)(2,1)S(1)}, u32[]{:S(2)}, u32[]{:S(2)}) collective-permute-start(bf16[256,384]{1,0:T(8,128)(2,1)} %v0_ref.1), channel_id=1, source_target_pairs={{16,48},{24,56},{32,64},{40,72},{48,16},{56,24},{64,32},{72,40},{8... | collective-permute-start | bytes 589832 | tf_op jit(solution)/shard_map/ppermute | solution.py:40
  20.1 0.0 collective-permute-done.2.k1_ref
  20.1 6.6 %collective-permute-start.5 = (bf16[256,384]{1,0:T(8,128)(2,1)}, bf16[256,384]{1,0:T(8,128)(2,1)S(1)}, u32[]{:S(2)}, u32[]{:S(2)}) collective-permute-start(bf16[256,384]{1,0:T(8,128)(2,1)} %v0_ref.1), channel_id=1, source_target_pairs={{0,32},{8,40},{32,0},{40,8},{48,80},{56,88},{64,96},{72,104},{80,4... | collective-permute-start | bytes 589832 | tf_op jit(solution)/shard_map/ppermute | solution.py:40
  26.8 4.6 %collective-permute-done.3.k2_ref = bf16[256,384]{1,0:T(8,128)(2,1)S(1)} collective-permute-done((bf16[256,384]{1,0:T(8,128)(2,1)}, bf16[256,384]{1,0:T(8,128)(2,1)S(1)}, u32[]{:S(2)}, u32[]{:S(2)}) %collective-permute-start.3) | collective-permute-done | bytes 196640 | tf_op jit(solution)/shard_map/ppermute | solution.py:40
  31.3 0.0 collective-permute-done.pair_ref
  31.3 0.0 collective-permute-done.1.middle_ref
  31.4 0.9 %copy-done.4 = bf16[272,384]{1,0:T(8,128)(2,1)S(1)} copy-done((bf16[272,384]{1,0:T(8,128)(2,1)S(1)}, bf16[272,384]{1,0:T(8,128)(2,1)}, u32[]{:S(2)}) %copy-start.4) | copy-done | bytes 208920
  32.3 0.9 %copy-done.5 = bf16[256,384]{1,0:T(8,128)(2,1)S(1)} copy-done((bf16[256,384]{1,0:T(8,128)(2,1)S(1)}, bf16[256,384]{1,0:T(8,128)(2,1)}, u32[]{:S(2)}) %copy-start.5) | copy-done | bytes 196632
  33.2 3.1 %scores.1 = (bf16[9,256,768]{2,1,0:T(8,128)(2,1)S(1)}, f32[3,256,128]{2,1,0:T(8,128)S(1)}) custom-call(bf16[272,384]{1,0:T(8,128)(2,1)S(1)} %copy-done.4, bf16[272,384]{1,0:T(8,128)(2,1)S(1)} %collective-permute-done.pair_ref, bf16[272,384]{1,0:T(8,128)(2,1)S(1)} %collective-permute-done.1.middle_ref, bf16[256,384]{1,0:T(8,128)(2,1)S(1)} %copy-done.5, ...), custom_call_target="tpu_custom_call" | custom-call | flops 452984832 | bytes 6000000 | tf_op jit(solution)/shard_map/scores/pallas_call | solution.py:113
  36.3 0.0 copy-start
  36.3 0.0 copy-start.3
  36.3 0.0 collective-permute-done.4.v1_ref
  36.3 1.5 %collective-permute-done.5.v2_ref = bf16[256,384]{1,0:T(8,128)(2,1)S(1)} collective-permute-done((bf16[256,384]{1,0:T(8,128)(2,1)}, bf16[256,384]{1,0:T(8,128)(2,1)S(1)}, u32[]{:S(2)}, u32[]{:S(2)}) %collective-permute-start.5) | collective-permute-done | bytes 196640 | tf_op jit(solution)/shard_map/ppermute | solution.py:40
  37.8 0.0 copy-done.1
  37.8 1.6 %mix.1 = (f32[256,384]{1,0:T(8,128)S(1)}, f32[3,8,256]{2,1,0:T(8,128)S(1)}, bf16[272,384]{1,0:T(8,128)(2,1)S(1)}, bf16[272,384]{1,0:T(8,128)(2,1)S(1)}) custom-call(bf16[9,256,768]{2,1,0:T(8,128)(2,1)S(1)} %get-tuple-element.15.probs_ref, f32[3,256,128]{2,1,0:T(8,128)S(1)} %get-tuple-element.16.stats_ref, bf16[256,384]{1,0:T(8,128)(2,1)S(1)} %copy-done.1, ...), custom_call_target="tpu_custom_call" | custom-call | flops 452984832 | bytes 6000000 | tf_op jit(solution)/shard_map/mix/pallas_call | solution.py:167
  39.4 1.9 %collective-permute-start.6 = (bf16[272,384]{1,0:T(8,128)(2,1)S(1)}, bf16[272,384]{1,0:T(8,128)(2,1)S(1)}, u32[]{:S(2)}, u32[]{:S(2)}) collective-permute-start(bf16[272,384]{1,0:T(8,128)(2,1)S(1)} %get-tuple-element.19), channel_id=1, source_target_pairs={{0,8},{8,0},{16,24},{24,16},{32,40},{40,32},{48,56},{56,48},{64,72... | collective-permute-start | bytes 626696 | tf_op jit(solution)/shard_map/ppermute | solution.py:44
  41.4 1.9 %collective-permute-start.7 = (bf16[272,384]{1,0:T(8,128)(2,1)S(1)}, bf16[272,384]{1,0:T(8,128)(2,1)S(1)}, u32[]{:S(2)}, u32[]{:S(2)}) collective-permute-start(bf16[272,384]{1,0:T(8,128)(2,1)S(1)} %get-tuple-element.20), channel_id=1, source_target_pairs={{8,16},{16,8},{40,48},{48,40},{72,80},{80,72},{104,112},{112,104},... | collective-permute-start | bytes 626696 | tf_op jit(solution)/shard_map/ppermute | solution.py:49
  43.3 0.0 collective-permute-done.6.pair_ref
  43.3 5.2 %collective-permute-done.7.middle_ref = bf16[272,384]{1,0:T(8,128)(2,1)S(1)} collective-permute-done((bf16[272,384]{1,0:T(8,128)(2,1)S(1)}, bf16[272,384]{1,0:T(8,128)(2,1)S(1)}, u32[]{:S(2)}, u32[]{:S(2)}) %collective-permute-start.7) | collective-permute-done | bytes 208928 | tf_op jit(solution)/shard_map/ppermute | solution.py:49
  48.5 0.0 copy-done
  48.5 0.0 copy-done.3
  48.5 3.4 %project.1 = bf16[8,256,384]{2,1,0:T(8,128)(2,1)} custom-call(s32[1,3]{1,0:T(1,128)S(1)} %copy-done.3, f32[256,384]{1,0:T(8,128)S(1)} %get-tuple-element.17.own_ref, f32[3,8,256]{2,1,0:T(8,128)S(1)} %get-tuple-element.18.stats_ref, bf16[272,384]{1,0:T(8,128)(2,1)S(1)} %collective-permute-done.6.pair_ref, ...), custom_call_target="tpu_custom_call" | custom-call | flops 603979776 | bytes 5000000 | tf_op jit(solution)/shard_map/project/pallas_call | solution.py:235
  52.0 7.0 %all-to-all-start = ((bf16[8,256,384]{2,1,0:T(8,128)(2,1)}), bf16[8,256,384]{2,1,0:T(8,128)(2,1)S(1)}, u32[]{:S(2)}, u32[]{:S(2)}) async-start(bf16[8,256,384]{2,1,0:T(8,128)(2,1)} %project.1), calls=%async_computation | async-start | bytes 3145728 | tf_op jit(solution)/shard_map/all_to_all | solution.py:278
  59.0 0.0 copy-done.6
  59.0 16.0 %all-to-all-done.terms_ref = bf16[8,256,384]{2,1,0:T(8,128)(2,1)S(1)} async-done(((bf16[8,256,384]{2,1,0:T(8,128)(2,1)}), bf16[8,256,384]{2,1,0:T(8,128)(2,1)S(1)}, u32[]{:S(2)}, u32[]{:S(2)}) %all-to-all-start) | async-done | bytes 1572896 | tf_op jit(solution)/shard_map/all_to_all | solution.py:278
  75.0 0.0 copy-done.2
  75.0 1.1 %finish.1 = bf16[256,384]{1,0:T(8,128)(2,1)} custom-call(bf16[8,256,384]{2,1,0:T(8,128)(2,1)S(1)} %all-to-all-done.terms_ref, bf16[256,384]{1,0:T(8,128)(2,1)S(1)} %copy-done.2, f32[1,384]{1,0:T(1,128)S(1)} %reshape.3.gate_ref), custom_call_target="tpu_custom_call" | custom-call | flops 7864320 | bytes 2000000 | tf_op jit(solution)/shard_map/finish/pallas_call | solution.py:255
  (6 shorter events, 0.0 us)
Async XLA Ops:
  0.0 37.8 %copy-start.1 = (bf16[256,384]{1,0:T(8,128)(2,1)S(1)}, bf16[256,384]{1,0:T(8,128)(2,1)}, u32[]{:S(2)}) copy-start(bf16[256,384]{1,0:T(8,128)(2,1)} %v0_ref.1) | copy-start | bytes 589828
  0.0 20.1 %collective-permute-start.2 = (bf16[256,384]{1,0:T(8,128)(2,1)}, bf16[256,384]{1,0:T(8,128)(2,1)S(1)}, u32[]{:S(2)}, u32[]{:S(2)}) collective-permute-start(bf16[256,384]{1,0:T(8,128)(2,1)} %k_ref.1), channel_id=1, source_target_pairs={{16,48},{24,56},{32,64},{40,72},{48,16},{56,24},{64,32},{72,40},{8... | collective-permute-start | bytes 589832 | tf_op jit(solution)/shard_map/ppermute | solution.py:40
  6.0 25.4 %collective-permute-start = (bf16[272,384]{1,0:T(8,128)(2,1)}, bf16[272,384]{1,0:T(8,128)(2,1)S(1)}, u32[]{:S(2)}, u32[]{:S(2)}) collective-permute-start(bf16[272,384]{1,0:T(8,128)(2,1)} %get-tuple-element.13.q_ref), channel_id=1, source_target_pairs={{0,8},{8,0},{16,24},{24,16},{32,40},{40,32},{48,56},{56,48},{64,72... | collective-permute-start | bytes 626696 | tf_op jit(solution)/shard_map/ppermute | solution.py:44
  7.9 23.5 %collective-permute-start.1 = (bf16[272,384]{1,0:T(8,128)(2,1)}, bf16[272,384]{1,0:T(8,128)(2,1)S(1)}, u32[]{:S(2)}, u32[]{:S(2)}) collective-permute-start(bf16[272,384]{1,0:T(8,128)(2,1)} %get-tuple-element.13.q_ref), channel_id=1, source_target_pairs={{8,16},{16,8},{40,48},{48,40},{72,80},{80,72},{104,112},{112,104},... | collective-permute-start | bytes 626696 | tf_op jit(solution)/shard_map/ppermute | solution.py:49
  13.8 17.5 %collective-permute-start.3 = (bf16[256,384]{1,0:T(8,128)(2,1)}, bf16[256,384]{1,0:T(8,128)(2,1)S(1)}, u32[]{:S(2)}, u32[]{:S(2)}) collective-permute-start(bf16[256,384]{1,0:T(8,128)(2,1)} %k_ref.1), channel_id=1, source_target_pairs={{0,32},{8,40},{32,0},{40,8},{48,80},{56,88},{64,96},{72,104},{80,4... | collective-permute-start | bytes 589832 | tf_op jit(solution)/shard_map/ppermute | solution.py:40
  18.2 18.1 %collective-permute-start.4 = (bf16[256,384]{1,0:T(8,128)(2,1)}, bf16[256,384]{1,0:T(8,128)(2,1)S(1)}, u32[]{:S(2)}, u32[]{:S(2)}) collective-permute-start(bf16[256,384]{1,0:T(8,128)(2,1)} %v0_ref.1), channel_id=1, source_target_pairs={{16,48},{24,56},{32,64},{40,72},{48,16},{56,24},{64,32},{72,40},{8... | collective-permute-start | bytes 589832 | tf_op jit(solution)/shard_map/ppermute | solution.py:40
  20.1 17.7 %collective-permute-start.5 = (bf16[256,384]{1,0:T(8,128)(2,1)}, bf16[256,384]{1,0:T(8,128)(2,1)S(1)}, u32[]{:S(2)}, u32[]{:S(2)}) collective-permute-start(bf16[256,384]{1,0:T(8,128)(2,1)} %v0_ref.1), channel_id=1, source_target_pairs={{0,32},{8,40},{32,0},{40,8},{48,80},{56,88},{64,96},{72,104},{80,4... | collective-permute-start | bytes 589832 | tf_op jit(solution)/shard_map/ppermute | solution.py:40
  31.3 0.9 %copy-start.4 = (bf16[272,384]{1,0:T(8,128)(2,1)S(1)}, bf16[272,384]{1,0:T(8,128)(2,1)}, u32[]{:S(2)}) copy-start(bf16[272,384]{1,0:T(8,128)(2,1)} %get-tuple-element.13.q_ref) | copy-start | bytes 626692
  32.3 0.9 %copy-start.5 = (bf16[256,384]{1,0:T(8,128)(2,1)S(1)}, bf16[256,384]{1,0:T(8,128)(2,1)}, u32[]{:S(2)}) copy-start(bf16[256,384]{1,0:T(8,128)(2,1)} %get-tuple-element.14.k0_ref) | copy-start | bytes 589828
  36.3 12.2 %copy-start = (bf16[384,3072]{1,0:T(8,128)(2,1)S(1)}, bf16[384,3072]{1,0:T(8,128)(2,1)}, u32[]{:S(2)}) copy-start(bf16[384,3072]{1,0:T(8,128)(2,1)} %weight_ref.1) | copy-start | bytes 7077892
  36.3 12.2 %copy-start.3 = (s32[1,3]{1,0:T(1,128)S(1)}, s32[1,3]{1,0:T(1,128)}, u32[]{:S(2)}) copy-start(s32[1,3]{1,0:T(1,128)} %windows_ref.3) | copy-start | bytes 40
  39.4 3.9 %collective-permute-start.6 = (bf16[272,384]{1,0:T(8,128)(2,1)S(1)}, bf16[272,384]{1,0:T(8,128)(2,1)S(1)}, u32[]{:S(2)}, u32[]{:S(2)}) collective-permute-start(bf16[272,384]{1,0:T(8,128)(2,1)S(1)} %get-tuple-element.19), channel_id=1, source_target_pairs={{0,8},{8,0},{16,24},{24,16},{32,40},{40,32},{48,56},{56,48},{64,72... | collective-permute-start | bytes 626696 | tf_op jit(solution)/shard_map/ppermute | solution.py:44
  41.4 7.1 %collective-permute-start.7 = (bf16[272,384]{1,0:T(8,128)(2,1)S(1)}, bf16[272,384]{1,0:T(8,128)(2,1)S(1)}, u32[]{:S(2)}, u32[]{:S(2)}) collective-permute-start(bf16[272,384]{1,0:T(8,128)(2,1)S(1)} %get-tuple-element.20), channel_id=1, source_target_pairs={{8,16},{16,8},{40,48},{48,40},{72,80},{80,72},{104,112},{112,104},... | collective-permute-start | bytes 626696 | tf_op jit(solution)/shard_map/ppermute | solution.py:49
  51.9 7.0 %copy-start.6 = (f32[384]{0:T(512)S(1)}, f32[384]{0:T(512)}, u32[]{:S(2)}) copy-start(f32[384]{0:T(512)} %param.13) | copy-start | bytes 4612
  51.9 23.1 %copy-start.2 = (bf16[256,384]{1,0:T(8,128)(2,1)S(1)}, bf16[256,384]{1,0:T(8,128)(2,1)}, u32[]{:S(2)}) copy-start(bf16[256,384]{1,0:T(8,128)(2,1)} %residual_ref.1) | copy-start | bytes 589828
  52.0 23.1 %all-to-all-start = ((bf16[8,256,384]{2,1,0:T(8,128)(2,1)}), bf16[8,256,384]{2,1,0:T(8,128)(2,1)S(1)}, u32[]{:S(2)}, u32[]{:S(2)}) async-start(bf16[8,256,384]{2,1,0:T(8,128)(2,1)} %project.1), calls=%async_computation | async-start | bytes 3145728 | tf_op jit(solution)/shard_map/all_to_all | solution.py:278

commit v3 on v2

v3 whole, which is shorter than its diff:
```python
import functools

import jax
import jax.numpy as jnp
from jax import lax
from jax.experimental import pallas as pl
from jax.experimental.pallas import tpu as pltpu
from jax.sharding import PartitionSpec as P

HD = 128
HEIGHT_TILES = 4
SIDE = 16
LOG2E = 1.4426950408889634
MASKED = -1e30
MESH_AXES = ("tile", "head")
VMEM = pltpu.VMEM
SMEM = pltpu.SMEM


def params(megabytes):
    return pltpu.CompilerParams(vmem_limit_bytes=megabytes * 1024 * 1024)


def places():
    tiles = lax.axis_size("tile")
    return [(tile, *divmod(tile, HEIGHT_TILES), tiles // HEIGHT_TILES) for tile in range(tiles)]


def time_partner(time, height, later):
    odd = (height < HEIGHT_TILES // 2) != later
    return time + 1 if time % 2 == int(odd) else time - 1


def swap_times(block, later):
    route = []
    for tile, time, height, times in places():
        partner = time_partner(time, height, later)
        if 0 <= partner < times:
            route.append((tile, partner * HEIGHT_TILES + height))
    return lax.ppermute(block, "tile", route)


def swap_pair(block):
    return lax.ppermute(block, "tile", [(tile, tile ^ 1) for tile, *_ in places()])


def swap_middle(block):
    route = [(tile, tile + (1 if height == 1 else -1)) for tile, _, height, _ in places() if height in (1, 2)]
    return lax.ppermute(block, "tile", route)


def pack_kernel(windows_ref, q_ref, k_ref, v_ref, packed_ref, block_ref):
    rows = q_ref.shape[0]
    block_ref[:rows] = k_ref[...]
    block_ref[rows:] = v_ref[...]
    packed_ref[:rows] = q_ref[...]
    extent = windows_ref[0, 0].astype(jnp.float32)
    packed_ref[rows:] = jnp.full((SIDE, q_ref.shape[1]), extent, jnp.float32).astype(packed_ref.dtype)


def pack(windows, queries, key_rows, value_rows):
    rows, width = queries.shape
    whole = pl.BlockSpec(memory_space=VMEM)
    return pl.pallas_call(
        pack_kernel,
        out_shape=(
            jax.ShapeDtypeStruct((rows + SIDE, width), queries.dtype),
            jax.ShapeDtypeStruct((2 * rows, width), queries.dtype),
        ),
        in_specs=[pl.BlockSpec(memory_space=SMEM)] + [whole] * 3,
        out_specs=(whole, whole),
        name="pack",
    )(windows, queries, key_rows, value_rows)


def column(values, index):
    return values[:, index : index + 1]


def split_float(value):
    high = value.astype(jnp.bfloat16).astype(jnp.float32)
    rest = value - high
    middle = rest.astype(jnp.bfloat16).astype(jnp.float32)
    return high, middle, (rest - middle).astype(jnp.bfloat16).astype(jnp.float32)


def attend_kernel(stage, *refs):
    query_refs, block_ref, refs = refs[:3], refs[3], refs[4:]
    if stage > 0:
        old_mix_ref, old_stats_ref = refs[:2]
        refs = refs[2:]
    rows, width = block_ref.shape[0] // 2, block_ref.shape[1]
    tile = lax.axis_index("tile")
    time, height = tile // HEIGHT_TILES, tile % HEIGHT_TILES
    inner = (time > 0) & (time < lax.axis_size("tile") // HEIGHT_TILES - 1)
    lower = height < HEIGHT_TILES // 2
    present = (None, inner | ~lower, inner | lower)[stage]
    scale = HD**-0.5 * LOG2E
    line = lax.broadcasted_iota(jnp.int32, (8, rows), 0)
    lane = lax.broadcasted_iota(jnp.int32, (rows, HD), 1)
    spread = lambda value: jnp.broadcast_to(value, (rows, HD))
    if stage > 0:
        biases = []
        for ref in query_refs:
            wide = jnp.max(ref[rows:].astype(jnp.float32)) > 0.5
            biases.append(jnp.where(wide & present, 0.0, MASKED))
    for head in range(width // HD):
        low = head * HD
        keys, values = block_ref[:rows, low : low + HD], block_ref[rows:, low : low + HD]
        stats = jnp.zeros((rows, HD), jnp.float32)
        for place, ref in enumerate(query_refs):
            part = lax.dot_general(
                ref[:rows, low : low + HD], keys, (((1,), (1,)), ((), ())), preferred_element_type=jnp.float32
            )
            largest = spread(jnp.max(part, axis=1, keepdims=True)) * scale
            bias = 0.0
            index = 3 * head + place
            if stage > 0:
                bias = biases[place]
                largest = jnp.maximum(largest + bias, old_stats_ref[2 * index])
            offset = jnp.concatenate([bias - largest] * (rows // HD), axis=1)
            weights = jnp.exp2(part * scale + offset)
            total = spread(jnp.sum(weights, axis=1, keepdims=True))
            mix = jnp.dot(weights.astype(values.dtype), values, preferred_element_type=jnp.float32)
            if stage > 0:
                shrink = jnp.exp2(old_stats_ref[2 * index] - largest)
                total += old_stats_ref[2 * index + 1] * shrink
                mix += old_mix_ref[index] * shrink
            if stage < 2:
                refs[0][index] = mix
                refs[1][2 * index] = largest
                refs[1][2 * index + 1] = total
                continue
            stats = jnp.where(lane == 2 * place, largest, stats)
            stats = jnp.where(lane == 2 * place + 1, total, stats)
            if place == 0:
                refs[0][:, low : low + HD] = mix
            else:
                refs[1 + place][:rows, low : low + HD] = mix.astype(refs[1 + place].dtype)
        if stage < 2:
            continue
        stats = jnp.transpose(stats)[:8]
        refs[1][head] = stats
        for place in (1, 2):
            side = jnp.zeros((8, rows), jnp.float32)
            pieces = split_float(stats[2 * place : 2 * place + 1]) + split_float(stats[2 * place + 1 : 2 * place + 2])
            for index, piece in enumerate(pieces):
                side = jnp.where(line == index, piece, side)
            side = jnp.concatenate([side[:, :HD], side[:, HD:]], axis=0)
            refs[1 + place][rows:, low : low + HD] = side.astype(refs[1 + place].dtype)


def attend(stage, queries, block, before=()):
    rows, width = block.shape[0] // 2, block.shape[1]
    heads = width // HD
    whole = pl.BlockSpec(memory_space=VMEM)
    if stage < 2:
        out_shape = (
            jax.ShapeDtypeStruct((3 * heads, rows, HD), jnp.float32),
            jax.ShapeDtypeStruct((6 * heads, rows, HD), jnp.float32),
        )
    else:
        out_shape = (
            jax.ShapeDtypeStruct((rows, width), jnp.float32),
            jax.ShapeDtypeStruct((heads, 8, rows), jnp.float32),
            jax.ShapeDtypeStruct((rows + SIDE, width), jnp.bfloat16),
            jax.ShapeDtypeStruct((rows + SIDE, width), jnp.bfloat16),
        )
    return pl.pallas_call(
        functools.partial(attend_kernel, stage),
        out_shape=out_shape,
        in_specs=[whole] * (4 + len(before)),
        out_specs=(whole,) * len(out_shape),
        compiler_params=params(24),
        cost_estimate=pl.CostEstimate(flops=12 * heads * rows * rows * HD, bytes_accessed=2_000_000, transcendentals=3 * heads * rows * rows),
        name=("attend_own", "attend_first", "attend_second")[stage],
    )(*queries, block, *before)


def merge_shares(windows_ref, stats_ref, pair_ref, middle_ref, rows, heads):
    height = lax.axis_index("tile") % HEIGHT_TILES
    wide = windows_ref[0, 1] >= 1
    valid = (wide, wide & (height > 0) & (height < HEIGHT_TILES - 1))
    line = lax.broadcasted_iota(jnp.int32, (16, rows), 0)
    shares = jnp.zeros((16, rows), jnp.float32)
    for head in range(heads):
        low = head * HD
        stats = stats_ref[head]
        largest, total = [stats[0:1]], [stats[1:2]]
        for ref, flag in zip((pair_ref, middle_ref), valid):
            side = ref[rows:, low : low + HD].astype(jnp.float32)
            side = jnp.concatenate([side[:8], side[8:]], axis=1)
            largest.append(jnp.where(flag, side[0:1] + side[1:2] + side[2:3], MASKED))
            total.append(jnp.where(flag, side[3:4] + side[4:5] + side[5:6], 0.0))
        peak = jnp.maximum(jnp.maximum(largest[0], largest[1]), largest[2])
        factors = [jnp.exp2(value - peak) for value in largest]
        whole = total[0] * factors[0] + total[1] * factors[1] + total[2] * factors[2]
        for index, factor in enumerate(factors):
            shares = jnp.where(line == 3 * head + index, factor / whole, shares)
    return jnp.transpose(shares)


def project_kernel(windows_ref, own_ref, stats_ref, pair_ref, middle_ref, weight_ref, out_ref):
    rows, width = own_ref.shape
    heads = width // HD
    shares = merge_shares(windows_ref, stats_ref, pair_ref, middle_ref, rows, heads)
    merged = []
    for head in range(heads):
        low = head * HD
        value = own_ref[:, low : low + HD] * column(shares, 3 * head)
        for index, ref in enumerate((pair_ref, middle_ref)):
            value += ref[:rows, low : low + HD].astype(jnp.float32) * column(shares, 3 * head + 1 + index)
        merged.append(value.astype(jnp.bfloat16))
    attention = jnp.concatenate(merged, axis=1)
    for group in range(out_ref.shape[0]):
        out_ref[group] = jnp.dot(
            attention, weight_ref[:, group * width : (group + 1) * width], preferred_element_type=jnp.float32
        ).astype(out_ref.dtype)


def project(windows, own, stats, pair, middle, out_weight):
    rows, width = own.shape
    features = out_weight.shape[1]
    whole = pl.BlockSpec(memory_space=VMEM)
    return pl.pallas_call(
        project_kernel,
        out_shape=jax.ShapeDtypeStruct((features // width, rows, width), jnp.bfloat16),
        in_specs=[pl.BlockSpec(memory_space=SMEM)] + [whole] * 5,
        out_specs=whole,
        compiler_params=params(24),
        cost_estimate=pl.CostEstimate(flops=2 * rows * width * features, bytes_accessed=5_000_000, transcendentals=0),
        name="project",
    )(windows, own, stats, pair, middle, out_weight)


def finish_kernel(terms_ref, residual_ref, gate_ref, out_ref):
    total = jnp.sum(terms_ref[...].astype(jnp.float32), axis=0)
    out_ref[...] = (residual_ref[...].astype(jnp.float32) + gate_ref[...] * total).astype(out_ref.dtype)


def finish(terms, residual, gate_scale):
    groups, rows, width = terms.shape
    steps = 2
    part = rows // steps
    return pl.pallas_call(
        finish_kernel,
        grid=(steps,),
        out_shape=jax.ShapeDtypeStruct((rows, width), residual.dtype),
        in_specs=[
            pl.BlockSpec((groups, part, width), lambda step: (0, step, 0)),
            pl.BlockSpec((part, width), lambda step: (step, 0)),
            pl.BlockSpec((1, width), lambda step: (0, 0)),
        ],
        out_specs=pl.BlockSpec((part, width), lambda step: (step, 0)),
        compiler_params=params(24),
        cost_estimate=pl.CostEstimate(flops=10 * groups * rows * width, bytes_accessed=2_000_000, transcendentals=0),
        name="finish",
    )(terms, residual, gate_scale.reshape(1, width))


def shards(queries, key_rows, value_rows, windows, residual, out_weight, gate_scale):
    packed, block = pack(windows, queries, key_rows, value_rows)
    first, second = swap_times(block, False), swap_times(block, True)
    asked = (packed, swap_pair(packed), swap_middle(packed))
    before = attend(0, asked, block)
    before = attend(1, asked, first, before)
    own, stats, for_pair, for_middle = attend(2, asked, second, before)
    terms = project(windows, own, stats, swap_pair(for_pair), swap_middle(for_middle), out_weight)
    terms = lax.all_to_all(terms, "head", 0, 0)
    return finish(terms, residual, gate_scale)


def solution(mesh):
    return jax.shard_map(
        shards,
        mesh=mesh,
        in_specs=(
            P("tile", "head"),
            P("tile", "head"),
            P("tile", "head"),
            P("tile", None),
            P("tile", "head"),
            P("head", None),
            P("head"),
        ),
        out_specs=P("tile", "head"),
        check_vma=False,
    )
```

time: 76.5 us -> 74.6 us (0.975)
  the two profiles are of different devices: /device:TPU:184 before, /device:TPU:1 now
where the time goes in v3:
time: 74.6 us; the launch traced here: 73.2 us
  waiting for transfers between devices  32.8 us (44%)
  starting transfers between devices  27.3 us (37%)
  Pallas kernels  11 us (15%)
  local copies, waits for them, and re-layouts  1.95 us (3%)
    ppermute x2, waiting for transfers between devices, swap_middle(): return lax.ppermute(block, 'tile', route)  16.5 us
    all_to_all x1, waiting for transfers between devices, shards(): terms = lax.all_to_all(terms, 'head', 0, 0)  16.3 us
    ppermute x2, starting transfers between devices, swap_times(): return lax.ppermute(block, 'tile', route)  10.5 us
    all_to_all x1, starting transfers between devices, shards(): terms = lax.all_to_all(terms, 'head', 0, 0)  6.53 us
    ppermute x2, starting transfers between devices, swap_middle(): return lax.ppermute(block, 'tile', route)  5.28 us
    ppermute x2, starting transfers between devices, swap_pair(): lax.ppermute(block, 'tile', [(tile, tile ^ 1) for tile, *_ in places()])  5.06 us
    pallas_call x3, Pallas kernels, attend(): pl.pallas_call(functools.partial(attend_kernel, stage), out_shape=out_sha...  4.47 us
    pallas_call x1, Pallas kernels, project(): pl.pallas_call(project_kernel, out_shape=jax.ShapeDtypeStruct((features /...  3.44 us
  transfers between devices with their start and end apart: 7, of which 3 were waited for; matrix products, arithmetic and copies ran while one was open for 0% of the time, Pallas kernels for 4%

profile of v3, /device:TPU:1, one launch (start us, length us, event | category | flops | bytes accessed | tf_op | source)
XLA Modules:
  0.0 73.2 jit_solution(1106726403232458094)
XLA Ops:
  0.0 2.0 %pack.1 = (bf16[272,384]{1,0:T(8,128)(2,1)}, bf16[512,384]{1,0:T(8,128)(2,1)}) custom-call(s32[1,3]{1,0:T(1,128)} %windows_ref.3, bf16[256,384]{1,0:T(8,128)(2,1)} %q_ref.1, bf16[256,384]{1,0:T(8,128)(2,1)} %k_ref.1, bf16[256,384]{1,0:T(8,128)(2,1)} %v_ref.1), custom_call_target="tpu_custom_call" | custom-call | tf_op jit(solution)/shard_map/pack/pallas_call | solution.py:64
  2.0 0.7 collective-permute-start.3
  2.7 9.8 %collective-permute-start.2 = (bf16[512,384]{1,0:T(8,128)(2,1)}, bf16[512,384]{1,0:T(8,128)(2,1)S(1)}, u32[]{:S(2)}, u32[]{:S(2)}) collective-permute-start(bf16[512,384]{1,0:T(8,128)(2,1)} %get-tuple-element.16.refs_3_), channel_id=1, source_target_pairs={{0,32},{8,40},{32,0},{40,8},{48,80},{56,88},{64,96},{72,104},{80,4... | collective-permute-start | bytes 1179656 | tf_op jit(solution)/shard_map/ppermute | solution.py:40
  12.5 3.1 %collective-permute-start = (bf16[272,384]{1,0:T(8,128)(2,1)}, bf16[272,384]{1,0:T(8,128)(2,1)S(1)}, u32[]{:S(2)}, u32[]{:S(2)}) collective-permute-start(bf16[272,384]{1,0:T(8,128)(2,1)} %get-tuple-element.15.refs_0_), channel_id=1, source_target_pairs={{0,8},{8,0},{16,24},{24,16},{32,40},{40,32},{48,56},{56,48},{64,72... | collective-permute-start | bytes 626696 | tf_op jit(solution)/shard_map/ppermute | solution.py:44
  15.6 1.9 %collective-permute-start.1 = (bf16[272,384]{1,0:T(8,128)(2,1)}, bf16[272,384]{1,0:T(8,128)(2,1)S(1)}, u32[]{:S(2)}, u32[]{:S(2)}) collective-permute-start(bf16[272,384]{1,0:T(8,128)(2,1)} %get-tuple-element.15.refs_0_), channel_id=1, source_target_pairs={{8,16},{16,8},{40,48},{48,40},{72,80},{80,72},{104,112},{112,104},... | collective-permute-start | bytes 626696 | tf_op jit(solution)/shard_map/ppermute | solution.py:49
  17.5 0.0 collective-permute-done.refs_1_
  17.6 12.7 %collective-permute-done.1.refs_2_ = bf16[272,384]{1,0:T(8,128)(2,1)S(1)} collective-permute-done((bf16[272,384]{1,0:T(8,128)(2,1)}, bf16[272,384]{1,0:T(8,128)(2,1)S(1)}, u32[]{:S(2)}, u32[]{:S(2)}) %collective-permute-start.1) | collective-permute-done | bytes 208928 | tf_op jit(solution)/shard_map/ppermute | solution.py:49
  30.3 0.0 copy-start.1
  30.3 0.9 %copy-done.1 = bf16[272,384]{1,0:T(8,128)(2,1)S(1)} copy-done((bf16[272,384]{1,0:T(8,128)(2,1)S(1)}, bf16[272,384]{1,0:T(8,128)(2,1)}, u32[]{:S(2)}) %copy-start.1) | copy-done | bytes 208920
  31.2 0.0 copy-start.4
  31.2 1.0 %copy-done.4 = bf16[512,384]{1,0:T(8,128)(2,1)S(1)} copy-done((bf16[512,384]{1,0:T(8,128)(2,1)S(1)}, bf16[512,384]{1,0:T(8,128)(2,1)}, u32[]{:S(2)}) %copy-start.4) | copy-done | bytes 393240
  32.2 1.2 %attend_own.1 = (f32[9,256,128]{2,1,0:T(8,128)S(1)}, f32[18,256,128]{2,1,0:T(8,128)S(1)}) custom-call(bf16[272,384]{1,0:T(8,128)(2,1)S(1)} %copy-done.1, bf16[272,384]{1,0:T(8,128)(2,1)S(1)} %collective-permute-done.refs_1_, bf16[272,384]{1,0:T(8,128)(2,1)S(1)} %collective-permute-done.1.refs_2_, bf16[512,384]{1,0:T(8,128)(2,1)S(1)} %copy-done.4), custom_call_target="tpu_custom_call" | custom-call | flops 301989888 | bytes 2000000 | tf_op jit(solution)/shard_map/attend_own/pallas_call | solution.py:169
  33.4 0.0 collective-permute-done.3.refs_3_
  33.4 1.6 %attend_first.1 = (f32[9,256,128]{2,1,0:T(8,128)S(1)}, f32[18,256,128]{2,1,0:T(8,128)S(1)}) custom-call(bf16[272,384]{1,0:T(8,128)(2,1)S(1)} %copy-done.1, bf16[272,384]{1,0:T(8,128)(2,1)S(1)} %collective-permute-done.refs_1_, bf16[272,384]{1,0:T(8,128)(2,1)S(1)} %collective-permute-done.1.refs_2_, bf16[512,384]{1,0:T(8,128)(2,1)S(1)} %collective-permute-done.3.refs_3_, ...), custom_call_target="tpu_custom_call" | custom-call | flops 301989888 | bytes 2000000 | tf_op jit(solution)/shard_map/attend_first/pallas_call | solution.py:169
  35.0 0.0 collective-permute-done.2.refs_3_
  35.0 0.0 copy-start
  35.0 0.0 copy-start.3
  35.0 1.7 %attend_second.1 = (f32[256,384]{1,0:T(8,128)S(1)}, f32[3,8,256]{2,1,0:T(8,128)S(1)}, bf16[272,384]{1,0:T(8,128)(2,1)S(1)}, bf16[272,384]{1,0:T(8,128)(2,1)S(1)}) custom-call(bf16[272,384]{1,0:T(8,128)(2,1)S(1)} %copy-done.1, bf16[272,384]{1,0:T(8,128)(2,1)S(1)} %collective-permute-done.refs_1_, bf16[272,384]{1,0:T(8,128)(2,1)S(1)} %collective-permute-done.1.refs_2_, ...), custom_call_target="tpu_custom_call" | custom-call | flops 301989888 | bytes 2000000 | tf_op jit(solution)/shard_map/attend_second/pallas_call | solution.py:169
  36.8 1.9 %collective-permute-start.4 = (bf16[272,384]{1,0:T(8,128)(2,1)S(1)}, bf16[272,384]{1,0:T(8,128)(2,1)S(1)}, u32[]{:S(2)}, u32[]{:S(2)}) collective-permute-start(bf16[272,384]{1,0:T(8,128)(2,1)S(1)} %get-tuple-element.23), channel_id=1, source_target_pairs={{0,8},{8,0},{16,24},{24,16},{32,40},{40,32},{48,56},{56,48},{64,72... | collective-permute-start | bytes 626696 | tf_op jit(solution)/shard_map/ppermute | solution.py:44
  38.7 3.4 %collective-permute-start.5 = (bf16[272,384]{1,0:T(8,128)(2,1)S(1)}, bf16[272,384]{1,0:T(8,128)(2,1)S(1)}, u32[]{:S(2)}, u32[]{:S(2)}) collective-permute-start(bf16[272,384]{1,0:T(8,128)(2,1)S(1)} %get-tuple-element.24), channel_id=1, source_target_pairs={{8,16},{16,8},{40,48},{48,40},{72,80},{80,72},{104,112},{112,104},... | collective-permute-start | bytes 626696 | tf_op jit(solution)/shard_map/ppermute | solution.py:49
  42.1 0.0 collective-permute-done.4.pair_ref
  42.1 3.7 %collective-permute-done.5.middle_ref = bf16[272,384]{1,0:T(8,128)(2,1)S(1)} collective-permute-done((bf16[272,384]{1,0:T(8,128)(2,1)S(1)}, bf16[272,384]{1,0:T(8,128)(2,1)S(1)}, u32[]{:S(2)}, u32[]{:S(2)}) %collective-permute-start.5) | collective-permute-done | bytes 208928 | tf_op jit(solution)/shard_map/ppermute | solution.py:49
  45.8 0.0 copy-done
  45.8 0.0 copy-done.3
  45.8 3.4 %project.1 = bf16[8,256,384]{2,1,0:T(8,128)(2,1)} custom-call(s32[1,3]{1,0:T(1,128)S(1)} %copy-done.3, f32[256,384]{1,0:T(8,128)S(1)} %get-tuple-element.21.own_ref, f32[3,8,256]{2,1,0:T(8,128)S(1)} %get-tuple-element.22.stats_ref, bf16[272,384]{1,0:T(8,128)(2,1)S(1)} %collective-permute-done.4.pair_ref, ...), custom_call_target="tpu_custom_call" | custom-call | flops 603979776 | bytes 5000000 | tf_op jit(solution)/shard_map/project/pallas_call | solution.py:225
  49.3 0.0 copy-start.5
  49.3 0.0 copy-start.2
  49.3 6.5 %all-to-all-start = ((bf16[8,256,384]{2,1,0:T(8,128)(2,1)}), bf16[8,256,384]{2,1,0:T(8,128)(2,1)S(1)}, u32[]{:S(2)}, u32[]{:S(2)}) async-start(bf16[8,256,384]{2,1,0:T(8,128)(2,1)} %project.1), calls=%async_computation | async-start | bytes 3145728 | tf_op jit(solution)/shard_map/all_to_all | solution.py:269
  55.8 0.0 copy-done.5
  55.8 16.3 %all-to-all-done.terms_ref = bf16[8,256,384]{2,1,0:T(8,128)(2,1)S(1)} async-done(((bf16[8,256,384]{2,1,0:T(8,128)(2,1)}), bf16[8,256,384]{2,1,0:T(8,128)(2,1)S(1)}, u32[]{:S(2)}, u32[]{:S(2)}) %all-to-all-start) | async-done | bytes 1572896 | tf_op jit(solution)/shard_map/all_to_all | solution.py:269
  72.1 0.0 copy-done.2
  72.1 1.1 %finish.1 = bf16[256,384]{1,0:T(8,128)(2,1)} custom-call(bf16[8,256,384]{2,1,0:T(8,128)(2,1)S(1)} %all-to-all-done.terms_ref, bf16[256,384]{1,0:T(8,128)(2,1)S(1)} %copy-done.2, f32[1,384]{1,0:T(1,128)S(1)} %reshape.3.gate_ref), custom_call_target="tpu_custom_call" | custom-call | flops 7864320 | bytes 2000000 | tf_op jit(solution)/shard_map/finish/pallas_call | solution.py:245
  (1 shorter events, 0.0 us)
Async XLA Ops:
  2.0 31.4 %collective-permute-start.3 = (bf16[512,384]{1,0:T(8,128)(2,1)}, bf16[512,384]{1,0:T(8,128)(2,1)S(1)}, u32[]{:S(2)}, u32[]{:S(2)}) collective-permute-start(bf16[512,384]{1,0:T(8,128)(2,1)} %get-tuple-element.16.refs_3_), channel_id=1, source_target_pairs={{16,48},{24,56},{32,64},{40,72},{48,16},{56,24},{64,32},{72,40},{8... | collective-permute-start | bytes 1179656 | tf_op jit(solution)/shard_map/ppermute | solution.py:40
  2.7 32.3 %collective-permute-start.2 = (bf16[512,384]{1,0:T(8,128)(2,1)}, bf16[512,384]{1,0:T(8,128)(2,1)S(1)}, u32[]{:S(2)}, u32[]{:S(2)}) collective-permute-start(bf16[512,384]{1,0:T(8,128)(2,1)} %get-tuple-element.16.refs_3_), channel_id=1, source_target_pairs={{0,32},{8,40},{32,0},{40,8},{48,80},{56,88},{64,96},{72,104},{80,4... | collective-permute-start | bytes 1179656 | tf_op jit(solution)/shard_map/ppermute | solution.py:40
  12.5 5.1 %collective-permute-start = (bf16[272,384]{1,0:T(8,128)(2,1)}, bf16[272,384]{1,0:T(8,128)(2,1)S(1)}, u32[]{:S(2)}, u32[]{:S(2)}) collective-permute-start(bf16[272,384]{1,0:T(8,128)(2,1)} %get-tuple-element.15.refs_0_), channel_id=1, source_target_pairs={{0,8},{8,0},{16,24},{24,16},{32,40},{40,32},{48,56},{56,48},{64,72... | collective-permute-start | bytes 626696 | tf_op jit(solution)/shard_map/ppermute | solution.py:44
  15.6 14.7 %collective-permute-start.1 = (bf16[272,384]{1,0:T(8,128)(2,1)}, bf16[272,384]{1,0:T(8,128)(2,1)S(1)}, u32[]{:S(2)}, u32[]{:S(2)}) collective-permute-start(bf16[272,384]{1,0:T(8,128)(2,1)} %get-tuple-element.15.refs_0_), channel_id=1, source_target_pairs={{8,16},{16,8},{40,48},{48,40},{72,80},{80,72},{104,112},{112,104},... | collective-permute-start | bytes 626696 | tf_op jit(solution)/shard_map/ppermute | solution.py:49
  30.3 0.9 %copy-start.1 = (bf16[272,384]{1,0:T(8,128)(2,1)S(1)}, bf16[272,384]{1,0:T(8,128)(2,1)}, u32[]{:S(2)}) copy-start(bf16[272,384]{1,0:T(8,128)(2,1)} %get-tuple-element.15.refs_0_) | copy-start | bytes 626692
  31.2 1.0 %copy-start.4 = (bf16[512,384]{1,0:T(8,128)(2,1)S(1)}, bf16[512,384]{1,0:T(8,128)(2,1)}, u32[]{:S(2)}) copy-start(bf16[512,384]{1,0:T(8,128)(2,1)} %get-tuple-element.16.refs_3_) | copy-start | bytes 1179652
  35.0 10.8 %copy-start = (bf16[384,3072]{1,0:T(8,128)(2,1)S(1)}, bf16[384,3072]{1,0:T(8,128)(2,1)}, u32[]{:S(2)}) copy-start(bf16[384,3072]{1,0:T(8,128)(2,1)} %weight_ref.1) | copy-start | bytes 7077892
  35.0 10.8 %copy-start.3 = (s32[1,3]{1,0:T(1,128)S(1)}, s32[1,3]{1,0:T(1,128)}, u32[]{:S(2)}) copy-start(s32[1,3]{1,0:T(1,128)} %windows_ref.3) | copy-start | bytes 40
  36.8 5.3 %collective-permute-start.4 = (bf16[272,384]{1,0:T(8,128)(2,1)S(1)}, bf16[272,384]{1,0:T(8,128)(2,1)S(1)}, u32[]{:S(2)}, u32[]{:S(2)}) collective-permute-start(bf16[272,384]{1,0:T(8,128)(2,1)S(1)} %get-tuple-element.23), channel_id=1, source_target_pairs={{0,8},{8,0},{16,24},{24,16},{32,40},{40,32},{48,56},{56,48},{64,72... | collective-permute-start | bytes 626696 | tf_op jit(solution)/shard_map/ppermute | solution.py:44
  38.7 7.1 %collective-permute-start.5 = (bf16[272,384]{1,0:T(8,128)(2,1)S(1)}, bf16[272,384]{1,0:T(8,128)(2,1)S(1)}, u32[]{:S(2)}, u32[]{:S(2)}) collective-permute-start(bf16[272,384]{1,0:T(8,128)(2,1)S(1)} %get-tuple-element.24), channel_id=1, source_target_pairs={{8,16},{16,8},{40,48},{48,40},{72,80},{80,72},{104,112},{112,104},... | collective-permute-start | bytes 626696 | tf_op jit(solution)/shard_map/ppermute | solution.py:49
  49.3 6.5 %copy-start.5 = (f32[384]{0:T(512)S(1)}, f32[384]{0:T(512)}, u32[]{:S(2)}) copy-start(f32[384]{0:T(512)} %param.13) | copy-start | bytes 4612
  49.3 22.8 %copy-start.2 = (bf16[256,384]{1,0:T(8,128)(2,1)S(1)}, bf16[256,384]{1,0:T(8,128)(2,1)}, u32[]{:S(2)}) copy-start(bf16[256,384]{1,0:T(8,128)(2,1)} %residual_ref.1) | copy-start | bytes 589828
  49.3 22.8 %all-to-all-start = ((bf16[8,256,384]{2,1,0:T(8,128)(2,1)}), bf16[8,256,384]{2,1,0:T(8,128)(2,1)S(1)}, u32[]{:S(2)}, u32[]{:S(2)}) async-start(bf16[8,256,384]{2,1,0:T(8,128)(2,1)} %project.1), calls=%async_computation | async-start | bytes 3145728 | tf_op jit(solution)/shard_map/all_to_all | solution.py:269

commit v4 on v3

--- a/solution.py
+++ b/solution.py
@@ -84,39 +84,54 @@
     return high, middle, (rest - middle).astype(jnp.bfloat16).astype(jnp.float32)
 
 
-def attend_kernel(stage, *refs):
-    query_refs, block_ref, refs = refs[:3], refs[3], refs[4:]
+def wide_window(ref, rows):
+    return jnp.max(ref[rows:].astype(jnp.float32)) > 0.5
+
+
+def presence():
+    tile = lax.axis_index("tile")
+    time, height = tile // HEIGHT_TILES, tile % HEIGHT_TILES
+    inner = (time > 0) & (time < lax.axis_size("tile") // HEIGHT_TILES - 1)
+    lower = height < HEIGHT_TILES // 2
+    return inner | ~lower, inner | lower
+
+
+def raw_scores(query, keys):
+    return lax.dot_general(query, keys, (((1,), (1,)), ((), ())), preferred_element_type=jnp.float32)
+
+
+def put_message(ref, head, mix, stats, row):
+    rows = mix.shape[0]
+    low = head * HD
+    line = lax.broadcasted_iota(jnp.int32, (8, rows), 0)
+    ref[:rows, low : low + HD] = mix.astype(ref.dtype)
+    side = jnp.zeros((8, rows), jnp.float32)
+    for index, piece in enumerate(split_float(stats[row : row + 1]) + split_float(stats[row + 1 : row + 2])):
+        side = jnp.where(line == index, piece, side)
+    ref[rows:, low : low + HD] = jnp.concatenate([side[:, :HD], side[:, HD:]], axis=0).astype(ref.dtype)
+
+
+def attend_kernel(stage, places, *refs):
+    query_refs, block_ref, refs = refs[:2], refs[2], refs[3:]
     if stage > 0:
         old_mix_ref, old_stats_ref = refs[:2]
         refs = refs[2:]
     rows, width = block_ref.shape[0] // 2, block_ref.shape[1]
-    tile = lax.axis_index("tile")
-    time, height = tile // HEIGHT_TILES, tile % HEIGHT_TILES
-    inner = (time > 0) & (time < lax.axis_size("tile") // HEIGHT_TILES - 1)
-    lower = height < HEIGHT_TILES // 2
-    present = (None, inner | ~lower, inner | lower)[stage]
     scale = HD**-0.5 * LOG2E
-    line = lax.broadcasted_iota(jnp.int32, (8, rows), 0)
     lane = lax.broadcasted_iota(jnp.int32, (rows, HD), 1)
     spread = lambda value: jnp.broadcast_to(value, (rows, HD))
-    if stage > 0:
-        biases = []
-        for ref in query_refs:
-            wide = jnp.max(ref[rows:].astype(jnp.float32)) > 0.5
-            biases.append(jnp.where(wide & present, 0.0, MASKED))
-    for head in range(width // HD):
-        low = head * HD
-        keys, values = block_ref[:rows, low : low + HD], block_ref[rows:, low : low + HD]
-        stats = jnp.zeros((rows, HD), jnp.float32)
-        for place, ref in enumerate(query_refs):
-            part = lax.dot_general(
-                ref[:rows, low : low + HD], keys, (((1,), (1,)), ((), ())), preferred_element_type=jnp.float32
-            )
+    for place in places:
+        ref = query_refs[place]
+        bias = 0.0
+        if stage > 0:
+            bias = jnp.where(wide_window(ref, rows) & presence()[stage - 1], 0.0, MASKED)
+        for head in range(width // HD):
+            low = head * HD
+            keys, values = block_ref[:rows, low : low + HD], block_ref[rows:, low : low + HD]
+            part = raw_scores(ref[:rows, low : low + HD], keys)
             largest = spread(jnp.max(part, axis=1, keepdims=True)) * scale
-            bias = 0.0
-            index = 3 * head + place
+            index = 2 * head + place
             if stage > 0:
-                bias = biases[place]
                 largest = jnp.maximum(largest + bias, old_stats_ref[2 * index])
             offset = jnp.concatenate([bias - largest] * (rows // HD), axis=1)
             weights = jnp.exp2(part * scale + offset)
@@ -131,50 +146,93 @@
                 refs[1][2 * index] = largest
                 refs[1][2 * index + 1] = total
                 continue
-            stats = jnp.where(lane == 2 * place, largest, stats)
-            stats = jnp.where(lane == 2 * place + 1, total, stats)
+            stats = jnp.transpose(jnp.where(lane == 0, largest, jnp.where(lane == 1, total, 0.0)))[:8]
             if place == 0:
                 refs[0][:, low : low + HD] = mix
+                refs[1][head] = stats
             else:
-                refs[1 + place][:rows, low : low + HD] = mix.astype(refs[1 + place].dtype)
-        if stage < 2:
-            continue
-        stats = jnp.transpose(stats)[:8]
-        refs[1][head] = stats
-        for place in (1, 2):
-            side = jnp.zeros((8, rows), jnp.float32)
-            pieces = split_float(stats[2 * place : 2 * place + 1]) + split_float(stats[2 * place + 1 : 2 * place + 2])
-            for index, piece in enumerate(pieces):
-                side = jnp.where(line == index, piece, side)
-            side = jnp.concatenate([side[:, :HD], side[:, HD:]], axis=0)
-            refs[1 + place][rows:, low : low + HD] = side.astype(refs[1 + place].dtype)
-
-
-def attend(stage, queries, block, before=()):
+                put_message(refs[0], head, mix, stats, 0)
+
+
+def attend(stage, queries, block, before=(), places=(0, 1)):
     rows, width = block.shape[0] // 2, block.shape[1]
     heads = width // HD
     whole = pl.BlockSpec(memory_space=VMEM)
     if stage < 2:
         out_shape = (
-            jax.ShapeDtypeStruct((3 * heads, rows, HD), jnp.float32),
-            jax.ShapeDtypeStruct((6 * heads, rows, HD), jnp.float32),
+            jax.ShapeDtypeStruct((2 * heads, rows, HD), jnp.float32),
+            jax.ShapeDtypeStruct((4 * heads, rows, HD), jnp.float32),
         )
-    else:
+    elif places == (0,):
         out_shape = (
             jax.ShapeDtypeStruct((rows, width), jnp.float32),
             jax.ShapeDtypeStruct((heads, 8, rows), jnp.float32),
-            jax.ShapeDtypeStruct((rows + SIDE, width), jnp.bfloat16),
-            jax.ShapeDtypeStruct((rows + SIDE, width), jnp.bfloat16),
         )
-    return pl.pallas_call(
-        functools.partial(attend_kernel, stage),
+    else:
+        out_shape = (jax.ShapeDtypeStruct((rows + SIDE, width), jnp.bfloat16),)
+    cost = len(places) * heads * rows * rows
+    return pl.pallas_call(
+        functools.partial(attend_kernel, stage, places),
         out_shape=out_shape,
-        in_specs=[whole] * (4 + len(before)),
+        in_specs=[whole] * (3 + len(before)),
         out_specs=(whole,) * len(out_shape),
         compiler_params=params(24),
+        cost_estimate=pl.CostEstimate(flops=4 * HD * cost, bytes_accessed=2_000_000, transcendentals=cost),
+        name=("attend_own", "attend_first", "attend_second")[stage] + "_".join(map(str, places)),
+    )(*queries, block, *before)
+
+
+def gate_kernel(in_ref, out_ref):
+    pass
+
+
+def gate(array):
+    anywhere = pl.BlockSpec(memory_space=pl.ANY)
+    return pl.pallas_call(
+        gate_kernel,
+        out_shape=jax.ShapeDtypeStruct(array.shape, array.dtype),
+        in_specs=[anywhere],
+        out_specs=anywhere,
+        input_output_aliases={0: 0},
+        cost_estimate=pl.CostEstimate(flops=20_000_000_000, bytes_accessed=0, transcendentals=0),
+        name="gate",
+    )(array)
+
+
+def middle_kernel(query_ref, own_ref, first_ref, second_ref, after_ref, out_ref):
+    rows, width = own_ref.shape[0] // 2, own_ref.shape[1]
+    scale = HD**-0.5 * LOG2E
+    lane = lax.broadcasted_iota(jnp.int32, (rows, HD), 1)
+    wide = wide_window(query_ref, rows)
+    biases = [0.0] + [jnp.where(wide & present, 0.0, MASKED) for present in presence()]
+    for head in range(width // HD):
+        low = head * HD
+        query = query_ref[:rows, low : low + HD]
+        parts = [raw_scores(query, ref[:rows, low : low + HD]) for ref in (own_ref, first_ref, second_ref)]
+        peaks = [jnp.max(part, axis=1, keepdims=True) * scale + bias for part, bias in zip(parts, biases)]
+        largest = jnp.maximum(jnp.maximum(peaks[0], peaks[1]), peaks[2])
+        weights = [jnp.exp2(part * scale + (bias - largest)) for part, bias in zip(parts, biases)]
+        total = jnp.sum(weights[0] + weights[1] + weights[2], axis=1, keepdims=True)
+        mix = jnp.zeros((rows, HD), jnp.float32)
+        for weight, ref in zip(weights, (own_ref, first_ref, second_ref)):
+            mix += jnp.dot(weight.astype(ref.dtype), ref[rows:, low : low + HD], preferred_element_type=jnp.float32)
+        stats = jnp.where(lane == 0, largest, jnp.where(lane == 1, total, 0.0))
+        put_message(out_ref, head, mix, jnp.transpose(stats)[:8], 0)
+
+
+def attend_middle(query, own, first, second, after):
+    rows, width = own.shape[0] // 2, own.shape[1]
+    heads = width // HD
+    whole = pl.BlockSpec(memory_space=VMEM)
+    return pl.pallas_call(
+        middle_kernel,
+        out_shape=jax.ShapeDtypeStruct((rows + SIDE, width), jnp.bfloat16),
+        in_specs=[whole] * 4 + [pl.BlockSpec(memory_space=pl.ANY)],
+        out_specs=whole,
+        compiler_params=params(24),
         cost_estimate=pl.CostEstimate(flops=12 * heads * rows * rows * HD, bytes_accessed=2_000_000, transcendentals=3 * heads * rows * rows),
-        name=("attend_own", "attend_first", "attend_second")[stage],
-    )(*queries, block, *before)
+        name="attend_middle",
+    )(query, own, first, second, after)
 
 
 def merge_shares(windows_ref, stats_ref, pair_ref, middle_ref, rows, heads):
@@ -261,11 +319,14 @@
 def shards(queries, key_rows, value_rows, windows, residual, out_weight, gate_scale):
     packed, block = pack(windows, queries, key_rows, value_rows)
     first, second = swap_times(block, False), swap_times(block, True)
-    asked = (packed, swap_pair(packed), swap_middle(packed))
+    asked = (packed, swap_pair(packed))
     before = attend(0, asked, block)
     before = attend(1, asked, first, before)
-    own, stats, for_pair, for_middle = attend(2, asked, second, before)
-    terms = project(windows, own, stats, swap_pair(for_pair), swap_middle(for_middle), out_weight)
+    for_middle = attend_middle(swap_middle(packed), block, first, second, before[1])
+    (for_pair,) = attend(2, asked, second, before, (1,))
+    own, stats = attend(2, asked, second, before, (0,))
+    from_middle = gate(swap_middle(for_middle))
+    terms = project(windows, own, stats, swap_pair(for_pair), from_middle, out_weight)
     terms = lax.all_to_all(terms, "head", 0, 0)
     return finish(terms, residual, gate_scale)
 

time: 74.6 us -> 79.2 us (1.062)
  the two profiles are of different devices: /device:TPU:1 before, /device:TPU:129 now
where the time goes in v4:
time: 79.2 us; the launch traced here: 78.7 us
  waiting for transfers between devices  35 us (44%)
  starting transfers between devices  26.5 us (33%)
  Pallas kernels  11.8 us (15%)
  local copies, waits for them, and re-layouts  5.21 us (7%)
    all_to_all x1, waiting for transfers between devices, shards(): terms = lax.all_to_all(terms, 'head', 0, 0)  21.8 us
    ppermute x2, waiting for transfers between devices, swap_times(): return lax.ppermute(block, 'tile', route)  12.8 us
    ppermute x2, starting transfers between devices, swap_times(): return lax.ppermute(block, 'tile', route)  9.63 us
    all_to_all x1, starting transfers between devices, shards(): terms = lax.all_to_all(terms, 'head', 0, 0)  6.79 us
    unnamed x20, local copies, waits for them, and re-layouts  5.2 us
    ppermute x2, starting transfers between devices, swap_pair(): lax.ppermute(block, 'tile', [(tile, tile ^ 1) for tile, *_ in places()])  5.06 us
    ppermute x2, starting transfers between devices, swap_middle(): return lax.ppermute(block, 'tile', route)  5.04 us
    pallas_call x4, Pallas kernels, attend(): pl.pallas_call(functools.partial(attend_kernel, stage, places), out_shape...  3.78 us
  transfers between devices with their start and end apart: 7, of which 3 were waited for; matrix products, arithmetic and copies ran while one was open for 0% of the time, Pallas kernels for 5%

profile of v4, /device:TPU:129, one launch (start us, length us, event | category | flops | bytes accessed | tf_op | source)
XLA Modules:
  0.0 78.7 jit_solution(16320656066541157414)
XLA Ops:
  0.0 2.0 %pack.1 = (bf16[272,384]{1,0:T(8,128)(2,1)}, bf16[512,384]{1,0:T(8,128)(2,1)}) custom-call(s32[1,3]{1,0:T(1,128)} %windows_ref.3, bf16[256,384]{1,0:T(8,128)(2,1)} %q_ref.1, bf16[256,384]{1,0:T(8,128)(2,1)} %k_ref.1, bf16[256,384]{1,0:T(8,128)(2,1)} %v_ref.1), custom_call_target="tpu_custom_call" | custom-call | tf_op jit(solution)/shard_map/pack/pallas_call | solution.py:64
  2.0 4.1 %collective-permute-start.2 = (bf16[512,384]{1,0:T(8,128)(2,1)}, bf16[512,384]{1,0:T(8,128)(2,1)S(1)}, u32[]{:S(2)}, u32[]{:S(2)}) collective-permute-start(bf16[512,384]{1,0:T(8,128)(2,1)} %get-tuple-element.14.refs_2_.own_ref), channel_id=1, source_target_pairs={{16,48},{24,56},{32,64},{40,72},{48,16},{56,24},{64,32},{72,40},{8... | collective-permute-start | bytes 1179656 | tf_op jit(solution)/shard_map/ppermute | solution.py:40
  6.0 5.6 %collective-permute-start.1 = (bf16[512,384]{1,0:T(8,128)(2,1)}, bf16[512,384]{1,0:T(8,128)(2,1)S(1)}, u32[]{:S(2)}, u32[]{:S(2)}) collective-permute-start(bf16[512,384]{1,0:T(8,128)(2,1)} %get-tuple-element.14.refs_2_.own_ref), channel_id=1, source_target_pairs={{0,32},{8,40},{32,0},{40,8},{48,80},{56,88},{64,96},{72,104},{80,4... | collective-permute-start | bytes 1179656 | tf_op jit(solution)/shard_map/ppermute | solution.py:40
  11.6 3.1 %collective-permute-start = (bf16[272,384]{1,0:T(8,128)(2,1)}, bf16[272,384]{1,0:T(8,128)(2,1)S(1)}, u32[]{:S(2)}, u32[]{:S(2)}) collective-permute-start(bf16[272,384]{1,0:T(8,128)(2,1)} %get-tuple-element.13.refs_0_), channel_id=1, source_target_pairs={{0,8},{8,0},{16,24},{24,16},{32,40},{40,32},{48,56},{56,48},{64,72... | collective-permute-start | bytes 626696 | tf_op jit(solution)/shard_map/ppermute | solution.py:44
  14.8 1.9 %collective-permute-start.4 = (bf16[272,384]{1,0:T(8,128)(2,1)}, bf16[272,384]{1,0:T(8,128)(2,1)S(1)}, u32[]{:S(2)}, u32[]{:S(2)}) collective-permute-start(bf16[272,384]{1,0:T(8,128)(2,1)} %get-tuple-element.13.refs_0_), channel_id=1, source_target_pairs={{8,16},{16,8},{40,48},{48,40},{72,80},{80,72},{104,112},{112,104},... | collective-permute-start | bytes 626696 | tf_op jit(solution)/shard_map/ppermute | solution.py:49
  16.7 0.0 collective-permute-done.refs_1_
  16.7 0.0 copy-start
  16.7 0.9 %copy-done = bf16[272,384]{1,0:T(8,128)(2,1)S(1)} copy-done((bf16[272,384]{1,0:T(8,128)(2,1)S(1)}, bf16[272,384]{1,0:T(8,128)(2,1)}, u32[]{:S(2)}) %copy-start) | copy-done | bytes 208920
  17.7 1.0 %copy-done.3 = bf16[512,384]{1,0:T(8,128)(2,1)S(1)} copy-done((bf16[512,384]{1,0:T(8,128)(2,1)S(1)}, bf16[512,384]{1,0:T(8,128)(2,1)}, u32[]{:S(2)}) %copy-start.3) | copy-done | bytes 393240
  18.7 1.0 %attend_own0_1.1 = (f32[6,256,128]{2,1,0:T(8,128)S(1)}, f32[12,256,128]{2,1,0:T(8,128)S(1)}) custom-call(bf16[272,384]{1,0:T(8,128)(2,1)S(1)} %copy-done, bf16[272,384]{1,0:T(8,128)(2,1)S(1)} %collective-permute-done.refs_1_, bf16[512,384]{1,0:T(8,128)(2,1)S(1)} %copy-done.3), custom_call_target="tpu_custom_call" | custom-call | flops 201326592 | bytes 2000000 | tf_op jit(solution)/shard_map/attend_own0_1/pallas_call | solution.py:174
  19.6 12.8 %collective-permute-done.2.refs_2_.first_ref = bf16[512,384]{1,0:T(8,128)(2,1)S(1)} collective-permute-done((bf16[512,384]{1,0:T(8,128)(2,1)}, bf16[512,384]{1,0:T(8,128)(2,1)S(1)}, u32[]{:S(2)}, u32[]{:S(2)}) %collective-permute-start.2) | collective-permute-done | bytes 393248 | tf_op jit(solution)/shard_map/ppermute | solution.py:40
  32.5 1.1 %attend_first0_1.1 = (f32[6,256,128]{2,1,0:T(8,128)S(1)}, f32[12,256,128]{2,1,0:T(8,128)S(1)}) custom-call(bf16[272,384]{1,0:T(8,128)(2,1)S(1)} %copy-done, bf16[272,384]{1,0:T(8,128)(2,1)S(1)} %collective-permute-done.refs_1_, bf16[512,384]{1,0:T(8,128)(2,1)S(1)} %collective-permute-done.2.refs_2_.first_ref, f32[6,256,128]{2,1,0:T(8,128)S(1)} %get-tuple-element.15.refs_3_, ...), custom_call_target="tpu_custom_call" | custom-call | flops 201326592 | bytes 2000000 | tf_op jit(solution)/shard_map/attend_first0_1/pallas_call | solution.py:174
  33.6 0.0 collective-permute-done.4.query_ref
  33.6 0.0 collective-permute-done.1.refs_2_.second_ref
  33.6 0.0 copy-done.4
  33.7 0.0 copy-start.1
  33.7 1.5 %attend_middle.1 = bf16[272,384]{1,0:T(8,128)(2,1)S(1)} custom-call(bf16[272,384]{1,0:T(8,128)(2,1)S(1)} %collective-permute-done.4.query_ref, bf16[512,384]{1,0:T(8,128)(2,1)S(1)} %copy-done.4, bf16[512,384]{1,0:T(8,128)(2,1)S(1)} %collective-permute-done.2.refs_2_.first_ref, bf16[512,384]{1,0:T(8,128)(2,1)S(1)} %collective-permute-done.1.refs_2_.second_ref, ...), custom_call_target="tpu_custom_call" | custom-call | flops 301989888 | bytes 2000000 | tf_op jit(solution)/shard_map/attend_middle/pallas_call | solution.py:227
  35.2 3.1 %collective-permute-start.5 = (bf16[272,384]{1,0:T(8,128)(2,1)S(1)}, bf16[272,384]{1,0:T(8,128)(2,1)S(1)}, u32[]{:S(2)}, u32[]{:S(2)}) collective-permute-start(bf16[272,384]{1,0:T(8,128)(2,1)S(1)} %attend_middle.1), channel_id=1, source_target_pairs={{8,16},{16,8},{40,48},{48,40},{72,80},{80,72},{104,112},{112,104},... | collective-permute-start | bytes 626696 | tf_op jit(solution)/shard_map/ppermute | solution.py:49
  38.3 0.0 copy-done.1
  38.3 0.8 %attend_second1.1 = bf16[272,384]{1,0:T(8,128)(2,1)S(1)} custom-call(bf16[272,384]{1,0:T(8,128)(2,1)S(1)} %copy-done.1, bf16[272,384]{1,0:T(8,128)(2,1)S(1)} %collective-permute-done.refs_1_, bf16[512,384]{1,0:T(8,128)(2,1)S(1)} %collective-permute-done.1.refs_2_.second_ref, f32[6,256,128]{2,1,0:T(8,128)S(1)} %get-tuple-element.17.refs_3_, ...), custom_call_target="tpu_custom_call" | custom-call | flops 100663296 | bytes 2000000 | tf_op jit(solution)/shard_map/attend_second1/pallas_call | solution.py:174
  39.2 1.9 %collective-permute-start.3 = (bf16[272,384]{1,0:T(8,128)(2,1)S(1)}, bf16[272,384]{1,0:T(8,128)(2,1)S(1)}, u32[]{:S(2)}, u32[]{:S(2)}) collective-permute-start(bf16[272,384]{1,0:T(8,128)(2,1)S(1)} %attend_second1.1), channel_id=1, source_target_pairs={{0,8},{8,0},{16,24},{24,16},{32,40},{40,32},{48,56},{56,48},{64,72... | collective-permute-start | bytes 626696 | tf_op jit(solution)/shard_map/ppermute | solution.py:44
  41.1 0.8 %attend_second0.1 = (f32[256,384]{1,0:T(8,128)S(1)}, f32[3,8,256]{2,1,0:T(8,128)S(1)}) custom-call(bf16[272,384]{1,0:T(8,128)(2,1)S(1)} %copy-done.1, bf16[272,384]{1,0:T(8,128)(2,1)S(1)} %collective-permute-done.refs_1_, bf16[512,384]{1,0:T(8,128)(2,1)S(1)} %collective-permute-done.1.refs_2_.second_ref, f32[6,256,128]{2,1,0:T(8,128)S(1)} %get-tuple-element.17.refs_3_, ...), custom_call_target="tpu_custom_call" | custom-call | flops 100663296 | bytes 2000000 | tf_op jit(solution)/shard_map/attend_second0/pallas_call | solution.py:174
  41.9 0.4 collective-permute-done.5.in_ref
  42.3 0.7 copy-done.5
  43.0 0.0 collective-permute-done.3.pair_ref
  43.0 0.0 copy-done.8
  43.0 1.7 %copy-done.2 = bf16[384,3072]{1,0:T(8,128)(2,1)S(1)} copy-done((bf16[384,3072]{1,0:T(8,128)(2,1)S(1)}, bf16[384,3072]{1,0:T(8,128)(2,1)}, u32[]{:S(2)}) %copy-start.2) | copy-done | bytes 2359320
  44.7 0.9 %copy-done.6 = bf16[272,384]{1,0:T(8,128)(2,1)S(1)} copy-done((bf16[272,384]{1,0:T(8,128)(2,1)S(1)}, bf16[272,384]{1,0:T(8,128)(2,1)}, u32[]{:S(2)}) %copy-start.6) | copy-done | bytes 208920
  45.6 3.4 %project.1 = bf16[8,256,384]{2,1,0:T(8,128)(2,1)} custom-call(s32[1,3]{1,0:T(1,128)S(1)} %copy-done.8, f32[256,384]{1,0:T(8,128)S(1)} %get-tuple-element.19.own_ref, f32[3,8,256]{2,1,0:T(8,128)S(1)} %get-tuple-element.20.stats_ref, bf16[272,384]{1,0:T(8,128)(2,1)S(1)} %collective-permute-done.3.pair_ref, bf16[272,384]{1,0:T(8,128)(2,1)S(1)} %copy-done.6, ...), custom_call_target="tpu_custom_call" | custom-call | flops 603979776 | bytes 5000000 | tf_op jit(solution)/shard_map/project/pallas_call | solution.py:283
  49.0 6.8 %all-to-all-start = ((bf16[8,256,384]{2,1,0:T(8,128)(2,1)}), bf16[8,256,384]{2,1,0:T(8,128)(2,1)S(1)}, u32[]{:S(2)}, u32[]{:S(2)}) async-start(bf16[8,256,384]{2,1,0:T(8,128)(2,1)} %project.1), calls=%async_computation | async-start | bytes 3145728 | tf_op jit(solution)/shard_map/all_to_all | solution.py:330
  55.9 21.8 %all-to-all-done.terms_ref = bf16[8,256,384]{2,1,0:T(8,128)(2,1)S(1)} async-done(((bf16[8,256,384]{2,1,0:T(8,128)(2,1)}), bf16[8,256,384]{2,1,0:T(8,128)(2,1)S(1)}, u32[]{:S(2)}, u32[]{:S(2)}) %all-to-all-start) | async-done | bytes 1572896 | tf_op jit(solution)/shard_map/all_to_all | solution.py:330
  77.6 1.1 %finish.1 = bf16[256,384]{1,0:T(8,128)(2,1)} custom-call(bf16[8,256,384]{2,1,0:T(8,128)(2,1)S(1)} %all-to-all-done.terms_ref, bf16[256,384]{1,0:T(8,128)(2,1)S(1)} %copy-done.7, f32[1,384]{1,0:T(1,128)S(1)} %reshape.3.gate_ref), custom_call_target="tpu_custom_call" | custom-call | flops 7864320 | bytes 2000000 | tf_op jit(solution)/shard_map/finish/pallas_call | solution.py:303
  (12 shorter events, 0.0 us)
Async XLA Ops:
  2.0 30.5 %collective-permute-start.2 = (bf16[512,384]{1,0:T(8,128)(2,1)}, bf16[512,384]{1,0:T(8,128)(2,1)S(1)}, u32[]{:S(2)}, u32[]{:S(2)}) collective-permute-start(bf16[512,384]{1,0:T(8,128)(2,1)} %get-tuple-element.14.refs_2_.own_ref), channel_id=1, source_target_pairs={{16,48},{24,56},{32,64},{40,72},{48,16},{56,24},{64,32},{72,40},{8... | collective-permute-start | bytes 1179656 | tf_op jit(solution)/shard_map/ppermute | solution.py:40
  6.0 27.6 %collective-permute-start.1 = (bf16[512,384]{1,0:T(8,128)(2,1)}, bf16[512,384]{1,0:T(8,128)(2,1)S(1)}, u32[]{:S(2)}, u32[]{:S(2)}) collective-permute-start(bf16[512,384]{1,0:T(8,128)(2,1)} %get-tuple-element.14.refs_2_.own_ref), channel_id=1, source_target_pairs={{0,32},{8,40},{32,0},{40,8},{48,80},{56,88},{64,96},{72,104},{80,4... | collective-permute-start | bytes 1179656 | tf_op jit(solution)/shard_map/ppermute | solution.py:40
  11.6 5.1 %collective-permute-start = (bf16[272,384]{1,0:T(8,128)(2,1)}, bf16[272,384]{1,0:T(8,128)(2,1)S(1)}, u32[]{:S(2)}, u32[]{:S(2)}) collective-permute-start(bf16[272,384]{1,0:T(8,128)(2,1)} %get-tuple-element.13.refs_0_), channel_id=1, source_target_pairs={{0,8},{8,0},{16,24},{24,16},{32,40},{40,32},{48,56},{56,48},{64,72... | collective-permute-start | bytes 626696 | tf_op jit(solution)/shard_map/ppermute | solution.py:44
  14.8 18.8 %collective-permute-start.4 = (bf16[272,384]{1,0:T(8,128)(2,1)}, bf16[272,384]{1,0:T(8,128)(2,1)S(1)}, u32[]{:S(2)}, u32[]{:S(2)}) collective-permute-start(bf16[272,384]{1,0:T(8,128)(2,1)} %get-tuple-element.13.refs_0_), channel_id=1, source_target_pairs={{8,16},{16,8},{40,48},{48,40},{72,80},{80,72},{104,112},{112,104},... | collective-permute-start | bytes 626696 | tf_op jit(solution)/shard_map/ppermute | solution.py:49
  16.7 0.9 %copy-start = (bf16[272,384]{1,0:T(8,128)(2,1)S(1)}, bf16[272,384]{1,0:T(8,128)(2,1)}, u32[]{:S(2)}) copy-start(bf16[272,384]{1,0:T(8,128)(2,1)} %get-tuple-element.13.refs_0_) | copy-start | bytes 626692
  17.7 1.0 %copy-start.3 = (bf16[512,384]{1,0:T(8,128)(2,1)S(1)}, bf16[512,384]{1,0:T(8,128)(2,1)}, u32[]{:S(2)}) copy-start(bf16[512,384]{1,0:T(8,128)(2,1)} %get-tuple-element.14.refs_2_.own_ref) | copy-start | bytes 1179652
  32.5 1.2 %copy-start.4 = (bf16[512,384]{1,0:T(8,128)(2,1)S(1)}, bf16[512,384]{1,0:T(8,128)(2,1)}, u32[]{:S(2)}) copy-start(bf16[512,384]{1,0:T(8,128)(2,1)} %get-tuple-element.14.refs_2_.own_ref) | copy-start | bytes 1179652
  33.7 4.7 %copy-start.1 = (bf16[272,384]{1,0:T(8,128)(2,1)S(1)}, bf16[272,384]{1,0:T(8,128)(2,1)}, u32[]{:S(2)}) copy-start(bf16[272,384]{1,0:T(8,128)(2,1)} %get-tuple-element.13.refs_0_) | copy-start | bytes 626692
  35.2 7.1 %collective-permute-start.5 = (bf16[272,384]{1,0:T(8,128)(2,1)S(1)}, bf16[272,384]{1,0:T(8,128)(2,1)S(1)}, u32[]{:S(2)}, u32[]{:S(2)}) collective-permute-start(bf16[272,384]{1,0:T(8,128)(2,1)S(1)} %attend_middle.1), channel_id=1, source_target_pairs={{8,16},{16,8},{40,48},{48,40},{72,80},{80,72},{104,112},{112,104},... | collective-permute-start | bytes 626696 | tf_op jit(solution)/shard_map/ppermute | solution.py:49
  39.2 3.8 %collective-permute-start.3 = (bf16[272,384]{1,0:T(8,128)(2,1)S(1)}, bf16[272,384]{1,0:T(8,128)(2,1)S(1)}, u32[]{:S(2)}, u32[]{:S(2)}) collective-permute-start(bf16[272,384]{1,0:T(8,128)(2,1)S(1)} %attend_second1.1), channel_id=1, source_target_pairs={{0,8},{8,0},{16,24},{24,16},{32,40},{40,32},{48,56},{56,48},{64,72... | collective-permute-start | bytes 626696 | tf_op jit(solution)/shard_map/ppermute | solution.py:44
  41.9 1.1 %copy-start.8 = (s32[1,3]{1,0:T(1,128)S(1)}, s32[1,3]{1,0:T(1,128)}, u32[]{:S(2)}) copy-start(s32[1,3]{1,0:T(1,128)} %windows_ref.3) | copy-start | bytes 40
  42.3 0.7 copy-start.5
  43.0 1.7 %copy-start.2 = (bf16[384,3072]{1,0:T(8,128)(2,1)S(1)}, bf16[384,3072]{1,0:T(8,128)(2,1)}, u32[]{:S(2)}) copy-start(bf16[384,3072]{1,0:T(8,128)(2,1)} %weight_ref.1) | copy-start | bytes 7077892
  44.7 0.9 %copy-start.6 = (bf16[272,384]{1,0:T(8,128)(2,1)S(1)}, bf16[272,384]{1,0:T(8,128)(2,1)}, u32[]{:S(2)}) copy-start(bf16[272,384]{1,0:T(8,128)(2,1)} %gate.1.middle_ref) | copy-start | bytes 626692
  49.0 6.8 %copy-start.9 = (f32[384]{0:T(512)S(1)}, f32[384]{0:T(512)}, u32[]{:S(2)}) copy-start(f32[384]{0:T(512)} %param.13) | copy-start | bytes 4612
  49.0 28.6 %copy-start.7 = (bf16[256,384]{1,0:T(8,128)(2,1)S(1)}, bf16[256,384]{1,0:T(8,128)(2,1)}, u32[]{:S(2)}) copy-start(bf16[256,384]{1,0:T(8,128)(2,1)} %residual_ref.1) | copy-start | bytes 589828
  49.0 28.6 %all-to-all-start = ((bf16[8,256,384]{2,1,0:T(8,128)(2,1)}), bf16[8,256,384]{2,1,0:T(8,128)(2,1)S(1)}, u32[]{:S(2)}, u32[]{:S(2)}) async-start(bf16[8,256,384]{2,1,0:T(8,128)(2,1)} %project.1), calls=%async_computation | async-start | bytes 3145728 | tf_op jit(solution)/shard_map/all_to_all | solution.py:330

commit v5 on v4

--- a/solution.py
+++ b/solution.py
@@ -54,8 +54,10 @@
     block_ref[:rows] = k_ref[...]
     block_ref[rows:] = v_ref[...]
     packed_ref[:rows] = q_ref[...]
-    extent = windows_ref[0, 0].astype(jnp.float32)
-    packed_ref[rows:] = jnp.full((SIDE, q_ref.shape[1]), extent, jnp.float32).astype(packed_ref.dtype)
+    for axis in (0, 1):
+        extent = windows_ref[0, axis].astype(jnp.float32)
+        packed_ref[rows:, axis * HD : (axis + 1) * HD] = jnp.full((SIDE, HD), extent, jnp.float32).astype(packed_ref.dtype)
+    packed_ref[rows:, 2 * HD :] = jnp.zeros((SIDE, q_ref.shape[1] - 2 * HD), packed_ref.dtype)
 
 
 def pack(windows, queries, key_rows, value_rows):
@@ -84,8 +86,8 @@
     return high, middle, (rest - middle).astype(jnp.bfloat16).astype(jnp.float32)
 
 
-def wide_window(ref, rows):
-    return jnp.max(ref[rows:].astype(jnp.float32)) > 0.5
+def wide_window(ref, rows, axis=0):
+    return jnp.max(ref[rows:, axis * HD : (axis + 1) * HD].astype(jnp.float32)) > 0.5
 
 
 def presence():
@@ -113,6 +115,10 @@
 
 def attend_kernel(stage, places, *refs):
     query_refs, block_ref, refs = refs[:2], refs[2], refs[3:]
+    if stage == 0:
+        weight_ref, refs, held_ref, sem = refs[0], refs[1:3], refs[3], refs[4]
+        copy = pltpu.make_async_copy(weight_ref, held_ref, sem)
+        copy.start()
     if stage > 0:
         old_mix_ref, old_stats_ref = refs[:2]
         refs = refs[2:]
@@ -149,12 +155,15 @@
             stats = jnp.transpose(jnp.where(lane == 0, largest, jnp.where(lane == 1, total, 0.0)))[:8]
             if place == 0:
                 refs[0][:, low : low + HD] = mix
-                refs[1][head] = stats
+                line = lax.broadcasted_iota(jnp.int32, stats.shape, 0)
+                refs[1][head] = jnp.where(line == 2, jnp.where(wide_window(ref, rows, 1), 1.0, 0.0), stats)
             else:
                 put_message(refs[0], head, mix, stats, 0)
-
-
-def attend(stage, queries, block, before=(), places=(0, 1)):
+    if stage == 0:
+        copy.wait()
+
+
+def attend(stage, queries, block, before=(), places=(0, 1), out_weight=None):
     rows, width = block.shape[0] // 2, block.shape[1]
     heads = width // HD
     whole = pl.BlockSpec(memory_space=VMEM)
@@ -171,15 +180,21 @@
     else:
         out_shape = (jax.ShapeDtypeStruct((rows + SIDE, width), jnp.bfloat16),)
     cost = len(places) * heads * rows * rows
+    extra, extra_specs, scratch = (), [], []
+    if stage == 0:
+        extra, extra_specs = (out_weight,), [pl.BlockSpec(memory_space=pl.ANY)]
+        out_shape += (jax.ShapeDtypeStruct(out_weight.shape, out_weight.dtype),)
+        scratch = [pltpu.SemaphoreType.DMA]
     return pl.pallas_call(
         functools.partial(attend_kernel, stage, places),
         out_shape=out_shape,
-        in_specs=[whole] * (3 + len(before)),
+        in_specs=[whole] * 3 + extra_specs + [whole] * len(before),
         out_specs=(whole,) * len(out_shape),
+        scratch_shapes=scratch,
         compiler_params=params(24),
         cost_estimate=pl.CostEstimate(flops=4 * HD * cost, bytes_accessed=2_000_000, transcendentals=cost),
         name=("attend_own", "attend_first", "attend_second")[stage] + "_".join(map(str, places)),
-    )(*queries, block, *before)
+    )(*queries, block, *extra, *before)
 
 
 def gate_kernel(in_ref, out_ref):
@@ -194,7 +209,7 @@
         in_specs=[anywhere],
         out_specs=anywhere,
         input_output_aliases={0: 0},
-        cost_estimate=pl.CostEstimate(flops=20_000_000_000, bytes_accessed=0, transcendentals=0),
+        cost_estimate=pl.CostEstimate(flops=3_500_000_000, bytes_accessed=0, transcendentals=0),
         name="gate",
     )(array)
 
@@ -203,21 +218,30 @@
     rows, width = own_ref.shape[0] // 2, own_ref.shape[1]
     scale = HD**-0.5 * LOG2E
     lane = lax.broadcasted_iota(jnp.int32, (rows, HD), 1)
-    wide = wide_window(query_ref, rows)
-    biases = [0.0] + [jnp.where(wide & present, 0.0, MASKED) for present in presence()]
-    for head in range(width // HD):
-        low = head * HD
-        query = query_ref[:rows, low : low + HD]
-        parts = [raw_scores(query, ref[:rows, low : low + HD]) for ref in (own_ref, first_ref, second_ref)]
-        peaks = [jnp.max(part, axis=1, keepdims=True) * scale + bias for part, bias in zip(parts, biases)]
-        largest = jnp.maximum(jnp.maximum(peaks[0], peaks[1]), peaks[2])
-        weights = [jnp.exp2(part * scale + (bias - largest)) for part, bias in zip(parts, biases)]
-        total = jnp.sum(weights[0] + weights[1] + weights[2], axis=1, keepdims=True)
-        mix = jnp.zeros((rows, HD), jnp.float32)
-        for weight, ref in zip(weights, (own_ref, first_ref, second_ref)):
-            mix += jnp.dot(weight.astype(ref.dtype), ref[rows:, low : low + HD], preferred_element_type=jnp.float32)
-        stats = jnp.where(lane == 0, largest, jnp.where(lane == 1, total, 0.0))
-        put_message(out_ref, head, mix, jnp.transpose(stats)[:8], 0)
+    height = lax.axis_index("tile") % HEIGHT_TILES
+    inside = (height > 0) & (height < HEIGHT_TILES - 1)
+
+    @pl.when(inside)
+    def compute():
+        wide = wide_window(query_ref, rows)
+        biases = [0.0] + [jnp.where(wide & present, 0.0, MASKED) for present in presence()]
+        for head in range(width // HD):
+            low = head * HD
+            query = query_ref[:rows, low : low + HD]
+            parts = [raw_scores(query, ref[:rows, low : low + HD]) for ref in (own_ref, first_ref, second_ref)]
+            peaks = [jnp.max(part, axis=1, keepdims=True) * scale + bias for part, bias in zip(parts, biases)]
+            largest = jnp.maximum(jnp.maximum(peaks[0], peaks[1]), peaks[2])
+            weights = [jnp.exp2(part * scale + (bias - largest)) for part, bias in zip(parts, biases)]
+            total = jnp.sum(weights[0] + weights[1] + weights[2], axis=1, keepdims=True)
+            mix = jnp.zeros((rows, HD), jnp.float32)
+            for weight, ref in zip(weights, (own_ref, first_ref, second_ref)):
+                mix += jnp.dot(weight.astype(ref.dtype), ref[rows:, low : low + HD], preferred_element_type=jnp.float32)
+            stats = jnp.where(lane == 0, largest, jnp.where(lane == 1, total, 0.0))
+            put_message(out_ref, head, mix, jnp.transpose(stats)[:8], 0)
+
+    @pl.when(jnp.logical_not(inside))
+    def skip():
+        out_ref[...] = jnp.zeros_like(out_ref)
 
 
 def attend_middle(query, own, first, second, after):
@@ -235,17 +259,17 @@
     )(query, own, first, second, after)
 
 
-def merge_shares(windows_ref, stats_ref, pair_ref, middle_ref, rows, heads):
+def merge_shares(stats_ref, pair_ref, middle_ref, rows, heads):
     height = lax.axis_index("tile") % HEIGHT_TILES
-    wide = windows_ref[0, 1] >= 1
-    valid = (wide, wide & (height > 0) & (height < HEIGHT_TILES - 1))
+    inside = jnp.where((height > 0) & (height < HEIGHT_TILES - 1), 1.0, 0.0)
     line = lax.broadcasted_iota(jnp.int32, (16, rows), 0)
     shares = jnp.zeros((16, rows), jnp.float32)
     for head in range(heads):
         low = head * HD
         stats = stats_ref[head]
         largest, total = [stats[0:1]], [stats[1:2]]
-        for ref, flag in zip((pair_ref, middle_ref), valid):
+        wide = stats[2:3]
+        for ref, flag in ((pair_ref, wide > 0.5), (middle_ref, wide * inside > 0.5)):
             side = ref[rows:, low : low + HD].astype(jnp.float32)
             side = jnp.concatenate([side[:8], side[8:]], axis=1)
             largest.append(jnp.where(flag, side[0:1] + side[1:2] + side[2:3], MASKED))
@@ -258,10 +282,10 @@
     return jnp.transpose(shares)
 
 
-def project_kernel(windows_ref, own_ref, stats_ref, pair_ref, middle_ref, weight_ref, out_ref):
+def project_kernel(own_ref, stats_ref, pair_ref, middle_ref, weight_ref, out_ref):
     rows, width = own_ref.shape
     heads = width // HD
-    shares = merge_shares(windows_ref, stats_ref, pair_ref, middle_ref, rows, heads)
+    shares = merge_shares(stats_ref, pair_ref, middle_ref, rows, heads)
     merged = []
     for head in range(heads):
         low = head * HD
@@ -276,19 +300,19 @@
         ).astype(out_ref.dtype)
 
 
-def project(windows, own, stats, pair, middle, out_weight):
+def project(own, stats, pair, middle, out_weight):
     rows, width = own.shape
     features = out_weight.shape[1]
     whole = pl.BlockSpec(memory_space=VMEM)
     return pl.pallas_call(
         project_kernel,
         out_shape=jax.ShapeDtypeStruct((features // width, rows, width), jnp.bfloat16),
-        in_specs=[pl.BlockSpec(memory_space=SMEM)] + [whole] * 5,
+        in_specs=[whole] * 5,
         out_specs=whole,
         compiler_params=params(24),
         cost_estimate=pl.CostEstimate(flops=2 * rows * width * features, bytes_accessed=5_000_000, transcendentals=0),
         name="project",
-    )(windows, own, stats, pair, middle, out_weight)
+    )(own, stats, pair, middle, out_weight)
 
 
 def finish_kernel(terms_ref, residual_ref, gate_ref, out_ref):
@@ -320,13 +344,13 @@
     packed, block = pack(windows, queries, key_rows, value_rows)
     first, second = swap_times(block, False), swap_times(block, True)
     asked = (packed, swap_pair(packed))
-    before = attend(0, asked, block)
+    *before, held_weight = attend(0, asked, block, out_weight=out_weight)
     before = attend(1, asked, first, before)
-    for_middle = attend_middle(swap_middle(packed), block, first, second, before[1])
     (for_pair,) = attend(2, asked, second, before, (1,))
+    for_middle = attend_middle(swap_middle(packed), block, first, second, for_pair)
     own, stats = attend(2, asked, second, before, (0,))
-    from_middle = gate(swap_middle(for_middle))
-    terms = project(windows, own, stats, swap_pair(for_pair), from_middle, out_weight)
+    from_pair = gate(swap_pair(for_pair))
+    terms = project(own, stats, from_pair, swap_middle(for_middle), held_weight)
     terms = lax.all_to_all(terms, "head", 0, 0)
     return finish(terms, residual, gate_scale)
 

time: 79.2 us -> 74.3 us (0.938)
  waiting for transfers between devices: 35 us -> 30.3 us
    all_to_all x1, waiting for transfers between devices: 21.8 us -> 16 us  [shards(): terms = lax.all_to_all(terms, 'head', 0, 0)]
    ppermute x2, waiting for transfers between devices: 0.4 us -> 3.33 us  [swap_middle(): return lax.ppermute(block, 'tile', route)]
    ppermute x2, waiting for transfers between devices: 12.8 us -> 11 us  [swap_times(): return lax.ppermute(block, 'tile', route)]
    ppermute x2, starting transfers between devices: 5.06 us -> 6.08 us  [swap_pair(): lax.ppermute(block, 'tile', [(tile, tile ^ 1) for tile, *_ in places()])]
    ppermute x2, starting transfers between devices: 5.04 us -> 4.17 us  [swap_middle(): return lax.ppermute(block, 'tile', route)]
    unnamed x20 -> x18, local copies, waits for them, and re-layouts: 5.2 us -> 5.19 us
  transfers between devices with their start and end apart: 7 -> 7, of which waited for: 3 -> 3; matrix products, arithmetic and copies ran while one was open for 0% -> 0% of each run, Pallas kernels for 5% -> 7%
where the time goes in v5:
time: 74.3 us; the launch traced here: 73.8 us
  waiting for transfers between devices  30.3 us (41%)
  starting transfers between devices  26.6 us (36%)
  Pallas kernels  11.5 us (15%)
  local copies, waits for them, and re-layouts  5.19 us (7%)
    all_to_all x1, waiting for transfers between devices, shards(): terms = lax.all_to_all(terms, 'head', 0, 0)  16 us
    ppermute x2, waiting for transfers between devices, swap_times(): return lax.ppermute(block, 'tile', route)  11 us
    ppermute x2, starting transfers between devices, swap_times(): return lax.ppermute(block, 'tile', route)  9.63 us
    all_to_all x1, starting transfers between devices, shards(): terms = lax.all_to_all(terms, 'head', 0, 0)  6.74 us
    ppermute x2, starting transfers between devices, swap_pair(): lax.ppermute(block, 'tile', [(tile, tile ^ 1) for tile, *_ in places()])  6.08 us
    unnamed x18, local copies, waits for them, and re-layouts  5.19 us
    ppermute x2, starting transfers between devices, swap_middle(): return lax.ppermute(block, 'tile', route)  4.17 us
    pallas_call x4, Pallas kernels, attend(): pl.pallas_call(functools.partial(attend_kernel, stage, places), out_shape...  3.98 us
  transfers between devices with their start and end apart: 7, of which 3 were waited for; matrix products, arithmetic and copies ran while one was open for 0% of the time, Pallas kernels for 7%

profile of v5, /device:TPU:129, one launch (start us, length us, event | category | flops | bytes accessed | tf_op | source)
XLA Modules:
  0.0 73.8 jit_solution(8744327493706557496)
XLA Ops:
  0.0 2.0 %pack.1 = (bf16[272,384]{1,0:T(8,128)(2,1)}, bf16[512,384]{1,0:T(8,128)(2,1)}) custom-call(s32[1,3]{1,0:T(1,128)} %windows_ref.1, bf16[256,384]{1,0:T(8,128)(2,1)} %q_ref.1, bf16[256,384]{1,0:T(8,128)(2,1)} %k_ref.1, bf16[256,384]{1,0:T(8,128)(2,1)} %v_ref.1), custom_call_target="tpu_custom_call" | custom-call | tf_op jit(solution)/shard_map/pack/pallas_call | solution.py:66
  2.0 4.1 %collective-permute-start.2 = (bf16[512,384]{1,0:T(8,128)(2,1)}, bf16[512,384]{1,0:T(8,128)(2,1)S(1)}, u32[]{:S(2)}, u32[]{:S(2)}) collective-permute-start(bf16[512,384]{1,0:T(8,128)(2,1)} %get-tuple-element.15.refs_2_.own_ref), channel_id=1, source_target_pairs={{16,48},{24,56},{32,64},{40,72},{48,16},{56,24},{64,32},{72,40},{8... | collective-permute-start | bytes 1179656 | tf_op jit(solution)/shard_map/ppermute | solution.py:40
  6.0 5.6 %collective-permute-start.1 = (bf16[512,384]{1,0:T(8,128)(2,1)}, bf16[512,384]{1,0:T(8,128)(2,1)S(1)}, u32[]{:S(2)}, u32[]{:S(2)}) collective-permute-start(bf16[512,384]{1,0:T(8,128)(2,1)} %get-tuple-element.15.refs_2_.own_ref), channel_id=1, source_target_pairs={{0,32},{8,40},{32,0},{40,8},{48,80},{56,88},{64,96},{72,104},{80,4... | collective-permute-start | bytes 1179656 | tf_op jit(solution)/shard_map/ppermute | solution.py:40
  11.6 3.1 %collective-permute-start = (bf16[272,384]{1,0:T(8,128)(2,1)}, bf16[272,384]{1,0:T(8,128)(2,1)S(1)}, u32[]{:S(2)}, u32[]{:S(2)}) collective-permute-start(bf16[272,384]{1,0:T(8,128)(2,1)} %get-tuple-element.14.refs_0_), channel_id=1, source_target_pairs={{0,8},{8,0},{16,24},{24,16},{32,40},{40,32},{48,56},{56,48},{64,72... | collective-permute-start | bytes 626696 | tf_op jit(solution)/shard_map/ppermute | solution.py:44
  14.8 1.9 %collective-permute-start.4 = (bf16[272,384]{1,0:T(8,128)(2,1)}, bf16[272,384]{1,0:T(8,128)(2,1)S(1)}, u32[]{:S(2)}, u32[]{:S(2)}) collective-permute-start(bf16[272,384]{1,0:T(8,128)(2,1)} %get-tuple-element.14.refs_0_), channel_id=1, source_target_pairs={{8,16},{16,8},{40,48},{48,40},{72,80},{80,72},{104,112},{112,104},... | collective-permute-start | bytes 626696 | tf_op jit(solution)/shard_map/ppermute | solution.py:49
  16.7 0.0 collective-permute-done.refs_1_
  16.7 0.0 copy-start
  16.7 0.9 %copy-done = bf16[272,384]{1,0:T(8,128)(2,1)S(1)} copy-done((bf16[272,384]{1,0:T(8,128)(2,1)S(1)}, bf16[272,384]{1,0:T(8,128)(2,1)}, u32[]{:S(2)}) %copy-start) | copy-done | bytes 208920
  17.7 1.7 %copy-done.2 = bf16[384,3072]{1,0:T(8,128)(2,1)S(1)} copy-done((bf16[384,3072]{1,0:T(8,128)(2,1)S(1)}, bf16[384,3072]{1,0:T(8,128)(2,1)}, u32[]{:S(2)}) %copy-start.2) | copy-done | bytes 2359320
  19.3 1.0 %copy-done.3 = bf16[512,384]{1,0:T(8,128)(2,1)S(1)} copy-done((bf16[512,384]{1,0:T(8,128)(2,1)S(1)}, bf16[512,384]{1,0:T(8,128)(2,1)}, u32[]{:S(2)}) %copy-start.3) | copy-done | bytes 393240
  20.3 1.1 %attend_own0_1.1 = (f32[6,256,128]{2,1,0:T(8,128)S(1)}, f32[12,256,128]{2,1,0:T(8,128)S(1)}, bf16[384,3072]{1,0:T(8,128)(2,1)S(1)}) custom-call(bf16[272,384]{1,0:T(8,128)(2,1)S(1)} %copy-done, bf16[272,384]{1,0:T(8,128)(2,1)S(1)} %collective-permute-done.refs_1_, bf16[512,384]{1,0:T(8,128)(2,1)S(1)} %copy-done.3, bf16[384,3072]{1,0:T(8,128)(2,1)S(1)} %copy-done.2), custom_call_target="tpu_custom_call" | custom-call | flops 201326592 | bytes 2000000 | tf_op jit(solution)/shard_map/attend_own0_1/pallas_call | solution.py:188
  21.5 11.0 %collective-permute-done.2.refs_2_.first_ref = bf16[512,384]{1,0:T(8,128)(2,1)S(1)} collective-permute-done((bf16[512,384]{1,0:T(8,128)(2,1)}, bf16[512,384]{1,0:T(8,128)(2,1)S(1)}, u32[]{:S(2)}, u32[]{:S(2)}) %collective-permute-start.2) | collective-permute-done | bytes 393248 | tf_op jit(solution)/shard_map/ppermute | solution.py:40
  32.5 1.1 %attend_first0_1.1 = (f32[6,256,128]{2,1,0:T(8,128)S(1)}, f32[12,256,128]{2,1,0:T(8,128)S(1)}) custom-call(bf16[272,384]{1,0:T(8,128)(2,1)S(1)} %copy-done, bf16[272,384]{1,0:T(8,128)(2,1)S(1)} %collective-permute-done.refs_1_, bf16[512,384]{1,0:T(8,128)(2,1)S(1)} %collective-permute-done.2.refs_2_.first_ref, f32[6,256,128]{2,1,0:T(8,128)S(1)} %get-tuple-element.16.refs_3_, ...), custom_call_target="tpu_custom_call" | custom-call | flops 201326592 | bytes 2000000 | tf_op jit(solution)/shard_map/attend_first0_1/pallas_call | solution.py:188
  33.6 0.0 collective-permute-done.1.refs_2_.second_ref
  33.6 0.0 copy-start.4
  33.7 0.8 %attend_second1.1.after_ref = bf16[272,384]{1,0:T(8,128)(2,1)S(1)} custom-call(bf16[272,384]{1,0:T(8,128)(2,1)S(1)} %copy-done, bf16[272,384]{1,0:T(8,128)(2,1)S(1)} %collective-permute-done.refs_1_, bf16[512,384]{1,0:T(8,128)(2,1)S(1)} %collective-permute-done.1.refs_2_.second_ref, f32[6,256,128]{2,1,0:T(8,128)S(1)} %get-tuple-element.18.refs_3_, ...), custom_call_target="tpu_custom_call" | custom-call | flops 100663296 | bytes 2000000 | tf_op jit(solution)/shard_map/attend_second1/pallas_call | solution.py:188
  34.5 2.9 %collective-permute-start.3 = (bf16[272,384]{1,0:T(8,128)(2,1)S(1)}, bf16[272,384]{1,0:T(8,128)(2,1)S(1)}, u32[]{:S(2)}, u32[]{:S(2)}) collective-permute-start(bf16[272,384]{1,0:T(8,128)(2,1)S(1)} %attend_second1.1.after_ref), channel_id=1, source_target_pairs={{0,8},{8,0},{16,24},{24,16},{32,40},{40,32},{48,56},{56,48},{64,72... | collective-permute-start | bytes 626696 | tf_op jit(solution)/shard_map/ppermute | solution.py:44
  37.4 0.0 collective-permute-done.4.query_ref
  37.5 0.0 copy-done.4
  37.5 1.5 %attend_middle.1 = bf16[272,384]{1,0:T(8,128)(2,1)S(1)} custom-call(bf16[272,384]{1,0:T(8,128)(2,1)S(1)} %collective-permute-done.4.query_ref, bf16[512,384]{1,0:T(8,128)(2,1)S(1)} %copy-done.4, bf16[512,384]{1,0:T(8,128)(2,1)S(1)} %collective-permute-done.2.refs_2_.first_ref, bf16[512,384]{1,0:T(8,128)(2,1)S(1)} %collective-permute-done.1.refs_2_.second_ref, ...), custom_call_target="tpu_custom_call" | custom-call | flops 301989888 | bytes 2000000 | tf_op jit(solution)/shard_map/attend_middle/pallas_call | solution.py:251
  39.0 2.2 %collective-permute-start.5 = (bf16[272,384]{1,0:T(8,128)(2,1)S(1)}, bf16[272,384]{1,0:T(8,128)(2,1)S(1)}, u32[]{:S(2)}, u32[]{:S(2)}) collective-permute-start(bf16[272,384]{1,0:T(8,128)(2,1)S(1)} %attend_middle.1), channel_id=1, source_target_pairs={{8,16},{16,8},{40,48},{48,40},{72,80},{80,72},{104,112},{112,104},... | collective-permute-start | bytes 626696 | tf_op jit(solution)/shard_map/ppermute | solution.py:49
  41.3 0.0 copy-done.1
  41.3 0.8 %attend_second0.1 = (f32[256,384]{1,0:T(8,128)S(1)}, f32[3,8,256]{2,1,0:T(8,128)S(1)}) custom-call(bf16[272,384]{1,0:T(8,128)(2,1)S(1)} %copy-done.1, bf16[272,384]{1,0:T(8,128)(2,1)S(1)} %collective-permute-done.refs_1_, bf16[512,384]{1,0:T(8,128)(2,1)S(1)} %collective-permute-done.1.refs_2_.second_ref, f32[6,256,128]{2,1,0:T(8,128)S(1)} %get-tuple-element.18.refs_3_, ...), custom_call_target="tpu_custom_call" | custom-call | flops 100663296 | bytes 2000000 | tf_op jit(solution)/shard_map/attend_second0/pallas_call | solution.py:188
  42.1 0.0 collective-permute-done.3.in_ref
  42.1 0.0 copy-start.5
  42.2 0.7 copy-done.5
  42.8 3.3 %collective-permute-done.5.middle_ref = bf16[272,384]{1,0:T(8,128)(2,1)S(1)} collective-permute-done((bf16[272,384]{1,0:T(8,128)(2,1)S(1)}, bf16[272,384]{1,0:T(8,128)(2,1)S(1)}, u32[]{:S(2)}, u32[]{:S(2)}) %collective-permute-start.5) | collective-permute-done | bytes 208928 | tf_op jit(solution)/shard_map/ppermute | solution.py:49
  46.1 0.9 %copy-done.6 = bf16[272,384]{1,0:T(8,128)(2,1)S(1)} copy-done((bf16[272,384]{1,0:T(8,128)(2,1)S(1)}, bf16[272,384]{1,0:T(8,128)(2,1)}, u32[]{:S(2)}) %copy-start.6) | copy-done | bytes 208920
  47.1 2.9 %project.1 = bf16[8,256,384]{2,1,0:T(8,128)(2,1)} custom-call(f32[256,384]{1,0:T(8,128)S(1)} %get-tuple-element.20.own_ref, f32[3,8,256]{2,1,0:T(8,128)S(1)} %get-tuple-element.21.stats_ref, bf16[272,384]{1,0:T(8,128)(2,1)S(1)} %copy-done.6, bf16[272,384]{1,0:T(8,128)(2,1)S(1)} %collective-permute-done.5.middle_ref, ...), custom_call_target="tpu_custom_call" | custom-call | flops 603979776 | bytes 5000000 | tf_op jit(solution)/shard_map/project/pallas_call | solution.py:307
  50.0 6.7 %all-to-all-start = ((bf16[8,256,384]{2,1,0:T(8,128)(2,1)}), bf16[8,256,384]{2,1,0:T(8,128)(2,1)S(1)}, u32[]{:S(2)}, u32[]{:S(2)}) async-start(bf16[8,256,384]{2,1,0:T(8,128)(2,1)} %project.1), calls=%async_computation | async-start | bytes 3145728 | tf_op jit(solution)/shard_map/all_to_all | solution.py:354
  56.7 16.0 %all-to-all-done.terms_ref = bf16[8,256,384]{2,1,0:T(8,128)(2,1)S(1)} async-done(((bf16[8,256,384]{2,1,0:T(8,128)(2,1)}), bf16[8,256,384]{2,1,0:T(8,128)(2,1)S(1)}, u32[]{:S(2)}, u32[]{:S(2)}) %all-to-all-start) | async-done | bytes 1572896 | tf_op jit(solution)/shard_map/all_to_all | solution.py:354
  72.7 1.1 %finish.1 = bf16[256,384]{1,0:T(8,128)(2,1)} custom-call(bf16[8,256,384]{2,1,0:T(8,128)(2,1)S(1)} %all-to-all-done.terms_ref, bf16[256,384]{1,0:T(8,128)(2,1)S(1)} %copy-done.7, f32[1,384]{1,0:T(1,128)S(1)} %reshape.3.gate_ref), custom_call_target="tpu_custom_call" | custom-call | flops 7864320 | bytes 2000000 | tf_op jit(solution)/shard_map/finish/pallas_call | solution.py:327
  (10 shorter events, 0.0 us)
Async XLA Ops:
  2.0 30.5 %collective-permute-start.2 = (bf16[512,384]{1,0:T(8,128)(2,1)}, bf16[512,384]{1,0:T(8,128)(2,1)S(1)}, u32[]{:S(2)}, u32[]{:S(2)}) collective-permute-start(bf16[512,384]{1,0:T(8,128)(2,1)} %get-tuple-element.15.refs_2_.own_ref), channel_id=1, source_target_pairs={{16,48},{24,56},{32,64},{40,72},{48,16},{56,24},{64,32},{72,40},{8... | collective-permute-start | bytes 1179656 | tf_op jit(solution)/shard_map/ppermute | solution.py:40
  6.0 27.6 %collective-permute-start.1 = (bf16[512,384]{1,0:T(8,128)(2,1)}, bf16[512,384]{1,0:T(8,128)(2,1)S(1)}, u32[]{:S(2)}, u32[]{:S(2)}) collective-permute-start(bf16[512,384]{1,0:T(8,128)(2,1)} %get-tuple-element.15.refs_2_.own_ref), channel_id=1, source_target_pairs={{0,32},{8,40},{32,0},{40,8},{48,80},{56,88},{64,96},{72,104},{80,4... | collective-permute-start | bytes 1179656 | tf_op jit(solution)/shard_map/ppermute | solution.py:40
  11.6 5.1 %collective-permute-start = (bf16[272,384]{1,0:T(8,128)(2,1)}, bf16[272,384]{1,0:T(8,128)(2,1)S(1)}, u32[]{:S(2)}, u32[]{:S(2)}) collective-permute-start(bf16[272,384]{1,0:T(8,128)(2,1)} %get-tuple-element.14.refs_0_), channel_id=1, source_target_pairs={{0,8},{8,0},{16,24},{24,16},{32,40},{40,32},{48,56},{56,48},{64,72... | collective-permute-start | bytes 626696 | tf_op jit(solution)/shard_map/ppermute | solution.py:44
  14.8 22.7 %collective-permute-start.4 = (bf16[272,384]{1,0:T(8,128)(2,1)}, bf16[272,384]{1,0:T(8,128)(2,1)S(1)}, u32[]{:S(2)}, u32[]{:S(2)}) collective-permute-start(bf16[272,384]{1,0:T(8,128)(2,1)} %get-tuple-element.14.refs_0_), channel_id=1, source_target_pairs={{8,16},{16,8},{40,48},{48,40},{72,80},{80,72},{104,112},{112,104},... | collective-permute-start | bytes 626696 | tf_op jit(solution)/shard_map/ppermute | solution.py:49
  16.7 0.9 %copy-start = (bf16[272,384]{1,0:T(8,128)(2,1)S(1)}, bf16[272,384]{1,0:T(8,128)(2,1)}, u32[]{:S(2)}) copy-start(bf16[272,384]{1,0:T(8,128)(2,1)} %get-tuple-element.14.refs_0_) | copy-start | bytes 626692
  17.7 1.7 %copy-start.2 = (bf16[384,3072]{1,0:T(8,128)(2,1)S(1)}, bf16[384,3072]{1,0:T(8,128)(2,1)}, u32[]{:S(2)}) copy-start(bf16[384,3072]{1,0:T(8,128)(2,1)} %refs_3_.1) | copy-start | bytes 7077892
  19.3 1.0 %copy-start.3 = (bf16[512,384]{1,0:T(8,128)(2,1)S(1)}, bf16[512,384]{1,0:T(8,128)(2,1)}, u32[]{:S(2)}) copy-start(bf16[512,384]{1,0:T(8,128)(2,1)} %get-tuple-element.15.refs_2_.own_ref) | copy-start | bytes 1179652
  33.6 3.8 %copy-start.4 = (bf16[512,384]{1,0:T(8,128)(2,1)S(1)}, bf16[512,384]{1,0:T(8,128)(2,1)}, u32[]{:S(2)}) copy-start(bf16[512,384]{1,0:T(8,128)(2,1)} %get-tuple-element.15.refs_2_.own_ref) | copy-start | bytes 1179652
  34.5 6.8 %copy-start.1 = (bf16[272,384]{1,0:T(8,128)(2,1)S(1)}, bf16[272,384]{1,0:T(8,128)(2,1)}, u32[]{:S(2)}) copy-start(bf16[272,384]{1,0:T(8,128)(2,1)} %get-tuple-element.14.refs_0_) | copy-start | bytes 626692
  34.5 7.6 %collective-permute-start.3 = (bf16[272,384]{1,0:T(8,128)(2,1)S(1)}, bf16[272,384]{1,0:T(8,128)(2,1)S(1)}, u32[]{:S(2)}, u32[]{:S(2)}) collective-permute-start(bf16[272,384]{1,0:T(8,128)(2,1)S(1)} %attend_second1.1.after_ref), channel_id=1, source_target_pairs={{0,8},{8,0},{16,24},{24,16},{32,40},{40,32},{48,56},{56,48},{64,72... | collective-permute-start | bytes 626696 | tf_op jit(solution)/shard_map/ppermute | solution.py:44
  39.0 7.1 %collective-permute-start.5 = (bf16[272,384]{1,0:T(8,128)(2,1)S(1)}, bf16[272,384]{1,0:T(8,128)(2,1)S(1)}, u32[]{:S(2)}, u32[]{:S(2)}) collective-permute-start(bf16[272,384]{1,0:T(8,128)(2,1)S(1)} %attend_middle.1), channel_id=1, source_target_pairs={{8,16},{16,8},{40,48},{48,40},{72,80},{80,72},{104,112},{112,104},... | collective-permute-start | bytes 626696 | tf_op jit(solution)/shard_map/ppermute | solution.py:49
  42.1 0.7 copy-start.5
  46.1 0.9 %copy-start.6 = (bf16[272,384]{1,0:T(8,128)(2,1)S(1)}, bf16[272,384]{1,0:T(8,128)(2,1)}, u32[]{:S(2)}) copy-start(bf16[272,384]{1,0:T(8,128)(2,1)} %gate.1.pair_ref) | copy-start | bytes 626692
  50.0 6.7 %copy-start.8 = (f32[384]{0:T(512)S(1)}, f32[384]{0:T(512)}, u32[]{:S(2)}) copy-start(f32[384]{0:T(512)} %param.13) | copy-start | bytes 4612
  50.0 22.8 %copy-start.7 = (bf16[256,384]{1,0:T(8,128)(2,1)S(1)}, bf16[256,384]{1,0:T(8,128)(2,1)}, u32[]{:S(2)}) copy-start(bf16[256,384]{1,0:T(8,128)(2,1)} %residual_ref.1) | copy-start | bytes 589828
  50.0 22.7 %all-to-all-start = ((bf16[8,256,384]{2,1,0:T(8,128)(2,1)}), bf16[8,256,384]{2,1,0:T(8,128)(2,1)S(1)}, u32[]{:S(2)}, u32[]{:S(2)}) async-start(bf16[8,256,384]{2,1,0:T(8,128)(2,1)} %project.1), calls=%async_computation | async-start | bytes 3145728 | tf_op jit(solution)/shard_map/all_to_all | solution.py:354

commit v6 on v5

--- a/solution.py
+++ b/solution.py
@@ -47,6 +47,38 @@
 def swap_middle(block):
     route = [(tile, tile + (1 if height == 1 else -1)) for tile, _, height, _ in places() if height in (1, 2)]
     return lax.ppermute(block, "tile", route)
+
+
+def shift_columns(block, step):
+    count = lax.axis_size("head")
+    return lax.ppermute(block, "head", [(i, (i + 2 * step) % count) for i in range(count)])
+
+
+def swap_depth(block):
+    return lax.ppermute(block, "head", [(i, i ^ 1) for i in range(lax.axis_size("head"))])
+
+
+def split_weight_kernel(weight_ref, *out_refs):
+    width = out_refs[0].shape[1]
+    mine = lax.axis_index("head") // 2
+    for step, ref in enumerate(out_refs):
+        start = pl.multiple_of(lax.rem(mine + step, len(out_refs)) * width, HD)
+        ref[...] = weight_ref[:, pl.ds(start, width)]
+
+
+def split_weight(out_weight):
+    rows, features = out_weight.shape
+    parts = lax.axis_size("head") // 2
+    whole = pl.BlockSpec(memory_space=VMEM)
+    return pl.pallas_call(
+        split_weight_kernel,
+        out_shape=(jax.ShapeDtypeStruct((rows, features // parts), out_weight.dtype),) * parts,
+        in_specs=[whole],
+        out_specs=(whole,) * parts,
+        compiler_params=params(24),
+        cost_estimate=pl.CostEstimate(flops=0, bytes_accessed=0, transcendentals=0),
+        name="split_weight",
+    )(out_weight)
 
 
 def pack_kernel(windows_ref, q_ref, k_ref, v_ref, packed_ref, block_ref):
@@ -113,15 +145,28 @@
     ref[rows:, low : low + HD] = jnp.concatenate([side[:, :HD], side[:, HD:]], axis=0).astype(ref.dtype)
 
 
+def message_stats(ref, head, rows):
+    side = ref[rows:, head * HD : (head + 1) * HD].astype(jnp.float32)
+    side = jnp.concatenate([side[:8], side[8:]], axis=1)
+    return side[0:1] + side[1:2] + side[2:3], side[3:4] + side[4:5] + side[5:6]
+
+
+def message_columns(ref, head, rows):
+    line = lax.broadcasted_iota(jnp.int32, (8, rows), 0)
+    largest, total = message_stats(ref, head, rows)
+    columns = jnp.transpose(jnp.where(line == 0, largest, jnp.where(line == 1, total, 0.0)))
+    return [jnp.broadcast_to(column(columns, index), (rows, HD)) for index in (0, 1)]
+
+
 def attend_kernel(stage, places, *refs):
     query_refs, block_ref, refs = refs[:2], refs[2], refs[3:]
-    if stage == 0:
-        weight_ref, refs, held_ref, sem = refs[0], refs[1:3], refs[3], refs[4]
-        copy = pltpu.make_async_copy(weight_ref, held_ref, sem)
-        copy.start()
     if stage > 0:
         old_mix_ref, old_stats_ref = refs[:2]
         refs = refs[2:]
+    if stage == 1:
+        refs = refs[-2:]
+    if places == (0,):
+        message_ref, refs = refs[0], refs[-2:]
     rows, width = block_ref.shape[0] // 2, block_ref.shape[1]
     scale = HD**-0.5 * LOG2E
     lane = lax.broadcasted_iota(jnp.int32, (rows, HD), 1)
@@ -152,21 +197,27 @@
                 refs[1][2 * index] = largest
                 refs[1][2 * index + 1] = total
                 continue
+            if place == 0:
+                wide = wide_window(ref, rows, 1)
+                their_largest, their_total = message_columns(message_ref, head, rows)
+                peak = jnp.maximum(largest, jnp.where(wide, their_largest, MASKED))
+                shrink, share = jnp.exp2(largest - peak), jnp.where(wide, jnp.exp2(their_largest - peak), 0.0)
+                largest, total = peak, total * shrink + their_total * share
+                mix = mix * shrink + message_ref[:rows, low : low + HD].astype(jnp.float32) * share
             stats = jnp.transpose(jnp.where(lane == 0, largest, jnp.where(lane == 1, total, 0.0)))[:8]
             if place == 0:
                 refs[0][:, low : low + HD] = mix
                 line = lax.broadcasted_iota(jnp.int32, stats.shape, 0)
-                refs[1][head] = jnp.where(line == 2, jnp.where(wide_window(ref, rows, 1), 1.0, 0.0), stats)
+                refs[1][head] = jnp.where(line == 2, jnp.where(wide, 1.0, 0.0), stats)
             else:
                 put_message(refs[0], head, mix, stats, 0)
-    if stage == 0:
-        copy.wait()
-
-
-def attend(stage, queries, block, before=(), places=(0, 1), out_weight=None):
+
+
+def attend(stage, queries, block, before=(), places=(0, 1), message=(), after=()):
     rows, width = block.shape[0] // 2, block.shape[1]
     heads = width // HD
     whole = pl.BlockSpec(memory_space=VMEM)
+    flops = 4 * HD * len(places) * heads * rows * rows
     if stage < 2:
         out_shape = (
             jax.ShapeDtypeStruct((2 * heads, rows, HD), jnp.float32),
@@ -177,41 +228,18 @@
             jax.ShapeDtypeStruct((rows, width), jnp.float32),
             jax.ShapeDtypeStruct((heads, 8, rows), jnp.float32),
         )
+        flops = 3_500_000_000
     else:
         out_shape = (jax.ShapeDtypeStruct((rows + SIDE, width), jnp.bfloat16),)
-    cost = len(places) * heads * rows * rows
-    extra, extra_specs, scratch = (), [], []
-    if stage == 0:
-        extra, extra_specs = (out_weight,), [pl.BlockSpec(memory_space=pl.ANY)]
-        out_shape += (jax.ShapeDtypeStruct(out_weight.shape, out_weight.dtype),)
-        scratch = [pltpu.SemaphoreType.DMA]
     return pl.pallas_call(
         functools.partial(attend_kernel, stage, places),
         out_shape=out_shape,
-        in_specs=[whole] * 3 + extra_specs + [whole] * len(before),
+        in_specs=[whole] * (3 + len(before) + len(message)) + [pl.BlockSpec(memory_space=pl.ANY)] * len(after),
         out_specs=(whole,) * len(out_shape),
-        scratch_shapes=scratch,
-        compiler_params=params(24),
-        cost_estimate=pl.CostEstimate(flops=4 * HD * cost, bytes_accessed=2_000_000, transcendentals=cost),
+        compiler_params=params(24),
+        cost_estimate=pl.CostEstimate(flops=flops, bytes_accessed=2_000_000, transcendentals=len(places) * heads * rows * rows),
         name=("attend_own", "attend_first", "attend_second")[stage] + "_".join(map(str, places)),
-    )(*queries, block, *extra, *before)
-
-
-def gate_kernel(in_ref, out_ref):
-    pass
-
-
-def gate(array):
-    anywhere = pl.BlockSpec(memory_space=pl.ANY)
-    return pl.pallas_call(
-        gate_kernel,
-        out_shape=jax.ShapeDtypeStruct(array.shape, array.dtype),
-        in_specs=[anywhere],
-        out_specs=anywhere,
-        input_output_aliases={0: 0},
-        cost_estimate=pl.CostEstimate(flops=3_500_000_000, bytes_accessed=0, transcendentals=0),
-        name="gate",
-    )(array)
+    )(*queries, block, *before, *message, *after)
 
 
 def middle_kernel(query_ref, own_ref, first_ref, second_ref, after_ref, out_ref):
@@ -259,100 +287,102 @@
     )(query, own, first, second, after)
 
 
-def merge_shares(stats_ref, pair_ref, middle_ref, rows, heads):
+def merge_kernel(own_ref, stats_ref, middle_ref, out_ref):
+    rows, width = own_ref.shape
     height = lax.axis_index("tile") % HEIGHT_TILES
     inside = jnp.where((height > 0) & (height < HEIGHT_TILES - 1), 1.0, 0.0)
-    line = lax.broadcasted_iota(jnp.int32, (16, rows), 0)
-    shares = jnp.zeros((16, rows), jnp.float32)
-    for head in range(heads):
+    line = lax.broadcasted_iota(jnp.int32, (8, rows), 0)
+    shares = jnp.zeros((8, rows), jnp.float32)
+    for head in range(width // HD):
+        stats = stats_ref[head]
+        their_largest, their_total = message_stats(middle_ref, head, rows)
+        valid = stats[2:3] * inside > 0.5
+        peak = jnp.maximum(stats[0:1], jnp.where(valid, their_largest, MASKED))
+        shrink = jnp.exp2(stats[0:1] - peak)
+        share = jnp.where(valid, jnp.exp2(their_largest - peak), 0.0)
+        whole = stats[1:2] * shrink + their_total * share
+        shares = jnp.where(line == 2 * head, shrink / whole, shares)
+        shares = jnp.where(line == 2 * head + 1, share / whole, shares)
+    shares = jnp.transpose(shares)
+    for head in range(width // HD):
         low = head * HD
-        stats = stats_ref[head]
-        largest, total = [stats[0:1]], [stats[1:2]]
-        wide = stats[2:3]
-        for ref, flag in ((pair_ref, wide > 0.5), (middle_ref, wide * inside > 0.5)):
-            side = ref[rows:, low : low + HD].astype(jnp.float32)
-            side = jnp.concatenate([side[:8], side[8:]], axis=1)
-            largest.append(jnp.where(flag, side[0:1] + side[1:2] + side[2:3], MASKED))
-            total.append(jnp.where(flag, side[3:4] + side[4:5] + side[5:6], 0.0))
-        peak = jnp.maximum(jnp.maximum(largest[0], largest[1]), largest[2])
-        factors = [jnp.exp2(value - peak) for value in largest]
-        whole = total[0] * factors[0] + total[1] * factors[1] + total[2] * factors[2]
-        for index, factor in enumerate(factors):
-            shares = jnp.where(line == 3 * head + index, factor / whole, shares)
-    return jnp.transpose(shares)
-
-
-def project_kernel(own_ref, stats_ref, pair_ref, middle_ref, weight_ref, out_ref):
-    rows, width = own_ref.shape
-    heads = width // HD
-    shares = merge_shares(stats_ref, pair_ref, middle_ref, rows, heads)
-    merged = []
-    for head in range(heads):
-        low = head * HD
-        value = own_ref[:, low : low + HD] * column(shares, 3 * head)
-        for index, ref in enumerate((pair_ref, middle_ref)):
-            value += ref[:rows, low : low + HD].astype(jnp.float32) * column(shares, 3 * head + 1 + index)
-        merged.append(value.astype(jnp.bfloat16))
-    attention = jnp.concatenate(merged, axis=1)
-    for group in range(out_ref.shape[0]):
-        out_ref[group] = jnp.dot(
-            attention, weight_ref[:, group * width : (group + 1) * width], preferred_element_type=jnp.float32
-        ).astype(out_ref.dtype)
-
-
-def project(own, stats, pair, middle, out_weight):
-    rows, width = own.shape
-    features = out_weight.shape[1]
+        value = own_ref[:, low : low + HD] * column(shares, 2 * head)
+        value += middle_ref[:rows, low : low + HD].astype(jnp.float32) * column(shares, 2 * head + 1)
+        out_ref[:, low : low + HD] = value.astype(out_ref.dtype)
+
+
+def merge(own, stats, middle):
+    whole = pl.BlockSpec(memory_space=VMEM)
+    return pl.pallas_call(
+        merge_kernel,
+        out_shape=jax.ShapeDtypeStruct(own.shape, jnp.bfloat16),
+        in_specs=[whole] * 3,
+        out_specs=whole,
+        compiler_params=params(24),
+        name="merge",
+    )(own, stats, middle)
+
+
+def project_kernel(*refs):
+    parts = (len(refs) - 2) // 2
+    attention_refs, weight_refs, (mine_ref, other_ref) = refs[:parts], refs[parts:-2], refs[-2:]
+    width = mine_ref.shape[1]
+    depth = lax.rem(lax.axis_index("head"), 2)
+    for ref, place in ((other_ref, 1 - depth), (mine_ref, depth)):
+        start = pl.multiple_of(place * width, HD)
+        total = jnp.zeros(mine_ref.shape, jnp.float32)
+        for attention_ref, weight_ref in zip(attention_refs, weight_refs):
+            total += jnp.dot(attention_ref[...], weight_ref[:, pl.ds(start, width)], preferred_element_type=jnp.float32)
+        ref[...] = total.astype(ref.dtype)
+
+
+def project(attention, weights):
+    shape = attention[0].shape
     whole = pl.BlockSpec(memory_space=VMEM)
     return pl.pallas_call(
         project_kernel,
-        out_shape=jax.ShapeDtypeStruct((features // width, rows, width), jnp.bfloat16),
-        in_specs=[whole] * 5,
+        out_shape=(jax.ShapeDtypeStruct(shape, jnp.float32), jax.ShapeDtypeStruct(shape, jnp.bfloat16)),
+        in_specs=[whole] * (len(attention) + len(weights)),
+        out_specs=(whole, whole),
+        compiler_params=params(24),
+        name="project",
+    )(*attention, *weights)
+
+
+def finish_kernel(mine_ref, other_ref, residual_ref, gate_ref, out_ref):
+    total = mine_ref[...] + other_ref[...].astype(jnp.float32)
+    out_ref[...] = (residual_ref[...].astype(jnp.float32) + gate_ref[...] * total).astype(out_ref.dtype)
+
+
+def finish(mine, other, residual, gate_scale):
+    whole = pl.BlockSpec(memory_space=VMEM)
+    return pl.pallas_call(
+        finish_kernel,
+        out_shape=jax.ShapeDtypeStruct(residual.shape, residual.dtype),
+        in_specs=[whole] * 4,
         out_specs=whole,
         compiler_params=params(24),
-        cost_estimate=pl.CostEstimate(flops=2 * rows * width * features, bytes_accessed=5_000_000, transcendentals=0),
-        name="project",
-    )(own, stats, pair, middle, out_weight)
-
-
-def finish_kernel(terms_ref, residual_ref, gate_ref, out_ref):
-    total = jnp.sum(terms_ref[...].astype(jnp.float32), axis=0)
-    out_ref[...] = (residual_ref[...].astype(jnp.float32) + gate_ref[...] * total).astype(out_ref.dtype)
-
-
-def finish(terms, residual, gate_scale):
-    groups, rows, width = terms.shape
-    steps = 2
-    part = rows // steps
-    return pl.pallas_call(
-        finish_kernel,
-        grid=(steps,),
-        out_shape=jax.ShapeDtypeStruct((rows, width), residual.dtype),
-        in_specs=[
-            pl.BlockSpec((groups, part, width), lambda step: (0, step, 0)),
-            pl.BlockSpec((part, width), lambda step: (step, 0)),
-            pl.BlockSpec((1, width), lambda step: (0, 0)),
-        ],
-        out_specs=pl.BlockSpec((part, width), lambda step: (step, 0)),
-        compiler_params=params(24),
-        cost_estimate=pl.CostEstimate(flops=10 * groups * rows * width, bytes_accessed=2_000_000, transcendentals=0),
         name="finish",
-    )(terms, residual, gate_scale.reshape(1, width))
+    )(mine, other, residual, gate_scale.reshape(1, -1))
 
 
 def shards(queries, key_rows, value_rows, windows, residual, out_weight, gate_scale):
     packed, block = pack(windows, queries, key_rows, value_rows)
     first, second = swap_times(block, False), swap_times(block, True)
     asked = (packed, swap_pair(packed))
-    *before, held_weight = attend(0, asked, block, out_weight=out_weight)
-    before = attend(1, asked, first, before)
+    weight, *to_send = split_weight(out_weight)
+    steps = range(1, len(to_send) + 1)
+    weights = [shift_columns(part, step) for step, part in zip(steps, to_send)]
+    middle_asks = swap_middle(packed)
+    before = attend(0, asked, block)
+    before = attend(1, asked, first, before, after=(middle_asks,))
     (for_pair,) = attend(2, asked, second, before, (1,))
-    for_middle = attend_middle(swap_middle(packed), block, first, second, for_pair)
-    own, stats = attend(2, asked, second, before, (0,))
-    from_pair = gate(swap_pair(for_pair))
-    terms = project(own, stats, from_pair, swap_middle(for_middle), held_weight)
-    terms = lax.all_to_all(terms, "head", 0, 0)
-    return finish(terms, residual, gate_scale)
+    for_middle = attend_middle(middle_asks, block, first, second, for_pair)
+    own, stats = attend(2, asked, second, before, (0,), (swap_pair(for_pair),), weights)
+    attention = merge(own, stats, swap_middle(for_middle))
+    gathered = [shift_columns(attention, step) for step in steps]
+    mine, other = project([attention, *gathered], [weight, *weights])
+    return finish(mine, swap_depth(other), residual, gate_scale)
 
 
 def solution(mesh):

time: 74.3 us -> 82.5 us (1.11)
  the two profiles are of different devices: /device:TPU:129 before, /device:TPU:128 now
where the time goes in v6:
time: 82.5 us; the launch traced here: 82 us
  starting transfers between devices  42.7 us (52%)
  waiting for transfers between devices  28.1 us (34%)
  Pallas kernels  9.25 us (11%)
  local copies, waits for them, and re-layouts  1.68 us (2%)
    ppermute x6, starting transfers between devices, shift_columns(): lax.ppermute(block, 'head', [(i, (i + 2 * step) % count) for i in range(c...  22.5 us
    ppermute x6, waiting for transfers between devices, shift_columns(): lax.ppermute(block, 'head', [(i, (i + 2 * step) % count) for i in range(c...  17.4 us
    ppermute x2, starting transfers between devices, swap_times(): return lax.ppermute(block, 'tile', route)  10.2 us
    ppermute x2, waiting for transfers between devices, swap_times(): return lax.ppermute(block, 'tile', route)  7.07 us
    pallas_call x4, Pallas kernels, attend(): pl.pallas_call(functools.partial(attend_kernel, stage, places), out_shape...  4.68 us
    ppermute x2, starting transfers between devices, swap_pair(): lax.ppermute(block, 'tile', [(tile, tile ^ 1) for tile, *_ in places()])  4.37 us
    ppermute x1, starting transfers between devices, swap_depth(): lax.ppermute(block, 'head', [(i, i ^ 1) for i in range(lax.axis_size('hea...  4.28 us
    ppermute x1, waiting for transfers between devices, swap_depth(): lax.ppermute(block, 'head', [(i, i ^ 1) for i in range(lax.axis_size('hea...  3.66 us
  transfers between devices with their start and end apart: 13, of which 6 were waited for; matrix products, arithmetic and copies ran while one was open for 0% of the time, Pallas kernels for 6%

profile of v6, /device:TPU:128, one launch (start us, length us, event | category | flops | bytes accessed | tf_op | source)
XLA Modules:
  0.0 82.0 jit_solution(15051874950387266543)
XLA Ops:
  0.0 2.0 %pack.1 = (bf16[272,384]{1,0:T(8,128)(2,1)}, bf16[512,384]{1,0:T(8,128)(2,1)}) custom-call(s32[1,3]{1,0:T(1,128)} %windows_ref.1, bf16[256,384]{1,0:T(8,128)(2,1)} %q_ref.1, bf16[256,384]{1,0:T(8,128)(2,1)} %k_ref.1, bf16[256,384]{1,0:T(8,128)(2,1)} %v_ref.1), custom_call_target="tpu_custom_call" | custom-call | tf_op jit(solution)/shard_map/pack/pallas_call | solution.py:98
  2.0 1.9 %collective-permute-start = (bf16[272,384]{1,0:T(8,128)(2,1)}, bf16[272,384]{1,0:T(8,128)(2,1)S(1)}, u32[]{:S(2)}, u32[]{:S(2)}) collective-permute-start(bf16[272,384]{1,0:T(8,128)(2,1)} %get-tuple-element.19.refs_0_), channel_id=1, source_target_pairs={{0,8},{8,0},{16,24},{24,16},{32,40},{40,32},{48,56},{56,48},{64,72... | collective-permute-start | bytes 626696 | tf_op jit(solution)/shard_map/ppermute | solution.py:44
  3.9 0.7 collective-permute-start.3
  4.6 4.3 %collective-permute-start.2 = (bf16[512,384]{1,0:T(8,128)(2,1)}, bf16[512,384]{1,0:T(8,128)(2,1)S(1)}, u32[]{:S(2)}, u32[]{:S(2)}) collective-permute-start(bf16[512,384]{1,0:T(8,128)(2,1)} %get-tuple-element.20.refs_2_.own_ref), channel_id=1, source_target_pairs={{16,48},{24,56},{32,64},{40,72},{48,16},{56,24},{64,32},{72,40},{8... | collective-permute-start | bytes 1179656 | tf_op jit(solution)/shard_map/ppermute | solution.py:40
  8.9 5.9 %collective-permute-start.1 = (bf16[512,384]{1,0:T(8,128)(2,1)}, bf16[512,384]{1,0:T(8,128)(2,1)S(1)}, u32[]{:S(2)}, u32[]{:S(2)}) collective-permute-start(bf16[512,384]{1,0:T(8,128)(2,1)} %get-tuple-element.20.refs_2_.own_ref), channel_id=1, source_target_pairs={{0,32},{8,40},{32,0},{40,8},{48,80},{56,88},{64,96},{72,104},{80,4... | collective-permute-start | bytes 1179656 | tf_op jit(solution)/shard_map/ppermute | solution.py:40
  14.8 0.0 copy-start
  14.8 1.7 %copy-done = bf16[384,3072]{1,0:T(8,128)(2,1)S(1)} copy-done((bf16[384,3072]{1,0:T(8,128)(2,1)S(1)}, bf16[384,3072]{1,0:T(8,128)(2,1)}, u32[]{:S(2)}) %copy-start) | copy-done | bytes 2359320
  16.5 0.2 split_weight.1
  16.6 3.5 %collective-permute-start.5 = (bf16[384,768]{1,0:T(8,128)(2,1)S(1)}, bf16[384,768]{1,0:T(8,128)(2,1)S(1)}, u32[]{:S(2)}, u32[]{:S(2)}) collective-permute-start(bf16[384,768]{1,0:T(8,128)(2,1)S(1)} %get-tuple-element.25), channel_id=1, source_target_pairs={{0,2},{1,3},{2,4},{3,5},{4,6},{5,7},{6,0},{7,1},{8,10},{9,11},{10,... | collective-permute-start | bytes 1769480 | tf_op jit(solution)/shard_map/ppermute | solution.py:54
  20.2 4.6 %collective-permute-start.6 = (bf16[384,768]{1,0:T(8,128)(2,1)S(1)}, bf16[384,768]{1,0:T(8,128)(2,1)S(1)}, u32[]{:S(2)}, u32[]{:S(2)}) collective-permute-start(bf16[384,768]{1,0:T(8,128)(2,1)S(1)} %get-tuple-element.26), channel_id=1, source_target_pairs={{0,4},{1,5},{2,6},{3,7},{4,0},{5,1},{6,2},{7,3},{8,12},{9,13},{10,... | collective-permute-start | bytes 1769480 | tf_op jit(solution)/shard_map/ppermute | solution.py:54
  24.8 3.3 %collective-permute-start.7 = (bf16[384,768]{1,0:T(8,128)(2,1)S(1)}, bf16[384,768]{1,0:T(8,128)(2,1)S(1)}, u32[]{:S(2)}, u32[]{:S(2)}) collective-permute-start(bf16[384,768]{1,0:T(8,128)(2,1)S(1)} %get-tuple-element.27), channel_id=1, source_target_pairs={{0,6},{1,7},{2,0},{3,1},{4,2},{5,3},{6,4},{7,5},{8,14},{9,15},{10,... | collective-permute-start | bytes 1769480 | tf_op jit(solution)/shard_map/ppermute | solution.py:54
  28.2 1.0 %attend_own0_1.1 = (f32[6,256,128]{2,1,0:T(8,128)S(1)}, f32[12,256,128]{2,1,0:T(8,128)S(1)}) custom-call(bf16[272,384]{1,0:T(8,128)(2,1)S(1)} %copy-done.1, bf16[272,384]{1,0:T(8,128)(2,1)S(1)} %collective-permute-done.refs_1_, bf16[512,384]{1,0:T(8,128)(2,1)S(1)} %copy-done.2), custom_call_target="tpu_custom_call" | custom-call | flops 201326592 | bytes 2000000 | tf_op jit(solution)/shard_map/attend_own0_1/pallas_call | solution.py:234
  29.2 7.1 %collective-permute-done.2.refs_2_.first_ref = bf16[512,384]{1,0:T(8,128)(2,1)S(1)} collective-permute-done((bf16[512,384]{1,0:T(8,128)(2,1)}, bf16[512,384]{1,0:T(8,128)(2,1)S(1)}, u32[]{:S(2)}, u32[]{:S(2)}) %collective-permute-start.2) | collective-permute-done | bytes 393248 | tf_op jit(solution)/shard_map/ppermute | solution.py:40
  36.3 1.1 %attend_first0_1.1 = (f32[6,256,128]{2,1,0:T(8,128)S(1)}, f32[12,256,128]{2,1,0:T(8,128)S(1)}) custom-call(bf16[272,384]{1,0:T(8,128)(2,1)S(1)} %copy-done.1, bf16[272,384]{1,0:T(8,128)(2,1)S(1)} %collective-permute-done.refs_1_, bf16[512,384]{1,0:T(8,128)(2,1)S(1)} %collective-permute-done.2.refs_2_.first_ref, ...), custom_call_target="tpu_custom_call" | custom-call | flops 201326592 | bytes 2000000 | tf_op jit(solution)/shard_map/attend_first0_1/pallas_call | solution.py:234
  37.4 0.0 collective-permute-done.1.refs_2_.second_ref
  37.4 0.8 %attend_second1.1.after_ref = bf16[272,384]{1,0:T(8,128)(2,1)S(1)} custom-call(bf16[272,384]{1,0:T(8,128)(2,1)S(1)} %copy-done.1, bf16[272,384]{1,0:T(8,128)(2,1)S(1)} %collective-permute-done.refs_1_, bf16[512,384]{1,0:T(8,128)(2,1)S(1)} %collective-permute-done.1.refs_2_.second_ref, f32[6,256,128]{2,1,0:T(8,128)S(1)} %get-tuple-element.23.refs_3_, ...), custom_call_target="tpu_custom_call" | custom-call | flops 100663296 | bytes 2000000 | tf_op jit(solution)/shard_map/attend_second1/pallas_call | solution.py:234
  38.3 2.5 %collective-permute-start.4 = (bf16[272,384]{1,0:T(8,128)(2,1)S(1)}, bf16[272,384]{1,0:T(8,128)(2,1)S(1)}, u32[]{:S(2)}, u32[]{:S(2)}) collective-permute-start(bf16[272,384]{1,0:T(8,128)(2,1)S(1)} %attend_second1.1.after_ref), channel_id=1, source_target_pairs={{0,8},{8,0},{16,24},{24,16},{32,40},{40,32},{48,56},{56,48},{64,72... | collective-permute-start | bytes 626696 | tf_op jit(solution)/shard_map/ppermute | solution.py:44
  40.8 0.7 collective-permute-start.8
  41.4 0.0 collective-permute-done.5.refs_6_.refs_5_
  41.5 7.8 %collective-permute-done.6.refs_7_.refs_6_ = bf16[384,768]{1,0:T(8,128)(2,1)S(1)} collective-permute-done((bf16[384,768]{1,0:T(8,128)(2,1)S(1)}, bf16[384,768]{1,0:T(8,128)(2,1)S(1)}, u32[]{:S(2)}, u32[]{:S(2)}) %collective-permute-start.6) | collective-permute-done | bytes 589856 | tf_op jit(solution)/shard_map/ppermute | solution.py:54
  49.3 2.1 %collective-permute-done.7.refs_8_.refs_7_ = bf16[384,768]{1,0:T(8,128)(2,1)S(1)} collective-permute-done((bf16[384,768]{1,0:T(8,128)(2,1)S(1)}, bf16[384,768]{1,0:T(8,128)(2,1)S(1)}, u32[]{:S(2)}, u32[]{:S(2)}) %collective-permute-start.7) | collective-permute-done | bytes 589856 | tf_op jit(solution)/shard_map/ppermute | solution.py:54
  51.3 1.7 %attend_second0.1 = (f32[256,384]{1,0:T(8,128)S(1)}, f32[3,8,256]{2,1,0:T(8,128)S(1)}) custom-call(bf16[272,384]{1,0:T(8,128)(2,1)S(1)} %copy-done.1, bf16[272,384]{1,0:T(8,128)(2,1)S(1)} %collective-permute-done.refs_1_, bf16[512,384]{1,0:T(8,128)(2,1)S(1)} %collective-permute-done.1.refs_2_.second_ref, f32[6,256,128]{2,1,0:T(8,128)S(1)} %get-tuple-element.23.refs_3_, ...), custom_call_target="tpu_custom_call" | custom-call | flops 3500000000 | bytes 2000000 | tf_op jit(solution)/shard_map/attend_second0/pallas_call | solution.py:234
  53.1 0.5 merge.1.refs_0_
  53.6 4.9 %collective-permute-start.10 = (bf16[256,384]{1,0:T(8,128)(2,1)S(1)}, bf16[256,384]{1,0:T(8,128)(2,1)S(1)}, u32[]{:S(2)}, u32[]{:S(2)}) collective-permute-start(bf16[256,384]{1,0:T(8,128)(2,1)S(1)} %merge.1.refs_0_), channel_id=1, source_target_pairs={{0,4},{1,5},{2,6},{3,7},{4,0},{5,1},{6,2},{7,3},{8,12},{9,13},{10,... | collective-permute-start | bytes 589832 | tf_op jit(solution)/shard_map/ppermute | solution.py:54
  58.5 4.2 %collective-permute-start.11 = (bf16[256,384]{1,0:T(8,128)(2,1)S(1)}, bf16[256,384]{1,0:T(8,128)(2,1)S(1)}, u32[]{:S(2)}, u32[]{:S(2)}) collective-permute-start(bf16[256,384]{1,0:T(8,128)(2,1)S(1)} %merge.1.refs_0_), channel_id=1, source_target_pairs={{0,6},{1,7},{2,0},{3,1},{4,2},{5,3},{6,4},{7,5},{8,14},{9,15},{10,... | collective-permute-start | bytes 589832 | tf_op jit(solution)/shard_map/ppermute | solution.py:54
  62.7 1.9 %collective-permute-start.9 = (bf16[256,384]{1,0:T(8,128)(2,1)S(1)}, bf16[256,384]{1,0:T(8,128)(2,1)S(1)}, u32[]{:S(2)}, u32[]{:S(2)}) collective-permute-start(bf16[256,384]{1,0:T(8,128)(2,1)S(1)} %merge.1.refs_0_), channel_id=1, source_target_pairs={{0,2},{1,3},{2,4},{3,5},{4,6},{5,7},{6,0},{7,1},{8,10},{9,11},{10,... | collective-permute-start | bytes 589832 | tf_op jit(solution)/shard_map/ppermute | solution.py:54
  64.6 3.7 %collective-permute-done.11.refs_3_ = bf16[256,384]{1,0:T(8,128)(2,1)S(1)} collective-permute-done((bf16[256,384]{1,0:T(8,128)(2,1)S(1)}, bf16[256,384]{1,0:T(8,128)(2,1)S(1)}, u32[]{:S(2)}, u32[]{:S(2)}) %collective-permute-start.11) | collective-permute-done | bytes 196640 | tf_op jit(solution)/shard_map/ppermute | solution.py:54
  68.3 3.9 %collective-permute-done.9.refs_1_ = bf16[256,384]{1,0:T(8,128)(2,1)S(1)} collective-permute-done((bf16[256,384]{1,0:T(8,128)(2,1)S(1)}, bf16[256,384]{1,0:T(8,128)(2,1)S(1)}, u32[]{:S(2)}, u32[]{:S(2)}) %collective-permute-start.9) | collective-permute-done | bytes 196640 | tf_op jit(solution)/shard_map/ppermute | solution.py:54
  72.1 1.1 %project.1 = (f32[256,384]{1,0:T(8,128)S(1)}, bf16[256,384]{1,0:T(8,128)(2,1)S(1)}) custom-call(bf16[256,384]{1,0:T(8,128)(2,1)S(1)} %merge.1.refs_0_, bf16[256,384]{1,0:T(8,128)(2,1)S(1)} %collective-permute-done.9.refs_1_, bf16[256,384]{1,0:T(8,128)(2,1)S(1)} %collective-permute-done.10.refs_2_, bf16[256,384]{1,0:T(8,128)(2,1)S(1)} %collective-permute-done.11.refs_3_, ...), custom_call_target="tpu_custom_call" | custom-call | tf_op jit(solution)/shard_map/project/pallas_call | solution.py:342
  73.3 4.3 %collective-permute-start.12 = (bf16[256,384]{1,0:T(8,128)(2,1)S(1)}, bf16[256,384]{1,0:T(8,128)(2,1)S(1)}, u32[]{:S(2)}, u32[]{:S(2)}) collective-permute-start(bf16[256,384]{1,0:T(8,128)(2,1)S(1)} %get-tuple-element.32), channel_id=1, source_target_pairs={{0,1},{1,0},{2,3},{3,2},{4,5},{5,4},{6,7},{7,6},{8,9},{9,8},{10,11... | collective-permute-start | bytes 589832 | tf_op jit(solution)/shard_map/ppermute | solution.py:58
  77.6 3.7 %collective-permute-done.12.other_ref = bf16[256,384]{1,0:T(8,128)(2,1)S(1)} collective-permute-done((bf16[256,384]{1,0:T(8,128)(2,1)S(1)}, bf16[256,384]{1,0:T(8,128)(2,1)S(1)}, u32[]{:S(2)}, u32[]{:S(2)}) %collective-permute-start.12) | collective-permute-done | bytes 196640 | tf_op jit(solution)/shard_map/ppermute | solution.py:58
  81.2 0.8 finish.1
  (15 shorter events, 0.1 us)
Async XLA Ops:
  2.0 18.2 %collective-permute-start = (bf16[272,384]{1,0:T(8,128)(2,1)}, bf16[272,384]{1,0:T(8,128)(2,1)S(1)}, u32[]{:S(2)}, u32[]{:S(2)}) collective-permute-start(bf16[272,384]{1,0:T(8,128)(2,1)} %get-tuple-element.19.refs_0_), channel_id=1, source_target_pairs={{0,8},{8,0},{16,24},{24,16},{32,40},{40,32},{48,56},{56,48},{64,72... | collective-permute-start | bytes 626696 | tf_op jit(solution)/shard_map/ppermute | solution.py:44
  3.9 20.9 %collective-permute-start.3 = (bf16[272,384]{1,0:T(8,128)(2,1)}, bf16[272,384]{1,0:T(8,128)(2,1)S(1)}, u32[]{:S(2)}, u32[]{:S(2)}) collective-permute-start(bf16[272,384]{1,0:T(8,128)(2,1)} %get-tuple-element.19.refs_0_), channel_id=1, source_target_pairs={{8,16},{16,8},{40,48},{48,40},{72,80},{80,72},{104,112},{112,104},... | collective-permute-start | bytes 626696 | tf_op jit(solution)/shard_map/ppermute | solution.py:49
  4.6 31.7 %collective-permute-start.2 = (bf16[512,384]{1,0:T(8,128)(2,1)}, bf16[512,384]{1,0:T(8,128)(2,1)S(1)}, u32[]{:S(2)}, u32[]{:S(2)}) collective-permute-start(bf16[512,384]{1,0:T(8,128)(2,1)} %get-tuple-element.20.refs_2_.own_ref), channel_id=1, source_target_pairs={{16,48},{24,56},{32,64},{40,72},{48,16},{56,24},{64,32},{72,40},{8... | collective-permute-start | bytes 1179656 | tf_op jit(solution)/shard_map/ppermute | solution.py:40
  8.9 28.5 %collective-permute-start.1 = (bf16[512,384]{1,0:T(8,128)(2,1)}, bf16[512,384]{1,0:T(8,128)(2,1)S(1)}, u32[]{:S(2)}, u32[]{:S(2)}) collective-permute-start(bf16[512,384]{1,0:T(8,128)(2,1)} %get-tuple-element.20.refs_2_.own_ref), channel_id=1, source_target_pairs={{0,32},{8,40},{32,0},{40,8},{48,80},{56,88},{64,96},{72,104},{80,4... | collective-permute-start | bytes 1179656 | tf_op jit(solution)/shard_map/ppermute | solution.py:40
  14.8 1.7 %copy-start = (bf16[384,3072]{1,0:T(8,128)(2,1)S(1)}, bf16[384,3072]{1,0:T(8,128)(2,1)}, u32[]{:S(2)}) copy-start(bf16[384,3072]{1,0:T(8,128)(2,1)} %weight_ref.1) | copy-start | bytes 7077892
  16.5 11.7 %copy-start.1 = (bf16[272,384]{1,0:T(8,128)(2,1)S(1)}, bf16[272,384]{1,0:T(8,128)(2,1)}, u32[]{:S(2)}) copy-start(bf16[272,384]{1,0:T(8,128)(2,1)} %get-tuple-element.19.refs_0_) | copy-start | bytes 626692
  16.5 11.7 %copy-start.2 = (bf16[512,384]{1,0:T(8,128)(2,1)S(1)}, bf16[512,384]{1,0:T(8,128)(2,1)}, u32[]{:S(2)}) copy-start(bf16[512,384]{1,0:T(8,128)(2,1)} %get-tuple-element.20.refs_2_.own_ref) | copy-start | bytes 1179652
  16.6 24.8 %collective-permute-start.5 = (bf16[384,768]{1,0:T(8,128)(2,1)S(1)}, bf16[384,768]{1,0:T(8,128)(2,1)S(1)}, u32[]{:S(2)}, u32[]{:S(2)}) collective-permute-start(bf16[384,768]{1,0:T(8,128)(2,1)S(1)} %get-tuple-element.25), channel_id=1, source_target_pairs={{0,2},{1,3},{2,4},{3,5},{4,6},{5,7},{6,0},{7,1},{8,10},{9,11},{10,... | collective-permute-start | bytes 1769480 | tf_op jit(solution)/shard_map/ppermute | solution.py:54
  20.2 29.1 %collective-permute-start.6 = (bf16[384,768]{1,0:T(8,128)(2,1)S(1)}, bf16[384,768]{1,0:T(8,128)(2,1)S(1)}, u32[]{:S(2)}, u32[]{:S(2)}) collective-permute-start(bf16[384,768]{1,0:T(8,128)(2,1)S(1)} %get-tuple-element.26), channel_id=1, source_target_pairs={{0,4},{1,5},{2,6},{3,7},{4,0},{5,1},{6,2},{7,3},{8,12},{9,13},{10,... | collective-permute-start | bytes 1769480 | tf_op jit(solution)/shard_map/ppermute | solution.py:54
  24.8 26.5 %collective-permute-start.7 = (bf16[384,768]{1,0:T(8,128)(2,1)S(1)}, bf16[384,768]{1,0:T(8,128)(2,1)S(1)}, u32[]{:S(2)}, u32[]{:S(2)}) collective-permute-start(bf16[384,768]{1,0:T(8,128)(2,1)S(1)} %get-tuple-element.27), channel_id=1, source_target_pairs={{0,6},{1,7},{2,0},{3,1},{4,2},{5,3},{6,4},{7,5},{8,14},{9,15},{10,... | collective-permute-start | bytes 1769480 | tf_op jit(solution)/shard_map/ppermute | solution.py:54
  38.3 13.1 %collective-permute-start.4 = (bf16[272,384]{1,0:T(8,128)(2,1)S(1)}, bf16[272,384]{1,0:T(8,128)(2,1)S(1)}, u32[]{:S(2)}, u32[]{:S(2)}) collective-permute-start(bf16[272,384]{1,0:T(8,128)(2,1)S(1)} %attend_second1.1.after_ref), channel_id=1, source_target_pairs={{0,8},{8,0},{16,24},{24,16},{32,40},{40,32},{48,56},{56,48},{64,72... | collective-permute-start | bytes 626696 | tf_op jit(solution)/shard_map/ppermute | solution.py:44
  40.8 12.3 %collective-permute-start.8 = (bf16[272,384]{1,0:T(8,128)(2,1)S(1)}, bf16[272,384]{1,0:T(8,128)(2,1)S(1)}, u32[]{:S(2)}, u32[]{:S(2)}) collective-permute-start(bf16[272,384]{1,0:T(8,128)(2,1)S(1)} %attend_middle.1), channel_id=1, source_target_pairs={{8,16},{16,8},{40,48},{48,40},{72,80},{80,72},{104,112},{112,104},... | collective-permute-start | bytes 626696 | tf_op jit(solution)/shard_map/ppermute | solution.py:49
  53.6 11.0 %collective-permute-start.10 = (bf16[256,384]{1,0:T(8,128)(2,1)S(1)}, bf16[256,384]{1,0:T(8,128)(2,1)S(1)}, u32[]{:S(2)}, u32[]{:S(2)}) collective-permute-start(bf16[256,384]{1,0:T(8,128)(2,1)S(1)} %merge.1.refs_0_), channel_id=1, source_target_pairs={{0,4},{1,5},{2,6},{3,7},{4,0},{5,1},{6,2},{7,3},{8,12},{9,13},{10,... | collective-permute-start | bytes 589832 | tf_op jit(solution)/shard_map/ppermute | solution.py:54
  58.5 9.8 %collective-permute-start.11 = (bf16[256,384]{1,0:T(8,128)(2,1)S(1)}, bf16[256,384]{1,0:T(8,128)(2,1)S(1)}, u32[]{:S(2)}, u32[]{:S(2)}) collective-permute-start(bf16[256,384]{1,0:T(8,128)(2,1)S(1)} %merge.1.refs_0_), channel_id=1, source_target_pairs={{0,6},{1,7},{2,0},{3,1},{4,2},{5,3},{6,4},{7,5},{8,14},{9,15},{10,... | collective-permute-start | bytes 589832 | tf_op jit(solution)/shard_map/ppermute | solution.py:54
  62.7 9.5 %collective-permute-start.9 = (bf16[256,384]{1,0:T(8,128)(2,1)S(1)}, bf16[256,384]{1,0:T(8,128)(2,1)S(1)}, u32[]{:S(2)}, u32[]{:S(2)}) collective-permute-start(bf16[256,384]{1,0:T(8,128)(2,1)S(1)} %merge.1.refs_0_), channel_id=1, source_target_pairs={{0,2},{1,3},{2,4},{3,5},{4,6},{5,7},{6,0},{7,1},{8,10},{9,11},{10,... | collective-permute-start | bytes 589832 | tf_op jit(solution)/shard_map/ppermute | solution.py:54
  72.1 5.4 %copy-start.4 = (f32[384]{0:T(512)S(1)}, f32[384]{0:T(512)}, u32[]{:S(2)}) copy-start(f32[384]{0:T(512)} %param.13) | copy-start | bytes 4612
  72.1 9.1 %copy-start.3 = (bf16[256,384]{1,0:T(8,128)(2,1)S(1)}, bf16[256,384]{1,0:T(8,128)(2,1)}, u32[]{:S(2)}) copy-start(bf16[256,384]{1,0:T(8,128)(2,1)} %residual_ref.1) | copy-start | bytes 589828
  73.3 8.0 %collective-permute-start.12 = (bf16[256,384]{1,0:T(8,128)(2,1)S(1)}, bf16[256,384]{1,0:T(8,128)(2,1)S(1)}, u32[]{:S(2)}, u32[]{:S(2)}) collective-permute-start(bf16[256,384]{1,0:T(8,128)(2,1)S(1)} %get-tuple-element.32), channel_id=1, source_target_pairs={{0,1},{1,0},{2,3},{3,2},{4,5},{5,4},{6,7},{7,6},{8,9},{9,8},{10,11... | collective-permute-start | bytes 589832 | tf_op jit(solution)/shard_map/ppermute | solution.py:58

commit v7 on v6

--- a/solution.py
+++ b/solution.py
@@ -2,6 +2,7 @@
 
 import jax
 import jax.numpy as jnp
+import numpy as np
 from jax import lax
 from jax.experimental import pallas as pl
 from jax.experimental.pallas import tpu as pltpu
@@ -49,32 +50,25 @@
     return lax.ppermute(block, "tile", route)
 
 
-def shift_columns(block, step):
-    count = lax.axis_size("head")
-    return lax.ppermute(block, "head", [(i, (i + 2 * step) % count) for i in range(count)])
-
-
 def swap_depth(block):
-    return lax.ppermute(block, "head", [(i, i ^ 1) for i in range(lax.axis_size("head"))])
-
-
-def split_weight_kernel(weight_ref, *out_refs):
-    width = out_refs[0].shape[1]
-    mine = lax.axis_index("head") // 2
-    for step, ref in enumerate(out_refs):
-        start = pl.multiple_of(lax.rem(mine + step, len(out_refs)) * width, HD)
-        ref[...] = weight_ref[:, pl.ds(start, width)]
+    return lax.ppermute(block, "depth", [(0, 1), (1, 0)])
+
+
+def split_weight_kernel(weight_ref, out_ref):
+    width = out_ref.shape[2]
+    for part in range(out_ref.shape[0]):
+        out_ref[part] = weight_ref[:, part * width : (part + 1) * width]
 
 
 def split_weight(out_weight):
     rows, features = out_weight.shape
-    parts = lax.axis_size("head") // 2
+    parts = lax.axis_size("x")
     whole = pl.BlockSpec(memory_space=VMEM)
     return pl.pallas_call(
         split_weight_kernel,
-        out_shape=(jax.ShapeDtypeStruct((rows, features // parts), out_weight.dtype),) * parts,
+        out_shape=jax.ShapeDtypeStruct((parts, rows, features // parts), out_weight.dtype),
         in_specs=[whole],
-        out_specs=(whole,) * parts,
+        out_specs=whole,
         compiler_params=params(24),
         cost_estimate=pl.CostEstimate(flops=0, bytes_accessed=0, transcendentals=0),
         name="split_weight",
@@ -228,7 +222,7 @@
             jax.ShapeDtypeStruct((rows, width), jnp.float32),
             jax.ShapeDtypeStruct((heads, 8, rows), jnp.float32),
         )
-        flops = 3_500_000_000
+        flops = 13_000_000_000
     else:
         out_shape = (jax.ShapeDtypeStruct((rows + SIDE, width), jnp.bfloat16),)
     return pl.pallas_call(
@@ -287,7 +281,7 @@
     )(query, own, first, second, after)
 
 
-def merge_kernel(own_ref, stats_ref, middle_ref, out_ref):
+def merge_kernel(own_ref, stats_ref, middle_ref, after_ref, out_ref):
     rows, width = own_ref.shape
     height = lax.axis_index("tile") % HEIGHT_TILES
     inside = jnp.where((height > 0) & (height < HEIGHT_TILES - 1), 1.0, 0.0)
@@ -308,45 +302,44 @@
         low = head * HD
         value = own_ref[:, low : low + HD] * column(shares, 2 * head)
         value += middle_ref[:rows, low : low + HD].astype(jnp.float32) * column(shares, 2 * head + 1)
-        out_ref[:, low : low + HD] = value.astype(out_ref.dtype)
-
-
-def merge(own, stats, middle):
+        for part in range(out_ref.shape[0]):
+            out_ref[part, :, low : low + HD] = value.astype(out_ref.dtype)
+
+
+def merge(own, stats, middle, after):
     whole = pl.BlockSpec(memory_space=VMEM)
     return pl.pallas_call(
         merge_kernel,
-        out_shape=jax.ShapeDtypeStruct(own.shape, jnp.bfloat16),
-        in_specs=[whole] * 3,
+        out_shape=jax.ShapeDtypeStruct((lax.axis_size("x"), *own.shape), jnp.bfloat16),
+        in_specs=[whole] * 3 + [pl.BlockSpec(memory_space=pl.ANY)],
         out_specs=whole,
         compiler_params=params(24),
         name="merge",
-    )(own, stats, middle)
-
-
-def project_kernel(*refs):
-    parts = (len(refs) - 2) // 2
-    attention_refs, weight_refs, (mine_ref, other_ref) = refs[:parts], refs[parts:-2], refs[-2:]
+    )(own, stats, middle, after)
+
+
+def project_kernel(attention_ref, weight_ref, mine_ref, other_ref):
     width = mine_ref.shape[1]
-    depth = lax.rem(lax.axis_index("head"), 2)
+    depth = lax.axis_index("depth")
     for ref, place in ((other_ref, 1 - depth), (mine_ref, depth)):
         start = pl.multiple_of(place * width, HD)
         total = jnp.zeros(mine_ref.shape, jnp.float32)
-        for attention_ref, weight_ref in zip(attention_refs, weight_refs):
-            total += jnp.dot(attention_ref[...], weight_ref[:, pl.ds(start, width)], preferred_element_type=jnp.float32)
+        for part in range(attention_ref.shape[0]):
+            total += jnp.dot(attention_ref[part], weight_ref[part, :, pl.ds(start, width)], preferred_element_type=jnp.float32)
         ref[...] = total.astype(ref.dtype)
 
 
-def project(attention, weights):
-    shape = attention[0].shape
+def project(attention, weight):
+    shape = attention.shape[1:]
     whole = pl.BlockSpec(memory_space=VMEM)
     return pl.pallas_call(
         project_kernel,
         out_shape=(jax.ShapeDtypeStruct(shape, jnp.float32), jax.ShapeDtypeStruct(shape, jnp.bfloat16)),
-        in_specs=[whole] * (len(attention) + len(weights)),
+        in_specs=[whole] * 2,
         out_specs=(whole, whole),
         compiler_params=params(24),
         name="project",
-    )(*attention, *weights)
+    )(attention, weight)
 
 
 def finish_kernel(mine_ref, other_ref, residual_ref, gate_ref, out_ref):
@@ -370,34 +363,35 @@
     packed, block = pack(windows, queries, key_rows, value_rows)
     first, second = swap_times(block, False), swap_times(block, True)
     asked = (packed, swap_pair(packed))
-    weight, *to_send = split_weight(out_weight)
-    steps = range(1, len(to_send) + 1)
-    weights = [shift_columns(part, step) for step, part in zip(steps, to_send)]
     middle_asks = swap_middle(packed)
+    weight = lax.all_to_all(split_weight(out_weight), "x", 0, 0)
     before = attend(0, asked, block)
-    before = attend(1, asked, first, before, after=(middle_asks,))
+    before = attend(1, asked, first, before)
     (for_pair,) = attend(2, asked, second, before, (1,))
     for_middle = attend_middle(middle_asks, block, first, second, for_pair)
-    own, stats = attend(2, asked, second, before, (0,), (swap_pair(for_pair),), weights)
-    attention = merge(own, stats, swap_middle(for_middle))
-    gathered = [shift_columns(attention, step) for step in steps]
-    mine, other = project([attention, *gathered], [weight, *weights])
+    own, stats = attend(2, asked, second, before, (0,), (swap_pair(for_pair),))
+    attention = merge(own, stats, swap_middle(for_middle), weight)
+    mine, other = project(lax.all_to_all(attention, "x", 0, 0), weight)
     return finish(mine, swap_depth(other), residual, gate_scale)
 
 
 def solution(mesh):
+    devices = np.asarray(mesh.devices)
+    tiles, heads = devices.shape
+    split = jax.sharding.Mesh(devices.reshape(tiles, heads // 2, 2), ("tile", "x", "depth"))
+    head = ("x", "depth")
     return jax.shard_map(
         shards,
-        mesh=mesh,
+        mesh=split,
         in_specs=(
-            P("tile", "head"),
-            P("tile", "head"),
-            P("tile", "head"),
+            P("tile", head),
+            P("tile", head),
+            P("tile", head),
             P("tile", None),
-            P("tile", "head"),
-            P("head", None),
-            P("head"),
+            P("tile", head),
+            P(head, None),
+            P(head),
         ),
-        out_specs=P("tile", "head"),
+        out_specs=P("tile", head),
         check_vma=False,
     )

time: 82.5 us -> 76.5 us (0.927)
  starting transfers between devices: 42.7 us -> 24.6 us
  blocking collectives: 0 us -> 14.9 us
  waiting for transfers between devices: 28.1 us -> 21.4 us
  local copies, waits for them, and re-layouts: 1.68 us -> 5.73 us
    ppermute x7 -> x1, starting transfers between devices: 26.8 us -> 4.8 us  [swap_depth(): return lax.ppermute(block, 'depth', [(0, 1), (1, 0)])]
    ppermute x7 -> x1, waiting for transfers between devices: 21.1 us -> 4.39 us  [swap_depth(): return lax.ppermute(block, 'depth', [(0, 1), (1, 0)])]
    all_to_all x0 -> x1, blocking collectives: none -> 14.9 us  [shards(): mine, other = project(lax.all_to_all(attention, 'x', 0, 0), weight)]
    all_to_all x0 -> x1, waiting for transfers between devices: none -> 8.04 us  [shards(): weight = lax.all_to_all(split_weight(out_weight), 'x', 0, 0)]
    all_to_all x0 -> x1, starting transfers between devices: none -> 4.42 us  [shards(): weight = lax.all_to_all(split_weight(out_weight), 'x', 0, 0)]
    unnamed x10 -> x16, local copies, waits for them, and re-layouts: 1.68 us -> 5.72 us
    ppermute x2, waiting for transfers between devices: 0.01 us -> 1.43 us  [swap_pair(): lax.ppermute(block, 'tile', [(tile, tile ^ 1) for tile, *_ in places()])]
  transfers between devices with their start and end apart: 13 -> 8, of which waited for: 6 -> 5; matrix products, arithmetic and copies ran while one was open for 0% -> 0% of each run, Pallas kernels for 6% -> 6%
where the time goes in v7:
time: 76.5 us; the launch traced here: 76 us
  starting transfers between devices  24.6 us (32%)
  waiting for transfers between devices  21.4 us (28%)
  blocking collectives  14.9 us (19%)
  Pallas kernels  9.17 us (12%)
  local copies, waits for them, and re-layouts  5.73 us (7%)
    all_to_all x1, blocking collectives, shards(): mine, other = project(lax.all_to_all(attention, 'x', 0, 0), weight)  14.9 us
    ppermute x2, starting transfers between devices, swap_times(): return lax.ppermute(block, 'tile', route)  10.2 us
    all_to_all x1, waiting for transfers between devices, shards(): weight = lax.all_to_all(split_weight(out_weight), 'x', 0, 0)  8.04 us
    ppermute x2, waiting for transfers between devices, swap_times(): return lax.ppermute(block, 'tile', route)  7.51 us
    unnamed x16, local copies, waits for them, and re-layouts  5.72 us
    ppermute x1, starting transfers between devices, swap_depth(): return lax.ppermute(block, 'depth', [(0, 1), (1, 0)])  4.8 us
    pallas_call x4, Pallas kernels, attend(): pl.pallas_call(functools.partial(attend_kernel, stage, places), out_shape...  4.62 us
    all_to_all x1, starting transfers between devices, shards(): weight = lax.all_to_all(split_weight(out_weight), 'x', 0, 0)  4.42 us
  transfers between devices with their start and end apart: 8, of which 5 were waited for; matrix products, arithmetic and copies ran while one was open for 0% of the time, Pallas kernels for 6%

profile of v7, /device:TPU:128, one launch (start us, length us, event | category | flops | bytes accessed | tf_op | source)
XLA Modules:
  0.0 76.0 jit_solution(13642158979239887203)
XLA Ops:
  0.0 2.0 %pack.1 = (bf16[272,384]{1,0:T(8,128)(2,1)}, bf16[512,384]{1,0:T(8,128)(2,1)}) custom-call(s32[1,3]{1,0:T(1,128)} %windows_ref.1, bf16[256,384]{1,0:T(8,128)(2,1)} %q_ref.1, bf16[256,384]{1,0:T(8,128)(2,1)} %k_ref.1, bf16[256,384]{1,0:T(8,128)(2,1)} %v_ref.1), custom_call_target="tpu_custom_call" | custom-call | tf_op jit(solution)/shard_map/pack/pallas_call | solution.py:92
  2.0 4.3 %collective-permute-start.2 = (bf16[512,384]{1,0:T(8,128)(2,1)}, bf16[512,384]{1,0:T(8,128)(2,1)S(1)}, u32[]{:S(2)}, u32[]{:S(2)}) collective-permute-start(bf16[512,384]{1,0:T(8,128)(2,1)} %get-tuple-element.16.refs_2_.own_ref), channel_id=1, source_target_pairs={{16,48},{24,56},{32,64},{40,72},{48,16},{56,24},{64,32},{72,40},{8... | collective-permute-start | bytes 1179656 | tf_op jit(solution)/shard_map/ppermute | solution.py:41
  6.3 5.9 %collective-permute-start.1 = (bf16[512,384]{1,0:T(8,128)(2,1)}, bf16[512,384]{1,0:T(8,128)(2,1)S(1)}, u32[]{:S(2)}, u32[]{:S(2)}) collective-permute-start(bf16[512,384]{1,0:T(8,128)(2,1)} %get-tuple-element.16.refs_2_.own_ref), channel_id=1, source_target_pairs={{0,32},{8,40},{32,0},{40,8},{48,80},{56,88},{64,96},{72,104},{80,4... | collective-permute-start | bytes 1179656 | tf_op jit(solution)/shard_map/ppermute | solution.py:41
  12.2 0.0 copy-start.1
  12.2 1.7 %copy-done.1 = bf16[384,3072]{1,0:T(8,128)(2,1)S(1)} copy-done((bf16[384,3072]{1,0:T(8,128)(2,1)S(1)}, bf16[384,3072]{1,0:T(8,128)(2,1)}, u32[]{:S(2)}) %copy-start.1) | copy-done | bytes 2359320
  13.9 0.2 split_weight.1
  14.0 1.4 %copy-done = bf16[4,384,768]{2,1,0:T(8,128)(2,1)} copy-done((bf16[4,384,768]{2,1,0:T(8,128)(2,1)}, bf16[4,384,768]{2,1,0:T(8,128)(2,1)S(1)}, u32[]{:S(2)}) %copy-start) | copy-done | bytes 2359320
  15.5 4.4 %all-to-all-start = ((bf16[4,384,768]{2,1,0:T(8,128)(2,1)}), bf16[4,384,768]{2,1,0:T(8,128)(2,1)S(1)}, u32[]{:S(2)}, u32[]{:S(2)}) async-start(bf16[4,384,768]{2,1,0:T(8,128)(2,1)} %copy-done), calls=%async_computation | async-start | bytes 4718592 | tf_op jit(solution)/shard_map/all_to_all | solution.py:367
  19.9 1.9 %collective-permute-start = (bf16[272,384]{1,0:T(8,128)(2,1)S(1)}, bf16[272,384]{1,0:T(8,128)(2,1)S(1)}, u32[]{:S(2)}, u32[]{:S(2)}) collective-permute-start(bf16[272,384]{1,0:T(8,128)(2,1)S(1)} %copy-done.2), channel_id=1, source_target_pairs={{0,8},{8,0},{16,24},{24,16},{32,40},{40,32},{48,56},{56,48},{64,72... | collective-permute-start | bytes 626696 | tf_op jit(solution)/shard_map/ppermute | solution.py:45
  21.8 0.7 collective-permute-start.4
  22.5 0.7 collective-permute-done.refs_1_
  23.2 1.0 %copy-done.3 = bf16[512,384]{1,0:T(8,128)(2,1)S(1)} copy-done((bf16[512,384]{1,0:T(8,128)(2,1)S(1)}, bf16[512,384]{1,0:T(8,128)(2,1)}, u32[]{:S(2)}) %copy-start.3) | copy-done | bytes 393240
  24.2 1.0 %attend_own0_1.1 = (f32[6,256,128]{2,1,0:T(8,128)S(1)}, f32[12,256,128]{2,1,0:T(8,128)S(1)}) custom-call(bf16[272,384]{1,0:T(8,128)(2,1)S(1)} %copy-done.2, bf16[272,384]{1,0:T(8,128)(2,1)S(1)} %collective-permute-done.refs_1_, bf16[512,384]{1,0:T(8,128)(2,1)S(1)} %copy-done.3), custom_call_target="tpu_custom_call" | custom-call | flops 201326592 | bytes 2000000 | tf_op jit(solution)/shard_map/attend_own0_1/pallas_call | solution.py:228
  25.2 7.5 %collective-permute-done.2.refs_2_.first_ref = bf16[512,384]{1,0:T(8,128)(2,1)S(1)} collective-permute-done((bf16[512,384]{1,0:T(8,128)(2,1)}, bf16[512,384]{1,0:T(8,128)(2,1)S(1)}, u32[]{:S(2)}, u32[]{:S(2)}) %collective-permute-start.2) | collective-permute-done | bytes 393248 | tf_op jit(solution)/shard_map/ppermute | solution.py:41
  32.7 1.1 %attend_first0_1.1 = (f32[6,256,128]{2,1,0:T(8,128)S(1)}, f32[12,256,128]{2,1,0:T(8,128)S(1)}) custom-call(bf16[272,384]{1,0:T(8,128)(2,1)S(1)} %copy-done.2, bf16[272,384]{1,0:T(8,128)(2,1)S(1)} %collective-permute-done.refs_1_, bf16[512,384]{1,0:T(8,128)(2,1)S(1)} %collective-permute-done.2.refs_2_.first_ref, ...), custom_call_target="tpu_custom_call" | custom-call | flops 201326592 | bytes 2000000 | tf_op jit(solution)/shard_map/attend_first0_1/pallas_call | solution.py:228
  33.8 0.0 collective-permute-done.1.refs_2_.second_ref
  33.8 0.8 %attend_second1.1.after_ref = bf16[272,384]{1,0:T(8,128)(2,1)S(1)} custom-call(bf16[272,384]{1,0:T(8,128)(2,1)S(1)} %copy-done.2, bf16[272,384]{1,0:T(8,128)(2,1)S(1)} %collective-permute-done.refs_1_, bf16[512,384]{1,0:T(8,128)(2,1)S(1)} %collective-permute-done.1.refs_2_.second_ref, f32[6,256,128]{2,1,0:T(8,128)S(1)} %get-tuple-element.19.refs_3_, ...), custom_call_target="tpu_custom_call" | custom-call | flops 100663296 | bytes 2000000 | tf_op jit(solution)/shard_map/attend_second1/pallas_call | solution.py:228
  34.6 1.9 %collective-permute-start.3 = (bf16[272,384]{1,0:T(8,128)(2,1)S(1)}, bf16[272,384]{1,0:T(8,128)(2,1)S(1)}, u32[]{:S(2)}, u32[]{:S(2)}) collective-permute-start(bf16[272,384]{1,0:T(8,128)(2,1)S(1)} %attend_second1.1.after_ref), channel_id=1, source_target_pairs={{0,8},{8,0},{16,24},{24,16},{32,40},{40,32},{48,56},{56,48},{64,72... | collective-permute-start | bytes 626696 | tf_op jit(solution)/shard_map/ppermute | solution.py:45
  36.6 0.7 collective-permute-start.5
  37.3 0.7 collective-permute-done.3.refs_5_
  38.0 1.7 %attend_second0.1 = (f32[256,384]{1,0:T(8,128)S(1)}, f32[3,8,256]{2,1,0:T(8,128)S(1)}) custom-call(bf16[272,384]{1,0:T(8,128)(2,1)S(1)} %copy-done.2, bf16[272,384]{1,0:T(8,128)(2,1)S(1)} %collective-permute-done.refs_1_, bf16[512,384]{1,0:T(8,128)(2,1)S(1)} %collective-permute-done.1.refs_2_.second_ref, f32[6,256,128]{2,1,0:T(8,128)S(1)} %get-tuple-element.19.refs_3_, ...), custom_call_target="tpu_custom_call" | custom-call | flops 12999999488 | bytes 2000000 | tf_op jit(solution)/shard_map/attend_second0/pallas_call | solution.py:228
  39.7 0.7 copy-done.4
  40.4 8.0 %all-to-all-done.after_ref.weight_ref = bf16[4,384,768]{2,1,0:T(8,128)(2,1)S(1)} async-done(((bf16[4,384,768]{2,1,0:T(8,128)(2,1)}), bf16[4,384,768]{2,1,0:T(8,128)(2,1)S(1)}, u32[]{:S(2)}, u32[]{:S(2)}) %all-to-all-start) | async-done | bytes 2359328 | tf_op jit(solution)/shard_map/all_to_all | solution.py:367
  48.5 0.9 %copy-done.5 = bf16[272,384]{1,0:T(8,128)(2,1)S(1)} copy-done((bf16[272,384]{1,0:T(8,128)(2,1)S(1)}, bf16[272,384]{1,0:T(8,128)(2,1)}, u32[]{:S(2)}) %copy-start.5) | copy-done | bytes 208920
  49.4 0.5 merge.1
  49.9 0.0 copy-start.7
  49.9 0.0 copy-start.6
  49.9 14.9 %all_to_all.10.attention_ref = bf16[4,256,384]{2,1,0:T(8,128)(2,1)S(1)} all-to-all(bf16[4,256,384]{2,1,0:T(8,128)(2,1)S(1)} %merge.1), channel_id=1, replica_groups=mesh['tile'=64,'x'=4,'depth'=2] {'x'}, dimensions={0} | all-to-all | bytes 1572864 | tf_op jit(solution)/shard_map/all_to_all | solution.py:374
  64.9 1.1 %project.1 = (f32[256,384]{1,0:T(8,128)S(1)}, bf16[256,384]{1,0:T(8,128)(2,1)S(1)}) custom-call(bf16[4,256,384]{2,1,0:T(8,128)(2,1)S(1)} %all_to_all.10.attention_ref, bf16[4,384,768]{2,1,0:T(8,128)(2,1)S(1)} %all-to-all-done.after_ref.weight_ref), custom_call_target="tpu_custom_call" | custom-call | tf_op jit(solution)/shard_map/project/pallas_call | solution.py:335
  66.0 4.8 %collective-permute-start.6 = (bf16[256,384]{1,0:T(8,128)(2,1)S(1)}, bf16[256,384]{1,0:T(8,128)(2,1)S(1)}, u32[]{:S(2)}, u32[]{:S(2)}) collective-permute-start(bf16[256,384]{1,0:T(8,128)(2,1)S(1)} %get-tuple-element.24), channel_id=1, source_target_pairs={{0,1},{1,0},{2,3},{3,2},{4,5},{5,4},{6,7},{7,6},{8,9},{9,8},{10,11... | collective-permute-start | bytes 589832 | tf_op jit(solution)/shard_map/ppermute | solution.py:54
  70.8 4.4 %collective-permute-done.6.other_ref = bf16[256,384]{1,0:T(8,128)(2,1)S(1)} collective-permute-done((bf16[256,384]{1,0:T(8,128)(2,1)S(1)}, bf16[256,384]{1,0:T(8,128)(2,1)S(1)}, u32[]{:S(2)}, u32[]{:S(2)}) %collective-permute-start.6) | collective-permute-done | bytes 196640 | tf_op jit(solution)/shard_map/ppermute | solution.py:54
  75.2 0.8 %finish.1 = bf16[256,384]{1,0:T(8,128)(2,1)} custom-call(f32[256,384]{1,0:T(8,128)S(1)} %get-tuple-element.23.mine_ref, bf16[256,384]{1,0:T(8,128)(2,1)S(1)} %collective-permute-done.6.other_ref, bf16[256,384]{1,0:T(8,128)(2,1)S(1)} %copy-done.6, f32[1,384]{1,0:T(1,128)S(1)} %reshape.3.gate_ref), custom_call_target="tpu_custom_call" | custom-call | tf_op jit(solution)/shard_map/finish/pallas_call | solution.py:352
  (12 shorter events, 0.1 us)
Async XLA Ops:
  2.0 30.7 %collective-permute-start.2 = (bf16[512,384]{1,0:T(8,128)(2,1)}, bf16[512,384]{1,0:T(8,128)(2,1)S(1)}, u32[]{:S(2)}, u32[]{:S(2)}) collective-permute-start(bf16[512,384]{1,0:T(8,128)(2,1)} %get-tuple-element.16.refs_2_.own_ref), channel_id=1, source_target_pairs={{16,48},{24,56},{32,64},{40,72},{48,16},{56,24},{64,32},{72,40},{8... | collective-permute-start | bytes 1179656 | tf_op jit(solution)/shard_map/ppermute | solution.py:41
  6.3 27.5 %collective-permute-start.1 = (bf16[512,384]{1,0:T(8,128)(2,1)}, bf16[512,384]{1,0:T(8,128)(2,1)S(1)}, u32[]{:S(2)}, u32[]{:S(2)}) collective-permute-start(bf16[512,384]{1,0:T(8,128)(2,1)} %get-tuple-element.16.refs_2_.own_ref), channel_id=1, source_target_pairs={{0,32},{8,40},{32,0},{40,8},{48,80},{56,88},{64,96},{72,104},{80,4... | collective-permute-start | bytes 1179656 | tf_op jit(solution)/shard_map/ppermute | solution.py:41
  12.2 1.7 %copy-start.1 = (bf16[384,3072]{1,0:T(8,128)(2,1)S(1)}, bf16[384,3072]{1,0:T(8,128)(2,1)}, u32[]{:S(2)}) copy-start(bf16[384,3072]{1,0:T(8,128)(2,1)} %weight_ref.1) | copy-start | bytes 7077892
  14.0 1.4 %copy-start = (bf16[4,384,768]{2,1,0:T(8,128)(2,1)}, bf16[4,384,768]{2,1,0:T(8,128)(2,1)S(1)}, u32[]{:S(2)}) copy-start(bf16[4,384,768]{2,1,0:T(8,128)(2,1)S(1)} %split_weight.1) | copy-start | bytes 7077892
  15.5 4.4 %copy-start.2 = (bf16[272,384]{1,0:T(8,128)(2,1)S(1)}, bf16[272,384]{1,0:T(8,128)(2,1)}, u32[]{:S(2)}) copy-start(bf16[272,384]{1,0:T(8,128)(2,1)} %get-tuple-element.15.refs_0_) | copy-start | bytes 626692
  15.5 33.0 %all-to-all-start = ((bf16[4,384,768]{2,1,0:T(8,128)(2,1)}), bf16[4,384,768]{2,1,0:T(8,128)(2,1)S(1)}, u32[]{:S(2)}, u32[]{:S(2)}) async-start(bf16[4,384,768]{2,1,0:T(8,128)(2,1)} %copy-done), calls=%async_computation | async-start | bytes 4718592 | tf_op jit(solution)/shard_map/all_to_all | solution.py:367
  19.9 3.3 %collective-permute-start = (bf16[272,384]{1,0:T(8,128)(2,1)S(1)}, bf16[272,384]{1,0:T(8,128)(2,1)S(1)}, u32[]{:S(2)}, u32[]{:S(2)}) collective-permute-start(bf16[272,384]{1,0:T(8,128)(2,1)S(1)} %copy-done.2), channel_id=1, source_target_pairs={{0,8},{8,0},{16,24},{24,16},{32,40},{40,32},{48,56},{56,48},{64,72... | collective-permute-start | bytes 626696 | tf_op jit(solution)/shard_map/ppermute | solution.py:45
  21.8 14.8 %collective-permute-start.4 = (bf16[272,384]{1,0:T(8,128)(2,1)S(1)}, bf16[272,384]{1,0:T(8,128)(2,1)S(1)}, u32[]{:S(2)}, u32[]{:S(2)}) collective-permute-start(bf16[272,384]{1,0:T(8,128)(2,1)S(1)} %copy-done.2), channel_id=1, source_target_pairs={{8,16},{16,8},{40,48},{48,40},{72,80},{80,72},{104,112},{112,104},... | collective-permute-start | bytes 626696 | tf_op jit(solution)/shard_map/ppermute | solution.py:50
  23.2 1.0 %copy-start.3 = (bf16[512,384]{1,0:T(8,128)(2,1)S(1)}, bf16[512,384]{1,0:T(8,128)(2,1)}, u32[]{:S(2)}) copy-start(bf16[512,384]{1,0:T(8,128)(2,1)} %get-tuple-element.16.refs_2_.own_ref) | copy-start | bytes 1179652
  34.6 3.3 %collective-permute-start.3 = (bf16[272,384]{1,0:T(8,128)(2,1)S(1)}, bf16[272,384]{1,0:T(8,128)(2,1)S(1)}, u32[]{:S(2)}, u32[]{:S(2)}) collective-permute-start(bf16[272,384]{1,0:T(8,128)(2,1)S(1)} %attend_second1.1.after_ref), channel_id=1, source_target_pairs={{0,8},{8,0},{16,24},{24,16},{32,40},{40,32},{48,56},{56,48},{64,72... | collective-permute-start | bytes 626696 | tf_op jit(solution)/shard_map/ppermute | solution.py:45
  36.6 3.1 %collective-permute-start.5 = (bf16[272,384]{1,0:T(8,128)(2,1)S(1)}, bf16[272,384]{1,0:T(8,128)(2,1)S(1)}, u32[]{:S(2)}, u32[]{:S(2)}) collective-permute-start(bf16[272,384]{1,0:T(8,128)(2,1)S(1)} %attend_middle.1), channel_id=1, source_target_pairs={{8,16},{16,8},{40,48},{48,40},{72,80},{80,72},{104,112},{112,104},... | collective-permute-start | bytes 626696 | tf_op jit(solution)/shard_map/ppermute | solution.py:50
  39.7 0.7 copy-start.4
  48.5 0.9 %copy-start.5 = (bf16[272,384]{1,0:T(8,128)(2,1)S(1)}, bf16[272,384]{1,0:T(8,128)(2,1)}, u32[]{:S(2)}) copy-start(bf16[272,384]{1,0:T(8,128)(2,1)} %copy-done.4) | copy-start | bytes 626692
  49.9 20.9 %copy-start.7 = (f32[384]{0:T(512)S(1)}, f32[384]{0:T(512)}, u32[]{:S(2)}) copy-start(f32[384]{0:T(512)} %param.13) | copy-start | bytes 4612
  49.9 25.3 %copy-start.6 = (bf16[256,384]{1,0:T(8,128)(2,1)S(1)}, bf16[256,384]{1,0:T(8,128)(2,1)}, u32[]{:S(2)}) copy-start(bf16[256,384]{1,0:T(8,128)(2,1)} %residual_ref.1) | copy-start | bytes 589828
  66.0 9.2 %collective-permute-start.6 = (bf16[256,384]{1,0:T(8,128)(2,1)S(1)}, bf16[256,384]{1,0:T(8,128)(2,1)S(1)}, u32[]{:S(2)}, u32[]{:S(2)}) collective-permute-start(bf16[256,384]{1,0:T(8,128)(2,1)S(1)} %get-tuple-element.24), channel_id=1, source_target_pairs={{0,1},{1,0},{2,3},{3,2},{4,5},{5,4},{6,7},{7,6},{8,9},{9,8},{10,11... | collective-permute-start | bytes 589832 | tf_op jit(solution)/shard_map/ppermute | solution.py:54

commit v8 on v5

--- a/solution.py
+++ b/solution.py
@@ -26,15 +26,10 @@
     return [(tile, *divmod(tile, HEIGHT_TILES), tiles // HEIGHT_TILES) for tile in range(tiles)]
 
 
-def time_partner(time, height, later):
-    odd = (height < HEIGHT_TILES // 2) != later
-    return time + 1 if time % 2 == int(odd) else time - 1
-
-
 def swap_times(block, later):
     route = []
     for tile, time, height, times in places():
-        partner = time_partner(time, height, later)
+        partner = time + 1 if time % 2 == int(not later) else time - 1
         if 0 <= partner < times:
             route.append((tile, partner * HEIGHT_TILES + height))
     return lax.ppermute(block, "tile", route)
@@ -90,12 +85,13 @@
     return jnp.max(ref[rows:, axis * HD : (axis + 1) * HD].astype(jnp.float32)) > 0.5
 
 
-def presence():
-    tile = lax.axis_index("tile")
-    time, height = tile // HEIGHT_TILES, tile % HEIGHT_TILES
-    inner = (time > 0) & (time < lax.axis_size("tile") // HEIGHT_TILES - 1)
-    lower = height < HEIGHT_TILES // 2
-    return inner | ~lower, inner | lower
+def has_first():
+    time = lax.axis_index("tile") // HEIGHT_TILES
+    return (time > 0) & (time < lax.axis_size("tile") // HEIGHT_TILES - 1)
+
+
+def block_bias(wide, stage):
+    return jnp.where(wide & has_first() if stage == 1 else wide, 0.0, MASKED)
 
 
 def raw_scores(query, keys):
@@ -113,6 +109,19 @@
     ref[rows:, low : low + HD] = jnp.concatenate([side[:, :HD], side[:, HD:]], axis=0).astype(ref.dtype)
 
 
+def message_stats(ref, head, rows):
+    side = ref[rows:, head * HD : (head + 1) * HD].astype(jnp.float32)
+    side = jnp.concatenate([side[:8], side[8:]], axis=1)
+    return side[0:1] + side[1:2] + side[2:3], side[3:4] + side[4:5] + side[5:6]
+
+
+def message_columns(ref, head, rows):
+    line = lax.broadcasted_iota(jnp.int32, (8, rows), 0)
+    largest, total = message_stats(ref, head, rows)
+    columns = jnp.transpose(jnp.where(line == 0, largest, jnp.where(line == 1, total, 0.0)))
+    return [jnp.broadcast_to(column(columns, index), (rows, HD)) for index in (0, 1)]
+
+
 def attend_kernel(stage, places, *refs):
     query_refs, block_ref, refs = refs[:2], refs[2], refs[3:]
     if stage == 0:
@@ -122,6 +131,8 @@
     if stage > 0:
         old_mix_ref, old_stats_ref = refs[:2]
         refs = refs[2:]
+    if places == (0,):
+        message_ref, refs = refs[0], refs[-2:]
     rows, width = block_ref.shape[0] // 2, block_ref.shape[1]
     scale = HD**-0.5 * LOG2E
     lane = lax.broadcasted_iota(jnp.int32, (rows, HD), 1)
@@ -130,7 +141,7 @@
         ref = query_refs[place]
         bias = 0.0
         if stage > 0:
-            bias = jnp.where(wide_window(ref, rows) & presence()[stage - 1], 0.0, MASKED)
+            bias = block_bias(wide_window(ref, rows), stage)
         for head in range(width // HD):
             low = head * HD
             keys, values = block_ref[:rows, low : low + HD], block_ref[rows:, low : low + HD]
@@ -152,21 +163,29 @@
                 refs[1][2 * index] = largest
                 refs[1][2 * index + 1] = total
                 continue
+            if place == 0:
+                wide = wide_window(ref, rows, 1)
+                their_largest, their_total = message_columns(message_ref, head, rows)
+                peak = jnp.maximum(largest, jnp.where(wide, their_largest, MASKED))
+                shrink, share = jnp.exp2(largest - peak), jnp.where(wide, jnp.exp2(their_largest - peak), 0.0)
+                largest, total = peak, total * shrink + their_total * share
+                mix = mix * shrink + message_ref[:rows, low : low + HD].astype(jnp.float32) * share
             stats = jnp.transpose(jnp.where(lane == 0, largest, jnp.where(lane == 1, total, 0.0)))[:8]
             if place == 0:
                 refs[0][:, low : low + HD] = mix
                 line = lax.broadcasted_iota(jnp.int32, stats.shape, 0)
-                refs[1][head] = jnp.where(line == 2, jnp.where(wide_window(ref, rows, 1), 1.0, 0.0), stats)
+                refs[1][head] = jnp.where(line == 2, jnp.where(wide, 1.0, 0.0), stats)
             else:
                 put_message(refs[0], head, mix, stats, 0)
     if stage == 0:
         copy.wait()
 
 
-def attend(stage, queries, block, before=(), places=(0, 1), out_weight=None):
+def attend(stage, queries, block, before=(), places=(0, 1), message=(), out_weight=None):
     rows, width = block.shape[0] // 2, block.shape[1]
     heads = width // HD
     whole = pl.BlockSpec(memory_space=VMEM)
+    flops = 4 * HD * len(places) * heads * rows * rows
     if stage < 2:
         out_shape = (
             jax.ShapeDtypeStruct((2 * heads, rows, HD), jnp.float32),
@@ -177,9 +196,9 @@
             jax.ShapeDtypeStruct((rows, width), jnp.float32),
             jax.ShapeDtypeStruct((heads, 8, rows), jnp.float32),
         )
+        flops = 3_500_000_000
     else:
         out_shape = (jax.ShapeDtypeStruct((rows + SIDE, width), jnp.bfloat16),)
-    cost = len(places) * heads * rows * rows
     extra, extra_specs, scratch = (), [], []
     if stage == 0:
         extra, extra_specs = (out_weight,), [pl.BlockSpec(memory_space=pl.ANY)]
@@ -188,30 +207,13 @@
     return pl.pallas_call(
         functools.partial(attend_kernel, stage, places),
         out_shape=out_shape,
-        in_specs=[whole] * 3 + extra_specs + [whole] * len(before),
+        in_specs=[whole] * 3 + extra_specs + [whole] * (len(before) + len(message)),
         out_specs=(whole,) * len(out_shape),
         scratch_shapes=scratch,
         compiler_params=params(24),
-        cost_estimate=pl.CostEstimate(flops=4 * HD * cost, bytes_accessed=2_000_000, transcendentals=cost),
+        cost_estimate=pl.CostEstimate(flops=flops, bytes_accessed=2_000_000, transcendentals=len(places) * heads * rows * rows),
         name=("attend_own", "attend_first", "attend_second")[stage] + "_".join(map(str, places)),
-    )(*queries, block, *extra, *before)
-
-
-def gate_kernel(in_ref, out_ref):
-    pass
-
-
-def gate(array):
-    anywhere = pl.BlockSpec(memory_space=pl.ANY)
-    return pl.pallas_call(
-        gate_kernel,
-        out_shape=jax.ShapeDtypeStruct(array.shape, array.dtype),
-        in_specs=[anywhere],
-        out_specs=anywhere,
-        input_output_aliases={0: 0},
-        cost_estimate=pl.CostEstimate(flops=3_500_000_000, bytes_accessed=0, transcendentals=0),
-        name="gate",
-    )(array)
+    )(*queries, block, *extra, *before, *message)
 
 
 def middle_kernel(query_ref, own_ref, first_ref, second_ref, after_ref, out_ref):
@@ -224,7 +226,7 @@
     @pl.when(inside)
     def compute():
         wide = wide_window(query_ref, rows)
-        biases = [0.0] + [jnp.where(wide & present, 0.0, MASKED) for present in presence()]
+        biases = [0.0] + [block_bias(wide, stage) for stage in (1, 2)]
         for head in range(width // HD):
             low = head * HD
             query = query_ref[:rows, low : low + HD]
@@ -259,39 +261,29 @@
     )(query, own, first, second, after)
 
 
-def merge_shares(stats_ref, pair_ref, middle_ref, rows, heads):
+def project_kernel(own_ref, stats_ref, middle_ref, weight_ref, out_ref):
+    rows, width = own_ref.shape
+    heads = width // HD
     height = lax.axis_index("tile") % HEIGHT_TILES
     inside = jnp.where((height > 0) & (height < HEIGHT_TILES - 1), 1.0, 0.0)
-    line = lax.broadcasted_iota(jnp.int32, (16, rows), 0)
-    shares = jnp.zeros((16, rows), jnp.float32)
+    line = lax.broadcasted_iota(jnp.int32, (8, rows), 0)
+    shares = jnp.zeros((8, rows), jnp.float32)
     for head in range(heads):
-        low = head * HD
         stats = stats_ref[head]
-        largest, total = [stats[0:1]], [stats[1:2]]
-        wide = stats[2:3]
-        for ref, flag in ((pair_ref, wide > 0.5), (middle_ref, wide * inside > 0.5)):
-            side = ref[rows:, low : low + HD].astype(jnp.float32)
-            side = jnp.concatenate([side[:8], side[8:]], axis=1)
-            largest.append(jnp.where(flag, side[0:1] + side[1:2] + side[2:3], MASKED))
-            total.append(jnp.where(flag, side[3:4] + side[4:5] + side[5:6], 0.0))
-        peak = jnp.maximum(jnp.maximum(largest[0], largest[1]), largest[2])
-        factors = [jnp.exp2(value - peak) for value in largest]
-        whole = total[0] * factors[0] + total[1] * factors[1] + total[2] * factors[2]
-        for index, factor in enumerate(factors):
-            shares = jnp.where(line == 3 * head + index, factor / whole, shares)
-    return jnp.transpose(shares)
-
-
-def project_kernel(own_ref, stats_ref, pair_ref, middle_ref, weight_ref, out_ref):
-    rows, width = own_ref.shape
-    heads = width // HD
-    shares = merge_shares(stats_ref, pair_ref, middle_ref, rows, heads)
+        their_largest, their_total = message_stats(middle_ref, head, rows)
+        valid = stats[2:3] * inside > 0.5
+        peak = jnp.maximum(stats[0:1], jnp.where(valid, their_largest, MASKED))
+        shrink = jnp.exp2(stats[0:1] - peak)
+        share = jnp.where(valid, jnp.exp2(their_largest - peak), 0.0)
+        whole = stats[1:2] * shrink + their_total * share
+        shares = jnp.where(line == 2 * head, shrink / whole, shares)
+        shares = jnp.where(line == 2 * head + 1, share / whole, shares)
+    shares = jnp.transpose(shares)
     merged = []
     for head in range(heads):
         low = head * HD
-        value = own_ref[:, low : low + HD] * column(shares, 3 * head)
-        for index, ref in enumerate((pair_ref, middle_ref)):
-            value += ref[:rows, low : low + HD].astype(jnp.float32) * column(shares, 3 * head + 1 + index)
+        value = own_ref[:, low : low + HD] * column(shares, 2 * head)
+        value += middle_ref[:rows, low : low + HD].astype(jnp.float32) * column(shares, 2 * head + 1)
         merged.append(value.astype(jnp.bfloat16))
     attention = jnp.concatenate(merged, axis=1)
     for group in range(out_ref.shape[0]):
@@ -300,19 +292,19 @@
         ).astype(out_ref.dtype)
 
 
-def project(own, stats, pair, middle, out_weight):
+def project(own, stats, middle, out_weight):
     rows, width = own.shape
     features = out_weight.shape[1]
     whole = pl.BlockSpec(memory_space=VMEM)
     return pl.pallas_call(
         project_kernel,
         out_shape=jax.ShapeDtypeStruct((features // width, rows, width), jnp.bfloat16),
-        in_specs=[whole] * 5,
+        in_specs=[whole] * 4,
         out_specs=whole,
         compiler_params=params(24),
         cost_estimate=pl.CostEstimate(flops=2 * rows * width * features, bytes_accessed=5_000_000, transcendentals=0),
         name="project",
-    )(own, stats, pair, middle, out_weight)
+    )(own, stats, middle, out_weight)
 
 
 def finish_kernel(terms_ref, residual_ref, gate_ref, out_ref):
@@ -321,23 +313,16 @@
 
 
 def finish(terms, residual, gate_scale):
-    groups, rows, width = terms.shape
-    steps = 2
-    part = rows // steps
+    whole = pl.BlockSpec(memory_space=VMEM)
     return pl.pallas_call(
         finish_kernel,
-        grid=(steps,),
-        out_shape=jax.ShapeDtypeStruct((rows, width), residual.dtype),
-        in_specs=[
-            pl.BlockSpec((groups, part, width), lambda step: (0, step, 0)),
-            pl.BlockSpec((part, width), lambda step: (step, 0)),
-            pl.BlockSpec((1, width), lambda step: (0, 0)),
-        ],
-        out_specs=pl.BlockSpec((part, width), lambda step: (step, 0)),
+        out_shape=jax.ShapeDtypeStruct(residual.shape, residual.dtype),
+        in_specs=[whole] * 3,
+        out_specs=whole,
         compiler_params=params(24),
-        cost_estimate=pl.CostEstimate(flops=10 * groups * rows * width, bytes_accessed=2_000_000, transcendentals=0),
+        cost_estimate=pl.CostEstimate(flops=10 * terms.size, bytes_accessed=2_000_000, transcendentals=0),
         name="finish",
-    )(terms, residual, gate_scale.reshape(1, width))
+    )(terms, residual, gate_scale.reshape(1, -1))
 
 
 def shards(queries, key_rows, value_rows, windows, residual, out_weight, gate_scale):
@@ -348,9 +333,8 @@
     before = attend(1, asked, first, before)
     (for_pair,) = attend(2, asked, second, before, (1,))
     for_middle = attend_middle(swap_middle(packed), block, first, second, for_pair)
-    own, stats = attend(2, asked, second, before, (0,))
-    from_pair = gate(swap_pair(for_pair))
-    terms = project(own, stats, from_pair, swap_middle(for_middle), held_weight)
+    own, stats = attend(2, asked, second, before, (0,), (swap_pair(for_pair),))
+    terms = project(own, stats, swap_middle(for_middle), held_weight)
     terms = lax.all_to_all(terms, "head", 0, 0)
     return finish(terms, residual, gate_scale)
 

time: 74.3 us -> 71.5 us (0.962)
  the two profiles are of different devices: /device:TPU:129 before, /device:TPU:177 now
where the time goes in v8:
time: 71.5 us; the launch traced here: 71.1 us
  waiting for transfers between devices  30.5 us (43%)
  starting transfers between devices  24.8 us (35%)
  Pallas kernels  12 us (17%)
  local copies, waits for them, and re-layouts  3.61 us (5%)
    all_to_all x1, waiting for transfers between devices, shards(): terms = lax.all_to_all(terms, 'head', 0, 0)  16.9 us
    ppermute x2, waiting for transfers between devices, swap_times(): return lax.ppermute(block, 'tile', route)  10.2 us
    ppermute x2, starting transfers between devices, swap_times(): return lax.ppermute(block, 'tile', route)  8.25 us
    ppermute x2, starting transfers between devices, swap_pair(): lax.ppermute(block, 'tile', [(tile, tile ^ 1) for tile, *_ in places()])  6.08 us
    all_to_all x1, starting transfers between devices, shards(): terms = lax.all_to_all(terms, 'head', 0, 0)  5.46 us
    ppermute x2, starting transfers between devices, swap_middle(): return lax.ppermute(block, 'tile', route)  5.02 us
    pallas_call x4, Pallas kernels, attend(): pl.pallas_call(functools.partial(attend_kernel, stage, places), out_shape...  4.85 us
    unnamed x14, local copies, waits for them, and re-layouts  3.6 us
  transfers between devices with their start and end apart: 7, of which 3 were waited for; matrix products, arithmetic and copies ran while one was open for 0% of the time, Pallas kernels for 9%

profile of v8, /device:TPU:177, one launch (start us, length us, event | category | flops | bytes accessed | tf_op | source)
XLA Modules:
  0.0 71.1 jit_solution(625890482911223452)
XLA Ops:
  0.0 2.0 %pack.1 = (bf16[272,384]{1,0:T(8,128)(2,1)}, bf16[512,384]{1,0:T(8,128)(2,1)}) custom-call(s32[1,3]{1,0:T(1,128)} %windows_ref.1, bf16[256,384]{1,0:T(8,128)(2,1)} %q_ref.1, bf16[256,384]{1,0:T(8,128)(2,1)} %k_ref.1, bf16[256,384]{1,0:T(8,128)(2,1)} %v_ref.1), custom_call_target="tpu_custom_call" | custom-call | tf_op jit(solution)/shard_map/pack/pallas_call | solution.py:61
  2.0 6.3 %collective-permute-start.2 = (bf16[512,384]{1,0:T(8,128)(2,1)}, bf16[512,384]{1,0:T(8,128)(2,1)S(1)}, u32[]{:S(2)}, u32[]{:S(2)}) collective-permute-start(bf16[512,384]{1,0:T(8,128)(2,1)} %get-tuple-element.15.refs_2_.own_ref), channel_id=1, source_target_pairs={{32,64},{40,72},{48,80},{56,88},{64,32},{72,40},{80,48},{88,56},{9... | collective-permute-start | bytes 1179656 | tf_op jit(solution)/shard_map/ppermute | solution.py:35
  8.3 1.9 %collective-permute-start.1 = (bf16[512,384]{1,0:T(8,128)(2,1)}, bf16[512,384]{1,0:T(8,128)(2,1)S(1)}, u32[]{:S(2)}, u32[]{:S(2)}) collective-permute-start(bf16[512,384]{1,0:T(8,128)(2,1)} %get-tuple-element.15.refs_2_.own_ref), channel_id=1, source_target_pairs={{0,32},{8,40},{16,48},{24,56},{32,0},{40,8},{48,16},{56,24},{64,96... | collective-permute-start | bytes 1179656 | tf_op jit(solution)/shard_map/ppermute | solution.py:35
  10.2 2.9 %collective-permute-start = (bf16[272,384]{1,0:T(8,128)(2,1)}, bf16[272,384]{1,0:T(8,128)(2,1)S(1)}, u32[]{:S(2)}, u32[]{:S(2)}) collective-permute-start(bf16[272,384]{1,0:T(8,128)(2,1)} %get-tuple-element.14.refs_0_), channel_id=1, source_target_pairs={{0,8},{8,0},{16,24},{24,16},{32,40},{40,32},{48,56},{56,48},{64,72... | collective-permute-start | bytes 626696 | tf_op jit(solution)/shard_map/ppermute | solution.py:39
  13.1 3.1 %collective-permute-start.4 = (bf16[272,384]{1,0:T(8,128)(2,1)}, bf16[272,384]{1,0:T(8,128)(2,1)S(1)}, u32[]{:S(2)}, u32[]{:S(2)}) collective-permute-start(bf16[272,384]{1,0:T(8,128)(2,1)} %get-tuple-element.14.refs_0_), channel_id=1, source_target_pairs={{8,16},{16,8},{40,48},{48,40},{72,80},{80,72},{104,112},{112,104},... | collective-permute-start | bytes 626696 | tf_op jit(solution)/shard_map/ppermute | solution.py:44
  16.2 0.0 collective-permute-done.refs_1_
  16.2 0.0 copy-start
  16.3 1.7 %copy-done = bf16[384,3072]{1,0:T(8,128)(2,1)S(1)} copy-done((bf16[384,3072]{1,0:T(8,128)(2,1)S(1)}, bf16[384,3072]{1,0:T(8,128)(2,1)}, u32[]{:S(2)}) %copy-start) | copy-done | bytes 2359320
  17.9 0.0 copy-start.1
  17.9 0.9 %copy-done.1 = bf16[272,384]{1,0:T(8,128)(2,1)S(1)} copy-done((bf16[272,384]{1,0:T(8,128)(2,1)S(1)}, bf16[272,384]{1,0:T(8,128)(2,1)}, u32[]{:S(2)}) %copy-start.1) | copy-done | bytes 208920
  18.8 1.0 %copy-done.3 = bf16[512,384]{1,0:T(8,128)(2,1)S(1)} copy-done((bf16[512,384]{1,0:T(8,128)(2,1)S(1)}, bf16[512,384]{1,0:T(8,128)(2,1)}, u32[]{:S(2)}) %copy-start.3) | copy-done | bytes 393240
  19.8 1.1 %attend_own0_1.1 = (f32[6,256,128]{2,1,0:T(8,128)S(1)}, f32[12,256,128]{2,1,0:T(8,128)S(1)}, bf16[384,3072]{1,0:T(8,128)(2,1)S(1)}) custom-call(bf16[272,384]{1,0:T(8,128)(2,1)S(1)} %copy-done.1, bf16[272,384]{1,0:T(8,128)(2,1)S(1)} %collective-permute-done.refs_1_, bf16[512,384]{1,0:T(8,128)(2,1)S(1)} %copy-done.3, bf16[384,3072]{1,0:T(8,128)(2,1)S(1)} %copy-done), custom_call_target="tpu_custom_call" | custom-call | flops 201326592 | bytes 2000000 | tf_op jit(solution)/shard_map/attend_own0_1/pallas_call | solution.py:207
  21.0 10.2 %collective-permute-done.2.refs_2_.first_ref = bf16[512,384]{1,0:T(8,128)(2,1)S(1)} collective-permute-done((bf16[512,384]{1,0:T(8,128)(2,1)}, bf16[512,384]{1,0:T(8,128)(2,1)S(1)}, u32[]{:S(2)}, u32[]{:S(2)}) %collective-permute-start.2) | collective-permute-done | bytes 393248 | tf_op jit(solution)/shard_map/ppermute | solution.py:35
  31.2 1.1 %attend_first0_1.1 = (f32[6,256,128]{2,1,0:T(8,128)S(1)}, f32[12,256,128]{2,1,0:T(8,128)S(1)}) custom-call(bf16[272,384]{1,0:T(8,128)(2,1)S(1)} %copy-done.1, bf16[272,384]{1,0:T(8,128)(2,1)S(1)} %collective-permute-done.refs_1_, bf16[512,384]{1,0:T(8,128)(2,1)S(1)} %collective-permute-done.2.refs_2_.first_ref, ...), custom_call_target="tpu_custom_call" | custom-call | flops 201326592 | bytes 2000000 | tf_op jit(solution)/shard_map/attend_first0_1/pallas_call | solution.py:207
  32.3 0.0 collective-permute-done.1.refs_2_.second_ref
  32.4 0.0 copy-start.4
  32.4 0.8 %attend_second1.1.after_ref = bf16[272,384]{1,0:T(8,128)(2,1)S(1)} custom-call(bf16[272,384]{1,0:T(8,128)(2,1)S(1)} %copy-done.1, bf16[272,384]{1,0:T(8,128)(2,1)S(1)} %collective-permute-done.refs_1_, bf16[512,384]{1,0:T(8,128)(2,1)S(1)} %collective-permute-done.1.refs_2_.second_ref, f32[6,256,128]{2,1,0:T(8,128)S(1)} %get-tuple-element.18.refs_3_, ...), custom_call_target="tpu_custom_call" | custom-call | flops 100663296 | bytes 2000000 | tf_op jit(solution)/shard_map/attend_second1/pallas_call | solution.py:207
  33.2 3.2 %collective-permute-start.3 = (bf16[272,384]{1,0:T(8,128)(2,1)S(1)}, bf16[272,384]{1,0:T(8,128)(2,1)S(1)}, u32[]{:S(2)}, u32[]{:S(2)}) collective-permute-start(bf16[272,384]{1,0:T(8,128)(2,1)S(1)} %attend_second1.1.after_ref), channel_id=1, source_target_pairs={{0,8},{8,0},{16,24},{24,16},{32,40},{40,32},{48,56},{56,48},{64,72... | collective-permute-start | bytes 626696 | tf_op jit(solution)/shard_map/ppermute | solution.py:39
  36.4 0.0 collective-permute-done.4.query_ref
  36.4 0.0 copy-done.4
  36.5 1.6 %attend_middle.1 = bf16[272,384]{1,0:T(8,128)(2,1)S(1)} custom-call(bf16[272,384]{1,0:T(8,128)(2,1)S(1)} %collective-permute-done.4.query_ref, bf16[512,384]{1,0:T(8,128)(2,1)S(1)} %copy-done.4, bf16[512,384]{1,0:T(8,128)(2,1)S(1)} %collective-permute-done.2.refs_2_.first_ref, bf16[512,384]{1,0:T(8,128)(2,1)S(1)} %collective-permute-done.1.refs_2_.second_ref, ...), custom_call_target="tpu_custom_call" | custom-call | flops 301989888 | bytes 2000000 | tf_op jit(solution)/shard_map/attend_middle/pallas_call | solution.py:253
  38.0 1.9 %collective-permute-start.5 = (bf16[272,384]{1,0:T(8,128)(2,1)S(1)}, bf16[272,384]{1,0:T(8,128)(2,1)S(1)}, u32[]{:S(2)}, u32[]{:S(2)}) collective-permute-start(bf16[272,384]{1,0:T(8,128)(2,1)S(1)} %attend_middle.1), channel_id=1, source_target_pairs={{8,16},{16,8},{40,48},{48,40},{72,80},{80,72},{104,112},{112,104},... | collective-permute-start | bytes 626696 | tf_op jit(solution)/shard_map/ppermute | solution.py:44
  39.9 0.0 collective-permute-done.3.refs_5_
  40.0 0.0 copy-done.2
  40.0 1.7 %attend_second0.1 = (f32[256,384]{1,0:T(8,128)S(1)}, f32[3,8,256]{2,1,0:T(8,128)S(1)}) custom-call(bf16[272,384]{1,0:T(8,128)(2,1)S(1)} %copy-done.2, bf16[272,384]{1,0:T(8,128)(2,1)S(1)} %collective-permute-done.refs_1_, bf16[512,384]{1,0:T(8,128)(2,1)S(1)} %collective-permute-done.1.refs_2_.second_ref, f32[6,256,128]{2,1,0:T(8,128)S(1)} %get-tuple-element.18.refs_3_, ...), custom_call_target="tpu_custom_call" | custom-call | flops 3500000000 | bytes 2000000 | tf_op jit(solution)/shard_map/attend_second0/pallas_call | solution.py:207
  41.7 3.4 %collective-permute-done.5.middle_ref = bf16[272,384]{1,0:T(8,128)(2,1)S(1)} collective-permute-done((bf16[272,384]{1,0:T(8,128)(2,1)S(1)}, bf16[272,384]{1,0:T(8,128)(2,1)S(1)}, u32[]{:S(2)}, u32[]{:S(2)}) %collective-permute-start.5) | collective-permute-done | bytes 208928 | tf_op jit(solution)/shard_map/ppermute | solution.py:44
  45.1 2.7 %project.1 = bf16[8,256,384]{2,1,0:T(8,128)(2,1)} custom-call(f32[256,384]{1,0:T(8,128)S(1)} %get-tuple-element.20.own_ref, f32[3,8,256]{2,1,0:T(8,128)S(1)} %get-tuple-element.21.stats_ref, bf16[272,384]{1,0:T(8,128)(2,1)S(1)} %collective-permute-done.5.middle_ref, bf16[384,3072]{1,0:T(8,128)(2,1)S(1)} %get-tuple-element.22.weight_ref), custom_call_target="tpu_custom_call" | custom-call | flops 603979776 | bytes 5000000 | tf_op jit(solution)/shard_map/project/pallas_call | solution.py:299
  47.8 5.5 %all-to-all-start = ((bf16[8,256,384]{2,1,0:T(8,128)(2,1)}), bf16[8,256,384]{2,1,0:T(8,128)(2,1)S(1)}, u32[]{:S(2)}, u32[]{:S(2)}) async-start(bf16[8,256,384]{2,1,0:T(8,128)(2,1)} %project.1), calls=%async_computation | async-start | bytes 3145728 | tf_op jit(solution)/shard_map/all_to_all | solution.py:338
  53.3 0.0 copy-done.6
  53.3 16.9 %all-to-all-done.terms_ref = bf16[8,256,384]{2,1,0:T(8,128)(2,1)S(1)} async-done(((bf16[8,256,384]{2,1,0:T(8,128)(2,1)}), bf16[8,256,384]{2,1,0:T(8,128)(2,1)S(1)}, u32[]{:S(2)}, u32[]{:S(2)}) %all-to-all-start) | async-done | bytes 1572896 | tf_op jit(solution)/shard_map/all_to_all | solution.py:338
  70.2 0.0 copy-done.5
  70.2 0.9 %finish.1 = bf16[256,384]{1,0:T(8,128)(2,1)} custom-call(bf16[8,256,384]{2,1,0:T(8,128)(2,1)S(1)} %all-to-all-done.terms_ref, bf16[256,384]{1,0:T(8,128)(2,1)S(1)} %copy-done.5, f32[1,384]{1,0:T(1,128)S(1)} %reshape.3.gate_ref), custom_call_target="tpu_custom_call" | custom-call | flops 7864320 | bytes 2000000 | tf_op jit(solution)/shard_map/finish/pallas_call | solution.py:317
  (5 shorter events, 0.0 us)
Async XLA Ops:
  2.0 29.2 %collective-permute-start.2 = (bf16[512,384]{1,0:T(8,128)(2,1)}, bf16[512,384]{1,0:T(8,128)(2,1)S(1)}, u32[]{:S(2)}, u32[]{:S(2)}) collective-permute-start(bf16[512,384]{1,0:T(8,128)(2,1)} %get-tuple-element.15.refs_2_.own_ref), channel_id=1, source_target_pairs={{32,64},{40,72},{48,80},{56,88},{64,32},{72,40},{80,48},{88,56},{9... | collective-permute-start | bytes 1179656 | tf_op jit(solution)/shard_map/ppermute | solution.py:35
  8.3 24.0 %collective-permute-start.1 = (bf16[512,384]{1,0:T(8,128)(2,1)}, bf16[512,384]{1,0:T(8,128)(2,1)S(1)}, u32[]{:S(2)}, u32[]{:S(2)}) collective-permute-start(bf16[512,384]{1,0:T(8,128)(2,1)} %get-tuple-element.15.refs_2_.own_ref), channel_id=1, source_target_pairs={{0,32},{8,40},{16,48},{24,56},{32,0},{40,8},{48,16},{56,24},{64,96... | collective-permute-start | bytes 1179656 | tf_op jit(solution)/shard_map/ppermute | solution.py:35
  10.2 6.0 %collective-permute-start = (bf16[272,384]{1,0:T(8,128)(2,1)}, bf16[272,384]{1,0:T(8,128)(2,1)S(1)}, u32[]{:S(2)}, u32[]{:S(2)}) collective-permute-start(bf16[272,384]{1,0:T(8,128)(2,1)} %get-tuple-element.14.refs_0_), channel_id=1, source_target_pairs={{0,8},{8,0},{16,24},{24,16},{32,40},{40,32},{48,56},{56,48},{64,72... | collective-permute-start | bytes 626696 | tf_op jit(solution)/shard_map/ppermute | solution.py:39
  13.1 23.3 %collective-permute-start.4 = (bf16[272,384]{1,0:T(8,128)(2,1)}, bf16[272,384]{1,0:T(8,128)(2,1)S(1)}, u32[]{:S(2)}, u32[]{:S(2)}) collective-permute-start(bf16[272,384]{1,0:T(8,128)(2,1)} %get-tuple-element.14.refs_0_), channel_id=1, source_target_pairs={{8,16},{16,8},{40,48},{48,40},{72,80},{80,72},{104,112},{112,104},... | collective-permute-start | bytes 626696 | tf_op jit(solution)/shard_map/ppermute | solution.py:44
  16.2 1.7 %copy-start = (bf16[384,3072]{1,0:T(8,128)(2,1)S(1)}, bf16[384,3072]{1,0:T(8,128)(2,1)}, u32[]{:S(2)}) copy-start(bf16[384,3072]{1,0:T(8,128)(2,1)} %refs_3_.1) | copy-start | bytes 7077892
  17.9 0.9 %copy-start.1 = (bf16[272,384]{1,0:T(8,128)(2,1)S(1)}, bf16[272,384]{1,0:T(8,128)(2,1)}, u32[]{:S(2)}) copy-start(bf16[272,384]{1,0:T(8,128)(2,1)} %get-tuple-element.14.refs_0_) | copy-start | bytes 626692
  18.8 1.0 %copy-start.3 = (bf16[512,384]{1,0:T(8,128)(2,1)S(1)}, bf16[512,384]{1,0:T(8,128)(2,1)}, u32[]{:S(2)}) copy-start(bf16[512,384]{1,0:T(8,128)(2,1)} %get-tuple-element.15.refs_2_.own_ref) | copy-start | bytes 1179652
  32.4 4.1 %copy-start.4 = (bf16[512,384]{1,0:T(8,128)(2,1)S(1)}, bf16[512,384]{1,0:T(8,128)(2,1)}, u32[]{:S(2)}) copy-start(bf16[512,384]{1,0:T(8,128)(2,1)} %get-tuple-element.15.refs_2_.own_ref) | copy-start | bytes 1179652
  33.2 6.8 %copy-start.2 = (bf16[272,384]{1,0:T(8,128)(2,1)S(1)}, bf16[272,384]{1,0:T(8,128)(2,1)}, u32[]{:S(2)}) copy-start(bf16[272,384]{1,0:T(8,128)(2,1)} %get-tuple-element.14.refs_0_) | copy-start | bytes 626692
  33.2 6.7 %collective-permute-start.3 = (bf16[272,384]{1,0:T(8,128)(2,1)S(1)}, bf16[272,384]{1,0:T(8,128)(2,1)S(1)}, u32[]{:S(2)}, u32[]{:S(2)}) collective-permute-start(bf16[272,384]{1,0:T(8,128)(2,1)S(1)} %attend_second1.1.after_ref), channel_id=1, source_target_pairs={{0,8},{8,0},{16,24},{24,16},{32,40},{40,32},{48,56},{56,48},{64,72... | collective-permute-start | bytes 626696 | tf_op jit(solution)/shard_map/ppermute | solution.py:39
  38.0 7.1 %collective-permute-start.5 = (bf16[272,384]{1,0:T(8,128)(2,1)S(1)}, bf16[272,384]{1,0:T(8,128)(2,1)S(1)}, u32[]{:S(2)}, u32[]{:S(2)}) collective-permute-start(bf16[272,384]{1,0:T(8,128)(2,1)S(1)} %attend_middle.1), channel_id=1, source_target_pairs={{8,16},{16,8},{40,48},{48,40},{72,80},{80,72},{104,112},{112,104},... | collective-permute-start | bytes 626696 | tf_op jit(solution)/shard_map/ppermute | solution.py:44
  47.8 5.5 %copy-start.6 = (f32[384]{0:T(512)S(1)}, f32[384]{0:T(512)}, u32[]{:S(2)}) copy-start(f32[384]{0:T(512)} %param.13) | copy-start | bytes 4612
  47.8 22.4 %copy-start.5 = (bf16[256,384]{1,0:T(8,128)(2,1)S(1)}, bf16[256,384]{1,0:T(8,128)(2,1)}, u32[]{:S(2)}) copy-start(bf16[256,384]{1,0:T(8,128)(2,1)} %residual_ref.1) | copy-start | bytes 589828
  47.8 22.4 %all-to-all-start = ((bf16[8,256,384]{2,1,0:T(8,128)(2,1)}), bf16[8,256,384]{2,1,0:T(8,128)(2,1)S(1)}, u32[]{:S(2)}, u32[]{:S(2)}) async-start(bf16[8,256,384]{2,1,0:T(8,128)(2,1)} %project.1), calls=%async_computation | async-start | bytes 3145728 | tf_op jit(solution)/shard_map/all_to_all | solution.py:338

commit v9 on v8

v9 whole, which is shorter than its diff:
```python
import functools

import jax
import jax.numpy as jnp
from jax import lax
from jax.experimental import pallas as pl
from jax.experimental.pallas import tpu as pltpu
from jax.sharding import PartitionSpec as P

HD = 128
HEIGHT_TILES = 4
SIDE = 16
LOG2E = 1.4426950408889634
MASKED = -1e30
LAST_FLOPS = 3_500_000_000
HERE_FLOPS = 2_000_000_000
MESH_AXES = ("tile", "head")
VMEM = pltpu.VMEM
SMEM = pltpu.SMEM


def params(megabytes):
    return pltpu.CompilerParams(vmem_limit_bytes=megabytes * 1024 * 1024)


def places():
    tiles = lax.axis_size("tile")
    return [(tile, *divmod(tile, HEIGHT_TILES), tiles // HEIGHT_TILES) for tile in range(tiles)]


def swap_times(block, later):
    route = []
    for tile, time, height, times in places():
        partner = time + 1 if time % 2 == int(not later) else time - 1
        if 0 <= partner < times:
            route.append((tile, partner * HEIGHT_TILES + height))
    return lax.ppermute(block, "tile", route)


def swap_pair(block):
    return lax.ppermute(block, "tile", [(tile, tile ^ 1) for tile, *_ in places()])


def swap_middle(block):
    route = [(tile, tile + (1 if height == 1 else -1)) for tile, _, height, _ in places() if height in (1, 2)]
    return lax.ppermute(block, "tile", route)


def pack_kernel(windows_ref, q_ref, packed_ref):
    rows = q_ref.shape[0]
    packed_ref[:rows] = q_ref[...]
    for axis in (0, 1):
        extent = windows_ref[0, axis].astype(jnp.float32)
        packed_ref[rows:, axis * HD : (axis + 1) * HD] = jnp.full((SIDE, HD), extent, jnp.float32).astype(packed_ref.dtype)
    packed_ref[rows:, 2 * HD :] = jnp.zeros((SIDE, q_ref.shape[1] - 2 * HD), packed_ref.dtype)


def pack(windows, queries):
    rows, width = queries.shape
    whole = pl.BlockSpec(memory_space=VMEM)
    return pl.pallas_call(
        pack_kernel,
        out_shape=jax.ShapeDtypeStruct((rows + SIDE, width), queries.dtype),
        in_specs=[pl.BlockSpec(memory_space=SMEM), whole],
        out_specs=whole,
        compiler_params=params(8),
        name="pack",
    )(windows, queries)


def column(values, index):
    return values[:, index : index + 1]


def split_float(value):
    high = value.astype(jnp.bfloat16).astype(jnp.float32)
    rest = value - high
    middle = rest.astype(jnp.bfloat16).astype(jnp.float32)
    return high, middle, (rest - middle).astype(jnp.bfloat16).astype(jnp.float32)


def wide_window(ref, rows, axis=0):
    return jnp.max(ref[rows:, axis * HD : (axis + 1) * HD].astype(jnp.float32)) > 0.5


def has_first():
    time = lax.axis_index("tile") // HEIGHT_TILES
    return (time > 0) & (time < lax.axis_size("tile") // HEIGHT_TILES - 1)


def block_bias(wide, stage):
    return jnp.where(wide & has_first() if stage == 1 else wide, 0.0, MASKED)


def raw_scores(query, keys):
    return lax.dot_general(query, keys, (((1,), (1,)), ((), ())), preferred_element_type=jnp.float32)


def put_message(ref, head, mix, stats, row):
    rows = mix.shape[0]
    low = head * HD
    line = lax.broadcasted_iota(jnp.int32, (8, rows), 0)
    ref[:rows, low : low + HD] = mix.astype(ref.dtype)
    side = jnp.zeros((8, rows), jnp.float32)
    for index, piece in enumerate(split_float(stats[row : row + 1]) + split_float(stats[row + 1 : row + 2])):
        side = jnp.where(line == index, piece, side)
    ref[rows:, low : low + HD] = jnp.concatenate([side[:, :HD], side[:, HD:]], axis=0).astype(ref.dtype)


def message_stats(ref, head, rows):
    side = ref[rows:, head * HD : (head + 1) * HD].astype(jnp.float32)
    side = jnp.concatenate([side[:8], side[8:]], axis=1)
    return side[0:1] + side[1:2] + side[2:3], side[3:4] + side[4:5] + side[5:6]


def message_columns(ref, head, rows):
    line = lax.broadcasted_iota(jnp.int32, (8, rows), 0)
    largest, total = message_stats(ref, head, rows)
    columns = jnp.transpose(jnp.where(line == 0, largest, jnp.where(line == 1, total, 0.0)))
    return [jnp.broadcast_to(column(columns, index), (rows, HD)) for index in (0, 1)]


def attend(query, blocks, biases, low, old=None):
    rows = blocks[0][0].shape[0]
    scale = HD**-0.5 * LOG2E
    spread = lambda value: jnp.broadcast_to(value, (rows, HD))
    parts = [raw_scores(query, keys[:, low : low + HD]) for keys, _ in blocks]
    largest = None if old is None else old[0]
    for part, bias in zip(parts, biases):
        peak = spread(jnp.max(part, axis=1, keepdims=True)) * scale + bias
        largest = peak if largest is None else jnp.maximum(largest, peak)
    summed, mix = None, None
    for part, bias, (_, values) in zip(parts, biases, blocks):
        offset = jnp.concatenate([bias - largest] * (rows // HD), axis=1)
        weights = jnp.exp2(part * scale + offset)
        product = jnp.dot(weights.astype(values.dtype), values[:, low : low + HD], preferred_element_type=jnp.float32)
        summed = weights if summed is None else summed + weights
        mix = product if mix is None else mix + product
    total = spread(jnp.sum(summed, axis=1, keepdims=True))
    if old is not None:
        shrink = jnp.exp2(old[0] - largest)
        total, mix = total + old[1] * shrink, mix + old[2] * shrink
    return largest, total, mix


def row_stats(largest, total):
    lane = lax.broadcasted_iota(jnp.int32, largest.shape, 1)
    return jnp.transpose(jnp.where(lane == 0, largest, jnp.where(lane == 1, total, 0.0)))[:8]


def own_kernel(query_ref, key_ref, value_ref, weight_ref, mix_ref, stats_ref, held_ref, sem):
    copy = pltpu.make_async_copy(weight_ref, held_ref, sem)
    copy.start()
    rows, width = key_ref.shape
    for head in range(width // HD):
        low = head * HD
        largest, total, mix = attend(query_ref[:rows, low : low + HD], [(key_ref, value_ref)], [0.0], low)
        mix_ref[head], stats_ref[2 * head], stats_ref[2 * head + 1] = mix, largest, total
    copy.wait()


def attend_own(queries, block, out_weight):
    rows, width = block[0].shape
    heads = width // HD
    whole = pl.BlockSpec(memory_space=VMEM)
    return pl.pallas_call(
        own_kernel,
        out_shape=(
            jax.ShapeDtypeStruct((heads, rows, HD), jnp.float32),
            jax.ShapeDtypeStruct((2 * heads, rows, HD), jnp.float32),
            jax.ShapeDtypeStruct(out_weight.shape, out_weight.dtype),
        ),
        in_specs=[whole] * 3 + [pl.BlockSpec(memory_space=pl.ANY)],
        out_specs=(whole,) * 3,
        scratch_shapes=[pltpu.SemaphoreType.DMA],
        compiler_params=params(24),
        cost_estimate=pl.CostEstimate(flops=0, bytes_accessed=0, transcendentals=0),
        name="attend_own",
    )(queries, *block, out_weight)


def neighbour_kernel(middle, query_ref, *refs):
    blocks = [(refs[2 * i], refs[2 * i + 1]) for i in range(3)]
    out_ref = refs[-1]
    rows, width = blocks[0][0].shape
    height = lax.axis_index("tile") % HEIGHT_TILES

    def compute():
        wide = wide_window(query_ref, rows)
        biases = [0.0] + [block_bias(wide, stage) for stage in (1, 2)]
        for head in range(width // HD):
            low = head * HD
            largest, total, mix = attend(query_ref[:rows, low : low + HD], blocks, biases, low)
            put_message(out_ref, head, mix, row_stats(largest, total), 0)

    if not middle:
        compute()
        return
    inside = (height > 0) & (height < HEIGHT_TILES - 1)
    pl.when(inside)(compute)

    @pl.when(jnp.logical_not(inside))
    def skip():
        out_ref[...] = jnp.zeros_like(out_ref)


def attend_neighbour(middle, query, blocks, after=()):
    rows, width = blocks[0][0].shape
    whole = pl.BlockSpec(memory_space=VMEM)
    cost = 3 * (width // HD) * rows * rows
    return pl.pallas_call(
        functools.partial(neighbour_kernel, middle),
        out_shape=jax.ShapeDtypeStruct((rows + SIDE, width), jnp.bfloat16),
        in_specs=[whole] * 7 + [pl.BlockSpec(memory_space=pl.ANY)] * len(after),
        out_specs=whole,
        compiler_params=params(24),
        cost_estimate=pl.CostEstimate(flops=4 * HD * cost, bytes_accessed=2_000_000, transcendentals=cost),
        name="attend_middle" if middle else "attend_pair",
    )(query, *[array for block in blocks for array in block], *after)


def here_kernel(*refs):
    refs[-1][...] = jnp.zeros_like(refs[-1])


def all_here(arrays):
    return pl.pallas_call(
        here_kernel,
        out_shape=jax.ShapeDtypeStruct((8, HD), jnp.float32),
        in_specs=[pl.BlockSpec(memory_space=pl.ANY)] * len(arrays),
        out_specs=pl.BlockSpec(memory_space=VMEM),
        compiler_params=params(4),
        cost_estimate=pl.CostEstimate(flops=HERE_FLOPS, bytes_accessed=0, transcendentals=0),
        name="all_here",
    )(*arrays)


def last_kernel(query_ref, k1_ref, v1_ref, k2_ref, v2_ref, old_mix_ref, old_stats_ref, message_ref, mix_ref, stats_ref):
    rows, width = k1_ref.shape
    wide = wide_window(query_ref, rows, 1)
    biases = [block_bias(wide_window(query_ref, rows), stage) for stage in (1, 2)]
    for head in range(width // HD):
        low = head * HD
        old = (old_stats_ref[2 * head], old_stats_ref[2 * head + 1], old_mix_ref[head])
        blocks = [(k1_ref, v1_ref), (k2_ref, v2_ref)]
        largest, total, mix = attend(query_ref[:rows, low : low + HD], blocks, biases, low, old)
        their_largest, their_total = message_columns(message_ref, head, rows)
        peak = jnp.maximum(largest, jnp.where(wide, their_largest, MASKED))
        shrink, share = jnp.exp2(largest - peak), jnp.where(wide, jnp.exp2(their_largest - peak), 0.0)
        stats = row_stats(peak, total * shrink + their_total * share)
        mix_ref[:, low : low + HD] = mix * shrink + message_ref[:rows, low : low + HD].astype(jnp.float32) * share
        line = lax.broadcasted_iota(jnp.int32, stats.shape, 0)
        stats_ref[head] = jnp.where(line == 2, jnp.where(wide, 1.0, 0.0), stats)


def attend_last(queries, first, second, mix, stats, message):
    rows, width = first[0].shape
    whole = pl.BlockSpec(memory_space=VMEM)
    return pl.pallas_call(
        last_kernel,
        out_shape=(
            jax.ShapeDtypeStruct((rows, width), jnp.float32),
            jax.ShapeDtypeStruct((width // HD, 8, rows), jnp.float32),
        ),
        in_specs=[whole] * 8,
        out_specs=(whole, whole),
        compiler_params=params(24),
        cost_estimate=pl.CostEstimate(flops=LAST_FLOPS, bytes_accessed=2_000_000, transcendentals=0),
        name="attend_last",
    )(queries, *first, *second, mix, stats, message)


def project_kernel(own_ref, stats_ref, middle_ref, weight_ref, out_ref):
    rows, width = own_ref.shape
    heads = width // HD
    height = lax.axis_index("tile") % HEIGHT_TILES
    inside = jnp.where((height > 0) & (height < HEIGHT_TILES - 1), 1.0, 0.0)
    line = lax.broadcasted_iota(jnp.int32, (8, rows), 0)
    shares = jnp.zeros((8, rows), jnp.float32)
    for head in range(heads):
        stats = stats_ref[head]
        their_largest, their_total = message_stats(middle_ref, head, rows)
        valid = stats[2:3] * inside > 0.5
        peak = jnp.maximum(stats[0:1], jnp.where(valid, their_largest, MASKED))
        shrink = jnp.exp2(stats[0:1] - peak)
        share = jnp.where(valid, jnp.exp2(their_largest - peak), 0.0)
        whole = stats[1:2] * shrink + their_total * share
        shares = jnp.where(line == 2 * head, shrink / whole, shares)
        shares = jnp.where(line == 2 * head + 1, share / whole, shares)
    shares = jnp.transpose(shares)
    merged = []
    for head in range(heads):
        low = head * HD
        value = own_ref[:, low : low + HD] * column(shares, 2 * head)
        value += middle_ref[:rows, low : low + HD].astype(jnp.float32) * column(shares, 2 * head + 1)
        merged.append(value.astype(jnp.bfloat16))
    attention = jnp.concatenate(merged, axis=1)
    for group in range(out_ref.shape[0]):
        out_ref[group] = jnp.dot(
            attention, weight_ref[:, group * width : (group + 1) * width], preferred_element_type=jnp.float32
        ).astype(out_ref.dtype)


def project(own, stats, middle, out_weight):
    rows, width = own.shape
    features = out_weight.shape[1]
    whole = pl.BlockSpec(memory_space=VMEM)
    return pl.pallas_call(
        project_kernel,
        out_shape=jax.ShapeDtypeStruct((features // width, rows, width), jnp.bfloat16),
        in_specs=[whole] * 4,
        out_specs=whole,
        compiler_params=params(24),
        cost_estimate=pl.CostEstimate(flops=2 * rows * width * features, bytes_accessed=5_000_000, transcendentals=0),
        name="project",
    )(own, stats, middle, out_weight)


def finish_kernel(terms_ref, residual_ref, gate_ref, out_ref):
    total = jnp.sum(terms_ref[...].astype(jnp.float32), axis=0)
    out_ref[...] = (residual_ref[...].astype(jnp.float32) + gate_ref[...] * total).astype(out_ref.dtype)


def finish(terms, residual, gate_scale):
    whole = pl.BlockSpec(memory_space=VMEM)
    return pl.pallas_call(
        finish_kernel,
        out_shape=jax.ShapeDtypeStruct(residual.shape, residual.dtype),
        in_specs=[whole] * 3,
        out_specs=whole,
        compiler_params=params(24),
        cost_estimate=pl.CostEstimate(flops=10 * terms.size, bytes_accessed=2_000_000, transcendentals=0),
        name="finish",
    )(terms, residual, gate_scale.reshape(1, -1))


def shards(queries, key_rows, value_rows, windows, residual, out_weight, gate_scale):
    own_block = (key_rows, value_rows)
    first, second = [[swap_times(array, later) for array in own_block] for later in (False, True)]
    packed = pack(windows, queries)
    blocks = (own_block, first, second)
    mix, stats, held_weight = attend_own(packed, own_block, out_weight)
    asked = swap_pair(packed), swap_middle(packed)
    for_pair = attend_neighbour(False, asked[0], blocks, (stats, all_here(first + second), asked[1]))
    for_middle = attend_neighbour(True, asked[1], blocks, (for_pair,))
    mix, stats = attend_last(packed, first, second, mix, stats, swap_pair(for_pair))
    terms = project(mix, stats, swap_middle(for_middle), held_weight)
    terms = lax.all_to_all(terms, "head", 0, 0)
    return finish(terms, residual, gate_scale)


def solution(mesh):
    return jax.shard_map(
        shards,
        mesh=mesh,
        in_specs=(
            P("tile", "head"),
            P("tile", "head"),
            P("tile", "head"),
            P("tile", None),
            P("tile", "head"),
            P("head", None),
            P("head"),
        ),
        out_specs=P("tile", "head"),
        check_vma=False,
    )
```

time: 71.5 us -> 72.4 us (1.013)
  the two profiles are of different devices: /device:TPU:177 before, /device:TPU:1 now
where the time goes in v9:
time: 72.4 us; the launch traced here: 71 us
  starting transfers between devices  32.9 us (45%)
  waiting for transfers between devices  22.6 us (31%)
  Pallas kernels  10.2 us (14%)
  local copies, waits for them, and re-layouts  5.11 us (7%)
    all_to_all x1, waiting for transfers between devices, shards(): terms = lax.all_to_all(terms, 'head', 0, 0)  16.6 us
    ppermute x4, starting transfers between devices, swap_times(): return lax.ppermute(block, 'tile', route)  14.4 us
    ppermute x2, starting transfers between devices, swap_middle(): return lax.ppermute(block, 'tile', route)  9 us
    ppermute x2, waiting for transfers between devices, swap_middle(): return lax.ppermute(block, 'tile', route)  5.77 us
    all_to_all x1, starting transfers between devices, shards(): terms = lax.all_to_all(terms, 'head', 0, 0)  5.74 us
    unnamed x18, local copies, waits for them, and re-layouts  5.11 us
    ppermute x2, starting transfers between devices, swap_pair(): lax.ppermute(block, 'tile', [(tile, tile ^ 1) for tile, *_ in places()])  3.84 us
    pallas_call x2, Pallas kernels, attend_neighbour(): pl.pallas_call(functools.partial(neighbour_kernel, middle), out_shape=jax...  3.04 us
  transfers between devices with their start and end apart: 9, of which 4 were waited for; matrix products, arithmetic and copies ran while one was open for 0% of the time, Pallas kernels for 7%

profile of v9, /device:TPU:1, one launch (start us, length us, event | category | flops | bytes accessed | tf_op | source)
XLA Modules:
  0.0 71.0 jit_solution(14442766250993359587)
XLA Ops:
  0.0 0.7 collective-permute-start
  0.7 0.7 collective-permute-start.1
  1.4 11.1 %collective-permute-start.2 = (bf16[256,384]{1,0:T(8,128)(2,1)}, bf16[256,384]{1,0:T(8,128)(2,1)S(1)}, u32[]{:S(2)}, u32[]{:S(2)}) collective-permute-start(bf16[256,384]{1,0:T(8,128)(2,1)} %refs_0_.3), channel_id=1, source_target_pairs={{0,32},{8,40},{16,48},{24,56},{32,0},{40,8},{48,16},{56,24},{64,96... | collective-permute-start | bytes 589832 | tf_op jit(solution)/shard_map/ppermute | solution.py:37
  12.5 1.9 %collective-permute-start.3 = (bf16[256,384]{1,0:T(8,128)(2,1)}, bf16[256,384]{1,0:T(8,128)(2,1)S(1)}, u32[]{:S(2)}, u32[]{:S(2)}) collective-permute-start(bf16[256,384]{1,0:T(8,128)(2,1)} %refs_1_.3), channel_id=1, source_target_pairs={{0,32},{8,40},{16,48},{24,56},{32,0},{40,8},{48,16},{56,24},{64,96... | collective-permute-start | bytes 589832 | tf_op jit(solution)/shard_map/ppermute | solution.py:37
  14.4 0.9 %copy-done.5 = bf16[256,384]{1,0:T(8,128)(2,1)S(1)} copy-done((bf16[256,384]{1,0:T(8,128)(2,1)S(1)}, bf16[256,384]{1,0:T(8,128)(2,1)}, u32[]{:S(2)}) %copy-start.5) | copy-done | bytes 196632
  15.3 0.7 copy-done.7
  16.0 0.6 pack.1.query_ref
  16.5 4.6 %collective-permute-start.5 = (bf16[272,384]{1,0:T(8,128)(2,1)S(1)}, bf16[272,384]{1,0:T(8,128)(2,1)S(1)}, u32[]{:S(2)}, u32[]{:S(2)}) collective-permute-start(bf16[272,384]{1,0:T(8,128)(2,1)S(1)} %pack.1.query_ref), channel_id=1, source_target_pairs={{8,16},{16,8},{40,48},{48,40},{72,80},{80,72},{104,112},{112,104},... | collective-permute-start | bytes 626696 | tf_op jit(solution)/shard_map/ppermute | solution.py:46
  21.2 0.0 collective-permute-done.refs_0_.refs_2_.k1_ref
  21.2 1.9 %collective-permute-start.4 = (bf16[272,384]{1,0:T(8,128)(2,1)S(1)}, bf16[272,384]{1,0:T(8,128)(2,1)S(1)}, u32[]{:S(2)}, u32[]{:S(2)}) collective-permute-start(bf16[272,384]{1,0:T(8,128)(2,1)S(1)} %pack.1.query_ref), channel_id=1, source_target_pairs={{0,8},{8,0},{16,24},{24,16},{32,40},{40,32},{48,56},{56,48},{64,72... | collective-permute-start | bytes 626696 | tf_op jit(solution)/shard_map/ppermute | solution.py:41
  23.1 0.0 copy-start
  23.1 1.7 %copy-done = bf16[384,3072]{1,0:T(8,128)(2,1)S(1)} copy-done((bf16[384,3072]{1,0:T(8,128)(2,1)S(1)}, bf16[384,3072]{1,0:T(8,128)(2,1)}, u32[]{:S(2)}) %copy-start) | copy-done | bytes 2359320
  24.8 0.9 %copy-done.1 = bf16[256,384]{1,0:T(8,128)(2,1)S(1)} copy-done((bf16[256,384]{1,0:T(8,128)(2,1)S(1)}, bf16[256,384]{1,0:T(8,128)(2,1)}, u32[]{:S(2)}) %copy-start.1) | copy-done | bytes 196632
  25.7 0.9 %copy-done.3 = bf16[256,384]{1,0:T(8,128)(2,1)S(1)} copy-done((bf16[256,384]{1,0:T(8,128)(2,1)S(1)}, bf16[256,384]{1,0:T(8,128)(2,1)}, u32[]{:S(2)}) %copy-start.3) | copy-done | bytes 196632
  26.6 0.9 %attend_own.1 = (f32[3,256,128]{2,1,0:T(8,128)S(1)}, f32[6,256,128]{2,1,0:T(8,128)S(1)}, bf16[384,3072]{1,0:T(8,128)(2,1)S(1)}) custom-call(bf16[272,384]{1,0:T(8,128)(2,1)S(1)} %pack.1.query_ref, bf16[256,384]{1,0:T(8,128)(2,1)S(1)} %copy-done.1, bf16[256,384]{1,0:T(8,128)(2,1)S(1)} %copy-done.3, bf16[384,3072]{1,0:T(8,128)(2,1)S(1)} %copy-done), custom_call_target="tpu_custom_call" | custom-call | tf_op jit(solution)/shard_map/attend_own/pallas_call | solution.py:166
  27.6 0.0 copy-start.2
  27.6 0.0 copy-start.4
  27.6 0.0 collective-permute-done.1.refs_1_.refs_3_.v1_ref
  27.6 0.2 collective-permute-done.3.refs_3_.refs_5_.v2_ref
  27.8 4.4 %collective-permute-done.5.refs_8_.query_ref = bf16[272,384]{1,0:T(8,128)(2,1)S(1)} collective-permute-done((bf16[272,384]{1,0:T(8,128)(2,1)S(1)}, bf16[272,384]{1,0:T(8,128)(2,1)S(1)}, u32[]{:S(2)}, u32[]{:S(2)}) %collective-permute-start.5) | collective-permute-done | bytes 208928 | tf_op jit(solution)/shard_map/ppermute | solution.py:46
  32.1 0.0 collective-permute-done.4.query_ref
  32.2 1.5 %attend_pair.1.refs_6_ = bf16[272,384]{1,0:T(8,128)(2,1)S(1)} custom-call(bf16[272,384]{1,0:T(8,128)(2,1)S(1)} %collective-permute-done.4.query_ref, bf16[256,384]{1,0:T(8,128)(2,1)S(1)} %copy-done.2, bf16[256,384]{1,0:T(8,128)(2,1)S(1)} %copy-done.4, bf16[256,384]{1,0:T(8,128)(2,1)S(1)} %collective-permute-done.refs_0_.refs_2_.k1_ref, ...), custom_call_target="tpu_custom_call" | custom-call | flops 301989888 | bytes 2000000 | tf_op jit(solution)/shard_map/attend_pair/pallas_call | solution.py:211
  33.7 1.9 %collective-permute-start.6 = (bf16[272,384]{1,0:T(8,128)(2,1)S(1)}, bf16[272,384]{1,0:T(8,128)(2,1)S(1)}, u32[]{:S(2)}, u32[]{:S(2)}) collective-permute-start(bf16[272,384]{1,0:T(8,128)(2,1)S(1)} %attend_pair.1.refs_6_), channel_id=1, source_target_pairs={{0,8},{8,0},{16,24},{24,16},{32,40},{40,32},{48,56},{56,48},{64,72... | collective-permute-start | bytes 626696 | tf_op jit(solution)/shard_map/ppermute | solution.py:41
  35.6 1.5 %attend_middle.1 = bf16[272,384]{1,0:T(8,128)(2,1)S(1)} custom-call(bf16[272,384]{1,0:T(8,128)(2,1)S(1)} %collective-permute-done.5.refs_8_.query_ref, bf16[256,384]{1,0:T(8,128)(2,1)S(1)} %copy-done.2, bf16[256,384]{1,0:T(8,128)(2,1)S(1)} %copy-done.4, bf16[256,384]{1,0:T(8,128)(2,1)S(1)} %collective-permute-done.refs_0_.refs_2_.k1_ref, ...), custom_call_target="tpu_custom_call" | custom-call | flops 301989888 | bytes 2000000 | tf_op jit(solution)/shard_map/attend_middle/pallas_call | solution.py:211
  37.1 4.4 %collective-permute-start.7 = (bf16[272,384]{1,0:T(8,128)(2,1)S(1)}, bf16[272,384]{1,0:T(8,128)(2,1)S(1)}, u32[]{:S(2)}, u32[]{:S(2)}) collective-permute-start(bf16[272,384]{1,0:T(8,128)(2,1)S(1)} %attend_middle.1), channel_id=1, source_target_pairs={{8,16},{16,8},{40,48},{48,40},{72,80},{80,72},{104,112},{112,104},... | collective-permute-start | bytes 626696 | tf_op jit(solution)/shard_map/ppermute | solution.py:46
  41.5 0.0 collective-permute-done.6.message_ref
  41.6 2.0 %attend_last.1 = (f32[256,384]{1,0:T(8,128)S(1)}, f32[3,8,256]{2,1,0:T(8,128)S(1)}) custom-call(bf16[272,384]{1,0:T(8,128)(2,1)S(1)} %pack.1.query_ref, bf16[256,384]{1,0:T(8,128)(2,1)S(1)} %collective-permute-done.refs_0_.refs_2_.k1_ref, bf16[256,384]{1,0:T(8,128)(2,1)S(1)} %collective-permute-done.1.refs_1_.refs_3_.v1_ref, ...), custom_call_target="tpu_custom_call" | custom-call | flops 3500000000 | bytes 2000000 | tf_op jit(solution)/shard_map/attend_last/pallas_call | solution.py:259
  43.6 1.4 %collective-permute-done.7.middle_ref = bf16[272,384]{1,0:T(8,128)(2,1)S(1)} collective-permute-done((bf16[272,384]{1,0:T(8,128)(2,1)S(1)}, bf16[272,384]{1,0:T(8,128)(2,1)S(1)}, u32[]{:S(2)}, u32[]{:S(2)}) %collective-permute-start.7) | collective-permute-done | bytes 208928 | tf_op jit(solution)/shard_map/ppermute | solution.py:46
  45.0 2.7 %project.1 = bf16[8,256,384]{2,1,0:T(8,128)(2,1)} custom-call(f32[256,384]{1,0:T(8,128)S(1)} %get-tuple-element.12.own_ref, f32[3,8,256]{2,1,0:T(8,128)S(1)} %get-tuple-element.13.stats_ref, bf16[272,384]{1,0:T(8,128)(2,1)S(1)} %collective-permute-done.7.middle_ref, bf16[384,3072]{1,0:T(8,128)(2,1)S(1)} %get-tuple-element.14.weight_ref), custom_call_target="tpu_custom_call" | custom-call | flops 603979776 | bytes 5000000 | tf_op jit(solution)/shard_map/project/pallas_call | solution.py:308
  47.7 5.7 %all-to-all-start = ((bf16[8,256,384]{2,1,0:T(8,128)(2,1)}), bf16[8,256,384]{2,1,0:T(8,128)(2,1)S(1)}, u32[]{:S(2)}, u32[]{:S(2)}) async-start(bf16[8,256,384]{2,1,0:T(8,128)(2,1)} %project.1), calls=%async_computation | async-start | bytes 3145728 | tf_op jit(solution)/shard_map/all_to_all | solution.py:348
  53.4 16.6 %all-to-all-done.terms_ref = bf16[8,256,384]{2,1,0:T(8,128)(2,1)S(1)} async-done(((bf16[8,256,384]{2,1,0:T(8,128)(2,1)}), bf16[8,256,384]{2,1,0:T(8,128)(2,1)S(1)}, u32[]{:S(2)}, u32[]{:S(2)}) %all-to-all-start) | async-done | bytes 1572896 | tf_op jit(solution)/shard_map/all_to_all | solution.py:348
  70.1 0.9 %finish.1 = bf16[256,384]{1,0:T(8,128)(2,1)} custom-call(bf16[8,256,384]{2,1,0:T(8,128)(2,1)S(1)} %all-to-all-done.terms_ref, bf16[256,384]{1,0:T(8,128)(2,1)S(1)} %copy-done.6, f32[1,384]{1,0:T(1,128)S(1)} %reshape.3.gate_ref), custom_call_target="tpu_custom_call" | custom-call | flops 7864320 | bytes 2000000 | tf_op jit(solution)/shard_map/finish/pallas_call | solution.py:326
  (13 shorter events, 0.0 us)
Async XLA Ops:
  0.0 21.2 %collective-permute-start = (bf16[256,384]{1,0:T(8,128)(2,1)}, bf16[256,384]{1,0:T(8,128)(2,1)S(1)}, u32[]{:S(2)}, u32[]{:S(2)}) collective-permute-start(bf16[256,384]{1,0:T(8,128)(2,1)} %refs_0_.3), channel_id=1, source_target_pairs={{32,64},{40,72},{48,80},{56,88},{64,32},{72,40},{80,48},{88,56},{9... | collective-permute-start | bytes 589832 | tf_op jit(solution)/shard_map/ppermute | solution.py:37
  0.7 26.9 %collective-permute-start.1 = (bf16[256,384]{1,0:T(8,128)(2,1)}, bf16[256,384]{1,0:T(8,128)(2,1)S(1)}, u32[]{:S(2)}, u32[]{:S(2)}) collective-permute-start(bf16[256,384]{1,0:T(8,128)(2,1)} %refs_1_.3), channel_id=1, source_target_pairs={{32,64},{40,72},{48,80},{56,88},{64,32},{72,40},{80,48},{88,56},{9... | collective-permute-start | bytes 589832 | tf_op jit(solution)/shard_map/ppermute | solution.py:37
  1.4 26.2 %collective-permute-start.2 = (bf16[256,384]{1,0:T(8,128)(2,1)}, bf16[256,384]{1,0:T(8,128)(2,1)S(1)}, u32[]{:S(2)}, u32[]{:S(2)}) collective-permute-start(bf16[256,384]{1,0:T(8,128)(2,1)} %refs_0_.3), channel_id=1, source_target_pairs={{0,32},{8,40},{16,48},{24,56},{32,0},{40,8},{48,16},{56,24},{64,96... | collective-permute-start | bytes 589832 | tf_op jit(solution)/shard_map/ppermute | solution.py:37
  12.5 15.3 %collective-permute-start.3 = (bf16[256,384]{1,0:T(8,128)(2,1)}, bf16[256,384]{1,0:T(8,128)(2,1)S(1)}, u32[]{:S(2)}, u32[]{:S(2)}) collective-permute-start(bf16[256,384]{1,0:T(8,128)(2,1)} %refs_1_.3), channel_id=1, source_target_pairs={{0,32},{8,40},{16,48},{24,56},{32,0},{40,8},{48,16},{56,24},{64,96... | collective-permute-start | bytes 589832 | tf_op jit(solution)/shard_map/ppermute | solution.py:37
  14.4 0.9 %copy-start.5 = (bf16[256,384]{1,0:T(8,128)(2,1)S(1)}, bf16[256,384]{1,0:T(8,128)(2,1)}, u32[]{:S(2)}) copy-start(bf16[256,384]{1,0:T(8,128)(2,1)} %q_ref.1) | copy-start | bytes 589828
  15.3 0.7 copy-start.7
  16.5 15.6 %collective-permute-start.5 = (bf16[272,384]{1,0:T(8,128)(2,1)S(1)}, bf16[272,384]{1,0:T(8,128)(2,1)S(1)}, u32[]{:S(2)}, u32[]{:S(2)}) collective-permute-start(bf16[272,384]{1,0:T(8,128)(2,1)S(1)} %pack.1.query_ref), channel_id=1, source_target_pairs={{8,16},{16,8},{40,48},{48,40},{72,80},{80,72},{104,112},{112,104},... | collective-permute-start | bytes 626696 | tf_op jit(solution)/shard_map/ppermute | solution.py:46
  21.2 11.0 %collective-permute-start.4 = (bf16[272,384]{1,0:T(8,128)(2,1)S(1)}, bf16[272,384]{1,0:T(8,128)(2,1)S(1)}, u32[]{:S(2)}, u32[]{:S(2)}) collective-permute-start(bf16[272,384]{1,0:T(8,128)(2,1)S(1)} %pack.1.query_ref), channel_id=1, source_target_pairs={{0,8},{8,0},{16,24},{24,16},{32,40},{40,32},{48,56},{56,48},{64,72... | collective-permute-start | bytes 626696 | tf_op jit(solution)/shard_map/ppermute | solution.py:41
  23.1 1.7 %copy-start = (bf16[384,3072]{1,0:T(8,128)(2,1)S(1)}, bf16[384,3072]{1,0:T(8,128)(2,1)}, u32[]{:S(2)}) copy-start(bf16[384,3072]{1,0:T(8,128)(2,1)} %weight_ref.1) | copy-start | bytes 7077892
  24.8 0.9 %copy-start.1 = (bf16[256,384]{1,0:T(8,128)(2,1)S(1)}, bf16[256,384]{1,0:T(8,128)(2,1)}, u32[]{:S(2)}) copy-start(bf16[256,384]{1,0:T(8,128)(2,1)} %refs_0_.3) | copy-start | bytes 589828
  25.7 0.9 %copy-start.3 = (bf16[256,384]{1,0:T(8,128)(2,1)S(1)}, bf16[256,384]{1,0:T(8,128)(2,1)}, u32[]{:S(2)}) copy-start(bf16[256,384]{1,0:T(8,128)(2,1)} %refs_1_.3) | copy-start | bytes 589828
  27.6 4.6 %copy-start.2 = (bf16[256,384]{1,0:T(8,128)(2,1)S(1)}, bf16[256,384]{1,0:T(8,128)(2,1)}, u32[]{:S(2)}) copy-start(bf16[256,384]{1,0:T(8,128)(2,1)} %refs_0_.3) | copy-start | bytes 589828
  27.6 4.6 %copy-start.4 = (bf16[256,384]{1,0:T(8,128)(2,1)S(1)}, bf16[256,384]{1,0:T(8,128)(2,1)}, u32[]{:S(2)}) copy-start(bf16[256,384]{1,0:T(8,128)(2,1)} %refs_1_.3) | copy-start | bytes 589828
  33.7 7.9 %collective-permute-start.6 = (bf16[272,384]{1,0:T(8,128)(2,1)S(1)}, bf16[272,384]{1,0:T(8,128)(2,1)S(1)}, u32[]{:S(2)}, u32[]{:S(2)}) collective-permute-start(bf16[272,384]{1,0:T(8,128)(2,1)S(1)} %attend_pair.1.refs_6_), channel_id=1, source_target_pairs={{0,8},{8,0},{16,24},{24,16},{32,40},{40,32},{48,56},{56,48},{64,72... | collective-permute-start | bytes 626696 | tf_op jit(solution)/shard_map/ppermute | solution.py:41
  37.1 7.9 %collective-permute-start.7 = (bf16[272,384]{1,0:T(8,128)(2,1)S(1)}, bf16[272,384]{1,0:T(8,128)(2,1)S(1)}, u32[]{:S(2)}, u32[]{:S(2)}) collective-permute-start(bf16[272,384]{1,0:T(8,128)(2,1)S(1)} %attend_middle.1), channel_id=1, source_target_pairs={{8,16},{16,8},{40,48},{48,40},{72,80},{80,72},{104,112},{112,104},... | collective-permute-start | bytes 626696 | tf_op jit(solution)/shard_map/ppermute | solution.py:46
  47.7 5.7 %copy-start.8 = (f32[384]{0:T(512)S(1)}, f32[384]{0:T(512)}, u32[]{:S(2)}) copy-start(f32[384]{0:T(512)} %param.13) | copy-start | bytes 4612
  47.7 22.4 %copy-start.6 = (bf16[256,384]{1,0:T(8,128)(2,1)S(1)}, bf16[256,384]{1,0:T(8,128)(2,1)}, u32[]{:S(2)}) copy-start(bf16[256,384]{1,0:T(8,128)(2,1)} %residual_ref.1) | copy-start | bytes 589828
  47.7 22.4 %all-to-all-start = ((bf16[8,256,384]{2,1,0:T(8,128)(2,1)}), bf16[8,256,384]{2,1,0:T(8,128)(2,1)S(1)}, u32[]{:S(2)}, u32[]{:S(2)}) async-start(bf16[8,256,384]{2,1,0:T(8,128)(2,1)} %project.1), calls=%async_computation | async-start | bytes 3145728 | tf_op jit(solution)/shard_map/all_to_all | solution.py:348

commit v10 on v9

--- a/solution.py
+++ b/solution.py
@@ -12,8 +12,7 @@
 SIDE = 16
 LOG2E = 1.4426950408889634
 MASKED = -1e30
-LAST_FLOPS = 3_500_000_000
-HERE_FLOPS = 2_000_000_000
+LAST_FLOPS = 400_000_000
 MESH_AXES = ("tile", "head")
 VMEM = pltpu.VMEM
 SMEM = pltpu.SMEM
@@ -46,8 +45,10 @@
     return lax.ppermute(block, "tile", route)
 
 
-def pack_kernel(windows_ref, q_ref, packed_ref):
+def pack_kernel(windows_ref, q_ref, k_ref, v_ref, packed_ref, block_ref):
     rows = q_ref.shape[0]
+    block_ref[:rows] = k_ref[...]
+    block_ref[rows:] = v_ref[...]
     packed_ref[:rows] = q_ref[...]
     for axis in (0, 1):
         extent = windows_ref[0, axis].astype(jnp.float32)
@@ -55,17 +56,19 @@
     packed_ref[rows:, 2 * HD :] = jnp.zeros((SIDE, q_ref.shape[1] - 2 * HD), packed_ref.dtype)
 
 
-def pack(windows, queries):
+def pack(windows, queries, key_rows, value_rows):
     rows, width = queries.shape
     whole = pl.BlockSpec(memory_space=VMEM)
     return pl.pallas_call(
         pack_kernel,
-        out_shape=jax.ShapeDtypeStruct((rows + SIDE, width), queries.dtype),
-        in_specs=[pl.BlockSpec(memory_space=SMEM), whole],
-        out_specs=whole,
-        compiler_params=params(8),
+        out_shape=(
+            jax.ShapeDtypeStruct((rows + SIDE, width), queries.dtype),
+            jax.ShapeDtypeStruct((2 * rows, width), queries.dtype),
+        ),
+        in_specs=[pl.BlockSpec(memory_space=SMEM)] + [whole] * 3,
+        out_specs=(whole, whole),
         name="pack",
-    )(windows, queries)
+    )(windows, queries, key_rows, value_rows)
 
 
 def column(values, index):
@@ -121,19 +124,19 @@
 
 
 def attend(query, blocks, biases, low, old=None):
-    rows = blocks[0][0].shape[0]
+    rows = blocks[0].shape[0] // 2
     scale = HD**-0.5 * LOG2E
     spread = lambda value: jnp.broadcast_to(value, (rows, HD))
-    parts = [raw_scores(query, keys[:, low : low + HD]) for keys, _ in blocks]
+    parts = [raw_scores(query, block[:rows, low : low + HD]) for block in blocks]
     largest = None if old is None else old[0]
     for part, bias in zip(parts, biases):
         peak = spread(jnp.max(part, axis=1, keepdims=True)) * scale + bias
         largest = peak if largest is None else jnp.maximum(largest, peak)
     summed, mix = None, None
-    for part, bias, (_, values) in zip(parts, biases, blocks):
+    for part, bias, block in zip(parts, biases, blocks):
         offset = jnp.concatenate([bias - largest] * (rows // HD), axis=1)
         weights = jnp.exp2(part * scale + offset)
-        product = jnp.dot(weights.astype(values.dtype), values[:, low : low + HD], preferred_element_type=jnp.float32)
+        product = jnp.dot(weights.astype(block.dtype), block[rows:, low : low + HD], preferred_element_type=jnp.float32)
         summed = weights if summed is None else summed + weights
         mix = product if mix is None else mix + product
     total = spread(jnp.sum(summed, axis=1, keepdims=True))
@@ -148,26 +151,32 @@
     return jnp.transpose(jnp.where(lane == 0, largest, jnp.where(lane == 1, total, 0.0)))[:8]
 
 
-def own_kernel(query_ref, key_ref, value_ref, weight_ref, mix_ref, stats_ref, held_ref, sem):
+def block_biases(query_ref, rows):
+    wide = wide_window(query_ref, rows)
+    return [block_bias(wide, stage) for stage in (1, 2)]
+
+
+def own_kernel(query_ref, pair_ref, block_ref, weight_ref, mix_ref, stats_ref, held_ref, sem):
     copy = pltpu.make_async_copy(weight_ref, held_ref, sem)
     copy.start()
-    rows, width = key_ref.shape
-    for head in range(width // HD):
-        low = head * HD
-        largest, total, mix = attend(query_ref[:rows, low : low + HD], [(key_ref, value_ref)], [0.0], low)
-        mix_ref[head], stats_ref[2 * head], stats_ref[2 * head + 1] = mix, largest, total
+    rows, width = block_ref.shape[0] // 2, block_ref.shape[1]
+    for place, ref in enumerate((query_ref, pair_ref)):
+        for head in range(width // HD):
+            low, index = head * HD, 2 * head + place
+            largest, total, mix = attend(ref[:rows, low : low + HD], [block_ref], [0.0], low)
+            mix_ref[index], stats_ref[2 * index], stats_ref[2 * index + 1] = mix, largest, total
     copy.wait()
 
 
-def attend_own(queries, block, out_weight):
-    rows, width = block[0].shape
+def attend_own(queries, pair, block, out_weight):
+    rows, width = block.shape[0] // 2, block.shape[1]
     heads = width // HD
     whole = pl.BlockSpec(memory_space=VMEM)
     return pl.pallas_call(
         own_kernel,
         out_shape=(
-            jax.ShapeDtypeStruct((heads, rows, HD), jnp.float32),
             jax.ShapeDtypeStruct((2 * heads, rows, HD), jnp.float32),
+            jax.ShapeDtypeStruct((4 * heads, rows, HD), jnp.float32),
             jax.ShapeDtypeStruct(out_weight.shape, out_weight.dtype),
         ),
         in_specs=[whole] * 3 + [pl.BlockSpec(memory_space=pl.ANY)],
@@ -176,74 +185,61 @@
         compiler_params=params(24),
         cost_estimate=pl.CostEstimate(flops=0, bytes_accessed=0, transcendentals=0),
         name="attend_own",
-    )(queries, *block, out_weight)
-
-
-def neighbour_kernel(middle, query_ref, *refs):
-    blocks = [(refs[2 * i], refs[2 * i + 1]) for i in range(3)]
-    out_ref = refs[-1]
-    rows, width = blocks[0][0].shape
+    )(queries, pair, block, out_weight)
+
+
+def old_parts(mix_ref, stats_ref, head, place):
+    index = 2 * head + place
+    return stats_ref[2 * index], stats_ref[2 * index + 1], mix_ref[index]
+
+
+def neighbours_kernel(pair_ref, middle_ref, own_ref, first_ref, second_ref, mix_ref, stats_ref, for_pair_ref, for_middle_ref):
+    rows, width = own_ref.shape[0] // 2, own_ref.shape[1]
     height = lax.axis_index("tile") % HEIGHT_TILES
-
+    inside = (height > 0) & (height < HEIGHT_TILES - 1)
+    biases = block_biases(pair_ref, rows)
+    for head in range(width // HD):
+        low = head * HD
+        old = old_parts(mix_ref, stats_ref, head, 1)
+        largest, total, mix = attend(pair_ref[:rows, low : low + HD], [first_ref, second_ref], biases, low, old)
+        put_message(for_pair_ref, head, mix, row_stats(largest, total), 0)
+
+    @pl.when(inside)
     def compute():
-        wide = wide_window(query_ref, rows)
-        biases = [0.0] + [block_bias(wide, stage) for stage in (1, 2)]
+        biases = [0.0] + block_biases(middle_ref, rows)
+        blocks = [own_ref, first_ref, second_ref]
         for head in range(width // HD):
             low = head * HD
-            largest, total, mix = attend(query_ref[:rows, low : low + HD], blocks, biases, low)
-            put_message(out_ref, head, mix, row_stats(largest, total), 0)
-
-    if not middle:
-        compute()
-        return
-    inside = (height > 0) & (height < HEIGHT_TILES - 1)
-    pl.when(inside)(compute)
+            largest, total, mix = attend(middle_ref[:rows, low : low + HD], blocks, biases, low)
+            put_message(for_middle_ref, head, mix, row_stats(largest, total), 0)
 
     @pl.when(jnp.logical_not(inside))
     def skip():
-        out_ref[...] = jnp.zeros_like(out_ref)
-
-
-def attend_neighbour(middle, query, blocks, after=()):
-    rows, width = blocks[0][0].shape
-    whole = pl.BlockSpec(memory_space=VMEM)
-    cost = 3 * (width // HD) * rows * rows
-    return pl.pallas_call(
-        functools.partial(neighbour_kernel, middle),
-        out_shape=jax.ShapeDtypeStruct((rows + SIDE, width), jnp.bfloat16),
-        in_specs=[whole] * 7 + [pl.BlockSpec(memory_space=pl.ANY)] * len(after),
-        out_specs=whole,
-        compiler_params=params(24),
-        cost_estimate=pl.CostEstimate(flops=4 * HD * cost, bytes_accessed=2_000_000, transcendentals=cost),
-        name="attend_middle" if middle else "attend_pair",
-    )(query, *[array for block in blocks for array in block], *after)
-
-
-def here_kernel(*refs):
-    refs[-1][...] = jnp.zeros_like(refs[-1])
-
-
-def all_here(arrays):
-    return pl.pallas_call(
-        here_kernel,
-        out_shape=jax.ShapeDtypeStruct((8, HD), jnp.float32),
-        in_specs=[pl.BlockSpec(memory_space=pl.ANY)] * len(arrays),
-        out_specs=pl.BlockSpec(memory_space=VMEM),
-        compiler_params=params(4),
-        cost_estimate=pl.CostEstimate(flops=HERE_FLOPS, bytes_accessed=0, transcendentals=0),
-        name="all_here",
-    )(*arrays)
-
-
-def last_kernel(query_ref, k1_ref, v1_ref, k2_ref, v2_ref, old_mix_ref, old_stats_ref, message_ref, mix_ref, stats_ref):
-    rows, width = k1_ref.shape
+        for_middle_ref[...] = jnp.zeros_like(for_middle_ref)
+
+
+def attend_neighbours(pair, middle, own, first, second, mix, stats):
+    whole = pl.BlockSpec(memory_space=VMEM)
+    shape = jax.ShapeDtypeStruct(pair.shape, jnp.bfloat16)
+    return pl.pallas_call(
+        neighbours_kernel,
+        out_shape=(shape, shape),
+        in_specs=[whole] * 7,
+        out_specs=(whole, whole),
+        compiler_params=params(24),
+        cost_estimate=pl.CostEstimate(flops=1_000_000_000, bytes_accessed=2_000_000, transcendentals=0),
+        name="attend_neighbours",
+    )(pair, middle, own, first, second, mix, stats)
+
+
+def last_kernel(query_ref, first_ref, second_ref, old_mix_ref, old_stats_ref, message_ref, mix_ref, stats_ref):
+    rows, width = first_ref.shape[0] // 2, first_ref.shape[1]
     wide = wide_window(query_ref, rows, 1)
-    biases = [block_bias(wide_window(query_ref, rows), stage) for stage in (1, 2)]
+    biases = block_biases(query_ref, rows)
     for head in range(width // HD):
         low = head * HD
-        old = (old_stats_ref[2 * head], old_stats_ref[2 * head + 1], old_mix_ref[head])
-        blocks = [(k1_ref, v1_ref), (k2_ref, v2_ref)]
-        largest, total, mix = attend(query_ref[:rows, low : low + HD], blocks, biases, low, old)
+        old = old_parts(old_mix_ref, old_stats_ref, head, 0)
+        largest, total, mix = attend(query_ref[:rows, low : low + HD], [first_ref, second_ref], biases, low, old)
         their_largest, their_total = message_columns(message_ref, head, rows)
         peak = jnp.maximum(largest, jnp.where(wide, their_largest, MASKED))
         shrink, share = jnp.exp2(largest - peak), jnp.where(wide, jnp.exp2(their_largest - peak), 0.0)
@@ -254,7 +250,7 @@
 
 
 def attend_last(queries, first, second, mix, stats, message):
-    rows, width = first[0].shape
+    rows, width = first.shape[0] // 2, first.shape[1]
     whole = pl.BlockSpec(memory_space=VMEM)
     return pl.pallas_call(
         last_kernel,
@@ -262,15 +258,15 @@
             jax.ShapeDtypeStruct((rows, width), jnp.float32),
             jax.ShapeDtypeStruct((width // HD, 8, rows), jnp.float32),
         ),
-        in_specs=[whole] * 8,
+        in_specs=[whole] * 6,
         out_specs=(whole, whole),
         compiler_params=params(24),
         cost_estimate=pl.CostEstimate(flops=LAST_FLOPS, bytes_accessed=2_000_000, transcendentals=0),
         name="attend_last",
-    )(queries, *first, *second, mix, stats, message)
-
-
-def project_kernel(own_ref, stats_ref, middle_ref, weight_ref, out_ref):
+    )(queries, first, second, mix, stats, message)
+
+
+def project_kernel(own_ref, stats_ref, middle_ref, weight_ref, out_ref, held_ref, sems):
     rows, width = own_ref.shape
     heads = width // HD
     height = lax.axis_index("tile") % HEIGHT_TILES
@@ -295,23 +291,30 @@
         value += middle_ref[:rows, low : low + HD].astype(jnp.float32) * column(shares, 2 * head + 1)
         merged.append(value.astype(jnp.bfloat16))
     attention = jnp.concatenate(merged, axis=1)
+    copies = []
     for group in range(out_ref.shape[0]):
-        out_ref[group] = jnp.dot(
+        held_ref[group] = jnp.dot(
             attention, weight_ref[:, group * width : (group + 1) * width], preferred_element_type=jnp.float32
-        ).astype(out_ref.dtype)
+        ).astype(held_ref.dtype)
+        copies.append(pltpu.make_async_copy(held_ref.at[group], out_ref.at[group], sems.at[group]))
+        copies[-1].start()
+    for copy in copies:
+        copy.wait()
 
 
 def project(own, stats, middle, out_weight):
     rows, width = own.shape
-    features = out_weight.shape[1]
-    whole = pl.BlockSpec(memory_space=VMEM)
+    groups = out_weight.shape[1] // width
+    whole = pl.BlockSpec(memory_space=VMEM)
+    shape = (groups, rows, width)
     return pl.pallas_call(
         project_kernel,
-        out_shape=jax.ShapeDtypeStruct((features // width, rows, width), jnp.bfloat16),
+        out_shape=jax.ShapeDtypeStruct(shape, jnp.bfloat16),
         in_specs=[whole] * 4,
-        out_specs=whole,
-        compiler_params=params(24),
-        cost_estimate=pl.CostEstimate(flops=2 * rows * width * features, bytes_accessed=5_000_000, transcendentals=0),
+        out_specs=pl.BlockSpec(memory_space=pl.ANY),
+        scratch_shapes=[pltpu.VMEM(shape, jnp.bfloat16), pltpu.SemaphoreType.DMA((groups,))],
+        compiler_params=params(24),
+        cost_estimate=pl.CostEstimate(flops=2 * groups * rows * width * width, bytes_accessed=5_000_000, transcendentals=0),
         name="project",
     )(own, stats, middle, out_weight)
 
@@ -335,14 +338,11 @@
 
 
 def shards(queries, key_rows, value_rows, windows, residual, out_weight, gate_scale):
-    own_block = (key_rows, value_rows)
-    first, second = [[swap_times(array, later) for array in own_block] for later in (False, True)]
-    packed = pack(windows, queries)
-    blocks = (own_block, first, second)
-    mix, stats, held_weight = attend_own(packed, own_block, out_weight)
-    asked = swap_pair(packed), swap_middle(packed)
-    for_pair = attend_neighbour(False, asked[0], blocks, (stats, all_here(first + second), asked[1]))
-    for_middle = attend_neighbour(True, asked[1], blocks, (for_pair,))
+    packed, block = pack(windows, queries, key_rows, value_rows)
+    first, second = swap_times(block, False), swap_times(block, True)
+    pair_asks, middle_asks = swap_pair(packed), swap_middle(packed)
+    mix, stats, held_weight = attend_own(packed, pair_asks, block, out_weight)
+    for_pair, for_middle = attend_neighbours(pair_asks, middle_asks, block, first, second, mix, stats)
     mix, stats = attend_last(packed, first, second, mix, stats, swap_pair(for_pair))
     terms = project(mix, stats, swap_middle(for_middle), held_weight)
     terms = lax.all_to_all(terms, "head", 0, 0)

time: 72.4 us -> 72.7 us (level); the launches traced: 71 us -> 72.3 us
  waiting for transfers between devices: 22.6 us -> 29.4 us
  starting transfers between devices: 32.9 us -> 28 us
  local copies, waits for them, and re-layouts: 5.11 us -> 3.61 us
  Pallas kernels: 10.2 us -> 11.2 us
    ppermute x2, waiting for transfers between devices: 5.77 us -> 11.1 us  [swap_middle(): return lax.ppermute(block, 'tile', route)]
    ppermute x4 -> x2, starting transfers between devices: 14.4 us -> 10.5 us  [swap_times(): return lax.ppermute(block, 'tile', route)]
    ppermute x2, starting transfers between devices: 9 us -> 6.48 us  [swap_middle(): return lax.ppermute(block, 'tile', route)]
    all_to_all x1, waiting for transfers between devices: 16.6 us -> 18.2 us  [shards(): terms = lax.all_to_all(terms, 'head', 0, 0)]
    unnamed x18 -> x12, local copies, waits for them, and re-layouts: 5.11 us -> 3.6 us
    ppermute x2, starting transfers between devices: 3.84 us -> 5.06 us  [swap_pair(): lax.ppermute(block, 'tile', [(tile, tile ^ 1) for tile, *_ in places()])]
    pallas_call x6 -> x4, Pallas kernels: 7.2 us -> 8.2 us  [the longest x1 2.83 us: attend_neighbours(): pl.pallas_call(neighbours_kernel, out_shape=(shape, shape), in_specs=[who...]
  transfers between devices with their start and end apart: 9 -> 7, of which waited for: 4 -> 3; matrix products, arithmetic and copies ran while one was open for 0% -> 0% of each run, Pallas kernels for 7% -> 4%
where the time goes in v10:
time: 72.7 us; the launch traced here: 72.3 us
  waiting for transfers between devices  29.4 us (40%)
  starting transfers between devices  28 us (39%)
  Pallas kernels  11.2 us (15%)
  local copies, waits for them, and re-layouts  3.61 us (5%)
    all_to_all x1, waiting for transfers between devices, shards(): terms = lax.all_to_all(terms, 'head', 0, 0)  18.2 us
    ppermute x2, waiting for transfers between devices, swap_middle(): return lax.ppermute(block, 'tile', route)  11.1 us
    ppermute x2, starting transfers between devices, swap_times(): return lax.ppermute(block, 'tile', route)  10.5 us
    ppermute x2, starting transfers between devices, swap_middle(): return lax.ppermute(block, 'tile', route)  6.48 us
    all_to_all x1, starting transfers between devices, shards(): terms = lax.all_to_all(terms, 'head', 0, 0)  5.97 us
    ppermute x2, starting transfers between devices, swap_pair(): lax.ppermute(block, 'tile', [(tile, tile ^ 1) for tile, *_ in places()])  5.06 us
    unnamed x12, local copies, waits for them, and re-layouts  3.6 us
    pallas_call x1, Pallas kernels, attend_neighbours(): pl.pallas_call(neighbours_kernel, out_shape=(shape, shape), in_specs=[who...  2.83 us
  transfers between devices with their start and end apart: 7, of which 3 were waited for; matrix products, arithmetic and copies ran while one was open for 0% of the time, Pallas kernels for 4%

profile of v10, /device:TPU:1, one launch (start us, length us, event | category | flops | bytes accessed | tf_op | source)
XLA Modules:
  0.0 72.3 jit_solution(13884992630077892453)
XLA Ops:
  0.0 2.0 %pack.1 = (bf16[272,384]{1,0:T(8,128)(2,1)}, bf16[512,384]{1,0:T(8,128)(2,1)}) custom-call(s32[1,3]{1,0:T(1,128)} %windows_ref.1, bf16[256,384]{1,0:T(8,128)(2,1)} %q_ref.1, bf16[256,384]{1,0:T(8,128)(2,1)} %k_ref.1, bf16[256,384]{1,0:T(8,128)(2,1)} %v_ref.1), custom_call_target="tpu_custom_call" | custom-call | tf_op jit(solution)/shard_map/pack/pallas_call | solution.py:62
  2.0 0.7 collective-permute-start
  2.7 9.8 %collective-permute-start.1 = (bf16[512,384]{1,0:T(8,128)(2,1)}, bf16[512,384]{1,0:T(8,128)(2,1)S(1)}, u32[]{:S(2)}, u32[]{:S(2)}) collective-permute-start(bf16[512,384]{1,0:T(8,128)(2,1)} %get-tuple-element.15.block_ref.own_ref), channel_id=1, source_target_pairs={{0,32},{8,40},{16,48},{24,56},{32,0},{40,8},{48,16},{56,24},{64,96... | collective-permute-start | bytes 1179656 | tf_op jit(solution)/shard_map/ppermute | solution.py:36
  12.5 3.1 %collective-permute-start.2 = (bf16[272,384]{1,0:T(8,128)(2,1)}, bf16[272,384]{1,0:T(8,128)(2,1)S(1)}, u32[]{:S(2)}, u32[]{:S(2)}) collective-permute-start(bf16[272,384]{1,0:T(8,128)(2,1)} %get-tuple-element.14.query_ref), channel_id=1, source_target_pairs={{0,8},{8,0},{16,24},{24,16},{32,40},{40,32},{48,56},{56,48},{64,72... | collective-permute-start | bytes 626696 | tf_op jit(solution)/shard_map/ppermute | solution.py:40
  15.6 2.2 %collective-permute-start.3 = (bf16[272,384]{1,0:T(8,128)(2,1)}, bf16[272,384]{1,0:T(8,128)(2,1)S(1)}, u32[]{:S(2)}, u32[]{:S(2)}) collective-permute-start(bf16[272,384]{1,0:T(8,128)(2,1)} %get-tuple-element.14.query_ref), channel_id=1, source_target_pairs={{8,16},{16,8},{40,48},{48,40},{72,80},{80,72},{104,112},{112,104},... | collective-permute-start | bytes 626696 | tf_op jit(solution)/shard_map/ppermute | solution.py:45
  17.8 0.0 collective-permute-done.2.pair_ref
  17.8 0.0 copy-start
  17.9 1.7 %copy-done = bf16[384,3072]{1,0:T(8,128)(2,1)S(1)} copy-done((bf16[384,3072]{1,0:T(8,128)(2,1)S(1)}, bf16[384,3072]{1,0:T(8,128)(2,1)}, u32[]{:S(2)}) %copy-start) | copy-done | bytes 2359320
  19.5 0.0 copy-start.1
  19.5 1.0 %copy-done.1 = bf16[512,384]{1,0:T(8,128)(2,1)S(1)} copy-done((bf16[512,384]{1,0:T(8,128)(2,1)S(1)}, bf16[512,384]{1,0:T(8,128)(2,1)}, u32[]{:S(2)}) %copy-start.1) | copy-done | bytes 393240
  20.5 0.0 copy-start.3
  20.5 0.9 %copy-done.3 = bf16[272,384]{1,0:T(8,128)(2,1)S(1)} copy-done((bf16[272,384]{1,0:T(8,128)(2,1)S(1)}, bf16[272,384]{1,0:T(8,128)(2,1)}, u32[]{:S(2)}) %copy-start.3) | copy-done | bytes 208920
  21.4 0.0 copy-start.2
  21.4 1.1 %attend_own.1 = (f32[6,256,128]{2,1,0:T(8,128)S(1)}, f32[12,256,128]{2,1,0:T(8,128)S(1)}, bf16[384,3072]{1,0:T(8,128)(2,1)S(1)}) custom-call(bf16[272,384]{1,0:T(8,128)(2,1)S(1)} %copy-done.3, bf16[272,384]{1,0:T(8,128)(2,1)S(1)} %collective-permute-done.2.pair_ref, bf16[512,384]{1,0:T(8,128)(2,1)S(1)} %copy-done.1, bf16[384,3072]{1,0:T(8,128)(2,1)S(1)} %copy-done), custom_call_target="tpu_custom_call" | custom-call | tf_op jit(solution)/shard_map/attend_own/pallas_call | solution.py:175
  22.6 9.7 %collective-permute-done.3.middle_ref = bf16[272,384]{1,0:T(8,128)(2,1)S(1)} collective-permute-done((bf16[272,384]{1,0:T(8,128)(2,1)}, bf16[272,384]{1,0:T(8,128)(2,1)S(1)}, u32[]{:S(2)}, u32[]{:S(2)}) %collective-permute-start.3) | collective-permute-done | bytes 208928 | tf_op jit(solution)/shard_map/ppermute | solution.py:45
  32.3 0.0 collective-permute-done.first_ref
  32.3 0.0 collective-permute-done.1.second_ref
  32.3 0.0 copy-done.2
  32.3 2.8 %attend_neighbours.1 = (bf16[272,384]{1,0:T(8,128)(2,1)S(1)}, bf16[272,384]{1,0:T(8,128)(2,1)S(1)}) custom-call(bf16[272,384]{1,0:T(8,128)(2,1)S(1)} %collective-permute-done.2.pair_ref, bf16[272,384]{1,0:T(8,128)(2,1)S(1)} %collective-permute-done.3.middle_ref, bf16[512,384]{1,0:T(8,128)(2,1)S(1)} %copy-done.2, ...), custom_call_target="tpu_custom_call" | custom-call | flops 1000000000 | bytes 2000000 | tf_op jit(solution)/shard_map/attend_neighbours/pallas_call | solution.py:224
  35.2 1.9 %collective-permute-start.4 = (bf16[272,384]{1,0:T(8,128)(2,1)S(1)}, bf16[272,384]{1,0:T(8,128)(2,1)S(1)}, u32[]{:S(2)}, u32[]{:S(2)}) collective-permute-start(bf16[272,384]{1,0:T(8,128)(2,1)S(1)} %get-tuple-element.18), channel_id=1, source_target_pairs={{0,8},{8,0},{16,24},{24,16},{32,40},{40,32},{48,56},{56,48},{64,72... | collective-permute-start | bytes 626696 | tf_op jit(solution)/shard_map/ppermute | solution.py:40
  37.1 4.3 %collective-permute-start.5 = (bf16[272,384]{1,0:T(8,128)(2,1)S(1)}, bf16[272,384]{1,0:T(8,128)(2,1)S(1)}, u32[]{:S(2)}, u32[]{:S(2)}) collective-permute-start(bf16[272,384]{1,0:T(8,128)(2,1)S(1)} %get-tuple-element.21), channel_id=1, source_target_pairs={{8,16},{16,8},{40,48},{48,40},{72,80},{80,72},{104,112},{112,104},... | collective-permute-start | bytes 626696 | tf_op jit(solution)/shard_map/ppermute | solution.py:45
  41.4 0.0 collective-permute-done.4.message_ref
  41.4 2.0 %attend_last.1 = (f32[256,384]{1,0:T(8,128)S(1)}, f32[3,8,256]{2,1,0:T(8,128)S(1)}) custom-call(bf16[272,384]{1,0:T(8,128)(2,1)S(1)} %copy-done.3, bf16[512,384]{1,0:T(8,128)(2,1)S(1)} %collective-permute-done.first_ref, bf16[512,384]{1,0:T(8,128)(2,1)S(1)} %collective-permute-done.1.second_ref, f32[6,256,128]{2,1,0:T(8,128)S(1)} %get-tuple-element.16.mix_ref.old_mix_ref, ...), custom_call_target="tpu_custom_call" | custom-call | flops 400000000 | bytes 2000000 | tf_op jit(solution)/shard_map/attend_last/pallas_call | solution.py:255
  43.4 1.4 %collective-permute-done.5.middle_ref = bf16[272,384]{1,0:T(8,128)(2,1)S(1)} collective-permute-done((bf16[272,384]{1,0:T(8,128)(2,1)S(1)}, bf16[272,384]{1,0:T(8,128)(2,1)S(1)}, u32[]{:S(2)}, u32[]{:S(2)}) %collective-permute-start.5) | collective-permute-done | bytes 208928 | tf_op jit(solution)/shard_map/ppermute | solution.py:45
  44.8 2.2 %project.1 = bf16[8,256,384]{2,1,0:T(8,128)(2,1)} custom-call(f32[256,384]{1,0:T(8,128)S(1)} %get-tuple-element.19.own_ref, f32[3,8,256]{2,1,0:T(8,128)S(1)} %get-tuple-element.20.stats_ref, bf16[272,384]{1,0:T(8,128)(2,1)S(1)} %collective-permute-done.5.middle_ref, bf16[384,3072]{1,0:T(8,128)(2,1)S(1)} %get-tuple-element.22.weight_ref), custom_call_target="tpu_custom_call" | custom-call | flops 603979776 | bytes 5000000 | tf_op jit(solution)/shard_map/project/pallas_call | solution.py:310
  47.1 0.0 copy-start.5
  47.1 0.0 copy-start.4
  47.1 6.0 %all-to-all-start = ((bf16[8,256,384]{2,1,0:T(8,128)(2,1)}), bf16[8,256,384]{2,1,0:T(8,128)(2,1)S(1)}, u32[]{:S(2)}, u32[]{:S(2)}) async-start(bf16[8,256,384]{2,1,0:T(8,128)(2,1)} %project.1), calls=%async_computation | async-start | bytes 3145728 | tf_op jit(solution)/shard_map/all_to_all | solution.py:348
  53.1 0.0 copy-done.5
  53.1 18.2 %all-to-all-done.terms_ref = bf16[8,256,384]{2,1,0:T(8,128)(2,1)S(1)} async-done(((bf16[8,256,384]{2,1,0:T(8,128)(2,1)}), bf16[8,256,384]{2,1,0:T(8,128)(2,1)S(1)}, u32[]{:S(2)}, u32[]{:S(2)}) %all-to-all-start) | async-done | bytes 1572896 | tf_op jit(solution)/shard_map/all_to_all | solution.py:348
  71.4 0.0 copy-done.4
  71.4 0.9 %finish.1 = bf16[256,384]{1,0:T(8,128)(2,1)} custom-call(bf16[8,256,384]{2,1,0:T(8,128)(2,1)S(1)} %all-to-all-done.terms_ref, bf16[256,384]{1,0:T(8,128)(2,1)S(1)} %copy-done.4, f32[1,384]{1,0:T(1,128)S(1)} %reshape.3.gate_ref), custom_call_target="tpu_custom_call" | custom-call | flops 7864320 | bytes 2000000 | tf_op jit(solution)/shard_map/finish/pallas_call | solution.py:329
  (1 shorter events, 0.0 us)
Async XLA Ops:
  2.0 30.3 %collective-permute-start = (bf16[512,384]{1,0:T(8,128)(2,1)}, bf16[512,384]{1,0:T(8,128)(2,1)S(1)}, u32[]{:S(2)}, u32[]{:S(2)}) collective-permute-start(bf16[512,384]{1,0:T(8,128)(2,1)} %get-tuple-element.15.block_ref.own_ref), channel_id=1, source_target_pairs={{32,64},{40,72},{48,80},{56,88},{64,32},{72,40},{80,48},{88,56},{9... | collective-permute-start | bytes 1179656 | tf_op jit(solution)/shard_map/ppermute | solution.py:36
  2.7 29.6 %collective-permute-start.1 = (bf16[512,384]{1,0:T(8,128)(2,1)}, bf16[512,384]{1,0:T(8,128)(2,1)S(1)}, u32[]{:S(2)}, u32[]{:S(2)}) collective-permute-start(bf16[512,384]{1,0:T(8,128)(2,1)} %get-tuple-element.15.block_ref.own_ref), channel_id=1, source_target_pairs={{0,32},{8,40},{16,48},{24,56},{32,0},{40,8},{48,16},{56,24},{64,96... | collective-permute-start | bytes 1179656 | tf_op jit(solution)/shard_map/ppermute | solution.py:36
  12.5 5.4 %collective-permute-start.2 = (bf16[272,384]{1,0:T(8,128)(2,1)}, bf16[272,384]{1,0:T(8,128)(2,1)S(1)}, u32[]{:S(2)}, u32[]{:S(2)}) collective-permute-start(bf16[272,384]{1,0:T(8,128)(2,1)} %get-tuple-element.14.query_ref), channel_id=1, source_target_pairs={{0,8},{8,0},{16,24},{24,16},{32,40},{40,32},{48,56},{56,48},{64,72... | collective-permute-start | bytes 626696 | tf_op jit(solution)/shard_map/ppermute | solution.py:40
  15.6 16.7 %collective-permute-start.3 = (bf16[272,384]{1,0:T(8,128)(2,1)}, bf16[272,384]{1,0:T(8,128)(2,1)S(1)}, u32[]{:S(2)}, u32[]{:S(2)}) collective-permute-start(bf16[272,384]{1,0:T(8,128)(2,1)} %get-tuple-element.14.query_ref), channel_id=1, source_target_pairs={{8,16},{16,8},{40,48},{48,40},{72,80},{80,72},{104,112},{112,104},... | collective-permute-start | bytes 626696 | tf_op jit(solution)/shard_map/ppermute | solution.py:45
  17.8 1.7 %copy-start = (bf16[384,3072]{1,0:T(8,128)(2,1)S(1)}, bf16[384,3072]{1,0:T(8,128)(2,1)}, u32[]{:S(2)}) copy-start(bf16[384,3072]{1,0:T(8,128)(2,1)} %weight_ref.1) | copy-start | bytes 7077892
  19.5 1.0 %copy-start.1 = (bf16[512,384]{1,0:T(8,128)(2,1)S(1)}, bf16[512,384]{1,0:T(8,128)(2,1)}, u32[]{:S(2)}) copy-start(bf16[512,384]{1,0:T(8,128)(2,1)} %get-tuple-element.15.block_ref.own_ref) | copy-start | bytes 1179652
  20.5 0.9 %copy-start.3 = (bf16[272,384]{1,0:T(8,128)(2,1)S(1)}, bf16[272,384]{1,0:T(8,128)(2,1)}, u32[]{:S(2)}) copy-start(bf16[272,384]{1,0:T(8,128)(2,1)} %get-tuple-element.14.query_ref) | copy-start | bytes 626692
  21.4 10.9 %copy-start.2 = (bf16[512,384]{1,0:T(8,128)(2,1)S(1)}, bf16[512,384]{1,0:T(8,128)(2,1)}, u32[]{:S(2)}) copy-start(bf16[512,384]{1,0:T(8,128)(2,1)} %get-tuple-element.15.block_ref.own_ref) | copy-start | bytes 1179652
  35.2 6.2 %collective-permute-start.4 = (bf16[272,384]{1,0:T(8,128)(2,1)S(1)}, bf16[272,384]{1,0:T(8,128)(2,1)S(1)}, u32[]{:S(2)}, u32[]{:S(2)}) collective-permute-start(bf16[272,384]{1,0:T(8,128)(2,1)S(1)} %get-tuple-element.18), channel_id=1, source_target_pairs={{0,8},{8,0},{16,24},{24,16},{32,40},{40,32},{48,56},{56,48},{64,72... | collective-permute-start | bytes 626696 | tf_op jit(solution)/shard_map/ppermute | solution.py:40
  37.1 7.8 %collective-permute-start.5 = (bf16[272,384]{1,0:T(8,128)(2,1)S(1)}, bf16[272,384]{1,0:T(8,128)(2,1)S(1)}, u32[]{:S(2)}, u32[]{:S(2)}) collective-permute-start(bf16[272,384]{1,0:T(8,128)(2,1)S(1)} %get-tuple-element.21), channel_id=1, source_target_pairs={{8,16},{16,8},{40,48},{48,40},{72,80},{80,72},{104,112},{112,104},... | collective-permute-start | bytes 626696 | tf_op jit(solution)/shard_map/ppermute | solution.py:45
  47.1 6.0 %copy-start.5 = (f32[384]{0:T(512)S(1)}, f32[384]{0:T(512)}, u32[]{:S(2)}) copy-start(f32[384]{0:T(512)} %param.13) | copy-start | bytes 4612
  47.1 24.3 %copy-start.4 = (bf16[256,384]{1,0:T(8,128)(2,1)S(1)}, bf16[256,384]{1,0:T(8,128)(2,1)}, u32[]{:S(2)}) copy-start(bf16[256,384]{1,0:T(8,128)(2,1)} %residual_ref.1) | copy-start | bytes 589828
  47.1 24.2 %all-to-all-start = ((bf16[8,256,384]{2,1,0:T(8,128)(2,1)}), bf16[8,256,384]{2,1,0:T(8,128)(2,1)S(1)}, u32[]{:S(2)}, u32[]{:S(2)}) async-start(bf16[8,256,384]{2,1,0:T(8,128)(2,1)} %project.1), calls=%async_computation | async-start | bytes 3145728 | tf_op jit(solution)/shard_map/all_to_all | solution.py:348

commit v11 on v10

--- a/solution.py
+++ b/solution.py
@@ -193,43 +193,59 @@
     return stats_ref[2 * index], stats_ref[2 * index + 1], mix_ref[index]
 
 
-def neighbours_kernel(pair_ref, middle_ref, own_ref, first_ref, second_ref, mix_ref, stats_ref, for_pair_ref, for_middle_ref):
+def pair_kernel(query_ref, first_ref, second_ref, mix_ref, stats_ref, out_ref):
+    rows, width = first_ref.shape[0] // 2, first_ref.shape[1]
+    biases = block_biases(query_ref, rows)
+    for head in range(width // HD):
+        low = head * HD
+        old = old_parts(mix_ref, stats_ref, head, 1)
+        largest, total, mix = attend(query_ref[:rows, low : low + HD], [first_ref, second_ref], biases, low, old)
+        put_message(out_ref, head, mix, row_stats(largest, total), 0)
+
+
+def attend_pair(query, first, second, mix, stats):
+    whole = pl.BlockSpec(memory_space=VMEM)
+    return pl.pallas_call(
+        pair_kernel,
+        out_shape=jax.ShapeDtypeStruct(query.shape, jnp.bfloat16),
+        in_specs=[whole] * 5,
+        out_specs=whole,
+        compiler_params=params(24),
+        cost_estimate=pl.CostEstimate(flops=400_000_000, bytes_accessed=2_000_000, transcendentals=0),
+        name="attend_pair",
+    )(query, first, second, mix, stats)
+
+
+def middle_kernel(query_ref, own_ref, first_ref, second_ref, after_ref, out_ref):
     rows, width = own_ref.shape[0] // 2, own_ref.shape[1]
     height = lax.axis_index("tile") % HEIGHT_TILES
     inside = (height > 0) & (height < HEIGHT_TILES - 1)
-    biases = block_biases(pair_ref, rows)
-    for head in range(width // HD):
-        low = head * HD
-        old = old_parts(mix_ref, stats_ref, head, 1)
-        largest, total, mix = attend(pair_ref[:rows, low : low + HD], [first_ref, second_ref], biases, low, old)
-        put_message(for_pair_ref, head, mix, row_stats(largest, total), 0)
 
     @pl.when(inside)
     def compute():
-        biases = [0.0] + block_biases(middle_ref, rows)
+        biases = [0.0] + block_biases(query_ref, rows)
         blocks = [own_ref, first_ref, second_ref]
         for head in range(width // HD):
             low = head * HD
-            largest, total, mix = attend(middle_ref[:rows, low : low + HD], blocks, biases, low)
-            put_message(for_middle_ref, head, mix, row_stats(largest, total), 0)
+            largest, total, mix = attend(query_ref[:rows, low : low + HD], blocks, biases, low)
+            put_message(out_ref, head, mix, row_stats(largest, total), 0)
 
     @pl.when(jnp.logical_not(inside))
     def skip():
-        for_middle_ref[...] = jnp.zeros_like(for_middle_ref)
-
-
-def attend_neighbours(pair, middle, own, first, second, mix, stats):
-    whole = pl.BlockSpec(memory_space=VMEM)
-    shape = jax.ShapeDtypeStruct(pair.shape, jnp.bfloat16)
-    return pl.pallas_call(
-        neighbours_kernel,
-        out_shape=(shape, shape),
-        in_specs=[whole] * 7,
-        out_specs=(whole, whole),
-        compiler_params=params(24),
-        cost_estimate=pl.CostEstimate(flops=1_000_000_000, bytes_accessed=2_000_000, transcendentals=0),
-        name="attend_neighbours",
-    )(pair, middle, own, first, second, mix, stats)
+        out_ref[...] = jnp.zeros_like(out_ref)
+
+
+def attend_middle(query, own, first, second, after):
+    whole = pl.BlockSpec(memory_space=VMEM)
+    return pl.pallas_call(
+        middle_kernel,
+        out_shape=jax.ShapeDtypeStruct(query.shape, jnp.bfloat16),
+        in_specs=[whole] * 4 + [pl.BlockSpec(memory_space=pl.ANY)],
+        out_specs=whole,
+        compiler_params=params(24),
+        cost_estimate=pl.CostEstimate(flops=600_000_000, bytes_accessed=2_000_000, transcendentals=0),
+        name="attend_middle",
+    )(query, own, first, second, after)
 
 
 def last_kernel(query_ref, first_ref, second_ref, old_mix_ref, old_stats_ref, message_ref, mix_ref, stats_ref):
@@ -342,7 +358,8 @@
     first, second = swap_times(block, False), swap_times(block, True)
     pair_asks, middle_asks = swap_pair(packed), swap_middle(packed)
     mix, stats, held_weight = attend_own(packed, pair_asks, block, out_weight)
-    for_pair, for_middle = attend_neighbours(pair_asks, middle_asks, block, first, second, mix, stats)
+    for_pair = attend_pair(pair_asks, first, second, mix, stats)
+    for_middle = attend_middle(middle_asks, block, first, second, for_pair)
     mix, stats = attend_last(packed, first, second, mix, stats, swap_pair(for_pair))
     terms = project(mix, stats, swap_middle(for_middle), held_weight)
     terms = lax.all_to_all(terms, "head", 0, 0)

time: 72.7 us -> 70.7 us (0.972)
  starting transfers between devices: 28 us -> 26.4 us
  waiting for transfers between devices: 29.4 us -> 28.3 us
    ppermute x2, waiting for transfers between devices: 11.1 us -> 3.13 us  [swap_middle(): return lax.ppermute(block, 'tile', route)]
    ppermute x2, waiting for transfers between devices: 0.01 us -> 7.99 us  [swap_times(): return lax.ppermute(block, 'tile', route)]
    ppermute x2, starting transfers between devices: 6.48 us -> 4.12 us  [swap_middle(): return lax.ppermute(block, 'tile', route)]
    ppermute x2, starting transfers between devices: 5.06 us -> 6.48 us  [swap_pair(): lax.ppermute(block, 'tile', [(tile, tile ^ 1) for tile, *_ in places()])]
    all_to_all x1, waiting for transfers between devices: 18.2 us -> 17.2 us  [shards(): terms = lax.all_to_all(terms, 'head', 0, 0)]
    pallas_call x1 -> x2, Pallas kernels: 2.83 us -> 2.84 us  [the longest x1 1.55 us: attend_middle(): pl.pallas_call(middle_kernel, out_shape=jax.ShapeDtypeStruct(query.shape,...]
  transfers between devices with their start and end apart: 7 -> 7, of which waited for: 3 -> 3; matrix products, arithmetic and copies ran while one was open for 0% -> 0% of each run, Pallas kernels for 4% -> 9%
where the time goes in v11:
time: 70.7 us; the launch traced here: 69.6 us
  waiting for transfers between devices  28.3 us (40%)
  starting transfers between devices  26.4 us (37%)
  Pallas kernels  11.2 us (16%)
  local copies, waits for them, and re-layouts  3.61 us (5%)
    all_to_all x1, waiting for transfers between devices, shards(): terms = lax.all_to_all(terms, 'head', 0, 0)  17.2 us
    ppermute x2, starting transfers between devices, swap_times(): return lax.ppermute(block, 'tile', route)  10.5 us
    ppermute x2, waiting for transfers between devices, swap_times(): return lax.ppermute(block, 'tile', route)  7.99 us
    ppermute x2, starting transfers between devices, swap_pair(): lax.ppermute(block, 'tile', [(tile, tile ^ 1) for tile, *_ in places()])  6.48 us
    all_to_all x1, starting transfers between devices, shards(): terms = lax.all_to_all(terms, 'head', 0, 0)  5.29 us
    ppermute x2, starting transfers between devices, swap_middle(): return lax.ppermute(block, 'tile', route)  4.12 us
    unnamed x12, local copies, waits for them, and re-layouts  3.6 us
    ppermute x2, waiting for transfers between devices, swap_middle(): return lax.ppermute(block, 'tile', route)  3.13 us
  transfers between devices with their start and end apart: 7, of which 3 were waited for; matrix products, arithmetic and copies ran while one was open for 0% of the time, Pallas kernels for 9%

profile of v11, /device:TPU:1, one launch (start us, length us, event | category | flops | bytes accessed | tf_op | source)
XLA Modules:
  0.0 69.6 jit_solution(10505368469215805188)
XLA Ops:
  0.0 2.0 %pack.1 = (bf16[272,384]{1,0:T(8,128)(2,1)}, bf16[512,384]{1,0:T(8,128)(2,1)}) custom-call(s32[1,3]{1,0:T(1,128)} %windows_ref.1, bf16[256,384]{1,0:T(8,128)(2,1)} %q_ref.1, bf16[256,384]{1,0:T(8,128)(2,1)} %k_ref.1, bf16[256,384]{1,0:T(8,128)(2,1)} %v_ref.1), custom_call_target="tpu_custom_call" | custom-call | tf_op jit(solution)/shard_map/pack/pallas_call | solution.py:62
  2.0 0.7 collective-permute-start
  2.7 9.8 %collective-permute-start.1 = (bf16[512,384]{1,0:T(8,128)(2,1)}, bf16[512,384]{1,0:T(8,128)(2,1)S(1)}, u32[]{:S(2)}, u32[]{:S(2)}) collective-permute-start(bf16[512,384]{1,0:T(8,128)(2,1)} %get-tuple-element.13.block_ref.own_ref), channel_id=1, source_target_pairs={{0,32},{8,40},{16,48},{24,56},{32,0},{40,8},{48,16},{56,24},{64,96... | collective-permute-start | bytes 1179656 | tf_op jit(solution)/shard_map/ppermute | solution.py:36
  12.5 3.1 %collective-permute-start.2 = (bf16[272,384]{1,0:T(8,128)(2,1)}, bf16[272,384]{1,0:T(8,128)(2,1)S(1)}, u32[]{:S(2)}, u32[]{:S(2)}) collective-permute-start(bf16[272,384]{1,0:T(8,128)(2,1)} %get-tuple-element.12.query_ref), channel_id=1, source_target_pairs={{0,8},{8,0},{16,24},{24,16},{32,40},{40,32},{48,56},{56,48},{64,72... | collective-permute-start | bytes 626696 | tf_op jit(solution)/shard_map/ppermute | solution.py:40
  15.6 2.2 %collective-permute-start.4 = (bf16[272,384]{1,0:T(8,128)(2,1)}, bf16[272,384]{1,0:T(8,128)(2,1)S(1)}, u32[]{:S(2)}, u32[]{:S(2)}) collective-permute-start(bf16[272,384]{1,0:T(8,128)(2,1)} %get-tuple-element.12.query_ref), channel_id=1, source_target_pairs={{8,16},{16,8},{40,48},{48,40},{72,80},{80,72},{104,112},{112,104},... | collective-permute-start | bytes 626696 | tf_op jit(solution)/shard_map/ppermute | solution.py:45
  17.8 0.0 collective-permute-done.2.pair_ref.query_ref
  17.8 0.0 copy-start
  17.9 1.7 %copy-done = bf16[384,3072]{1,0:T(8,128)(2,1)S(1)} copy-done((bf16[384,3072]{1,0:T(8,128)(2,1)S(1)}, bf16[384,3072]{1,0:T(8,128)(2,1)}, u32[]{:S(2)}) %copy-start) | copy-done | bytes 2359320
  19.5 0.0 copy-start.1
  19.5 0.9 %copy-done.1 = bf16[272,384]{1,0:T(8,128)(2,1)S(1)} copy-done((bf16[272,384]{1,0:T(8,128)(2,1)S(1)}, bf16[272,384]{1,0:T(8,128)(2,1)}, u32[]{:S(2)}) %copy-start.1) | copy-done | bytes 208920
  20.4 1.0 %copy-done.3 = bf16[512,384]{1,0:T(8,128)(2,1)S(1)} copy-done((bf16[512,384]{1,0:T(8,128)(2,1)S(1)}, bf16[512,384]{1,0:T(8,128)(2,1)}, u32[]{:S(2)}) %copy-start.3) | copy-done | bytes 393240
  21.4 1.1 %attend_own.1 = (f32[6,256,128]{2,1,0:T(8,128)S(1)}, f32[12,256,128]{2,1,0:T(8,128)S(1)}, bf16[384,3072]{1,0:T(8,128)(2,1)S(1)}) custom-call(bf16[272,384]{1,0:T(8,128)(2,1)S(1)} %copy-done.1, bf16[272,384]{1,0:T(8,128)(2,1)S(1)} %collective-permute-done.2.pair_ref.query_ref, bf16[512,384]{1,0:T(8,128)(2,1)S(1)} %copy-done.3, bf16[384,3072]{1,0:T(8,128)(2,1)S(1)} %copy-done), custom_call_target="tpu_custom_call" | custom-call | tf_op jit(solution)/shard_map/attend_own/pallas_call | solution.py:175
  22.6 0.0 collective-permute-done.first_ref
  22.6 8.0 %collective-permute-done.1.second_ref = bf16[512,384]{1,0:T(8,128)(2,1)S(1)} collective-permute-done((bf16[512,384]{1,0:T(8,128)(2,1)}, bf16[512,384]{1,0:T(8,128)(2,1)S(1)}, u32[]{:S(2)}, u32[]{:S(2)}) %collective-permute-start.1) | collective-permute-done | bytes 393248 | tf_op jit(solution)/shard_map/ppermute | solution.py:36
  30.6 1.3 %attend_pair.1.after_ref = bf16[272,384]{1,0:T(8,128)(2,1)S(1)} custom-call(bf16[272,384]{1,0:T(8,128)(2,1)S(1)} %collective-permute-done.2.pair_ref.query_ref, bf16[512,384]{1,0:T(8,128)(2,1)S(1)} %collective-permute-done.first_ref, bf16[512,384]{1,0:T(8,128)(2,1)S(1)} %collective-permute-done.1.second_ref, ...), custom_call_target="tpu_custom_call" | custom-call | flops 400000000 | bytes 2000000 | tf_op jit(solution)/shard_map/attend_pair/pallas_call | solution.py:208
  31.9 0.0 copy-start.2
  31.9 3.3 %collective-permute-start.3 = (bf16[272,384]{1,0:T(8,128)(2,1)S(1)}, bf16[272,384]{1,0:T(8,128)(2,1)S(1)}, u32[]{:S(2)}, u32[]{:S(2)}) collective-permute-start(bf16[272,384]{1,0:T(8,128)(2,1)S(1)} %attend_pair.1.after_ref), channel_id=1, source_target_pairs={{0,8},{8,0},{16,24},{24,16},{32,40},{40,32},{48,56},{56,48},{64,72... | collective-permute-start | bytes 626696 | tf_op jit(solution)/shard_map/ppermute | solution.py:40
  35.2 0.0 collective-permute-done.4.query_ref
  35.3 1.6 %attend_middle.1 = bf16[272,384]{1,0:T(8,128)(2,1)S(1)} custom-call(bf16[272,384]{1,0:T(8,128)(2,1)S(1)} %collective-permute-done.4.query_ref, bf16[512,384]{1,0:T(8,128)(2,1)S(1)} %copy-done.3, bf16[512,384]{1,0:T(8,128)(2,1)S(1)} %collective-permute-done.first_ref, bf16[512,384]{1,0:T(8,128)(2,1)S(1)} %collective-permute-done.1.second_ref, ...), custom_call_target="tpu_custom_call" | custom-call | flops 600000000 | bytes 2000000 | tf_op jit(solution)/shard_map/attend_middle/pallas_call | solution.py:240
  36.8 1.9 %collective-permute-start.5 = (bf16[272,384]{1,0:T(8,128)(2,1)S(1)}, bf16[272,384]{1,0:T(8,128)(2,1)S(1)}, u32[]{:S(2)}, u32[]{:S(2)}) collective-permute-start(bf16[272,384]{1,0:T(8,128)(2,1)S(1)} %attend_middle.1), channel_id=1, source_target_pairs={{8,16},{16,8},{40,48},{48,40},{72,80},{80,72},{104,112},{112,104},... | collective-permute-start | bytes 626696 | tf_op jit(solution)/shard_map/ppermute | solution.py:45
  38.7 0.0 collective-permute-done.3.message_ref
  38.8 0.0 copy-done.2
  38.8 2.0 %attend_last.1 = (f32[256,384]{1,0:T(8,128)S(1)}, f32[3,8,256]{2,1,0:T(8,128)S(1)}) custom-call(bf16[272,384]{1,0:T(8,128)(2,1)S(1)} %copy-done.2, bf16[512,384]{1,0:T(8,128)(2,1)S(1)} %collective-permute-done.first_ref, bf16[512,384]{1,0:T(8,128)(2,1)S(1)} %collective-permute-done.1.second_ref, f32[6,256,128]{2,1,0:T(8,128)S(1)} %get-tuple-element.14.mix_ref.old_mix_ref, ...), custom_call_target="tpu_custom_call" | custom-call | flops 400000000 | bytes 2000000 | tf_op jit(solution)/shard_map/attend_last/pallas_call | solution.py:271
  40.8 3.1 %collective-permute-done.5.middle_ref = bf16[272,384]{1,0:T(8,128)(2,1)S(1)} collective-permute-done((bf16[272,384]{1,0:T(8,128)(2,1)S(1)}, bf16[272,384]{1,0:T(8,128)(2,1)S(1)}, u32[]{:S(2)}, u32[]{:S(2)}) %collective-permute-start.5) | collective-permute-done | bytes 208928 | tf_op jit(solution)/shard_map/ppermute | solution.py:45
  43.9 2.2 %project.1 = bf16[8,256,384]{2,1,0:T(8,128)(2,1)} custom-call(f32[256,384]{1,0:T(8,128)S(1)} %get-tuple-element.16.own_ref, f32[3,8,256]{2,1,0:T(8,128)S(1)} %get-tuple-element.17.stats_ref, bf16[272,384]{1,0:T(8,128)(2,1)S(1)} %collective-permute-done.5.middle_ref, bf16[384,3072]{1,0:T(8,128)(2,1)S(1)} %get-tuple-element.18.weight_ref), custom_call_target="tpu_custom_call" | custom-call | flops 603979776 | bytes 5000000 | tf_op jit(solution)/shard_map/project/pallas_call | solution.py:326
  46.2 0.0 copy-start.5
  46.2 0.0 copy-start.4
  46.2 5.3 %all-to-all-start = ((bf16[8,256,384]{2,1,0:T(8,128)(2,1)}), bf16[8,256,384]{2,1,0:T(8,128)(2,1)S(1)}, u32[]{:S(2)}, u32[]{:S(2)}) async-start(bf16[8,256,384]{2,1,0:T(8,128)(2,1)} %project.1), calls=%async_computation | async-start | bytes 3145728 | tf_op jit(solution)/shard_map/all_to_all | solution.py:365
  51.5 0.0 copy-done.5
  51.5 17.2 %all-to-all-done.terms_ref = bf16[8,256,384]{2,1,0:T(8,128)(2,1)S(1)} async-done(((bf16[8,256,384]{2,1,0:T(8,128)(2,1)}), bf16[8,256,384]{2,1,0:T(8,128)(2,1)S(1)}, u32[]{:S(2)}, u32[]{:S(2)}) %all-to-all-start) | async-done | bytes 1572896 | tf_op jit(solution)/shard_map/all_to_all | solution.py:365
  68.7 0.0 copy-done.4
  68.7 0.9 %finish.1 = bf16[256,384]{1,0:T(8,128)(2,1)} custom-call(bf16[8,256,384]{2,1,0:T(8,128)(2,1)S(1)} %all-to-all-done.terms_ref, bf16[256,384]{1,0:T(8,128)(2,1)S(1)} %copy-done.4, f32[1,384]{1,0:T(1,128)S(1)} %reshape.3.gate_ref), custom_call_target="tpu_custom_call" | custom-call | flops 7864320 | bytes 2000000 | tf_op jit(solution)/shard_map/finish/pallas_call | solution.py:345
  (2 shorter events, 0.0 us)
Async XLA Ops:
  2.0 20.6 %collective-permute-start = (bf16[512,384]{1,0:T(8,128)(2,1)}, bf16[512,384]{1,0:T(8,128)(2,1)S(1)}, u32[]{:S(2)}, u32[]{:S(2)}) collective-permute-start(bf16[512,384]{1,0:T(8,128)(2,1)} %get-tuple-element.13.block_ref.own_ref), channel_id=1, source_target_pairs={{32,64},{40,72},{48,80},{56,88},{64,32},{72,40},{80,48},{88,56},{9... | collective-permute-start | bytes 1179656 | tf_op jit(solution)/shard_map/ppermute | solution.py:36
  2.7 27.9 %collective-permute-start.1 = (bf16[512,384]{1,0:T(8,128)(2,1)}, bf16[512,384]{1,0:T(8,128)(2,1)S(1)}, u32[]{:S(2)}, u32[]{:S(2)}) collective-permute-start(bf16[512,384]{1,0:T(8,128)(2,1)} %get-tuple-element.13.block_ref.own_ref), channel_id=1, source_target_pairs={{0,32},{8,40},{16,48},{24,56},{32,0},{40,8},{48,16},{56,24},{64,96... | collective-permute-start | bytes 1179656 | tf_op jit(solution)/shard_map/ppermute | solution.py:36
  12.5 5.4 %collective-permute-start.2 = (bf16[272,384]{1,0:T(8,128)(2,1)}, bf16[272,384]{1,0:T(8,128)(2,1)S(1)}, u32[]{:S(2)}, u32[]{:S(2)}) collective-permute-start(bf16[272,384]{1,0:T(8,128)(2,1)} %get-tuple-element.12.query_ref), channel_id=1, source_target_pairs={{0,8},{8,0},{16,24},{24,16},{32,40},{40,32},{48,56},{56,48},{64,72... | collective-permute-start | bytes 626696 | tf_op jit(solution)/shard_map/ppermute | solution.py:40
  15.6 19.6 %collective-permute-start.4 = (bf16[272,384]{1,0:T(8,128)(2,1)}, bf16[272,384]{1,0:T(8,128)(2,1)S(1)}, u32[]{:S(2)}, u32[]{:S(2)}) collective-permute-start(bf16[272,384]{1,0:T(8,128)(2,1)} %get-tuple-element.12.query_ref), channel_id=1, source_target_pairs={{8,16},{16,8},{40,48},{48,40},{72,80},{80,72},{104,112},{112,104},... | collective-permute-start | bytes 626696 | tf_op jit(solution)/shard_map/ppermute | solution.py:45
  17.8 1.7 %copy-start = (bf16[384,3072]{1,0:T(8,128)(2,1)S(1)}, bf16[384,3072]{1,0:T(8,128)(2,1)}, u32[]{:S(2)}) copy-start(bf16[384,3072]{1,0:T(8,128)(2,1)} %weight_ref.1) | copy-start | bytes 7077892
  19.5 0.9 %copy-start.1 = (bf16[272,384]{1,0:T(8,128)(2,1)S(1)}, bf16[272,384]{1,0:T(8,128)(2,1)}, u32[]{:S(2)}) copy-start(bf16[272,384]{1,0:T(8,128)(2,1)} %get-tuple-element.12.query_ref) | copy-start | bytes 626692
  20.4 1.0 %copy-start.3 = (bf16[512,384]{1,0:T(8,128)(2,1)S(1)}, bf16[512,384]{1,0:T(8,128)(2,1)}, u32[]{:S(2)}) copy-start(bf16[512,384]{1,0:T(8,128)(2,1)} %get-tuple-element.13.block_ref.own_ref) | copy-start | bytes 1179652
  31.9 6.9 %copy-start.2 = (bf16[272,384]{1,0:T(8,128)(2,1)S(1)}, bf16[272,384]{1,0:T(8,128)(2,1)}, u32[]{:S(2)}) copy-start(bf16[272,384]{1,0:T(8,128)(2,1)} %get-tuple-element.12.query_ref) | copy-start | bytes 626692
  31.9 6.8 %collective-permute-start.3 = (bf16[272,384]{1,0:T(8,128)(2,1)S(1)}, bf16[272,384]{1,0:T(8,128)(2,1)S(1)}, u32[]{:S(2)}, u32[]{:S(2)}) collective-permute-start(bf16[272,384]{1,0:T(8,128)(2,1)S(1)} %attend_pair.1.after_ref), channel_id=1, source_target_pairs={{0,8},{8,0},{16,24},{24,16},{32,40},{40,32},{48,56},{56,48},{64,72... | collective-permute-start | bytes 626696 | tf_op jit(solution)/shard_map/ppermute | solution.py:40
  36.8 7.1 %collective-permute-start.5 = (bf16[272,384]{1,0:T(8,128)(2,1)S(1)}, bf16[272,384]{1,0:T(8,128)(2,1)S(1)}, u32[]{:S(2)}, u32[]{:S(2)}) collective-permute-start(bf16[272,384]{1,0:T(8,128)(2,1)S(1)} %attend_middle.1), channel_id=1, source_target_pairs={{8,16},{16,8},{40,48},{48,40},{72,80},{80,72},{104,112},{112,104},... | collective-permute-start | bytes 626696 | tf_op jit(solution)/shard_map/ppermute | solution.py:45
  46.2 5.3 %copy-start.5 = (f32[384]{0:T(512)S(1)}, f32[384]{0:T(512)}, u32[]{:S(2)}) copy-start(f32[384]{0:T(512)} %param.13) | copy-start | bytes 4612
  46.2 22.5 %copy-start.4 = (bf16[256,384]{1,0:T(8,128)(2,1)S(1)}, bf16[256,384]{1,0:T(8,128)(2,1)}, u32[]{:S(2)}) copy-start(bf16[256,384]{1,0:T(8,128)(2,1)} %residual_ref.1) | copy-start | bytes 589828
  46.2 22.5 %all-to-all-start = ((bf16[8,256,384]{2,1,0:T(8,128)(2,1)}), bf16[8,256,384]{2,1,0:T(8,128)(2,1)S(1)}, u32[]{:S(2)}, u32[]{:S(2)}) async-start(bf16[8,256,384]{2,1,0:T(8,128)(2,1)} %project.1), calls=%async_computation | async-start | bytes 3145728 | tf_op jit(solution)/shard_map/all_to_all | solution.py:365

commit v12 on v11

--- a/solution.py
+++ b/solution.py
@@ -216,7 +216,8 @@
     )(query, first, second, mix, stats)
 
 
-def middle_kernel(query_ref, own_ref, first_ref, second_ref, after_ref, out_ref):
+def middle_kernel(query_ref, own_ref, first_ref, second_ref, pair_ref, out_ref, same_pair_ref):
+    same_pair_ref[...] = pair_ref[...]
     rows, width = own_ref.shape[0] // 2, own_ref.shape[1]
     height = lax.axis_index("tile") % HEIGHT_TILES
     inside = (height > 0) & (height < HEIGHT_TILES - 1)
@@ -235,17 +236,17 @@
         out_ref[...] = jnp.zeros_like(out_ref)
 
 
-def attend_middle(query, own, first, second, after):
+def attend_middle(query, own, first, second, for_pair):
     whole = pl.BlockSpec(memory_space=VMEM)
     return pl.pallas_call(
         middle_kernel,
-        out_shape=jax.ShapeDtypeStruct(query.shape, jnp.bfloat16),
-        in_specs=[whole] * 4 + [pl.BlockSpec(memory_space=pl.ANY)],
-        out_specs=whole,
+        out_shape=(jax.ShapeDtypeStruct(query.shape, jnp.bfloat16),) * 2,
+        in_specs=[whole] * 5,
+        out_specs=(whole, whole),
         compiler_params=params(24),
         cost_estimate=pl.CostEstimate(flops=600_000_000, bytes_accessed=2_000_000, transcendentals=0),
         name="attend_middle",
-    )(query, own, first, second, after)
+    )(query, own, first, second, for_pair)
 
 
 def last_kernel(query_ref, first_ref, second_ref, old_mix_ref, old_stats_ref, message_ref, mix_ref, stats_ref):
@@ -359,7 +360,7 @@
     pair_asks, middle_asks = swap_pair(packed), swap_middle(packed)
     mix, stats, held_weight = attend_own(packed, pair_asks, block, out_weight)
     for_pair = attend_pair(pair_asks, first, second, mix, stats)
-    for_middle = attend_middle(middle_asks, block, first, second, for_pair)
+    for_middle, for_pair = attend_middle(middle_asks, block, first, second, for_pair)
     mix, stats = attend_last(packed, first, second, mix, stats, swap_pair(for_pair))
     terms = project(mix, stats, swap_middle(for_middle), held_weight)
     terms = lax.all_to_all(terms, "head", 0, 0)

time: 70.7 us -> 71.4 us (level)
  starting transfers between devices: 26.4 us -> 28 us
    ppermute x2, starting transfers between devices: 4.12 us -> 6.49 us  [swap_middle(): return lax.ppermute(block, 'tile', route)]
    ppermute x2, starting transfers between devices: 6.48 us -> 5.06 us  [swap_pair(): lax.ppermute(block, 'tile', [(tile, tile ^ 1) for tile, *_ in places()])]
    ppermute x2, waiting for transfers between devices: 3.13 us -> 1.81 us  [swap_middle(): return lax.ppermute(block, 'tile', route)]
    all_to_all x1, waiting for transfers between devices: 17.2 us -> 18.3 us  [shards(): terms = lax.all_to_all(terms, 'head', 0, 0)]
  transfers between devices with their start and end apart: 7 -> 7, of which waited for: 3 -> 4; matrix products, arithmetic and copies ran while one was open for 0% -> 0% of each run, Pallas kernels for 9% -> 6%
where the time goes in v12:
time: 71.4 us; the launch traced here: 71 us
  waiting for transfers between devices  28.1 us (39%)
  starting transfers between devices  28 us (39%)
  Pallas kernels  11.2 us (16%)
  local copies, waits for them, and re-layouts  3.61 us (5%)
    all_to_all x1, waiting for transfers between devices, shards(): terms = lax.all_to_all(terms, 'head', 0, 0)  18.3 us
    ppermute x2, starting transfers between devices, swap_times(): return lax.ppermute(block, 'tile', route)  10.5 us
    ppermute x2, waiting for transfers between devices, swap_times(): return lax.ppermute(block, 'tile', route)  7.99 us
    ppermute x2, starting transfers between devices, swap_middle(): return lax.ppermute(block, 'tile', route)  6.49 us
    all_to_all x1, starting transfers between devices, shards(): terms = lax.all_to_all(terms, 'head', 0, 0)  5.97 us
    ppermute x2, starting transfers between devices, swap_pair(): lax.ppermute(block, 'tile', [(tile, tile ^ 1) for tile, *_ in places()])  5.06 us
    unnamed x12, local copies, waits for them, and re-layouts  3.6 us
    pallas_call x1, Pallas kernels, project(): pl.pallas_call(project_kernel, out_shape=jax.ShapeDtypeStruct(shape, jnp....  2.23 us
  transfers between devices with their start and end apart: 7, of which 4 were waited for; matrix products, arithmetic and copies ran while one was open for 0% of the time, Pallas kernels for 6%

profile of v12, /device:TPU:1, one launch (start us, length us, event | category | flops | bytes accessed | tf_op | source)
XLA Modules:
  0.0 71.0 jit_solution(4724674089038478987)
XLA Ops:
  0.0 2.0 %pack.1 = (bf16[272,384]{1,0:T(8,128)(2,1)}, bf16[512,384]{1,0:T(8,128)(2,1)}) custom-call(s32[1,3]{1,0:T(1,128)} %windows_ref.1, bf16[256,384]{1,0:T(8,128)(2,1)} %q_ref.1, bf16[256,384]{1,0:T(8,128)(2,1)} %k_ref.1, bf16[256,384]{1,0:T(8,128)(2,1)} %v_ref.1), custom_call_target="tpu_custom_call" | custom-call | tf_op jit(solution)/shard_map/pack/pallas_call | solution.py:62
  2.0 0.7 collective-permute-start
  2.7 9.8 %collective-permute-start.1 = (bf16[512,384]{1,0:T(8,128)(2,1)}, bf16[512,384]{1,0:T(8,128)(2,1)S(1)}, u32[]{:S(2)}, u32[]{:S(2)}) collective-permute-start(bf16[512,384]{1,0:T(8,128)(2,1)} %get-tuple-element.15.block_ref.own_ref), channel_id=1, source_target_pairs={{0,32},{8,40},{16,48},{24,56},{32,0},{40,8},{48,16},{56,24},{64,96... | collective-permute-start | bytes 1179656 | tf_op jit(solution)/shard_map/ppermute | solution.py:36
  12.5 3.1 %collective-permute-start.2 = (bf16[272,384]{1,0:T(8,128)(2,1)}, bf16[272,384]{1,0:T(8,128)(2,1)S(1)}, u32[]{:S(2)}, u32[]{:S(2)}) collective-permute-start(bf16[272,384]{1,0:T(8,128)(2,1)} %get-tuple-element.14.query_ref), channel_id=1, source_target_pairs={{0,8},{8,0},{16,24},{24,16},{32,40},{40,32},{48,56},{56,48},{64,72... | collective-permute-start | bytes 626696 | tf_op jit(solution)/shard_map/ppermute | solution.py:40
  15.6 2.2 %collective-permute-start.3 = (bf16[272,384]{1,0:T(8,128)(2,1)}, bf16[272,384]{1,0:T(8,128)(2,1)S(1)}, u32[]{:S(2)}, u32[]{:S(2)}) collective-permute-start(bf16[272,384]{1,0:T(8,128)(2,1)} %get-tuple-element.14.query_ref), channel_id=1, source_target_pairs={{8,16},{16,8},{40,48},{48,40},{72,80},{80,72},{104,112},{112,104},... | collective-permute-start | bytes 626696 | tf_op jit(solution)/shard_map/ppermute | solution.py:45
  17.8 0.0 collective-permute-done.2.pair_ref.query_ref
  17.8 0.0 copy-start
  17.9 1.7 %copy-done = bf16[384,3072]{1,0:T(8,128)(2,1)S(1)} copy-done((bf16[384,3072]{1,0:T(8,128)(2,1)S(1)}, bf16[384,3072]{1,0:T(8,128)(2,1)}, u32[]{:S(2)}) %copy-start) | copy-done | bytes 2359320
  19.5 0.0 copy-start.1
  19.5 0.9 %copy-done.1 = bf16[272,384]{1,0:T(8,128)(2,1)S(1)} copy-done((bf16[272,384]{1,0:T(8,128)(2,1)S(1)}, bf16[272,384]{1,0:T(8,128)(2,1)}, u32[]{:S(2)}) %copy-start.1) | copy-done | bytes 208920
  20.4 1.0 %copy-done.3 = bf16[512,384]{1,0:T(8,128)(2,1)S(1)} copy-done((bf16[512,384]{1,0:T(8,128)(2,1)S(1)}, bf16[512,384]{1,0:T(8,128)(2,1)}, u32[]{:S(2)}) %copy-start.3) | copy-done | bytes 393240
  21.4 1.1 %attend_own.1 = (f32[6,256,128]{2,1,0:T(8,128)S(1)}, f32[12,256,128]{2,1,0:T(8,128)S(1)}, bf16[384,3072]{1,0:T(8,128)(2,1)S(1)}) custom-call(bf16[272,384]{1,0:T(8,128)(2,1)S(1)} %copy-done.1, bf16[272,384]{1,0:T(8,128)(2,1)S(1)} %collective-permute-done.2.pair_ref.query_ref, bf16[512,384]{1,0:T(8,128)(2,1)S(1)} %copy-done.3, bf16[384,3072]{1,0:T(8,128)(2,1)S(1)} %copy-done), custom_call_target="tpu_custom_call" | custom-call | tf_op jit(solution)/shard_map/attend_own/pallas_call | solution.py:175
  22.6 0.0 collective-permute-done.first_ref
  22.6 8.0 %collective-permute-done.1.second_ref = bf16[512,384]{1,0:T(8,128)(2,1)S(1)} collective-permute-done((bf16[512,384]{1,0:T(8,128)(2,1)}, bf16[512,384]{1,0:T(8,128)(2,1)S(1)}, u32[]{:S(2)}, u32[]{:S(2)}) %collective-permute-start.1) | collective-permute-done | bytes 393248 | tf_op jit(solution)/shard_map/ppermute | solution.py:36
  30.6 1.3 %attend_pair.1.pair_ref = bf16[272,384]{1,0:T(8,128)(2,1)S(1)} custom-call(bf16[272,384]{1,0:T(8,128)(2,1)S(1)} %collective-permute-done.2.pair_ref.query_ref, bf16[512,384]{1,0:T(8,128)(2,1)S(1)} %collective-permute-done.first_ref, bf16[512,384]{1,0:T(8,128)(2,1)S(1)} %collective-permute-done.1.second_ref, ...), custom_call_target="tpu_custom_call" | custom-call | flops 400000000 | bytes 2000000 | tf_op jit(solution)/shard_map/attend_pair/pallas_call | solution.py:208
  31.9 0.0 copy-start.2
  31.9 0.4 collective-permute-done.3.query_ref
  32.3 1.6 %attend_middle.1 = (bf16[272,384]{1,0:T(8,128)(2,1)S(1)}, bf16[272,384]{1,0:T(8,128)(2,1)S(1)}) custom-call(bf16[272,384]{1,0:T(8,128)(2,1)S(1)} %collective-permute-done.3.query_ref, bf16[512,384]{1,0:T(8,128)(2,1)S(1)} %copy-done.3, bf16[512,384]{1,0:T(8,128)(2,1)S(1)} %collective-permute-done.first_ref, ...), custom_call_target="tpu_custom_call" | custom-call | flops 600000000 | bytes 2000000 | tf_op jit(solution)/shard_map/attend_middle/pallas_call | solution.py:241
  33.9 1.9 %collective-permute-start.4 = (bf16[272,384]{1,0:T(8,128)(2,1)S(1)}, bf16[272,384]{1,0:T(8,128)(2,1)S(1)}, u32[]{:S(2)}, u32[]{:S(2)}) collective-permute-start(bf16[272,384]{1,0:T(8,128)(2,1)S(1)} %get-tuple-element.18), channel_id=1, source_target_pairs={{0,8},{8,0},{16,24},{24,16},{32,40},{40,32},{48,56},{56,48},{64,72... | collective-permute-start | bytes 626696 | tf_op jit(solution)/shard_map/ppermute | solution.py:40
  35.8 4.3 %collective-permute-start.5 = (bf16[272,384]{1,0:T(8,128)(2,1)S(1)}, bf16[272,384]{1,0:T(8,128)(2,1)S(1)}, u32[]{:S(2)}, u32[]{:S(2)}) collective-permute-start(bf16[272,384]{1,0:T(8,128)(2,1)S(1)} %get-tuple-element.21), channel_id=1, source_target_pairs={{8,16},{16,8},{40,48},{48,40},{72,80},{80,72},{104,112},{112,104},... | collective-permute-start | bytes 626696 | tf_op jit(solution)/shard_map/ppermute | solution.py:45
  40.1 0.0 collective-permute-done.4.message_ref
  40.1 0.0 copy-done.2
  40.1 2.0 %attend_last.1 = (f32[256,384]{1,0:T(8,128)S(1)}, f32[3,8,256]{2,1,0:T(8,128)S(1)}) custom-call(bf16[272,384]{1,0:T(8,128)(2,1)S(1)} %copy-done.2, bf16[512,384]{1,0:T(8,128)(2,1)S(1)} %collective-permute-done.first_ref, bf16[512,384]{1,0:T(8,128)(2,1)S(1)} %collective-permute-done.1.second_ref, f32[6,256,128]{2,1,0:T(8,128)S(1)} %get-tuple-element.16.mix_ref.old_mix_ref, ...), custom_call_target="tpu_custom_call" | custom-call | flops 400000000 | bytes 2000000 | tf_op jit(solution)/shard_map/attend_last/pallas_call | solution.py:272
  42.2 1.4 %collective-permute-done.5.middle_ref = bf16[272,384]{1,0:T(8,128)(2,1)S(1)} collective-permute-done((bf16[272,384]{1,0:T(8,128)(2,1)S(1)}, bf16[272,384]{1,0:T(8,128)(2,1)S(1)}, u32[]{:S(2)}, u32[]{:S(2)}) %collective-permute-start.5) | collective-permute-done | bytes 208928 | tf_op jit(solution)/shard_map/ppermute | solution.py:45
  43.6 2.2 %project.1 = bf16[8,256,384]{2,1,0:T(8,128)(2,1)} custom-call(f32[256,384]{1,0:T(8,128)S(1)} %get-tuple-element.19.own_ref, f32[3,8,256]{2,1,0:T(8,128)S(1)} %get-tuple-element.20.stats_ref, bf16[272,384]{1,0:T(8,128)(2,1)S(1)} %collective-permute-done.5.middle_ref, bf16[384,3072]{1,0:T(8,128)(2,1)S(1)} %get-tuple-element.22.weight_ref), custom_call_target="tpu_custom_call" | custom-call | flops 603979776 | bytes 5000000 | tf_op jit(solution)/shard_map/project/pallas_call | solution.py:327
  45.8 0.0 copy-start.5
  45.8 0.0 copy-start.4
  45.8 6.0 %all-to-all-start = ((bf16[8,256,384]{2,1,0:T(8,128)(2,1)}), bf16[8,256,384]{2,1,0:T(8,128)(2,1)S(1)}, u32[]{:S(2)}, u32[]{:S(2)}) async-start(bf16[8,256,384]{2,1,0:T(8,128)(2,1)} %project.1), calls=%async_computation | async-start | bytes 3145728 | tf_op jit(solution)/shard_map/all_to_all | solution.py:366
  51.8 0.0 copy-done.5
  51.8 18.3 %all-to-all-done.terms_ref = bf16[8,256,384]{2,1,0:T(8,128)(2,1)S(1)} async-done(((bf16[8,256,384]{2,1,0:T(8,128)(2,1)}), bf16[8,256,384]{2,1,0:T(8,128)(2,1)S(1)}, u32[]{:S(2)}, u32[]{:S(2)}) %all-to-all-start) | async-done | bytes 1572896 | tf_op jit(solution)/shard_map/all_to_all | solution.py:366
  70.1 0.0 copy-done.4
  70.1 0.9 %finish.1 = bf16[256,384]{1,0:T(8,128)(2,1)} custom-call(bf16[8,256,384]{2,1,0:T(8,128)(2,1)S(1)} %all-to-all-done.terms_ref, bf16[256,384]{1,0:T(8,128)(2,1)S(1)} %copy-done.4, f32[1,384]{1,0:T(1,128)S(1)} %reshape.3.gate_ref), custom_call_target="tpu_custom_call" | custom-call | flops 7864320 | bytes 2000000 | tf_op jit(solution)/shard_map/finish/pallas_call | solution.py:346
  (2 shorter events, 0.0 us)
Async XLA Ops:
  2.0 20.6 %collective-permute-start = (bf16[512,384]{1,0:T(8,128)(2,1)}, bf16[512,384]{1,0:T(8,128)(2,1)S(1)}, u32[]{:S(2)}, u32[]{:S(2)}) collective-permute-start(bf16[512,384]{1,0:T(8,128)(2,1)} %get-tuple-element.15.block_ref.own_ref), channel_id=1, source_target_pairs={{32,64},{40,72},{48,80},{56,88},{64,32},{72,40},{80,48},{88,56},{9... | collective-permute-start | bytes 1179656 | tf_op jit(solution)/shard_map/ppermute | solution.py:36
  2.7 27.9 %collective-permute-start.1 = (bf16[512,384]{1,0:T(8,128)(2,1)}, bf16[512,384]{1,0:T(8,128)(2,1)S(1)}, u32[]{:S(2)}, u32[]{:S(2)}) collective-permute-start(bf16[512,384]{1,0:T(8,128)(2,1)} %get-tuple-element.15.block_ref.own_ref), channel_id=1, source_target_pairs={{0,32},{8,40},{16,48},{24,56},{32,0},{40,8},{48,16},{56,24},{64,96... | collective-permute-start | bytes 1179656 | tf_op jit(solution)/shard_map/ppermute | solution.py:36
  12.5 5.4 %collective-permute-start.2 = (bf16[272,384]{1,0:T(8,128)(2,1)}, bf16[272,384]{1,0:T(8,128)(2,1)S(1)}, u32[]{:S(2)}, u32[]{:S(2)}) collective-permute-start(bf16[272,384]{1,0:T(8,128)(2,1)} %get-tuple-element.14.query_ref), channel_id=1, source_target_pairs={{0,8},{8,0},{16,24},{24,16},{32,40},{40,32},{48,56},{56,48},{64,72... | collective-permute-start | bytes 626696 | tf_op jit(solution)/shard_map/ppermute | solution.py:40
  15.6 16.7 %collective-permute-start.3 = (bf16[272,384]{1,0:T(8,128)(2,1)}, bf16[272,384]{1,0:T(8,128)(2,1)S(1)}, u32[]{:S(2)}, u32[]{:S(2)}) collective-permute-start(bf16[272,384]{1,0:T(8,128)(2,1)} %get-tuple-element.14.query_ref), channel_id=1, source_target_pairs={{8,16},{16,8},{40,48},{48,40},{72,80},{80,72},{104,112},{112,104},... | collective-permute-start | bytes 626696 | tf_op jit(solution)/shard_map/ppermute | solution.py:45
  17.8 1.7 %copy-start = (bf16[384,3072]{1,0:T(8,128)(2,1)S(1)}, bf16[384,3072]{1,0:T(8,128)(2,1)}, u32[]{:S(2)}) copy-start(bf16[384,3072]{1,0:T(8,128)(2,1)} %weight_ref.1) | copy-start | bytes 7077892
  19.5 0.9 %copy-start.1 = (bf16[272,384]{1,0:T(8,128)(2,1)S(1)}, bf16[272,384]{1,0:T(8,128)(2,1)}, u32[]{:S(2)}) copy-start(bf16[272,384]{1,0:T(8,128)(2,1)} %get-tuple-element.14.query_ref) | copy-start | bytes 626692
  20.4 1.0 %copy-start.3 = (bf16[512,384]{1,0:T(8,128)(2,1)S(1)}, bf16[512,384]{1,0:T(8,128)(2,1)}, u32[]{:S(2)}) copy-start(bf16[512,384]{1,0:T(8,128)(2,1)} %get-tuple-element.15.block_ref.own_ref) | copy-start | bytes 1179652
  31.9 8.2 %copy-start.2 = (bf16[272,384]{1,0:T(8,128)(2,1)S(1)}, bf16[272,384]{1,0:T(8,128)(2,1)}, u32[]{:S(2)}) copy-start(bf16[272,384]{1,0:T(8,128)(2,1)} %get-tuple-element.14.query_ref) | copy-start | bytes 626692
  33.9 6.2 %collective-permute-start.4 = (bf16[272,384]{1,0:T(8,128)(2,1)S(1)}, bf16[272,384]{1,0:T(8,128)(2,1)S(1)}, u32[]{:S(2)}, u32[]{:S(2)}) collective-permute-start(bf16[272,384]{1,0:T(8,128)(2,1)S(1)} %get-tuple-element.18), channel_id=1, source_target_pairs={{0,8},{8,0},{16,24},{24,16},{32,40},{40,32},{48,56},{56,48},{64,72... | collective-permute-start | bytes 626696 | tf_op jit(solution)/shard_map/ppermute | solution.py:40
  35.8 7.8 %collective-permute-start.5 = (bf16[272,384]{1,0:T(8,128)(2,1)S(1)}, bf16[272,384]{1,0:T(8,128)(2,1)S(1)}, u32[]{:S(2)}, u32[]{:S(2)}) collective-permute-start(bf16[272,384]{1,0:T(8,128)(2,1)S(1)} %get-tuple-element.21), channel_id=1, source_target_pairs={{8,16},{16,8},{40,48},{48,40},{72,80},{80,72},{104,112},{112,104},... | collective-permute-start | bytes 626696 | tf_op jit(solution)/shard_map/ppermute | solution.py:45
  45.8 6.0 %copy-start.5 = (f32[384]{0:T(512)S(1)}, f32[384]{0:T(512)}, u32[]{:S(2)}) copy-start(f32[384]{0:T(512)} %param.13) | copy-start | bytes 4612
  45.8 24.3 %copy-start.4 = (bf16[256,384]{1,0:T(8,128)(2,1)S(1)}, bf16[256,384]{1,0:T(8,128)(2,1)}, u32[]{:S(2)}) copy-start(bf16[256,384]{1,0:T(8,128)(2,1)} %residual_ref.1) | copy-start | bytes 589828
  45.8 24.2 %all-to-all-start = ((bf16[8,256,384]{2,1,0:T(8,128)(2,1)}), bf16[8,256,384]{2,1,0:T(8,128)(2,1)S(1)}, u32[]{:S(2)}, u32[]{:S(2)}) async-start(bf16[8,256,384]{2,1,0:T(8,128)(2,1)} %project.1), calls=%async_computation | async-start | bytes 3145728 | tf_op jit(solution)/shard_map/all_to_all | solution.py:366

commit v13 on v11

--- a/solution.py
+++ b/solution.py
@@ -2,6 +2,7 @@
 
 import jax
 import jax.numpy as jnp
+import numpy as np
 from jax import lax
 from jax.experimental import pallas as pl
 from jax.experimental.pallas import tpu as pltpu
@@ -12,7 +13,7 @@
 SIDE = 16
 LOG2E = 1.4426950408889634
 MASKED = -1e30
-LAST_FLOPS = 400_000_000
+LAST_FLOPS = 8_000_000_000
 MESH_AXES = ("tile", "head")
 VMEM = pltpu.VMEM
 SMEM = pltpu.SMEM
@@ -43,6 +44,31 @@
 def swap_middle(block):
     route = [(tile, tile + (1 if height == 1 else -1)) for tile, _, height, _ in places() if height in (1, 2)]
     return lax.ppermute(block, "tile", route)
+
+
+def swap_far(block):
+    return lax.ppermute(block, "far", [(0, 1), (1, 0)])
+
+
+def split_weight_kernel(weight_ref, mine_ref, theirs_ref):
+    width = mine_ref.shape[1]
+    far = lax.axis_index("far")
+    mine_ref[...] = weight_ref[:, pl.ds(pl.multiple_of(far * width, HD), width)]
+    theirs_ref[...] = weight_ref[:, pl.ds(pl.multiple_of((1 - far) * width, HD), width)]
+
+
+def split_weight(out_weight):
+    rows, features = out_weight.shape
+    whole = pl.BlockSpec(memory_space=VMEM)
+    return pl.pallas_call(
+        split_weight_kernel,
+        out_shape=(jax.ShapeDtypeStruct((rows, features // 2), out_weight.dtype),) * 2,
+        in_specs=[whole],
+        out_specs=(whole,) * 2,
+        compiler_params=params(24),
+        cost_estimate=pl.CostEstimate(flops=0, bytes_accessed=0, transcendentals=0),
+        name="split_weight",
+    )(out_weight)
 
 
 def pack_kernel(windows_ref, q_ref, k_ref, v_ref, packed_ref, block_ref):
@@ -156,19 +182,16 @@
     return [block_bias(wide, stage) for stage in (1, 2)]
 
 
-def own_kernel(query_ref, pair_ref, block_ref, weight_ref, mix_ref, stats_ref, held_ref, sem):
-    copy = pltpu.make_async_copy(weight_ref, held_ref, sem)
-    copy.start()
+def own_kernel(query_ref, pair_ref, block_ref, mix_ref, stats_ref):
     rows, width = block_ref.shape[0] // 2, block_ref.shape[1]
     for place, ref in enumerate((query_ref, pair_ref)):
         for head in range(width // HD):
             low, index = head * HD, 2 * head + place
             largest, total, mix = attend(ref[:rows, low : low + HD], [block_ref], [0.0], low)
             mix_ref[index], stats_ref[2 * index], stats_ref[2 * index + 1] = mix, largest, total
-    copy.wait()
-
-
-def attend_own(queries, pair, block, out_weight):
+
+
+def attend_own(queries, pair, block):
     rows, width = block.shape[0] // 2, block.shape[1]
     heads = width // HD
     whole = pl.BlockSpec(memory_space=VMEM)
@@ -177,15 +200,13 @@
         out_shape=(
             jax.ShapeDtypeStruct((2 * heads, rows, HD), jnp.float32),
             jax.ShapeDtypeStruct((4 * heads, rows, HD), jnp.float32),
-            jax.ShapeDtypeStruct(out_weight.shape, out_weight.dtype),
         ),
-        in_specs=[whole] * 3 + [pl.BlockSpec(memory_space=pl.ANY)],
-        out_specs=(whole,) * 3,
-        scratch_shapes=[pltpu.SemaphoreType.DMA],
+        in_specs=[whole] * 3,
+        out_specs=(whole,) * 2,
         compiler_params=params(24),
         cost_estimate=pl.CostEstimate(flops=0, bytes_accessed=0, transcendentals=0),
         name="attend_own",
-    )(queries, pair, block, out_weight)
+    )(queries, pair, block)
 
 
 def old_parts(mix_ref, stats_ref, head, place):
@@ -282,7 +303,7 @@
     )(queries, first, second, mix, stats, message)
 
 
-def project_kernel(own_ref, stats_ref, middle_ref, weight_ref, out_ref, held_ref, sems):
+def merge_kernel(own_ref, stats_ref, middle_ref, out_ref):
     rows, width = own_ref.shape
     heads = width // HD
     height = lax.axis_index("tile") % HEIGHT_TILES
@@ -300,17 +321,33 @@
         shares = jnp.where(line == 2 * head, shrink / whole, shares)
         shares = jnp.where(line == 2 * head + 1, share / whole, shares)
     shares = jnp.transpose(shares)
-    merged = []
     for head in range(heads):
         low = head * HD
         value = own_ref[:, low : low + HD] * column(shares, 2 * head)
         value += middle_ref[:rows, low : low + HD].astype(jnp.float32) * column(shares, 2 * head + 1)
-        merged.append(value.astype(jnp.bfloat16))
-    attention = jnp.concatenate(merged, axis=1)
+        out_ref[:, low : low + HD] = value.astype(out_ref.dtype)
+
+
+def merge(own, stats, middle):
+    whole = pl.BlockSpec(memory_space=VMEM)
+    return pl.pallas_call(
+        merge_kernel,
+        out_shape=jax.ShapeDtypeStruct(own.shape, jnp.bfloat16),
+        in_specs=[whole] * 3,
+        out_specs=whole,
+        compiler_params=params(24),
+        name="merge",
+    )(own, stats, middle)
+
+
+def project_kernel(mine_ref, theirs_ref, my_weight_ref, their_weight_ref, out_ref, held_ref, sems):
+    width = mine_ref.shape[1]
     copies = []
     for group in range(out_ref.shape[0]):
-        held_ref[group] = jnp.dot(
-            attention, weight_ref[:, group * width : (group + 1) * width], preferred_element_type=jnp.float32
+        low = group * width
+        held_ref[group] = (
+            jnp.dot(mine_ref[...], my_weight_ref[:, low : low + width], preferred_element_type=jnp.float32)
+            + jnp.dot(theirs_ref[...], their_weight_ref[:, low : low + width], preferred_element_type=jnp.float32)
         ).astype(held_ref.dtype)
         copies.append(pltpu.make_async_copy(held_ref.at[group], out_ref.at[group], sems.at[group]))
         copies[-1].start()
@@ -318,9 +355,9 @@
         copy.wait()
 
 
-def project(own, stats, middle, out_weight):
-    rows, width = own.shape
-    groups = out_weight.shape[1] // width
+def project(mine, theirs, my_weight, their_weight):
+    rows, width = mine.shape
+    groups = my_weight.shape[1] // width
     whole = pl.BlockSpec(memory_space=VMEM)
     shape = (groups, rows, width)
     return pl.pallas_call(
@@ -330,9 +367,9 @@
         out_specs=pl.BlockSpec(memory_space=pl.ANY),
         scratch_shapes=[pltpu.VMEM(shape, jnp.bfloat16), pltpu.SemaphoreType.DMA((groups,))],
         compiler_params=params(24),
-        cost_estimate=pl.CostEstimate(flops=2 * groups * rows * width * width, bytes_accessed=5_000_000, transcendentals=0),
+        cost_estimate=pl.CostEstimate(flops=4 * groups * rows * width * width, bytes_accessed=5_000_000, transcendentals=0),
         name="project",
-    )(own, stats, middle, out_weight)
+    )(mine, theirs, my_weight, their_weight)
 
 
 def finish_kernel(terms_ref, residual_ref, gate_ref, out_ref):
@@ -357,28 +394,35 @@
     packed, block = pack(windows, queries, key_rows, value_rows)
     first, second = swap_times(block, False), swap_times(block, True)
     pair_asks, middle_asks = swap_pair(packed), swap_middle(packed)
-    mix, stats, held_weight = attend_own(packed, pair_asks, block, out_weight)
+    my_weight, to_send = split_weight(out_weight)
+    their_weight = swap_far(to_send)
+    mix, stats = attend_own(packed, pair_asks, block)
     for_pair = attend_pair(pair_asks, first, second, mix, stats)
     for_middle = attend_middle(middle_asks, block, first, second, for_pair)
     mix, stats = attend_last(packed, first, second, mix, stats, swap_pair(for_pair))
-    terms = project(mix, stats, swap_middle(for_middle), held_weight)
-    terms = lax.all_to_all(terms, "head", 0, 0)
+    attention = merge(mix, stats, swap_middle(for_middle))
+    terms = project(attention, swap_far(attention), my_weight, their_weight)
+    terms = lax.all_to_all(terms, "group", 0, 0)
     return finish(terms, residual, gate_scale)
 
 
 def solution(mesh):
+    devices = np.asarray(mesh.devices)
+    tiles, heads = devices.shape
+    split = jax.sharding.Mesh(devices.reshape(tiles, 2, heads // 2), ("tile", "far", "group"))
+    head = ("far", "group")
     return jax.shard_map(
         shards,
-        mesh=mesh,
+        mesh=split,
         in_specs=(
-            P("tile", "head"),
-            P("tile", "head"),
-            P("tile", "head"),
+            P("tile", head),
+            P("tile", head),
+            P("tile", head),
             P("tile", None),
-            P("tile", "head"),
-            P("head", None),
-            P("head"),
+            P("tile", head),
+            P(head, None),
+            P(head),
         ),
-        out_specs=P("tile", "head"),
+        out_specs=P("tile", head),
         check_vma=False,
     )

time: 70.7 us -> 72.7 us (1.028)
  starting transfers between devices: 26.4 us -> 34.8 us
  waiting for transfers between devices: 28.3 us -> 24.5 us
  local copies, waits for them, and re-layouts: 3.61 us -> 1.68 us
    ppermute x0 -> x2, starting transfers between devices: none -> 9.43 us  [swap_far(): return lax.ppermute(block, 'far', [(0, 1), (1, 0)])]
    all_to_all x1, waiting for transfers between devices: 17.2 us -> 11.1 us  [shards(): terms = lax.all_to_all(terms, 'group', 0, 0)]
    ppermute x0 -> x2, waiting for transfers between devices: none -> 4.84 us  [swap_far(): return lax.ppermute(block, 'far', [(0, 1), (1, 0)])]
    ppermute x2, waiting for transfers between devices: 7.99 us -> 5.11 us  [swap_times(): return lax.ppermute(block, 'tile', route)]
    unnamed x12 -> x10, local copies, waits for them, and re-layouts: 3.6 us -> 1.68 us
    all_to_all x1, starting transfers between devices: 5.29 us -> 4.43 us  [shards(): terms = lax.all_to_all(terms, 'group', 0, 0)]
  transfers between devices with their start and end apart: 7 -> 9, of which waited for: 3 -> 4; matrix products, arithmetic and copies ran while one was open for 0% -> 0% of each run, Pallas kernels for 9% -> 9%
where the time goes in v13:
time: 72.7 us; the launch traced here: 72.3 us
  starting transfers between devices  34.8 us (48%)
  waiting for transfers between devices  24.5 us (34%)
  Pallas kernels  11.1 us (15%)
  local copies, waits for them, and re-layouts  1.68 us (2%)
    all_to_all x1, waiting for transfers between devices, shards(): terms = lax.all_to_all(terms, 'group', 0, 0)  11.1 us
    ppermute x2, starting transfers between devices, swap_times(): return lax.ppermute(block, 'tile', route)  10.5 us
    ppermute x2, starting transfers between devices, swap_far(): return lax.ppermute(block, 'far', [(0, 1), (1, 0)])  9.43 us
    ppermute x2, starting transfers between devices, swap_pair(): lax.ppermute(block, 'tile', [(tile, tile ^ 1) for tile, *_ in places()])  6.35 us
    ppermute x2, waiting for transfers between devices, swap_times(): return lax.ppermute(block, 'tile', route)  5.11 us
    ppermute x2, waiting for transfers between devices, swap_far(): return lax.ppermute(block, 'far', [(0, 1), (1, 0)])  4.84 us
    all_to_all x1, starting transfers between devices, shards(): terms = lax.all_to_all(terms, 'group', 0, 0)  4.43 us
    ppermute x2, starting transfers between devices, swap_middle(): return lax.ppermute(block, 'tile', route)  4.12 us
  transfers between devices with their start and end apart: 9, of which 4 were waited for; matrix products, arithmetic and copies ran while one was open for 0% of the time, Pallas kernels for 9%

profile of v13, /device:TPU:1, one launch (start us, length us, event | category | flops | bytes accessed | tf_op | source)
XLA Modules:
  0.0 72.3 jit_solution(9629264890246848107)
XLA Ops:
  0.0 2.0 %pack.1 = (bf16[272,384]{1,0:T(8,128)(2,1)}, bf16[512,384]{1,0:T(8,128)(2,1)}) custom-call(s32[1,3]{1,0:T(1,128)} %windows_ref.1, bf16[256,384]{1,0:T(8,128)(2,1)} %q_ref.1, bf16[256,384]{1,0:T(8,128)(2,1)} %k_ref.1, bf16[256,384]{1,0:T(8,128)(2,1)} %v_ref.1), custom_call_target="tpu_custom_call" | custom-call | tf_op jit(solution)/shard_map/pack/pallas_call | solution.py:88
  2.0 0.7 collective-permute-start
  2.7 9.8 %collective-permute-start.1 = (bf16[512,384]{1,0:T(8,128)(2,1)}, bf16[512,384]{1,0:T(8,128)(2,1)S(1)}, u32[]{:S(2)}, u32[]{:S(2)}) collective-permute-start(bf16[512,384]{1,0:T(8,128)(2,1)} %get-tuple-element.14.block_ref.own_ref), channel_id=1, source_target_pairs={{0,32},{8,40},{16,48},{24,56},{32,0},{40,8},{48,16},{56,24},{64,96... | collective-permute-start | bytes 1179656 | tf_op jit(solution)/shard_map/ppermute | solution.py:37
  12.5 3.1 %collective-permute-start.2 = (bf16[272,384]{1,0:T(8,128)(2,1)}, bf16[272,384]{1,0:T(8,128)(2,1)S(1)}, u32[]{:S(2)}, u32[]{:S(2)}) collective-permute-start(bf16[272,384]{1,0:T(8,128)(2,1)} %get-tuple-element.13.query_ref), channel_id=1, source_target_pairs={{0,8},{8,0},{16,24},{24,16},{32,40},{40,32},{48,56},{56,48},{64,72... | collective-permute-start | bytes 626696 | tf_op jit(solution)/shard_map/ppermute | solution.py:41
  15.6 2.2 %collective-permute-start.4 = (bf16[272,384]{1,0:T(8,128)(2,1)}, bf16[272,384]{1,0:T(8,128)(2,1)S(1)}, u32[]{:S(2)}, u32[]{:S(2)}) collective-permute-start(bf16[272,384]{1,0:T(8,128)(2,1)} %get-tuple-element.13.query_ref), channel_id=1, source_target_pairs={{8,16},{16,8},{40,48},{48,40},{72,80},{80,72},{104,112},{112,104},... | collective-permute-start | bytes 626696 | tf_op jit(solution)/shard_map/ppermute | solution.py:46
  17.8 0.0 copy-start
  17.8 1.7 %copy-done = bf16[384,3072]{1,0:T(8,128)(2,1)S(1)} copy-done((bf16[384,3072]{1,0:T(8,128)(2,1)S(1)}, bf16[384,3072]{1,0:T(8,128)(2,1)}, u32[]{:S(2)}) %copy-start) | copy-done | bytes 2359320
  19.5 0.2 split_weight.1
  19.7 4.8 %collective-permute-start.7 = (bf16[384,1536]{1,0:T(8,128)(2,1)S(1)}, bf16[384,1536]{1,0:T(8,128)(2,1)S(1)}, u32[]{:S(2)}, u32[]{:S(2)}) collective-permute-start(bf16[384,1536]{1,0:T(8,128)(2,1)S(1)} %get-tuple-element.20), channel_id=1, source_target_pairs={{0,4},{4,0},{1,5},{5,1},{2,6},{6,2},{3,7},{7,3},{8,12},{12,8},{9,1... | collective-permute-start | bytes 3538952 | tf_op jit(solution)/shard_map/ppermute | solution.py:50
  24.5 0.0 collective-permute-done.2.pair_ref.query_ref
  24.5 0.0 copy-done.1
  24.5 1.0 %attend_own.1 = (f32[6,256,128]{2,1,0:T(8,128)S(1)}, f32[12,256,128]{2,1,0:T(8,128)S(1)}) custom-call(bf16[272,384]{1,0:T(8,128)(2,1)S(1)} %copy-done.2, bf16[272,384]{1,0:T(8,128)(2,1)S(1)} %collective-permute-done.2.pair_ref.query_ref, bf16[512,384]{1,0:T(8,128)(2,1)S(1)} %copy-done.1), custom_call_target="tpu_custom_call" | custom-call | tf_op jit(solution)/shard_map/attend_own/pallas_call | solution.py:198
  25.5 0.0 collective-permute-done.first_ref
  25.5 5.1 %collective-permute-done.1.second_ref = bf16[512,384]{1,0:T(8,128)(2,1)S(1)} collective-permute-done((bf16[512,384]{1,0:T(8,128)(2,1)}, bf16[512,384]{1,0:T(8,128)(2,1)S(1)}, u32[]{:S(2)}, u32[]{:S(2)}) %collective-permute-start.1) | collective-permute-done | bytes 393248 | tf_op jit(solution)/shard_map/ppermute | solution.py:37
  30.6 1.3 %attend_pair.1.after_ref = bf16[272,384]{1,0:T(8,128)(2,1)S(1)} custom-call(bf16[272,384]{1,0:T(8,128)(2,1)S(1)} %collective-permute-done.2.pair_ref.query_ref, bf16[512,384]{1,0:T(8,128)(2,1)S(1)} %collective-permute-done.first_ref, bf16[512,384]{1,0:T(8,128)(2,1)S(1)} %collective-permute-done.1.second_ref, ...), custom_call_target="tpu_custom_call" | custom-call | flops 400000000 | bytes 2000000 | tf_op jit(solution)/shard_map/attend_pair/pallas_call | solution.py:229
  31.9 3.2 %collective-permute-start.3 = (bf16[272,384]{1,0:T(8,128)(2,1)S(1)}, bf16[272,384]{1,0:T(8,128)(2,1)S(1)}, u32[]{:S(2)}, u32[]{:S(2)}) collective-permute-start(bf16[272,384]{1,0:T(8,128)(2,1)S(1)} %attend_pair.1.after_ref), channel_id=1, source_target_pairs={{0,8},{8,0},{16,24},{24,16},{32,40},{40,32},{48,56},{56,48},{64,72... | collective-permute-start | bytes 626696 | tf_op jit(solution)/shard_map/ppermute | solution.py:41
  35.1 0.0 collective-permute-done.4.query_ref
  35.1 1.5 %attend_middle.1 = bf16[272,384]{1,0:T(8,128)(2,1)S(1)} custom-call(bf16[272,384]{1,0:T(8,128)(2,1)S(1)} %collective-permute-done.4.query_ref, bf16[512,384]{1,0:T(8,128)(2,1)S(1)} %copy-done.1, bf16[512,384]{1,0:T(8,128)(2,1)S(1)} %collective-permute-done.first_ref, bf16[512,384]{1,0:T(8,128)(2,1)S(1)} %collective-permute-done.1.second_ref, ...), custom_call_target="tpu_custom_call" | custom-call | flops 600000000 | bytes 2000000 | tf_op jit(solution)/shard_map/attend_middle/pallas_call | solution.py:261
  36.6 1.9 %collective-permute-start.5 = (bf16[272,384]{1,0:T(8,128)(2,1)S(1)}, bf16[272,384]{1,0:T(8,128)(2,1)S(1)}, u32[]{:S(2)}, u32[]{:S(2)}) collective-permute-start(bf16[272,384]{1,0:T(8,128)(2,1)S(1)} %attend_middle.1), channel_id=1, source_target_pairs={{8,16},{16,8},{40,48},{48,40},{72,80},{80,72},{104,112},{112,104},... | collective-permute-start | bytes 626696 | tf_op jit(solution)/shard_map/ppermute | solution.py:46
  38.6 0.0 collective-permute-done.3.message_ref
  38.6 2.0 %attend_last.1 = (f32[256,384]{1,0:T(8,128)S(1)}, f32[3,8,256]{2,1,0:T(8,128)S(1)}) custom-call(bf16[272,384]{1,0:T(8,128)(2,1)S(1)} %copy-done.2, bf16[512,384]{1,0:T(8,128)(2,1)S(1)} %collective-permute-done.first_ref, bf16[512,384]{1,0:T(8,128)(2,1)S(1)} %collective-permute-done.1.second_ref, f32[6,256,128]{2,1,0:T(8,128)S(1)} %get-tuple-element.15.mix_ref.old_mix_ref, ...), custom_call_target="tpu_custom_call" | custom-call | flops 8000000000 | bytes 2000000 | tf_op jit(solution)/shard_map/attend_last/pallas_call | solution.py:292
  40.6 3.4 %collective-permute-done.5.middle_ref = bf16[272,384]{1,0:T(8,128)(2,1)S(1)} collective-permute-done((bf16[272,384]{1,0:T(8,128)(2,1)S(1)}, bf16[272,384]{1,0:T(8,128)(2,1)S(1)}, u32[]{:S(2)}, u32[]{:S(2)}) %collective-permute-start.5) | collective-permute-done | bytes 208928 | tf_op jit(solution)/shard_map/ppermute | solution.py:46
  44.1 0.5 merge.1.mine_ref
  44.6 4.6 %collective-permute-start.6 = (bf16[256,384]{1,0:T(8,128)(2,1)S(1)}, bf16[256,384]{1,0:T(8,128)(2,1)S(1)}, u32[]{:S(2)}, u32[]{:S(2)}) collective-permute-start(bf16[256,384]{1,0:T(8,128)(2,1)S(1)} %merge.1.mine_ref), channel_id=1, source_target_pairs={{0,4},{4,0},{1,5},{5,1},{2,6},{6,2},{3,7},{7,3},{8,12},{12,8},{9,1... | collective-permute-start | bytes 589832 | tf_op jit(solution)/shard_map/ppermute | solution.py:50
  49.2 4.8 %collective-permute-done.6.theirs_ref = bf16[256,384]{1,0:T(8,128)(2,1)S(1)} collective-permute-done((bf16[256,384]{1,0:T(8,128)(2,1)S(1)}, bf16[256,384]{1,0:T(8,128)(2,1)S(1)}, u32[]{:S(2)}, u32[]{:S(2)}) %collective-permute-start.6) | collective-permute-done | bytes 196640 | tf_op jit(solution)/shard_map/ppermute | solution.py:50
  54.0 0.0 collective-permute-done.7.their_weight_ref
  54.0 1.9 %project.1 = bf16[4,256,384]{2,1,0:T(8,128)(2,1)} custom-call(bf16[256,384]{1,0:T(8,128)(2,1)S(1)} %merge.1.mine_ref, bf16[256,384]{1,0:T(8,128)(2,1)S(1)} %collective-permute-done.6.theirs_ref, bf16[384,1536]{1,0:T(8,128)(2,1)S(1)} %get-tuple-element.19.my_weight_ref, bf16[384,1536]{1,0:T(8,128)(2,1)S(1)} %collective-permute-done.7.their_weight_ref), custom_call_target="tpu_custom_call" | custom-call | flops 603979776 | bytes 5000000 | tf_op jit(solution)/shard_map/project/pallas_call | solution.py:363
  55.9 0.0 copy-start.4
  55.9 0.0 copy-start.3
  55.9 4.4 %all-to-all-start = ((bf16[4,256,384]{2,1,0:T(8,128)(2,1)}), bf16[4,256,384]{2,1,0:T(8,128)(2,1)S(1)}, u32[]{:S(2)}, u32[]{:S(2)}) async-start(bf16[4,256,384]{2,1,0:T(8,128)(2,1)} %project.1), calls=%async_computation | async-start | bytes 1572864 | tf_op jit(solution)/shard_map/all_to_all | solution.py:405
  60.4 11.1 %all-to-all-done.terms_ref = bf16[4,256,384]{2,1,0:T(8,128)(2,1)S(1)} async-done(((bf16[4,256,384]{2,1,0:T(8,128)(2,1)}), bf16[4,256,384]{2,1,0:T(8,128)(2,1)S(1)}, u32[]{:S(2)}, u32[]{:S(2)}) %all-to-all-start) | async-done | bytes 786464 | tf_op jit(solution)/shard_map/all_to_all | solution.py:405
  71.5 0.8 %finish.1 = bf16[256,384]{1,0:T(8,128)(2,1)} custom-call(bf16[4,256,384]{2,1,0:T(8,128)(2,1)S(1)} %all-to-all-done.terms_ref, bf16[256,384]{1,0:T(8,128)(2,1)S(1)} %copy-done.3, f32[1,384]{1,0:T(1,128)S(1)} %reshape.3.gate_ref), custom_call_target="tpu_custom_call" | custom-call | flops 3932160 | bytes 2000000 | tf_op jit(solution)/shard_map/finish/pallas_call | solution.py:382
  (6 shorter events, 0.0 us)
Async XLA Ops:
  2.0 23.5 %collective-permute-start = (bf16[512,384]{1,0:T(8,128)(2,1)}, bf16[512,384]{1,0:T(8,128)(2,1)S(1)}, u32[]{:S(2)}, u32[]{:S(2)}) collective-permute-start(bf16[512,384]{1,0:T(8,128)(2,1)} %get-tuple-element.14.block_ref.own_ref), channel_id=1, source_target_pairs={{32,64},{40,72},{48,80},{56,88},{64,32},{72,40},{80,48},{88,56},{9... | collective-permute-start | bytes 1179656 | tf_op jit(solution)/shard_map/ppermute | solution.py:37
  2.7 27.9 %collective-permute-start.1 = (bf16[512,384]{1,0:T(8,128)(2,1)}, bf16[512,384]{1,0:T(8,128)(2,1)S(1)}, u32[]{:S(2)}, u32[]{:S(2)}) collective-permute-start(bf16[512,384]{1,0:T(8,128)(2,1)} %get-tuple-element.14.block_ref.own_ref), channel_id=1, source_target_pairs={{0,32},{8,40},{16,48},{24,56},{32,0},{40,8},{48,16},{56,24},{64,96... | collective-permute-start | bytes 1179656 | tf_op jit(solution)/shard_map/ppermute | solution.py:37
  12.5 12.0 %collective-permute-start.2 = (bf16[272,384]{1,0:T(8,128)(2,1)}, bf16[272,384]{1,0:T(8,128)(2,1)S(1)}, u32[]{:S(2)}, u32[]{:S(2)}) collective-permute-start(bf16[272,384]{1,0:T(8,128)(2,1)} %get-tuple-element.13.query_ref), channel_id=1, source_target_pairs={{0,8},{8,0},{16,24},{24,16},{32,40},{40,32},{48,56},{56,48},{64,72... | collective-permute-start | bytes 626696 | tf_op jit(solution)/shard_map/ppermute | solution.py:41
  15.6 19.5 %collective-permute-start.4 = (bf16[272,384]{1,0:T(8,128)(2,1)}, bf16[272,384]{1,0:T(8,128)(2,1)S(1)}, u32[]{:S(2)}, u32[]{:S(2)}) collective-permute-start(bf16[272,384]{1,0:T(8,128)(2,1)} %get-tuple-element.13.query_ref), channel_id=1, source_target_pairs={{8,16},{16,8},{40,48},{48,40},{72,80},{80,72},{104,112},{112,104},... | collective-permute-start | bytes 626696 | tf_op jit(solution)/shard_map/ppermute | solution.py:46
  17.8 1.7 %copy-start = (bf16[384,3072]{1,0:T(8,128)(2,1)S(1)}, bf16[384,3072]{1,0:T(8,128)(2,1)}, u32[]{:S(2)}) copy-start(bf16[384,3072]{1,0:T(8,128)(2,1)} %weight_ref.1) | copy-start | bytes 7077892
  19.5 5.0 %copy-start.1 = (bf16[512,384]{1,0:T(8,128)(2,1)S(1)}, bf16[512,384]{1,0:T(8,128)(2,1)}, u32[]{:S(2)}) copy-start(bf16[512,384]{1,0:T(8,128)(2,1)} %get-tuple-element.14.block_ref.own_ref) | copy-start | bytes 1179652
  19.5 5.0 %copy-start.2 = (bf16[272,384]{1,0:T(8,128)(2,1)S(1)}, bf16[272,384]{1,0:T(8,128)(2,1)}, u32[]{:S(2)}) copy-start(bf16[272,384]{1,0:T(8,128)(2,1)} %get-tuple-element.13.query_ref) | copy-start | bytes 626692
  19.7 34.4 %collective-permute-start.7 = (bf16[384,1536]{1,0:T(8,128)(2,1)S(1)}, bf16[384,1536]{1,0:T(8,128)(2,1)S(1)}, u32[]{:S(2)}, u32[]{:S(2)}) collective-permute-start(bf16[384,1536]{1,0:T(8,128)(2,1)S(1)} %get-tuple-element.20), channel_id=1, source_target_pairs={{0,4},{4,0},{1,5},{5,1},{2,6},{6,2},{3,7},{7,3},{8,12},{12,8},{9,1... | collective-permute-start | bytes 3538952 | tf_op jit(solution)/shard_map/ppermute | solution.py:50
  31.9 6.7 %collective-permute-start.3 = (bf16[272,384]{1,0:T(8,128)(2,1)S(1)}, bf16[272,384]{1,0:T(8,128)(2,1)S(1)}, u32[]{:S(2)}, u32[]{:S(2)}) collective-permute-start(bf16[272,384]{1,0:T(8,128)(2,1)S(1)} %attend_pair.1.after_ref), channel_id=1, source_target_pairs={{0,8},{8,0},{16,24},{24,16},{32,40},{40,32},{48,56},{56,48},{64,72... | collective-permute-start | bytes 626696 | tf_op jit(solution)/shard_map/ppermute | solution.py:41
  36.6 7.4 %collective-permute-start.5 = (bf16[272,384]{1,0:T(8,128)(2,1)S(1)}, bf16[272,384]{1,0:T(8,128)(2,1)S(1)}, u32[]{:S(2)}, u32[]{:S(2)}) collective-permute-start(bf16[272,384]{1,0:T(8,128)(2,1)S(1)} %attend_middle.1), channel_id=1, source_target_pairs={{8,16},{16,8},{40,48},{48,40},{72,80},{80,72},{104,112},{112,104},... | collective-permute-start | bytes 626696 | tf_op jit(solution)/shard_map/ppermute | solution.py:46
  44.6 9.5 %collective-permute-start.6 = (bf16[256,384]{1,0:T(8,128)(2,1)S(1)}, bf16[256,384]{1,0:T(8,128)(2,1)S(1)}, u32[]{:S(2)}, u32[]{:S(2)}) collective-permute-start(bf16[256,384]{1,0:T(8,128)(2,1)S(1)} %merge.1.mine_ref), channel_id=1, source_target_pairs={{0,4},{4,0},{1,5},{5,1},{2,6},{6,2},{3,7},{7,3},{8,12},{12,8},{9,1... | collective-permute-start | bytes 589832 | tf_op jit(solution)/shard_map/ppermute | solution.py:50
  55.9 4.5 %copy-start.4 = (f32[384]{0:T(512)S(1)}, f32[384]{0:T(512)}, u32[]{:S(2)}) copy-start(f32[384]{0:T(512)} %param.13) | copy-start | bytes 4612
  55.9 15.6 %copy-start.3 = (bf16[256,384]{1,0:T(8,128)(2,1)S(1)}, bf16[256,384]{1,0:T(8,128)(2,1)}, u32[]{:S(2)}) copy-start(bf16[256,384]{1,0:T(8,128)(2,1)} %residual_ref.1) | copy-start | bytes 589828
  55.9 15.5 %all-to-all-start = ((bf16[4,256,384]{2,1,0:T(8,128)(2,1)}), bf16[4,256,384]{2,1,0:T(8,128)(2,1)S(1)}, u32[]{:S(2)}, u32[]{:S(2)}) async-start(bf16[4,256,384]{2,1,0:T(8,128)(2,1)} %project.1), calls=%async_computation | async-start | bytes 1572864 | tf_op jit(solution)/shard_map/all_to_all | solution.py:405

commit v14 on v13

--- a/solution.py
+++ b/solution.py
@@ -13,7 +13,7 @@
 SIDE = 16
 LOG2E = 1.4426950408889634
 MASKED = -1e30
-LAST_FLOPS = 8_000_000_000
+LAST_FLOPS = 6_000_000_000
 MESH_AXES = ("tile", "head")
 VMEM = pltpu.VMEM
 SMEM = pltpu.SMEM
@@ -51,10 +51,11 @@
 
 
 def split_weight_kernel(weight_ref, mine_ref, theirs_ref):
-    width = mine_ref.shape[1]
+    width, half = mine_ref.shape[1], theirs_ref.shape[1]
     far = lax.axis_index("far")
+    core = lax.rem(lax.axis_index("tile"), 2)
     mine_ref[...] = weight_ref[:, pl.ds(pl.multiple_of(far * width, HD), width)]
-    theirs_ref[...] = weight_ref[:, pl.ds(pl.multiple_of((1 - far) * width, HD), width)]
+    theirs_ref[...] = weight_ref[:, pl.ds(pl.multiple_of((1 - far) * width + core * half, HD), half)]
 
 
 def split_weight(out_weight):
@@ -62,7 +63,10 @@
     whole = pl.BlockSpec(memory_space=VMEM)
     return pl.pallas_call(
         split_weight_kernel,
-        out_shape=(jax.ShapeDtypeStruct((rows, features // 2), out_weight.dtype),) * 2,
+        out_shape=(
+            jax.ShapeDtypeStruct((rows, features // 2), out_weight.dtype),
+            jax.ShapeDtypeStruct((rows, features // 4), out_weight.dtype),
+        ),
         in_specs=[whole],
         out_specs=(whole,) * 2,
         compiler_params=params(24),
@@ -340,14 +344,17 @@
     )(own, stats, middle)
 
 
-def project_kernel(mine_ref, theirs_ref, my_weight_ref, their_weight_ref, out_ref, held_ref, sems):
-    width = mine_ref.shape[1]
+def project_kernel(mine_ref, theirs_ref, my_weight_ref, this_ref, other_ref, out_ref, held_ref, sems):
+    width, half = mine_ref.shape[1], this_ref.shape[1]
+    core = lax.rem(lax.axis_index("tile"), 2)
     copies = []
     for group in range(out_ref.shape[0]):
         low = group * width
+        side, start = divmod(low, half)
+        their_weight = jnp.where(side == core, this_ref[:, start : start + width], other_ref[:, start : start + width])
         held_ref[group] = (
             jnp.dot(mine_ref[...], my_weight_ref[:, low : low + width], preferred_element_type=jnp.float32)
-            + jnp.dot(theirs_ref[...], their_weight_ref[:, low : low + width], preferred_element_type=jnp.float32)
+            + jnp.dot(theirs_ref[...], their_weight, preferred_element_type=jnp.float32)
         ).astype(held_ref.dtype)
         copies.append(pltpu.make_async_copy(held_ref.at[group], out_ref.at[group], sems.at[group]))
         copies[-1].start()
@@ -355,7 +362,7 @@
         copy.wait()
 
 
-def project(mine, theirs, my_weight, their_weight):
+def project(mine, theirs, my_weight, this_half, other_half):
     rows, width = mine.shape
     groups = my_weight.shape[1] // width
     whole = pl.BlockSpec(memory_space=VMEM)
@@ -363,13 +370,13 @@
     return pl.pallas_call(
         project_kernel,
         out_shape=jax.ShapeDtypeStruct(shape, jnp.bfloat16),
-        in_specs=[whole] * 4,
+        in_specs=[whole] * 5,
         out_specs=pl.BlockSpec(memory_space=pl.ANY),
         scratch_shapes=[pltpu.VMEM(shape, jnp.bfloat16), pltpu.SemaphoreType.DMA((groups,))],
         compiler_params=params(24),
         cost_estimate=pl.CostEstimate(flops=4 * groups * rows * width * width, bytes_accessed=5_000_000, transcendentals=0),
         name="project",
-    )(mine, theirs, my_weight, their_weight)
+    )(mine, theirs, my_weight, this_half, other_half)
 
 
 def finish_kernel(terms_ref, residual_ref, gate_ref, out_ref):
@@ -395,13 +402,13 @@
     first, second = swap_times(block, False), swap_times(block, True)
     pair_asks, middle_asks = swap_pair(packed), swap_middle(packed)
     my_weight, to_send = split_weight(out_weight)
-    their_weight = swap_far(to_send)
+    this_half = swap_far(to_send)
     mix, stats = attend_own(packed, pair_asks, block)
     for_pair = attend_pair(pair_asks, first, second, mix, stats)
     for_middle = attend_middle(middle_asks, block, first, second, for_pair)
     mix, stats = attend_last(packed, first, second, mix, stats, swap_pair(for_pair))
     attention = merge(mix, stats, swap_middle(for_middle))
-    terms = project(attention, swap_far(attention), my_weight, their_weight)
+    terms = project(attention, swap_far(attention), my_weight, this_half, swap_pair(this_half))
     terms = lax.all_to_all(terms, "group", 0, 0)
     return finish(terms, residual, gate_scale)
 

time: 72.7 us -> 73.1 us (level)
  the two profiles are of different devices: /device:TPU:1 before, /device:TPU:184 now
where the time goes in v14:
time: 73.1 us; the launch traced here: 72.7 us
  starting transfers between devices  35.4 us (48%)
  waiting for transfers between devices  24.3 us (33%)
  Pallas kernels  11.1 us (15%)
  local copies, waits for them, and re-layouts  1.68 us (2%)
    all_to_all x1, waiting for transfers between devices, shards(): terms = lax.all_to_all(terms, 'group', 0, 0)  10.7 us
    ppermute x2, starting transfers between devices, swap_far(): return lax.ppermute(block, 'far', [(0, 1), (1, 0)])  9.99 us
    ppermute x2, starting transfers between devices, swap_times(): return lax.ppermute(block, 'tile', route)  9.42 us
    ppermute x2, waiting for transfers between devices, swap_times(): return lax.ppermute(block, 'tile', route)  7.79 us
    ppermute x2, starting transfers between devices, swap_middle(): return lax.ppermute(block, 'tile', route)  6.04 us
    ppermute x2, waiting for transfers between devices, swap_far(): return lax.ppermute(block, 'far', [(0, 1), (1, 0)])  5.76 us
    ppermute x3, starting transfers between devices, swap_pair(): lax.ppermute(block, 'tile', [(tile, tile ^ 1) for tile, *_ in places()])  5.76 us
    all_to_all x1, starting transfers between devices, shards(): terms = lax.all_to_all(terms, 'group', 0, 0)  4.21 us
  transfers between devices with their start and end apart: 10, of which 4 were waited for; matrix products, arithmetic and copies ran while one was open for 0% of the time, Pallas kernels for 9%

profile of v14, /device:TPU:184, one launch (start us, length us, event | category | flops | bytes accessed | tf_op | source)
XLA Modules:
  0.0 72.7 jit_solution(4278079397501443967)
XLA Ops:
  0.0 2.0 %pack.1 = (bf16[272,384]{1,0:T(8,128)(2,1)}, bf16[512,384]{1,0:T(8,128)(2,1)}) custom-call(s32[1,3]{1,0:T(1,128)} %windows_ref.1, bf16[256,384]{1,0:T(8,128)(2,1)} %q_ref.1, bf16[256,384]{1,0:T(8,128)(2,1)} %k_ref.1, bf16[256,384]{1,0:T(8,128)(2,1)} %v_ref.1), custom_call_target="tpu_custom_call" | custom-call | tf_op jit(solution)/shard_map/pack/pallas_call | solution.py:92
  2.0 7.5 %collective-permute-start = (bf16[512,384]{1,0:T(8,128)(2,1)}, bf16[512,384]{1,0:T(8,128)(2,1)S(1)}, u32[]{:S(2)}, u32[]{:S(2)}) collective-permute-start(bf16[512,384]{1,0:T(8,128)(2,1)} %get-tuple-element.14.block_ref.own_ref), channel_id=1, source_target_pairs={{32,64},{40,72},{48,80},{56,88},{64,32},{72,40},{80,48},{88,56},{9... | collective-permute-start | bytes 1179656 | tf_op jit(solution)/shard_map/ppermute | solution.py:37
  9.5 1.9 %collective-permute-start.1 = (bf16[512,384]{1,0:T(8,128)(2,1)}, bf16[512,384]{1,0:T(8,128)(2,1)S(1)}, u32[]{:S(2)}, u32[]{:S(2)}) collective-permute-start(bf16[512,384]{1,0:T(8,128)(2,1)} %get-tuple-element.14.block_ref.own_ref), channel_id=1, source_target_pairs={{0,32},{8,40},{16,48},{24,56},{32,0},{40,8},{48,16},{56,24},{64,96... | collective-permute-start | bytes 1179656 | tf_op jit(solution)/shard_map/ppermute | solution.py:37
  11.4 0.0 copy-start
  11.4 1.7 %copy-done = bf16[384,3072]{1,0:T(8,128)(2,1)S(1)} copy-done((bf16[384,3072]{1,0:T(8,128)(2,1)S(1)}, bf16[384,3072]{1,0:T(8,128)(2,1)}, u32[]{:S(2)}) %copy-start) | copy-done | bytes 2359320
  13.1 0.1 split_weight.1
  13.2 5.1 %collective-permute-start.7 = (bf16[384,768]{1,0:T(8,128)(2,1)S(1)}, bf16[384,768]{1,0:T(8,128)(2,1)S(1)}, u32[]{:S(2)}, u32[]{:S(2)}) collective-permute-start(bf16[384,768]{1,0:T(8,128)(2,1)S(1)} %get-tuple-element.20), channel_id=1, source_target_pairs={{0,4},{4,0},{1,5},{5,1},{2,6},{6,2},{3,7},{7,3},{8,12},{12,8},{9,1... | collective-permute-start | bytes 1769480 | tf_op jit(solution)/shard_map/ppermute | solution.py:50
  18.3 1.9 %collective-permute-start.2 = (bf16[272,384]{1,0:T(8,128)(2,1)S(1)}, bf16[272,384]{1,0:T(8,128)(2,1)S(1)}, u32[]{:S(2)}, u32[]{:S(2)}) collective-permute-start(bf16[272,384]{1,0:T(8,128)(2,1)S(1)} %copy-done.2), channel_id=1, source_target_pairs={{0,8},{8,0},{16,24},{24,16},{32,40},{40,32},{48,56},{56,48},{64,72... | collective-permute-start | bytes 626696 | tf_op jit(solution)/shard_map/ppermute | solution.py:41
  20.2 2.5 %collective-permute-start.4 = (bf16[272,384]{1,0:T(8,128)(2,1)S(1)}, bf16[272,384]{1,0:T(8,128)(2,1)S(1)}, u32[]{:S(2)}, u32[]{:S(2)}) collective-permute-start(bf16[272,384]{1,0:T(8,128)(2,1)S(1)} %copy-done.2), channel_id=1, source_target_pairs={{8,16},{16,8},{40,48},{48,40},{72,80},{80,72},{104,112},{112,104},... | collective-permute-start | bytes 626696 | tf_op jit(solution)/shard_map/ppermute | solution.py:46
  22.7 0.0 collective-permute-done.2.pair_ref.query_ref
  22.7 1.0 %attend_own.1 = (f32[6,256,128]{2,1,0:T(8,128)S(1)}, f32[12,256,128]{2,1,0:T(8,128)S(1)}) custom-call(bf16[272,384]{1,0:T(8,128)(2,1)S(1)} %copy-done.2, bf16[272,384]{1,0:T(8,128)(2,1)S(1)} %collective-permute-done.2.pair_ref.query_ref, bf16[512,384]{1,0:T(8,128)(2,1)S(1)} %copy-done.1), custom_call_target="tpu_custom_call" | custom-call | tf_op jit(solution)/shard_map/attend_own/pallas_call | solution.py:202
  23.7 2.9 %collective-permute-done.first_ref = bf16[512,384]{1,0:T(8,128)(2,1)S(1)} collective-permute-done((bf16[512,384]{1,0:T(8,128)(2,1)}, bf16[512,384]{1,0:T(8,128)(2,1)S(1)}, u32[]{:S(2)}, u32[]{:S(2)}) %collective-permute-start) | collective-permute-done | bytes 393248 | tf_op jit(solution)/shard_map/ppermute | solution.py:37
  26.6 4.9 %collective-permute-done.1.second_ref = bf16[512,384]{1,0:T(8,128)(2,1)S(1)} collective-permute-done((bf16[512,384]{1,0:T(8,128)(2,1)}, bf16[512,384]{1,0:T(8,128)(2,1)S(1)}, u32[]{:S(2)}, u32[]{:S(2)}) %collective-permute-start.1) | collective-permute-done | bytes 393248 | tf_op jit(solution)/shard_map/ppermute | solution.py:37
  31.5 1.3 %attend_pair.1.after_ref = bf16[272,384]{1,0:T(8,128)(2,1)S(1)} custom-call(bf16[272,384]{1,0:T(8,128)(2,1)S(1)} %collective-permute-done.2.pair_ref.query_ref, bf16[512,384]{1,0:T(8,128)(2,1)S(1)} %collective-permute-done.first_ref, bf16[512,384]{1,0:T(8,128)(2,1)S(1)} %collective-permute-done.1.second_ref, ...), custom_call_target="tpu_custom_call" | custom-call | flops 400000000 | bytes 2000000 | tf_op jit(solution)/shard_map/attend_pair/pallas_call | solution.py:233
  32.8 1.9 %collective-permute-start.3 = (bf16[272,384]{1,0:T(8,128)(2,1)S(1)}, bf16[272,384]{1,0:T(8,128)(2,1)S(1)}, u32[]{:S(2)}, u32[]{:S(2)}) collective-permute-start(bf16[272,384]{1,0:T(8,128)(2,1)S(1)} %attend_pair.1.after_ref), channel_id=1, source_target_pairs={{0,8},{8,0},{16,24},{24,16},{32,40},{40,32},{48,56},{56,48},{64,72... | collective-permute-start | bytes 626696 | tf_op jit(solution)/shard_map/ppermute | solution.py:41
  34.7 0.0 collective-permute-done.4.query_ref
  34.7 1.5 %attend_middle.1 = bf16[272,384]{1,0:T(8,128)(2,1)S(1)} custom-call(bf16[272,384]{1,0:T(8,128)(2,1)S(1)} %collective-permute-done.4.query_ref, bf16[512,384]{1,0:T(8,128)(2,1)S(1)} %copy-done.1, bf16[512,384]{1,0:T(8,128)(2,1)S(1)} %collective-permute-done.first_ref, bf16[512,384]{1,0:T(8,128)(2,1)S(1)} %collective-permute-done.1.second_ref, ...), custom_call_target="tpu_custom_call" | custom-call | flops 600000000 | bytes 2000000 | tf_op jit(solution)/shard_map/attend_middle/pallas_call | solution.py:265
  36.3 3.6 %collective-permute-start.5 = (bf16[272,384]{1,0:T(8,128)(2,1)S(1)}, bf16[272,384]{1,0:T(8,128)(2,1)S(1)}, u32[]{:S(2)}, u32[]{:S(2)}) collective-permute-start(bf16[272,384]{1,0:T(8,128)(2,1)S(1)} %attend_middle.1), channel_id=1, source_target_pairs={{8,16},{16,8},{40,48},{48,40},{72,80},{80,72},{104,112},{112,104},... | collective-permute-start | bytes 626696 | tf_op jit(solution)/shard_map/ppermute | solution.py:46
  39.8 0.0 collective-permute-done.7.this_ref
  39.9 1.9 %collective-permute-start.8 = (bf16[384,768]{1,0:T(8,128)(2,1)S(1)}, bf16[384,768]{1,0:T(8,128)(2,1)S(1)}, u32[]{:S(2)}, u32[]{:S(2)}) collective-permute-start(bf16[384,768]{1,0:T(8,128)(2,1)S(1)} %collective-permute-done.7.this_ref), channel_id=1, source_target_pairs={{0,8},{8,0},{16,24},{24,16},{32,40},{40,32},{48,56},{56,48},{64,72... | collective-permute-start | bytes 1769480 | tf_op jit(solution)/shard_map/ppermute | solution.py:41
  41.8 0.0 collective-permute-done.3.message_ref
  41.8 2.0 %attend_last.1 = (f32[256,384]{1,0:T(8,128)S(1)}, f32[3,8,256]{2,1,0:T(8,128)S(1)}) custom-call(bf16[272,384]{1,0:T(8,128)(2,1)S(1)} %copy-done.2, bf16[512,384]{1,0:T(8,128)(2,1)S(1)} %collective-permute-done.first_ref, bf16[512,384]{1,0:T(8,128)(2,1)S(1)} %collective-permute-done.1.second_ref, f32[6,256,128]{2,1,0:T(8,128)S(1)} %get-tuple-element.15.mix_ref.old_mix_ref, ...), custom_call_target="tpu_custom_call" | custom-call | flops 6000000000 | bytes 2000000 | tf_op jit(solution)/shard_map/attend_last/pallas_call | solution.py:296
  43.8 0.5 merge.1.mine_ref
  44.3 4.9 %collective-permute-start.6 = (bf16[256,384]{1,0:T(8,128)(2,1)S(1)}, bf16[256,384]{1,0:T(8,128)(2,1)S(1)}, u32[]{:S(2)}, u32[]{:S(2)}) collective-permute-start(bf16[256,384]{1,0:T(8,128)(2,1)S(1)} %merge.1.mine_ref), channel_id=1, source_target_pairs={{0,4},{4,0},{1,5},{5,1},{2,6},{6,2},{3,7},{7,3},{8,12},{12,8},{9,1... | collective-permute-start | bytes 589832 | tf_op jit(solution)/shard_map/ppermute | solution.py:50
  49.3 5.8 %collective-permute-done.6.theirs_ref = bf16[256,384]{1,0:T(8,128)(2,1)S(1)} collective-permute-done((bf16[256,384]{1,0:T(8,128)(2,1)S(1)}, bf16[256,384]{1,0:T(8,128)(2,1)S(1)}, u32[]{:S(2)}, u32[]{:S(2)}) %collective-permute-start.6) | collective-permute-done | bytes 196640 | tf_op jit(solution)/shard_map/ppermute | solution.py:50
  55.0 0.0 collective-permute-done.8.other_ref
  55.0 1.9 %project.1 = bf16[4,256,384]{2,1,0:T(8,128)(2,1)} custom-call(bf16[256,384]{1,0:T(8,128)(2,1)S(1)} %merge.1.mine_ref, bf16[256,384]{1,0:T(8,128)(2,1)S(1)} %collective-permute-done.6.theirs_ref, bf16[384,1536]{1,0:T(8,128)(2,1)S(1)} %get-tuple-element.19.my_weight_ref, bf16[384,768]{1,0:T(8,128)(2,1)S(1)} %collective-permute-done.7.this_ref, ...), custom_call_target="tpu_custom_call" | custom-call | flops 603979776 | bytes 5000000 | tf_op jit(solution)/shard_map/project/pallas_call | solution.py:370
  56.9 0.0 copy-start.4
  56.9 0.0 copy-start.3
  56.9 4.2 %all-to-all-start = ((bf16[4,256,384]{2,1,0:T(8,128)(2,1)}), bf16[4,256,384]{2,1,0:T(8,128)(2,1)S(1)}, u32[]{:S(2)}, u32[]{:S(2)}) async-start(bf16[4,256,384]{2,1,0:T(8,128)(2,1)} %project.1), calls=%async_computation | async-start | bytes 1572864 | tf_op jit(solution)/shard_map/all_to_all | solution.py:412
  61.2 10.7 %all-to-all-done.terms_ref = bf16[4,256,384]{2,1,0:T(8,128)(2,1)S(1)} async-done(((bf16[4,256,384]{2,1,0:T(8,128)(2,1)}), bf16[4,256,384]{2,1,0:T(8,128)(2,1)S(1)}, u32[]{:S(2)}, u32[]{:S(2)}) %all-to-all-start) | async-done | bytes 786464 | tf_op jit(solution)/shard_map/all_to_all | solution.py:412
  71.9 0.8 %finish.1 = bf16[256,384]{1,0:T(8,128)(2,1)} custom-call(bf16[4,256,384]{2,1,0:T(8,128)(2,1)S(1)} %all-to-all-done.terms_ref, bf16[256,384]{1,0:T(8,128)(2,1)S(1)} %copy-done.3, f32[1,384]{1,0:T(1,128)S(1)} %reshape.3.gate_ref), custom_call_target="tpu_custom_call" | custom-call | flops 3932160 | bytes 2000000 | tf_op jit(solution)/shard_map/finish/pallas_call | solution.py:389
  (8 shorter events, 0.0 us)
Async XLA Ops:
  2.0 24.6 %collective-permute-start = (bf16[512,384]{1,0:T(8,128)(2,1)}, bf16[512,384]{1,0:T(8,128)(2,1)S(1)}, u32[]{:S(2)}, u32[]{:S(2)}) collective-permute-start(bf16[512,384]{1,0:T(8,128)(2,1)} %get-tuple-element.14.block_ref.own_ref), channel_id=1, source_target_pairs={{32,64},{40,72},{48,80},{56,88},{64,32},{72,40},{80,48},{88,56},{9... | collective-permute-start | bytes 1179656 | tf_op jit(solution)/shard_map/ppermute | solution.py:37
  9.5 22.0 %collective-permute-start.1 = (bf16[512,384]{1,0:T(8,128)(2,1)}, bf16[512,384]{1,0:T(8,128)(2,1)S(1)}, u32[]{:S(2)}, u32[]{:S(2)}) collective-permute-start(bf16[512,384]{1,0:T(8,128)(2,1)} %get-tuple-element.14.block_ref.own_ref), channel_id=1, source_target_pairs={{0,32},{8,40},{16,48},{24,56},{32,0},{40,8},{48,16},{56,24},{64,96... | collective-permute-start | bytes 1179656 | tf_op jit(solution)/shard_map/ppermute | solution.py:37
  11.4 1.7 %copy-start = (bf16[384,3072]{1,0:T(8,128)(2,1)S(1)}, bf16[384,3072]{1,0:T(8,128)(2,1)}, u32[]{:S(2)}) copy-start(bf16[384,3072]{1,0:T(8,128)(2,1)} %weight_ref.1) | copy-start | bytes 7077892
  13.1 5.2 %copy-start.2 = (bf16[272,384]{1,0:T(8,128)(2,1)S(1)}, bf16[272,384]{1,0:T(8,128)(2,1)}, u32[]{:S(2)}) copy-start(bf16[272,384]{1,0:T(8,128)(2,1)} %get-tuple-element.13.query_ref) | copy-start | bytes 626692
  13.1 9.6 %copy-start.1 = (bf16[512,384]{1,0:T(8,128)(2,1)S(1)}, bf16[512,384]{1,0:T(8,128)(2,1)}, u32[]{:S(2)}) copy-start(bf16[512,384]{1,0:T(8,128)(2,1)} %get-tuple-element.14.block_ref.own_ref) | copy-start | bytes 1179652
  13.2 26.6 %collective-permute-start.7 = (bf16[384,768]{1,0:T(8,128)(2,1)S(1)}, bf16[384,768]{1,0:T(8,128)(2,1)S(1)}, u32[]{:S(2)}, u32[]{:S(2)}) collective-permute-start(bf16[384,768]{1,0:T(8,128)(2,1)S(1)} %get-tuple-element.20), channel_id=1, source_target_pairs={{0,4},{4,0},{1,5},{5,1},{2,6},{6,2},{3,7},{7,3},{8,12},{12,8},{9,1... | collective-permute-start | bytes 1769480 | tf_op jit(solution)/shard_map/ppermute | solution.py:50
  18.3 4.4 %collective-permute-start.2 = (bf16[272,384]{1,0:T(8,128)(2,1)S(1)}, bf16[272,384]{1,0:T(8,128)(2,1)S(1)}, u32[]{:S(2)}, u32[]{:S(2)}) collective-permute-start(bf16[272,384]{1,0:T(8,128)(2,1)S(1)} %copy-done.2), channel_id=1, source_target_pairs={{0,8},{8,0},{16,24},{24,16},{32,40},{40,32},{48,56},{56,48},{64,72... | collective-permute-start | bytes 626696 | tf_op jit(solution)/shard_map/ppermute | solution.py:41
  20.2 14.5 %collective-permute-start.4 = (bf16[272,384]{1,0:T(8,128)(2,1)S(1)}, bf16[272,384]{1,0:T(8,128)(2,1)S(1)}, u32[]{:S(2)}, u32[]{:S(2)}) collective-permute-start(bf16[272,384]{1,0:T(8,128)(2,1)S(1)} %copy-done.2), channel_id=1, source_target_pairs={{8,16},{16,8},{40,48},{48,40},{72,80},{80,72},{104,112},{112,104},... | collective-permute-start | bytes 626696 | tf_op jit(solution)/shard_map/ppermute | solution.py:46
  32.8 9.0 %collective-permute-start.3 = (bf16[272,384]{1,0:T(8,128)(2,1)S(1)}, bf16[272,384]{1,0:T(8,128)(2,1)S(1)}, u32[]{:S(2)}, u32[]{:S(2)}) collective-permute-start(bf16[272,384]{1,0:T(8,128)(2,1)S(1)} %attend_pair.1.after_ref), channel_id=1, source_target_pairs={{0,8},{8,0},{16,24},{24,16},{32,40},{40,32},{48,56},{56,48},{64,72... | collective-permute-start | bytes 626696 | tf_op jit(solution)/shard_map/ppermute | solution.py:41
  36.3 7.6 %collective-permute-start.5 = (bf16[272,384]{1,0:T(8,128)(2,1)S(1)}, bf16[272,384]{1,0:T(8,128)(2,1)S(1)}, u32[]{:S(2)}, u32[]{:S(2)}) collective-permute-start(bf16[272,384]{1,0:T(8,128)(2,1)S(1)} %attend_middle.1), channel_id=1, source_target_pairs={{8,16},{16,8},{40,48},{48,40},{72,80},{80,72},{104,112},{112,104},... | collective-permute-start | bytes 626696 | tf_op jit(solution)/shard_map/ppermute | solution.py:46
  39.9 15.2 %collective-permute-start.8 = (bf16[384,768]{1,0:T(8,128)(2,1)S(1)}, bf16[384,768]{1,0:T(8,128)(2,1)S(1)}, u32[]{:S(2)}, u32[]{:S(2)}) collective-permute-start(bf16[384,768]{1,0:T(8,128)(2,1)S(1)} %collective-permute-done.7.this_ref), channel_id=1, source_target_pairs={{0,8},{8,0},{16,24},{24,16},{32,40},{40,32},{48,56},{56,48},{64,72... | collective-permute-start | bytes 1769480 | tf_op jit(solution)/shard_map/ppermute | solution.py:41
  44.3 10.7 %collective-permute-start.6 = (bf16[256,384]{1,0:T(8,128)(2,1)S(1)}, bf16[256,384]{1,0:T(8,128)(2,1)S(1)}, u32[]{:S(2)}, u32[]{:S(2)}) collective-permute-start(bf16[256,384]{1,0:T(8,128)(2,1)S(1)} %merge.1.mine_ref), channel_id=1, source_target_pairs={{0,4},{4,0},{1,5},{5,1},{2,6},{6,2},{3,7},{7,3},{8,12},{12,8},{9,1... | collective-permute-start | bytes 589832 | tf_op jit(solution)/shard_map/ppermute | solution.py:50
  56.9 4.2 %copy-start.4 = (f32[384]{0:T(512)S(1)}, f32[384]{0:T(512)}, u32[]{:S(2)}) copy-start(f32[384]{0:T(512)} %param.13) | copy-start | bytes 4612
  56.9 14.9 %copy-start.3 = (bf16[256,384]{1,0:T(8,128)(2,1)S(1)}, bf16[256,384]{1,0:T(8,128)(2,1)}, u32[]{:S(2)}) copy-start(bf16[256,384]{1,0:T(8,128)(2,1)} %residual_ref.1) | copy-start | bytes 589828
  56.9 14.9 %all-to-all-start = ((bf16[4,256,384]{2,1,0:T(8,128)(2,1)}), bf16[4,256,384]{2,1,0:T(8,128)(2,1)S(1)}, u32[]{:S(2)}, u32[]{:S(2)}) async-start(bf16[4,256,384]{2,1,0:T(8,128)(2,1)} %project.1), calls=%async_computation | async-start | bytes 1572864 | tf_op jit(solution)/shard_map/all_to_all | solution.py:412

commit v15 on v14

--- a/solution.py
+++ b/solution.py
@@ -13,7 +13,8 @@
 SIDE = 16
 LOG2E = 1.4426950408889634
 MASKED = -1e30
-LAST_FLOPS = 6_000_000_000
+LAST_FLOPS = 400_000_000
+MIDDLE_FLOPS = 6000_000_000
 MESH_AXES = ("tile", "head")
 VMEM = pltpu.VMEM
 SMEM = pltpu.SMEM
@@ -236,7 +237,7 @@
         in_specs=[whole] * 5,
         out_specs=whole,
         compiler_params=params(24),
-        cost_estimate=pl.CostEstimate(flops=400_000_000, bytes_accessed=2_000_000, transcendentals=0),
+        cost_estimate=pl.CostEstimate(flops=4_000_000_000, bytes_accessed=2_000_000, transcendentals=0),
         name="attend_pair",
     )(query, first, second, mix, stats)
 
@@ -268,12 +269,12 @@
         in_specs=[whole] * 4 + [pl.BlockSpec(memory_space=pl.ANY)],
         out_specs=whole,
         compiler_params=params(24),
-        cost_estimate=pl.CostEstimate(flops=600_000_000, bytes_accessed=2_000_000, transcendentals=0),
+        cost_estimate=pl.CostEstimate(flops=MIDDLE_FLOPS, bytes_accessed=2_000_000, transcendentals=0),
         name="attend_middle",
     )(query, own, first, second, after)
 
 
-def last_kernel(query_ref, first_ref, second_ref, old_mix_ref, old_stats_ref, message_ref, mix_ref, stats_ref):
+def last_kernel(query_ref, first_ref, second_ref, old_mix_ref, old_stats_ref, message_ref, after_ref, mix_ref, stats_ref):
     rows, width = first_ref.shape[0] // 2, first_ref.shape[1]
     wide = wide_window(query_ref, rows, 1)
     biases = block_biases(query_ref, rows)
@@ -290,7 +291,7 @@
         stats_ref[head] = jnp.where(line == 2, jnp.where(wide, 1.0, 0.0), stats)
 
 
-def attend_last(queries, first, second, mix, stats, message):
+def attend_last(queries, first, second, mix, stats, message, after):
     rows, width = first.shape[0] // 2, first.shape[1]
     whole = pl.BlockSpec(memory_space=VMEM)
     return pl.pallas_call(
@@ -299,12 +300,12 @@
             jax.ShapeDtypeStruct((rows, width), jnp.float32),
             jax.ShapeDtypeStruct((width // HD, 8, rows), jnp.float32),
         ),
-        in_specs=[whole] * 6,
+        in_specs=[whole] * 6 + [pl.BlockSpec(memory_space=pl.ANY)],
         out_specs=(whole, whole),
         compiler_params=params(24),
         cost_estimate=pl.CostEstimate(flops=LAST_FLOPS, bytes_accessed=2_000_000, transcendentals=0),
         name="attend_last",
-    )(queries, first, second, mix, stats, message)
+    )(queries, first, second, mix, stats, message, after)
 
 
 def merge_kernel(own_ref, stats_ref, middle_ref, out_ref):
@@ -406,9 +407,10 @@
     mix, stats = attend_own(packed, pair_asks, block)
     for_pair = attend_pair(pair_asks, first, second, mix, stats)
     for_middle = attend_middle(middle_asks, block, first, second, for_pair)
-    mix, stats = attend_last(packed, first, second, mix, stats, swap_pair(for_pair))
+    other_half = swap_pair(this_half)
+    mix, stats = attend_last(packed, first, second, mix, stats, swap_pair(for_pair), other_half)
     attention = merge(mix, stats, swap_middle(for_middle))
-    terms = project(attention, swap_far(attention), my_weight, this_half, swap_pair(this_half))
+    terms = project(attention, swap_far(attention), my_weight, this_half, other_half)
     terms = lax.all_to_all(terms, "group", 0, 0)
     return finish(terms, residual, gate_scale)
 

time: 73.1 us -> 70.4 us (0.963)
  the two profiles are of different devices: /device:TPU:184 before, /device:TPU:1 now
where the time goes in v15:
time: 70.4 us; the launch traced here: 69.1 us
  starting transfers between devices  36.7 us (52%)
  waiting for transfers between devices  19.5 us (28%)
  Pallas kernels  11.1 us (16%)
  local copies, waits for them, and re-layouts  1.68 us (2%)
    ppermute x2, starting transfers between devices, swap_times(): return lax.ppermute(block, 'tile', route)  10.5 us
    ppermute x2, starting transfers between devices, swap_far(): return lax.ppermute(block, 'far', [(0, 1), (1, 0)])  10 us
    all_to_all x1, waiting for transfers between devices, shards(): terms = lax.all_to_all(terms, 'group', 0, 0)  8.44 us
    ppermute x3, starting transfers between devices, swap_pair(): lax.ppermute(block, 'tile', [(tile, tile ^ 1) for tile, *_ in places()])  7.97 us
    ppermute x2, waiting for transfers between devices, swap_times(): return lax.ppermute(block, 'tile', route)  4.83 us
    ppermute x2, starting transfers between devices, swap_middle(): return lax.ppermute(block, 'tile', route)  4.12 us
    all_to_all x1, starting transfers between devices, shards(): terms = lax.all_to_all(terms, 'group', 0, 0)  4.08 us
    ppermute x2, waiting for transfers between devices, swap_middle(): return lax.ppermute(block, 'tile', route)  3.16 us
  transfers between devices with their start and end apart: 10, of which 4 were waited for; matrix products, arithmetic and copies ran while one was open for 0% of the time, Pallas kernels for 9%

profile of v15, /device:TPU:1, one launch (start us, length us, event | category | flops | bytes accessed | tf_op | source)
XLA Modules:
  0.0 69.1 jit_solution(1907973855018421880)
XLA Ops:
  0.0 2.0 %pack.1 = (bf16[272,384]{1,0:T(8,128)(2,1)}, bf16[512,384]{1,0:T(8,128)(2,1)}) custom-call(s32[1,3]{1,0:T(1,128)} %windows_ref.1, bf16[256,384]{1,0:T(8,128)(2,1)} %q_ref.1, bf16[256,384]{1,0:T(8,128)(2,1)} %k_ref.1, bf16[256,384]{1,0:T(8,128)(2,1)} %v_ref.1), custom_call_target="tpu_custom_call" | custom-call | tf_op jit(solution)/shard_map/pack/pallas_call | solution.py:93
  2.0 0.7 collective-permute-start
  2.7 9.8 %collective-permute-start.1 = (bf16[512,384]{1,0:T(8,128)(2,1)}, bf16[512,384]{1,0:T(8,128)(2,1)S(1)}, u32[]{:S(2)}, u32[]{:S(2)}) collective-permute-start(bf16[512,384]{1,0:T(8,128)(2,1)} %get-tuple-element.14.block_ref.own_ref), channel_id=1, source_target_pairs={{0,32},{8,40},{16,48},{24,56},{32,0},{40,8},{48,16},{56,24},{64,96... | collective-permute-start | bytes 1179656 | tf_op jit(solution)/shard_map/ppermute | solution.py:38
  12.5 0.0 copy-start
  12.5 1.7 %copy-done = bf16[384,3072]{1,0:T(8,128)(2,1)S(1)} copy-done((bf16[384,3072]{1,0:T(8,128)(2,1)S(1)}, bf16[384,3072]{1,0:T(8,128)(2,1)}, u32[]{:S(2)}) %copy-start) | copy-done | bytes 2359320
  14.1 0.1 split_weight.1
  14.3 4.8 %collective-permute-start.4 = (bf16[384,768]{1,0:T(8,128)(2,1)S(1)}, bf16[384,768]{1,0:T(8,128)(2,1)S(1)}, u32[]{:S(2)}, u32[]{:S(2)}) collective-permute-start(bf16[384,768]{1,0:T(8,128)(2,1)S(1)} %get-tuple-element.17), channel_id=1, source_target_pairs={{0,4},{4,0},{1,5},{5,1},{2,6},{6,2},{3,7},{7,3},{8,12},{12,8},{9,1... | collective-permute-start | bytes 1769480 | tf_op jit(solution)/shard_map/ppermute | solution.py:51
  19.1 3.4 %collective-permute-start.2 = (bf16[272,384]{1,0:T(8,128)(2,1)S(1)}, bf16[272,384]{1,0:T(8,128)(2,1)S(1)}, u32[]{:S(2)}, u32[]{:S(2)}) collective-permute-start(bf16[272,384]{1,0:T(8,128)(2,1)S(1)} %copy-done.1), channel_id=1, source_target_pairs={{0,8},{8,0},{16,24},{24,16},{32,40},{40,32},{48,56},{56,48},{64,72... | collective-permute-start | bytes 626696 | tf_op jit(solution)/shard_map/ppermute | solution.py:42
  22.5 2.2 %collective-permute-start.6 = (bf16[272,384]{1,0:T(8,128)(2,1)S(1)}, bf16[272,384]{1,0:T(8,128)(2,1)S(1)}, u32[]{:S(2)}, u32[]{:S(2)}) collective-permute-start(bf16[272,384]{1,0:T(8,128)(2,1)S(1)} %copy-done.1), channel_id=1, source_target_pairs={{8,16},{16,8},{40,48},{48,40},{72,80},{80,72},{104,112},{112,104},... | collective-permute-start | bytes 626696 | tf_op jit(solution)/shard_map/ppermute | solution.py:47
  24.7 0.0 collective-permute-done.2.pair_ref.query_ref
  24.7 1.0 %attend_own.1 = (f32[6,256,128]{2,1,0:T(8,128)S(1)}, f32[12,256,128]{2,1,0:T(8,128)S(1)}) custom-call(bf16[272,384]{1,0:T(8,128)(2,1)S(1)} %copy-done.1, bf16[272,384]{1,0:T(8,128)(2,1)S(1)} %collective-permute-done.2.pair_ref.query_ref, bf16[512,384]{1,0:T(8,128)(2,1)S(1)} %copy-done.2), custom_call_target="tpu_custom_call" | custom-call | tf_op jit(solution)/shard_map/attend_own/pallas_call | solution.py:203
  25.7 4.8 %collective-permute-done.1.second_ref = bf16[512,384]{1,0:T(8,128)(2,1)S(1)} collective-permute-done((bf16[512,384]{1,0:T(8,128)(2,1)}, bf16[512,384]{1,0:T(8,128)(2,1)S(1)}, u32[]{:S(2)}, u32[]{:S(2)}) %collective-permute-start.1) | collective-permute-done | bytes 393248 | tf_op jit(solution)/shard_map/ppermute | solution.py:38
  30.6 1.3 %attend_pair.1.after_ref = bf16[272,384]{1,0:T(8,128)(2,1)S(1)} custom-call(bf16[272,384]{1,0:T(8,128)(2,1)S(1)} %collective-permute-done.2.pair_ref.query_ref, bf16[512,384]{1,0:T(8,128)(2,1)S(1)} %collective-permute-done.first_ref, bf16[512,384]{1,0:T(8,128)(2,1)S(1)} %collective-permute-done.1.second_ref, ...), custom_call_target="tpu_custom_call" | custom-call | flops 4000000000 | bytes 2000000 | tf_op jit(solution)/shard_map/attend_pair/pallas_call | solution.py:234
  31.8 2.6 %collective-permute-start.3 = (bf16[272,384]{1,0:T(8,128)(2,1)S(1)}, bf16[272,384]{1,0:T(8,128)(2,1)S(1)}, u32[]{:S(2)}, u32[]{:S(2)}) collective-permute-start(bf16[272,384]{1,0:T(8,128)(2,1)S(1)} %attend_pair.1.after_ref), channel_id=1, source_target_pairs={{0,8},{8,0},{16,24},{24,16},{32,40},{40,32},{48,56},{56,48},{64,72... | collective-permute-start | bytes 626696 | tf_op jit(solution)/shard_map/ppermute | solution.py:42
  34.5 0.0 collective-permute-done.4.this_ref
  34.5 1.9 %collective-permute-start.5 = (bf16[384,768]{1,0:T(8,128)(2,1)S(1)}, bf16[384,768]{1,0:T(8,128)(2,1)S(1)}, u32[]{:S(2)}, u32[]{:S(2)}) collective-permute-start(bf16[384,768]{1,0:T(8,128)(2,1)S(1)} %collective-permute-done.4.this_ref), channel_id=1, source_target_pairs={{0,8},{8,0},{16,24},{24,16},{32,40},{40,32},{48,56},{56,48},{64,72... | collective-permute-start | bytes 1769480 | tf_op jit(solution)/shard_map/ppermute | solution.py:42
  36.4 0.0 collective-permute-done.6.query_ref
  36.4 1.5 %attend_middle.1 = bf16[272,384]{1,0:T(8,128)(2,1)S(1)} custom-call(bf16[272,384]{1,0:T(8,128)(2,1)S(1)} %collective-permute-done.6.query_ref, bf16[512,384]{1,0:T(8,128)(2,1)S(1)} %copy-done.2, bf16[512,384]{1,0:T(8,128)(2,1)S(1)} %collective-permute-done.first_ref, bf16[512,384]{1,0:T(8,128)(2,1)S(1)} %collective-permute-done.1.second_ref, ...), custom_call_target="tpu_custom_call" | custom-call | flops 6000000000 | bytes 2000000 | tf_op jit(solution)/shard_map/attend_middle/pallas_call | solution.py:266
  38.0 1.9 %collective-permute-start.7 = (bf16[272,384]{1,0:T(8,128)(2,1)S(1)}, bf16[272,384]{1,0:T(8,128)(2,1)S(1)}, u32[]{:S(2)}, u32[]{:S(2)}) collective-permute-start(bf16[272,384]{1,0:T(8,128)(2,1)S(1)} %attend_middle.1), channel_id=1, source_target_pairs={{8,16},{16,8},{40,48},{48,40},{72,80},{80,72},{104,112},{112,104},... | collective-permute-start | bytes 626696 | tf_op jit(solution)/shard_map/ppermute | solution.py:47
  39.9 0.0 collective-permute-done.3.message_ref
  39.9 0.0 collective-permute-done.5.after_ref.other_ref
  39.9 2.0 %attend_last.1 = (f32[256,384]{1,0:T(8,128)S(1)}, f32[3,8,256]{2,1,0:T(8,128)S(1)}) custom-call(bf16[272,384]{1,0:T(8,128)(2,1)S(1)} %copy-done.1, bf16[512,384]{1,0:T(8,128)(2,1)S(1)} %collective-permute-done.first_ref, bf16[512,384]{1,0:T(8,128)(2,1)S(1)} %collective-permute-done.1.second_ref, f32[6,256,128]{2,1,0:T(8,128)S(1)} %get-tuple-element.15.mix_ref.old_mix_ref, ...), custom_call_target="tpu_custom_call" | custom-call | flops 400000000 | bytes 2000000 | tf_op jit(solution)/shard_map/attend_last/pallas_call | solution.py:297
  41.9 3.2 %collective-permute-done.7.middle_ref = bf16[272,384]{1,0:T(8,128)(2,1)S(1)} collective-permute-done((bf16[272,384]{1,0:T(8,128)(2,1)S(1)}, bf16[272,384]{1,0:T(8,128)(2,1)S(1)}, u32[]{:S(2)}, u32[]{:S(2)}) %collective-permute-start.7) | collective-permute-done | bytes 208928 | tf_op jit(solution)/shard_map/ppermute | solution.py:47
  45.1 0.5 merge.1.mine_ref
  45.6 5.3 %collective-permute-start.8 = (bf16[256,384]{1,0:T(8,128)(2,1)S(1)}, bf16[256,384]{1,0:T(8,128)(2,1)S(1)}, u32[]{:S(2)}, u32[]{:S(2)}) collective-permute-start(bf16[256,384]{1,0:T(8,128)(2,1)S(1)} %merge.1.mine_ref), channel_id=1, source_target_pairs={{0,4},{4,0},{1,5},{5,1},{2,6},{6,2},{3,7},{7,3},{8,12},{12,8},{9,1... | collective-permute-start | bytes 589832 | tf_op jit(solution)/shard_map/ppermute | solution.py:51
  50.9 3.0 %collective-permute-done.8.theirs_ref = bf16[256,384]{1,0:T(8,128)(2,1)S(1)} collective-permute-done((bf16[256,384]{1,0:T(8,128)(2,1)S(1)}, bf16[256,384]{1,0:T(8,128)(2,1)S(1)}, u32[]{:S(2)}, u32[]{:S(2)}) %collective-permute-start.8) | collective-permute-done | bytes 196640 | tf_op jit(solution)/shard_map/ppermute | solution.py:51
  53.9 1.8 %project.1 = bf16[4,256,384]{2,1,0:T(8,128)(2,1)} custom-call(bf16[256,384]{1,0:T(8,128)(2,1)S(1)} %merge.1.mine_ref, bf16[256,384]{1,0:T(8,128)(2,1)S(1)} %collective-permute-done.8.theirs_ref, bf16[384,1536]{1,0:T(8,128)(2,1)S(1)} %get-tuple-element.20.my_weight_ref, bf16[384,768]{1,0:T(8,128)(2,1)S(1)} %collective-permute-done.4.this_ref, ...), custom_call_target="tpu_custom_call" | custom-call | flops 603979776 | bytes 5000000 | tf_op jit(solution)/shard_map/project/pallas_call | solution.py:371
  55.8 0.0 copy-start.4
  55.8 0.0 copy-start.3
  55.8 4.1 %all-to-all-start = ((bf16[4,256,384]{2,1,0:T(8,128)(2,1)}), bf16[4,256,384]{2,1,0:T(8,128)(2,1)S(1)}, u32[]{:S(2)}, u32[]{:S(2)}) async-start(bf16[4,256,384]{2,1,0:T(8,128)(2,1)} %project.1), calls=%async_computation | async-start | bytes 1572864 | tf_op jit(solution)/shard_map/all_to_all | solution.py:414
  59.9 8.4 %all-to-all-done.terms_ref = bf16[4,256,384]{2,1,0:T(8,128)(2,1)S(1)} async-done(((bf16[4,256,384]{2,1,0:T(8,128)(2,1)}), bf16[4,256,384]{2,1,0:T(8,128)(2,1)S(1)}, u32[]{:S(2)}, u32[]{:S(2)}) %all-to-all-start) | async-done | bytes 786464 | tf_op jit(solution)/shard_map/all_to_all | solution.py:414
  68.3 0.8 %finish.1 = bf16[256,384]{1,0:T(8,128)(2,1)} custom-call(bf16[4,256,384]{2,1,0:T(8,128)(2,1)S(1)} %all-to-all-done.terms_ref, bf16[256,384]{1,0:T(8,128)(2,1)S(1)} %copy-done.3, f32[1,384]{1,0:T(1,128)S(1)} %reshape.3.gate_ref), custom_call_target="tpu_custom_call" | custom-call | flops 3932160 | bytes 2000000 | tf_op jit(solution)/shard_map/finish/pallas_call | solution.py:390
  (8 shorter events, 0.0 us)
Async XLA Ops:
  2.0 23.7 %collective-permute-start = (bf16[512,384]{1,0:T(8,128)(2,1)}, bf16[512,384]{1,0:T(8,128)(2,1)S(1)}, u32[]{:S(2)}, u32[]{:S(2)}) collective-permute-start(bf16[512,384]{1,0:T(8,128)(2,1)} %get-tuple-element.14.block_ref.own_ref), channel_id=1, source_target_pairs={{32,64},{40,72},{48,80},{56,88},{64,32},{72,40},{80,48},{88,56},{9... | collective-permute-start | bytes 1179656 | tf_op jit(solution)/shard_map/ppermute | solution.py:38
  2.7 27.9 %collective-permute-start.1 = (bf16[512,384]{1,0:T(8,128)(2,1)}, bf16[512,384]{1,0:T(8,128)(2,1)S(1)}, u32[]{:S(2)}, u32[]{:S(2)}) collective-permute-start(bf16[512,384]{1,0:T(8,128)(2,1)} %get-tuple-element.14.block_ref.own_ref), channel_id=1, source_target_pairs={{0,32},{8,40},{16,48},{24,56},{32,0},{40,8},{48,16},{56,24},{64,96... | collective-permute-start | bytes 1179656 | tf_op jit(solution)/shard_map/ppermute | solution.py:38
  12.5 1.7 %copy-start = (bf16[384,3072]{1,0:T(8,128)(2,1)S(1)}, bf16[384,3072]{1,0:T(8,128)(2,1)}, u32[]{:S(2)}) copy-start(bf16[384,3072]{1,0:T(8,128)(2,1)} %weight_ref.1) | copy-start | bytes 7077892
  14.1 4.9 %copy-start.1 = (bf16[272,384]{1,0:T(8,128)(2,1)S(1)}, bf16[272,384]{1,0:T(8,128)(2,1)}, u32[]{:S(2)}) copy-start(bf16[272,384]{1,0:T(8,128)(2,1)} %get-tuple-element.13.query_ref) | copy-start | bytes 626692
  14.1 10.6 %copy-start.2 = (bf16[512,384]{1,0:T(8,128)(2,1)S(1)}, bf16[512,384]{1,0:T(8,128)(2,1)}, u32[]{:S(2)}) copy-start(bf16[512,384]{1,0:T(8,128)(2,1)} %get-tuple-element.14.block_ref.own_ref) | copy-start | bytes 1179652
  14.3 20.2 %collective-permute-start.4 = (bf16[384,768]{1,0:T(8,128)(2,1)S(1)}, bf16[384,768]{1,0:T(8,128)(2,1)S(1)}, u32[]{:S(2)}, u32[]{:S(2)}) collective-permute-start(bf16[384,768]{1,0:T(8,128)(2,1)S(1)} %get-tuple-element.17), channel_id=1, source_target_pairs={{0,4},{4,0},{1,5},{5,1},{2,6},{6,2},{3,7},{7,3},{8,12},{12,8},{9,1... | collective-permute-start | bytes 1769480 | tf_op jit(solution)/shard_map/ppermute | solution.py:51
  19.1 5.6 %collective-permute-start.2 = (bf16[272,384]{1,0:T(8,128)(2,1)S(1)}, bf16[272,384]{1,0:T(8,128)(2,1)S(1)}, u32[]{:S(2)}, u32[]{:S(2)}) collective-permute-start(bf16[272,384]{1,0:T(8,128)(2,1)S(1)} %copy-done.1), channel_id=1, source_target_pairs={{0,8},{8,0},{16,24},{24,16},{32,40},{40,32},{48,56},{56,48},{64,72... | collective-permute-start | bytes 626696 | tf_op jit(solution)/shard_map/ppermute | solution.py:42
  22.5 13.9 %collective-permute-start.6 = (bf16[272,384]{1,0:T(8,128)(2,1)S(1)}, bf16[272,384]{1,0:T(8,128)(2,1)S(1)}, u32[]{:S(2)}, u32[]{:S(2)}) collective-permute-start(bf16[272,384]{1,0:T(8,128)(2,1)S(1)} %copy-done.1), channel_id=1, source_target_pairs={{8,16},{16,8},{40,48},{48,40},{72,80},{80,72},{104,112},{112,104},... | collective-permute-start | bytes 626696 | tf_op jit(solution)/shard_map/ppermute | solution.py:47
  31.8 8.1 %collective-permute-start.3 = (bf16[272,384]{1,0:T(8,128)(2,1)S(1)}, bf16[272,384]{1,0:T(8,128)(2,1)S(1)}, u32[]{:S(2)}, u32[]{:S(2)}) collective-permute-start(bf16[272,384]{1,0:T(8,128)(2,1)S(1)} %attend_pair.1.after_ref), channel_id=1, source_target_pairs={{0,8},{8,0},{16,24},{24,16},{32,40},{40,32},{48,56},{56,48},{64,72... | collective-permute-start | bytes 626696 | tf_op jit(solution)/shard_map/ppermute | solution.py:42
  34.5 5.4 %collective-permute-start.5 = (bf16[384,768]{1,0:T(8,128)(2,1)S(1)}, bf16[384,768]{1,0:T(8,128)(2,1)S(1)}, u32[]{:S(2)}, u32[]{:S(2)}) collective-permute-start(bf16[384,768]{1,0:T(8,128)(2,1)S(1)} %collective-permute-done.4.this_ref), channel_id=1, source_target_pairs={{0,8},{8,0},{16,24},{24,16},{32,40},{40,32},{48,56},{56,48},{64,72... | collective-permute-start | bytes 1769480 | tf_op jit(solution)/shard_map/ppermute | solution.py:42
  38.0 7.1 %collective-permute-start.7 = (bf16[272,384]{1,0:T(8,128)(2,1)S(1)}, bf16[272,384]{1,0:T(8,128)(2,1)S(1)}, u32[]{:S(2)}, u32[]{:S(2)}) collective-permute-start(bf16[272,384]{1,0:T(8,128)(2,1)S(1)} %attend_middle.1), channel_id=1, source_target_pairs={{8,16},{16,8},{40,48},{48,40},{72,80},{80,72},{104,112},{112,104},... | collective-permute-start | bytes 626696 | tf_op jit(solution)/shard_map/ppermute | solution.py:47
  45.6 8.3 %collective-permute-start.8 = (bf16[256,384]{1,0:T(8,128)(2,1)S(1)}, bf16[256,384]{1,0:T(8,128)(2,1)S(1)}, u32[]{:S(2)}, u32[]{:S(2)}) collective-permute-start(bf16[256,384]{1,0:T(8,128)(2,1)S(1)} %merge.1.mine_ref), channel_id=1, source_target_pairs={{0,4},{4,0},{1,5},{5,1},{2,6},{6,2},{3,7},{7,3},{8,12},{12,8},{9,1... | collective-permute-start | bytes 589832 | tf_op jit(solution)/shard_map/ppermute | solution.py:51
  55.8 4.1 %copy-start.4 = (f32[384]{0:T(512)S(1)}, f32[384]{0:T(512)}, u32[]{:S(2)}) copy-start(f32[384]{0:T(512)} %param.13) | copy-start | bytes 4612
  55.8 12.5 %copy-start.3 = (bf16[256,384]{1,0:T(8,128)(2,1)S(1)}, bf16[256,384]{1,0:T(8,128)(2,1)}, u32[]{:S(2)}) copy-start(bf16[256,384]{1,0:T(8,128)(2,1)} %residual_ref.1) | copy-start | bytes 589828
  55.8 12.5 %all-to-all-start = ((bf16[4,256,384]{2,1,0:T(8,128)(2,1)}), bf16[4,256,384]{2,1,0:T(8,128)(2,1)S(1)}, u32[]{:S(2)}, u32[]{:S(2)}) async-start(bf16[4,256,384]{2,1,0:T(8,128)(2,1)} %project.1), calls=%async_computation | async-start | bytes 1572864 | tf_op jit(solution)/shard_map/all_to_all | solution.py:414

commit v16 on v15

--- a/solution.py
+++ b/solution.py
@@ -345,39 +345,55 @@
     )(own, stats, middle)
 
 
-def project_kernel(mine_ref, theirs_ref, my_weight_ref, this_ref, other_ref, out_ref, held_ref, sems):
-    width, half = mine_ref.shape[1], this_ref.shape[1]
+def project_mine_kernel(mine_ref, weight_ref, out_ref):
+    width = mine_ref.shape[1]
+    for group in range(out_ref.shape[0]):
+        low = group * width
+        out_ref[group] = jnp.dot(mine_ref[...], weight_ref[:, low : low + width], preferred_element_type=jnp.float32)
+
+
+def project_mine(mine, my_weight):
+    rows, width = mine.shape
+    groups = my_weight.shape[1] // width
+    whole = pl.BlockSpec(memory_space=VMEM)
+    return pl.pallas_call(
+        project_mine_kernel,
+        out_shape=jax.ShapeDtypeStruct((groups, rows, width), jnp.float32),
+        in_specs=[whole] * 2,
+        out_specs=whole,
+        compiler_params=params(24),
+        cost_estimate=pl.CostEstimate(flops=2 * groups * rows * width * width, bytes_accessed=0, transcendentals=0),
+        name="project_mine",
+    )(mine, my_weight)
+
+
+def project_kernel(mine_ref, theirs_ref, this_ref, other_ref, out_ref, held_ref, sems):
+    width, half = theirs_ref.shape[1], this_ref.shape[1]
     core = lax.rem(lax.axis_index("tile"), 2)
     copies = []
     for group in range(out_ref.shape[0]):
-        low = group * width
-        side, start = divmod(low, half)
+        side, start = divmod(group * width, half)
         their_weight = jnp.where(side == core, this_ref[:, start : start + width], other_ref[:, start : start + width])
-        held_ref[group] = (
-            jnp.dot(mine_ref[...], my_weight_ref[:, low : low + width], preferred_element_type=jnp.float32)
-            + jnp.dot(theirs_ref[...], their_weight, preferred_element_type=jnp.float32)
-        ).astype(held_ref.dtype)
+        product = jnp.dot(theirs_ref[...], their_weight, preferred_element_type=jnp.float32)
+        held_ref[group] = (mine_ref[group] + product).astype(held_ref.dtype)
         copies.append(pltpu.make_async_copy(held_ref.at[group], out_ref.at[group], sems.at[group]))
         copies[-1].start()
     for copy in copies:
         copy.wait()
 
 
-def project(mine, theirs, my_weight, this_half, other_half):
-    rows, width = mine.shape
-    groups = my_weight.shape[1] // width
-    whole = pl.BlockSpec(memory_space=VMEM)
-    shape = (groups, rows, width)
+def project(mine, theirs, this_half, other_half):
+    whole = pl.BlockSpec(memory_space=VMEM)
     return pl.pallas_call(
         project_kernel,
-        out_shape=jax.ShapeDtypeStruct(shape, jnp.bfloat16),
-        in_specs=[whole] * 5,
+        out_shape=jax.ShapeDtypeStruct(mine.shape, jnp.bfloat16),
+        in_specs=[whole] * 4,
         out_specs=pl.BlockSpec(memory_space=pl.ANY),
-        scratch_shapes=[pltpu.VMEM(shape, jnp.bfloat16), pltpu.SemaphoreType.DMA((groups,))],
-        compiler_params=params(24),
-        cost_estimate=pl.CostEstimate(flops=4 * groups * rows * width * width, bytes_accessed=5_000_000, transcendentals=0),
+        scratch_shapes=[pltpu.VMEM(mine.shape, jnp.bfloat16), pltpu.SemaphoreType.DMA((mine.shape[0],))],
+        compiler_params=params(24),
+        cost_estimate=pl.CostEstimate(flops=300_000_000, bytes_accessed=5_000_000, transcendentals=0),
         name="project",
-    )(mine, theirs, my_weight, this_half, other_half)
+    )(mine, theirs, this_half, other_half)
 
 
 def finish_kernel(terms_ref, residual_ref, gate_ref, out_ref):
@@ -410,7 +426,8 @@
     other_half = swap_pair(this_half)
     mix, stats = attend_last(packed, first, second, mix, stats, swap_pair(for_pair), other_half)
     attention = merge(mix, stats, swap_middle(for_middle))
-    terms = project(attention, swap_far(attention), my_weight, this_half, other_half)
+    mine = project_mine(attention, my_weight)
+    terms = project(mine, swap_far(attention), this_half, other_half)
     terms = lax.all_to_all(terms, "group", 0, 0)
     return finish(terms, residual, gate_scale)
 

time: 70.4 us -> 70.7 us (level)
  the two profiles are of different devices: /device:TPU:1 before, /device:TPU:286 now
where the time goes in v16:
time: 70.7 us; the launch traced here: 70.2 us
  starting transfers between devices  36.3 us (51%)
  waiting for transfers between devices  20.8 us (29%)
  Pallas kernels  11.2 us (16%)
  local copies, waits for them, and re-layouts  1.68 us (2%)
    ppermute x2, starting transfers between devices, swap_middle(): return lax.ppermute(block, 'tile', route)  9.04 us
    all_to_all x1, starting transfers between devices, shards(): terms = lax.all_to_all(terms, 'group', 0, 0)  7.57 us
    all_to_all x1, waiting for transfers between devices, shards(): terms = lax.all_to_all(terms, 'group', 0, 0)  7.47 us
    ppermute x2, waiting for transfers between devices, swap_times(): return lax.ppermute(block, 'tile', route)  6.78 us
    ppermute x2, starting transfers between devices, swap_far(): return lax.ppermute(block, 'far', [(0, 1), (1, 0)])  6.75 us
    ppermute x2, starting transfers between devices, swap_times(): return lax.ppermute(block, 'tile', route)  6.72 us
    ppermute x3, starting transfers between devices, swap_pair(): lax.ppermute(block, 'tile', [(tile, tile ^ 1) for tile, *_ in places()])  6.25 us
    ppermute x2, waiting for transfers between devices, swap_far(): return lax.ppermute(block, 'far', [(0, 1), (1, 0)])  5.12 us
  transfers between devices with their start and end apart: 10, of which 5 were waited for; matrix products, arithmetic and copies ran while one was open for 0% of the time, Pallas kernels for 9%

profile of v16, /device:TPU:286, one launch (start us, length us, event | category | flops | bytes accessed | tf_op | source)
XLA Modules:
  0.0 70.2 jit_solution(7805140576893816717)
XLA Ops:
  0.0 2.0 %pack.1 = (bf16[272,384]{1,0:T(8,128)(2,1)}, bf16[512,384]{1,0:T(8,128)(2,1)}) custom-call(s32[1,3]{1,0:T(1,128)} %windows_ref.1, bf16[256,384]{1,0:T(8,128)(2,1)} %q_ref.1, bf16[256,384]{1,0:T(8,128)(2,1)} %k_ref.1, bf16[256,384]{1,0:T(8,128)(2,1)} %v_ref.1), custom_call_target="tpu_custom_call" | custom-call | tf_op jit(solution)/shard_map/pack/pallas_call | solution.py:93
  2.0 4.8 %collective-permute-start = (bf16[512,384]{1,0:T(8,128)(2,1)}, bf16[512,384]{1,0:T(8,128)(2,1)S(1)}, u32[]{:S(2)}, u32[]{:S(2)}) collective-permute-start(bf16[512,384]{1,0:T(8,128)(2,1)} %get-tuple-element.14.block_ref.own_ref), channel_id=1, source_target_pairs={{32,64},{40,72},{48,80},{56,88},{64,32},{72,40},{80,48},{88,56},{9... | collective-permute-start | bytes 1179656 | tf_op jit(solution)/shard_map/ppermute | solution.py:38
  6.8 1.9 %collective-permute-start.1 = (bf16[512,384]{1,0:T(8,128)(2,1)}, bf16[512,384]{1,0:T(8,128)(2,1)S(1)}, u32[]{:S(2)}, u32[]{:S(2)}) collective-permute-start(bf16[512,384]{1,0:T(8,128)(2,1)} %get-tuple-element.14.block_ref.own_ref), channel_id=1, source_target_pairs={{0,32},{8,40},{16,48},{24,56},{32,0},{40,8},{48,16},{56,24},{64,96... | collective-permute-start | bytes 1179656 | tf_op jit(solution)/shard_map/ppermute | solution.py:38
  8.7 0.0 copy-start
  8.7 1.7 %copy-done = bf16[384,3072]{1,0:T(8,128)(2,1)S(1)} copy-done((bf16[384,3072]{1,0:T(8,128)(2,1)S(1)}, bf16[384,3072]{1,0:T(8,128)(2,1)}, u32[]{:S(2)}) %copy-start) | copy-done | bytes 2359320
  10.4 0.1 split_weight.1
  10.5 3.4 %collective-permute-start.4 = (bf16[384,768]{1,0:T(8,128)(2,1)S(1)}, bf16[384,768]{1,0:T(8,128)(2,1)S(1)}, u32[]{:S(2)}, u32[]{:S(2)}) collective-permute-start(bf16[384,768]{1,0:T(8,128)(2,1)S(1)} %get-tuple-element.17), channel_id=1, source_target_pairs={{0,4},{4,0},{1,5},{5,1},{2,6},{6,2},{3,7},{7,3},{8,12},{12,8},{9,1... | collective-permute-start | bytes 1769480 | tf_op jit(solution)/shard_map/ppermute | solution.py:51
  14.0 1.9 %collective-permute-start.2 = (bf16[272,384]{1,0:T(8,128)(2,1)S(1)}, bf16[272,384]{1,0:T(8,128)(2,1)S(1)}, u32[]{:S(2)}, u32[]{:S(2)}) collective-permute-start(bf16[272,384]{1,0:T(8,128)(2,1)S(1)} %copy-done.1), channel_id=1, source_target_pairs={{0,8},{8,0},{16,24},{24,16},{32,40},{40,32},{48,56},{56,48},{64,72... | collective-permute-start | bytes 626696 | tf_op jit(solution)/shard_map/ppermute | solution.py:42
  15.9 3.4 %collective-permute-start.6 = (bf16[272,384]{1,0:T(8,128)(2,1)S(1)}, bf16[272,384]{1,0:T(8,128)(2,1)S(1)}, u32[]{:S(2)}, u32[]{:S(2)}) collective-permute-start(bf16[272,384]{1,0:T(8,128)(2,1)S(1)} %copy-done.1), channel_id=1, source_target_pairs={{8,16},{16,8},{40,48},{48,40},{72,80},{80,72},{104,112},{112,104},... | collective-permute-start | bytes 626696 | tf_op jit(solution)/shard_map/ppermute | solution.py:47
  19.3 0.0 collective-permute-done.2.pair_ref.query_ref
  19.3 1.0 %attend_own.1 = (f32[6,256,128]{2,1,0:T(8,128)S(1)}, f32[12,256,128]{2,1,0:T(8,128)S(1)}) custom-call(bf16[272,384]{1,0:T(8,128)(2,1)S(1)} %copy-done.1, bf16[272,384]{1,0:T(8,128)(2,1)S(1)} %collective-permute-done.2.pair_ref.query_ref, bf16[512,384]{1,0:T(8,128)(2,1)S(1)} %copy-done.2), custom_call_target="tpu_custom_call" | custom-call | tf_op jit(solution)/shard_map/attend_own/pallas_call | solution.py:203
  20.3 3.5 %collective-permute-done.first_ref = bf16[512,384]{1,0:T(8,128)(2,1)S(1)} collective-permute-done((bf16[512,384]{1,0:T(8,128)(2,1)}, bf16[512,384]{1,0:T(8,128)(2,1)S(1)}, u32[]{:S(2)}, u32[]{:S(2)}) %collective-permute-start) | collective-permute-done | bytes 393248 | tf_op jit(solution)/shard_map/ppermute | solution.py:38
  23.8 3.3 %collective-permute-done.1.second_ref = bf16[512,384]{1,0:T(8,128)(2,1)S(1)} collective-permute-done((bf16[512,384]{1,0:T(8,128)(2,1)}, bf16[512,384]{1,0:T(8,128)(2,1)S(1)}, u32[]{:S(2)}, u32[]{:S(2)}) %collective-permute-start.1) | collective-permute-done | bytes 393248 | tf_op jit(solution)/shard_map/ppermute | solution.py:38
  27.1 1.3 %attend_pair.1.after_ref = bf16[272,384]{1,0:T(8,128)(2,1)S(1)} custom-call(bf16[272,384]{1,0:T(8,128)(2,1)S(1)} %collective-permute-done.2.pair_ref.query_ref, bf16[512,384]{1,0:T(8,128)(2,1)S(1)} %collective-permute-done.first_ref, bf16[512,384]{1,0:T(8,128)(2,1)S(1)} %collective-permute-done.1.second_ref, ...), custom_call_target="tpu_custom_call" | custom-call | flops 4000000000 | bytes 2000000 | tf_op jit(solution)/shard_map/attend_pair/pallas_call | solution.py:234
  28.3 1.9 %collective-permute-start.3 = (bf16[272,384]{1,0:T(8,128)(2,1)S(1)}, bf16[272,384]{1,0:T(8,128)(2,1)S(1)}, u32[]{:S(2)}, u32[]{:S(2)}) collective-permute-start(bf16[272,384]{1,0:T(8,128)(2,1)S(1)} %attend_pair.1.after_ref), channel_id=1, source_target_pairs={{0,8},{8,0},{16,24},{24,16},{32,40},{40,32},{48,56},{56,48},{64,72... | collective-permute-start | bytes 626696 | tf_op jit(solution)/shard_map/ppermute | solution.py:42
  30.3 0.0 collective-permute-done.4.this_ref
  30.3 2.4 %collective-permute-start.5 = (bf16[384,768]{1,0:T(8,128)(2,1)S(1)}, bf16[384,768]{1,0:T(8,128)(2,1)S(1)}, u32[]{:S(2)}, u32[]{:S(2)}) collective-permute-start(bf16[384,768]{1,0:T(8,128)(2,1)S(1)} %collective-permute-done.4.this_ref), channel_id=1, source_target_pairs={{0,8},{8,0},{16,24},{24,16},{32,40},{40,32},{48,56},{56,48},{64,72... | collective-permute-start | bytes 1769480 | tf_op jit(solution)/shard_map/ppermute | solution.py:42
  32.7 0.0 collective-permute-done.6.query_ref
  32.7 1.5 %attend_middle.1 = bf16[272,384]{1,0:T(8,128)(2,1)S(1)} custom-call(bf16[272,384]{1,0:T(8,128)(2,1)S(1)} %collective-permute-done.6.query_ref, bf16[512,384]{1,0:T(8,128)(2,1)S(1)} %copy-done.2, bf16[512,384]{1,0:T(8,128)(2,1)S(1)} %collective-permute-done.first_ref, bf16[512,384]{1,0:T(8,128)(2,1)S(1)} %collective-permute-done.1.second_ref, ...), custom_call_target="tpu_custom_call" | custom-call | flops 6000000000 | bytes 2000000 | tf_op jit(solution)/shard_map/attend_middle/pallas_call | solution.py:266
  34.3 5.7 %collective-permute-start.7 = (bf16[272,384]{1,0:T(8,128)(2,1)S(1)}, bf16[272,384]{1,0:T(8,128)(2,1)S(1)}, u32[]{:S(2)}, u32[]{:S(2)}) collective-permute-start(bf16[272,384]{1,0:T(8,128)(2,1)S(1)} %attend_middle.1), channel_id=1, source_target_pairs={{8,16},{16,8},{40,48},{48,40},{72,80},{80,72},{104,112},{112,104},... | collective-permute-start | bytes 626696 | tf_op jit(solution)/shard_map/ppermute | solution.py:47
  40.0 2.0 %attend_last.1 = (f32[256,384]{1,0:T(8,128)S(1)}, f32[3,8,256]{2,1,0:T(8,128)S(1)}) custom-call(bf16[272,384]{1,0:T(8,128)(2,1)S(1)} %copy-done.1, bf16[512,384]{1,0:T(8,128)(2,1)S(1)} %collective-permute-done.first_ref, bf16[512,384]{1,0:T(8,128)(2,1)S(1)} %collective-permute-done.1.second_ref, f32[6,256,128]{2,1,0:T(8,128)S(1)} %get-tuple-element.15.mix_ref.old_mix_ref, ...), custom_call_target="tpu_custom_call" | custom-call | flops 400000000 | bytes 2000000 | tf_op jit(solution)/shard_map/attend_last/pallas_call | solution.py:297
  42.0 1.4 %collective-permute-done.7.middle_ref = bf16[272,384]{1,0:T(8,128)(2,1)S(1)} collective-permute-done((bf16[272,384]{1,0:T(8,128)(2,1)S(1)}, bf16[272,384]{1,0:T(8,128)(2,1)S(1)}, u32[]{:S(2)}, u32[]{:S(2)}) %collective-permute-start.7) | collective-permute-done | bytes 208928 | tf_op jit(solution)/shard_map/ppermute | solution.py:47
  43.4 0.5 merge.1.mine_ref
  43.9 3.3 %collective-permute-start.8 = (bf16[256,384]{1,0:T(8,128)(2,1)S(1)}, bf16[256,384]{1,0:T(8,128)(2,1)S(1)}, u32[]{:S(2)}, u32[]{:S(2)}) collective-permute-start(bf16[256,384]{1,0:T(8,128)(2,1)S(1)} %merge.1.mine_ref), channel_id=1, source_target_pairs={{0,4},{4,0},{1,5},{5,1},{2,6},{6,2},{3,7},{7,3},{8,12},{12,8},{9,1... | collective-permute-start | bytes 589832 | tf_op jit(solution)/shard_map/ppermute | solution.py:51
  47.2 0.6 project_mine.1.mine_ref
  47.9 5.1 %collective-permute-done.8.theirs_ref = bf16[256,384]{1,0:T(8,128)(2,1)S(1)} collective-permute-done((bf16[256,384]{1,0:T(8,128)(2,1)S(1)}, bf16[256,384]{1,0:T(8,128)(2,1)S(1)}, u32[]{:S(2)}, u32[]{:S(2)}) %collective-permute-start.8) | collective-permute-done | bytes 196640 | tf_op jit(solution)/shard_map/ppermute | solution.py:51
  53.0 1.4 %project.1 = bf16[4,256,384]{2,1,0:T(8,128)(2,1)} custom-call(f32[4,256,384]{2,1,0:T(8,128)S(1)} %project_mine.1.mine_ref, bf16[256,384]{1,0:T(8,128)(2,1)S(1)} %collective-permute-done.8.theirs_ref, bf16[384,768]{1,0:T(8,128)(2,1)S(1)} %collective-permute-done.4.this_ref, bf16[384,768]{1,0:T(8,128)(2,1)S(1)} %collective-permute-done.5.after_ref.other_ref), custom_call_target="tpu_custom_call" | custom-call | flops 300000000 | bytes 5000000 | tf_op jit(solution)/shard_map/project/pallas_call | solution.py:387
  54.3 0.0 copy-start.4
  54.4 0.0 copy-start.3
  54.4 7.6 %all-to-all-start = ((bf16[4,256,384]{2,1,0:T(8,128)(2,1)}), bf16[4,256,384]{2,1,0:T(8,128)(2,1)S(1)}, u32[]{:S(2)}, u32[]{:S(2)}) async-start(bf16[4,256,384]{2,1,0:T(8,128)(2,1)} %project.1), calls=%async_computation | async-start | bytes 1572864 | tf_op jit(solution)/shard_map/all_to_all | solution.py:431
  61.9 7.5 %all-to-all-done.terms_ref = bf16[4,256,384]{2,1,0:T(8,128)(2,1)S(1)} async-done(((bf16[4,256,384]{2,1,0:T(8,128)(2,1)}), bf16[4,256,384]{2,1,0:T(8,128)(2,1)S(1)}, u32[]{:S(2)}, u32[]{:S(2)}) %all-to-all-start) | async-done | bytes 786464 | tf_op jit(solution)/shard_map/all_to_all | solution.py:431
  69.4 0.8 %finish.1 = bf16[256,384]{1,0:T(8,128)(2,1)} custom-call(bf16[4,256,384]{2,1,0:T(8,128)(2,1)S(1)} %all-to-all-done.terms_ref, bf16[256,384]{1,0:T(8,128)(2,1)S(1)} %copy-done.3, f32[1,384]{1,0:T(1,128)S(1)} %reshape.3.gate_ref), custom_call_target="tpu_custom_call" | custom-call | flops 3932160 | bytes 2000000 | tf_op jit(solution)/shard_map/finish/pallas_call | solution.py:406
  (9 shorter events, 0.0 us)
Async XLA Ops:
  2.0 21.8 %collective-permute-start = (bf16[512,384]{1,0:T(8,128)(2,1)}, bf16[512,384]{1,0:T(8,128)(2,1)S(1)}, u32[]{:S(2)}, u32[]{:S(2)}) collective-permute-start(bf16[512,384]{1,0:T(8,128)(2,1)} %get-tuple-element.14.block_ref.own_ref), channel_id=1, source_target_pairs={{32,64},{40,72},{48,80},{56,88},{64,32},{72,40},{80,48},{88,56},{9... | collective-permute-start | bytes 1179656 | tf_op jit(solution)/shard_map/ppermute | solution.py:38
  6.8 20.3 %collective-permute-start.1 = (bf16[512,384]{1,0:T(8,128)(2,1)}, bf16[512,384]{1,0:T(8,128)(2,1)S(1)}, u32[]{:S(2)}, u32[]{:S(2)}) collective-permute-start(bf16[512,384]{1,0:T(8,128)(2,1)} %get-tuple-element.14.block_ref.own_ref), channel_id=1, source_target_pairs={{0,32},{8,40},{16,48},{24,56},{32,0},{40,8},{48,16},{56,24},{64,96... | collective-permute-start | bytes 1179656 | tf_op jit(solution)/shard_map/ppermute | solution.py:38
  8.7 1.7 %copy-start = (bf16[384,3072]{1,0:T(8,128)(2,1)S(1)}, bf16[384,3072]{1,0:T(8,128)(2,1)}, u32[]{:S(2)}) copy-start(bf16[384,3072]{1,0:T(8,128)(2,1)} %weight_ref.1) | copy-start | bytes 7077892
  10.4 3.6 %copy-start.1 = (bf16[272,384]{1,0:T(8,128)(2,1)S(1)}, bf16[272,384]{1,0:T(8,128)(2,1)}, u32[]{:S(2)}) copy-start(bf16[272,384]{1,0:T(8,128)(2,1)} %get-tuple-element.13.query_ref) | copy-start | bytes 626692
  10.4 8.9 %copy-start.2 = (bf16[512,384]{1,0:T(8,128)(2,1)S(1)}, bf16[512,384]{1,0:T(8,128)(2,1)}, u32[]{:S(2)}) copy-start(bf16[512,384]{1,0:T(8,128)(2,1)} %get-tuple-element.14.block_ref.own_ref) | copy-start | bytes 1179652
  10.5 19.8 %collective-permute-start.4 = (bf16[384,768]{1,0:T(8,128)(2,1)S(1)}, bf16[384,768]{1,0:T(8,128)(2,1)S(1)}, u32[]{:S(2)}, u32[]{:S(2)}) collective-permute-start(bf16[384,768]{1,0:T(8,128)(2,1)S(1)} %get-tuple-element.17), channel_id=1, source_target_pairs={{0,4},{4,0},{1,5},{5,1},{2,6},{6,2},{3,7},{7,3},{8,12},{12,8},{9,1... | collective-permute-start | bytes 1769480 | tf_op jit(solution)/shard_map/ppermute | solution.py:51
  14.0 5.3 %collective-permute-start.2 = (bf16[272,384]{1,0:T(8,128)(2,1)S(1)}, bf16[272,384]{1,0:T(8,128)(2,1)S(1)}, u32[]{:S(2)}, u32[]{:S(2)}) collective-permute-start(bf16[272,384]{1,0:T(8,128)(2,1)S(1)} %copy-done.1), channel_id=1, source_target_pairs={{0,8},{8,0},{16,24},{24,16},{32,40},{40,32},{48,56},{56,48},{64,72... | collective-permute-start | bytes 626696 | tf_op jit(solution)/shard_map/ppermute | solution.py:42
  15.9 16.8 %collective-permute-start.6 = (bf16[272,384]{1,0:T(8,128)(2,1)S(1)}, bf16[272,384]{1,0:T(8,128)(2,1)S(1)}, u32[]{:S(2)}, u32[]{:S(2)}) collective-permute-start(bf16[272,384]{1,0:T(8,128)(2,1)S(1)} %copy-done.1), channel_id=1, source_target_pairs={{8,16},{16,8},{40,48},{48,40},{72,80},{80,72},{104,112},{112,104},... | collective-permute-start | bytes 626696 | tf_op jit(solution)/shard_map/ppermute | solution.py:47
  28.3 11.6 %collective-permute-start.3 = (bf16[272,384]{1,0:T(8,128)(2,1)S(1)}, bf16[272,384]{1,0:T(8,128)(2,1)S(1)}, u32[]{:S(2)}, u32[]{:S(2)}) collective-permute-start(bf16[272,384]{1,0:T(8,128)(2,1)S(1)} %attend_pair.1.after_ref), channel_id=1, source_target_pairs={{0,8},{8,0},{16,24},{24,16},{32,40},{40,32},{48,56},{56,48},{64,72... | collective-permute-start | bytes 626696 | tf_op jit(solution)/shard_map/ppermute | solution.py:42
  30.3 9.7 %collective-permute-start.5 = (bf16[384,768]{1,0:T(8,128)(2,1)S(1)}, bf16[384,768]{1,0:T(8,128)(2,1)S(1)}, u32[]{:S(2)}, u32[]{:S(2)}) collective-permute-start(bf16[384,768]{1,0:T(8,128)(2,1)S(1)} %collective-permute-done.4.this_ref), channel_id=1, source_target_pairs={{0,8},{8,0},{16,24},{24,16},{32,40},{40,32},{48,56},{56,48},{64,72... | collective-permute-start | bytes 1769480 | tf_op jit(solution)/shard_map/ppermute | solution.py:42
  34.3 9.2 %collective-permute-start.7 = (bf16[272,384]{1,0:T(8,128)(2,1)S(1)}, bf16[272,384]{1,0:T(8,128)(2,1)S(1)}, u32[]{:S(2)}, u32[]{:S(2)}) collective-permute-start(bf16[272,384]{1,0:T(8,128)(2,1)S(1)} %attend_middle.1), channel_id=1, source_target_pairs={{8,16},{16,8},{40,48},{48,40},{72,80},{80,72},{104,112},{112,104},... | collective-permute-start | bytes 626696 | tf_op jit(solution)/shard_map/ppermute | solution.py:47
  43.9 9.1 %collective-permute-start.8 = (bf16[256,384]{1,0:T(8,128)(2,1)S(1)}, bf16[256,384]{1,0:T(8,128)(2,1)S(1)}, u32[]{:S(2)}, u32[]{:S(2)}) collective-permute-start(bf16[256,384]{1,0:T(8,128)(2,1)S(1)} %merge.1.mine_ref), channel_id=1, source_target_pairs={{0,4},{4,0},{1,5},{5,1},{2,6},{6,2},{3,7},{7,3},{8,12},{12,8},{9,1... | collective-permute-start | bytes 589832 | tf_op jit(solution)/shard_map/ppermute | solution.py:51
  54.3 7.6 %copy-start.4 = (f32[384]{0:T(512)S(1)}, f32[384]{0:T(512)}, u32[]{:S(2)}) copy-start(f32[384]{0:T(512)} %param.13) | copy-start | bytes 4612
  54.4 15.1 %copy-start.3 = (bf16[256,384]{1,0:T(8,128)(2,1)S(1)}, bf16[256,384]{1,0:T(8,128)(2,1)}, u32[]{:S(2)}) copy-start(bf16[256,384]{1,0:T(8,128)(2,1)} %residual_ref.1) | copy-start | bytes 589828
  54.4 15.0 %all-to-all-start = ((bf16[4,256,384]{2,1,0:T(8,128)(2,1)}), bf16[4,256,384]{2,1,0:T(8,128)(2,1)S(1)}, u32[]{:S(2)}, u32[]{:S(2)}) async-start(bf16[4,256,384]{2,1,0:T(8,128)(2,1)} %project.1), calls=%async_computation | async-start | bytes 1572864 | tf_op jit(solution)/shard_map/all_to_all | solution.py:431

commit v17 on v16

--- a/solution.py
+++ b/solution.py
@@ -14,7 +14,9 @@
 LOG2E = 1.4426950408889634
 MASKED = -1e30
 LAST_FLOPS = 400_000_000
-MIDDLE_FLOPS = 6000_000_000
+MIDDLE_FLOPS = 600_000_000
+PAIR_FLOPS = 400_000_000
+HERE_FLOPS = 3_000_000_000
 MESH_AXES = ("tile", "head")
 VMEM = pltpu.VMEM
 SMEM = pltpu.SMEM
@@ -138,11 +140,11 @@
     side = jnp.zeros((8, rows), jnp.float32)
     for index, piece in enumerate(split_float(stats[row : row + 1]) + split_float(stats[row + 1 : row + 2])):
         side = jnp.where(line == index, piece, side)
-    ref[rows:, low : low + HD] = jnp.concatenate([side[:, :HD], side[:, HD:]], axis=0).astype(ref.dtype)
+    ref[rows : rows + SIDE, low : low + HD] = jnp.concatenate([side[:, :HD], side[:, HD:]], axis=0).astype(ref.dtype)
 
 
 def message_stats(ref, head, rows):
-    side = ref[rows:, head * HD : (head + 1) * HD].astype(jnp.float32)
+    side = ref[rows : rows + SIDE, head * HD : (head + 1) * HD].astype(jnp.float32)
     side = jnp.concatenate([side[:8], side[8:]], axis=1)
     return side[0:1] + side[1:2] + side[2:3], side[3:4] + side[4:5] + side[5:6]
 
@@ -219,8 +221,30 @@
     return stats_ref[2 * index], stats_ref[2 * index + 1], mix_ref[index]
 
 
-def pair_kernel(query_ref, first_ref, second_ref, mix_ref, stats_ref, out_ref):
+def here_kernel(*refs):
+    refs[-1][...] = jnp.zeros_like(refs[-1])
+
+
+def all_here(*arrays):
+    return pl.pallas_call(
+        here_kernel,
+        out_shape=jax.ShapeDtypeStruct((8, HD), jnp.float32),
+        in_specs=[pl.BlockSpec(memory_space=pl.ANY)] * len(arrays),
+        out_specs=pl.BlockSpec(memory_space=VMEM),
+        compiler_params=params(4),
+        cost_estimate=pl.CostEstimate(flops=HERE_FLOPS, bytes_accessed=0, transcendentals=0),
+        name="all_here",
+    )(*arrays)
+
+
+def half_rows(weight_shape, rows, width):
+    return [rows + SIDE + part * weight_shape[0] for part in range(weight_shape[1] // width)]
+
+
+def pair_kernel(query_ref, first_ref, second_ref, mix_ref, stats_ref, weight_ref, after_ref, out_ref):
     rows, width = first_ref.shape[0] // 2, first_ref.shape[1]
+    for part, start in enumerate(half_rows(weight_ref.shape, rows, width)):
+        out_ref[start : start + weight_ref.shape[0]] = weight_ref[:, part * width : (part + 1) * width]
     biases = block_biases(query_ref, rows)
     for head in range(width // HD):
         low = head * HD
@@ -229,17 +253,18 @@
         put_message(out_ref, head, mix, row_stats(largest, total), 0)
 
 
-def attend_pair(query, first, second, mix, stats):
+def attend_pair(query, first, second, mix, stats, weight, after):
+    rows, width = query.shape
     whole = pl.BlockSpec(memory_space=VMEM)
     return pl.pallas_call(
         pair_kernel,
-        out_shape=jax.ShapeDtypeStruct(query.shape, jnp.bfloat16),
-        in_specs=[whole] * 5,
+        out_shape=jax.ShapeDtypeStruct((rows + weight.size // width, width), jnp.bfloat16),
+        in_specs=[whole] * 6 + [pl.BlockSpec(memory_space=pl.ANY)],
         out_specs=whole,
         compiler_params=params(24),
-        cost_estimate=pl.CostEstimate(flops=4_000_000_000, bytes_accessed=2_000_000, transcendentals=0),
+        cost_estimate=pl.CostEstimate(flops=PAIR_FLOPS, bytes_accessed=2_000_000, transcendentals=0),
         name="attend_pair",
-    )(query, first, second, mix, stats)
+    )(query, first, second, mix, stats, weight, after)
 
 
 def middle_kernel(query_ref, own_ref, first_ref, second_ref, after_ref, out_ref):
@@ -274,7 +299,7 @@
     )(query, own, first, second, after)
 
 
-def last_kernel(query_ref, first_ref, second_ref, old_mix_ref, old_stats_ref, message_ref, after_ref, mix_ref, stats_ref):
+def last_kernel(query_ref, first_ref, second_ref, old_mix_ref, old_stats_ref, message_ref, mix_ref, stats_ref):
     rows, width = first_ref.shape[0] // 2, first_ref.shape[1]
     wide = wide_window(query_ref, rows, 1)
     biases = block_biases(query_ref, rows)
@@ -291,7 +316,7 @@
         stats_ref[head] = jnp.where(line == 2, jnp.where(wide, 1.0, 0.0), stats)
 
 
-def attend_last(queries, first, second, mix, stats, message, after):
+def attend_last(queries, first, second, mix, stats, message):
     rows, width = first.shape[0] // 2, first.shape[1]
     whole = pl.BlockSpec(memory_space=VMEM)
     return pl.pallas_call(
@@ -300,12 +325,12 @@
             jax.ShapeDtypeStruct((rows, width), jnp.float32),
             jax.ShapeDtypeStruct((width // HD, 8, rows), jnp.float32),
         ),
-        in_specs=[whole] * 6 + [pl.BlockSpec(memory_space=pl.ANY)],
+        in_specs=[whole] * 6,
         out_specs=(whole, whole),
         compiler_params=params(24),
         cost_estimate=pl.CostEstimate(flops=LAST_FLOPS, bytes_accessed=2_000_000, transcendentals=0),
         name="attend_last",
-    )(queries, first, second, mix, stats, message, after)
+    )(queries, first, second, mix, stats, message)
 
 
 def merge_kernel(own_ref, stats_ref, middle_ref, out_ref):
@@ -368,12 +393,15 @@
 
 
 def project_kernel(mine_ref, theirs_ref, this_ref, other_ref, out_ref, held_ref, sems):
-    width, half = theirs_ref.shape[1], this_ref.shape[1]
+    rows, width = theirs_ref.shape
     core = lax.rem(lax.axis_index("tile"), 2)
+    starts = half_rows(this_ref.shape, rows, width)
     copies = []
     for group in range(out_ref.shape[0]):
-        side, start = divmod(group * width, half)
-        their_weight = jnp.where(side == core, this_ref[:, start : start + width], other_ref[:, start : start + width])
+        side, part = divmod(group, len(starts))
+        this = this_ref[:, part * width : (part + 1) * width]
+        other = other_ref[starts[part] : starts[part] + this.shape[0]]
+        their_weight = jnp.where(side == core, this, other)
         product = jnp.dot(theirs_ref[...], their_weight, preferred_element_type=jnp.float32)
         held_ref[group] = (mine_ref[group] + product).astype(held_ref.dtype)
         copies.append(pltpu.make_async_copy(held_ref.at[group], out_ref.at[group], sems.at[group]))
@@ -382,7 +410,7 @@
         copy.wait()
 
 
-def project(mine, theirs, this_half, other_half):
+def project(mine, theirs, this_half, pair_message):
     whole = pl.BlockSpec(memory_space=VMEM)
     return pl.pallas_call(
         project_kernel,
@@ -393,7 +421,7 @@
         compiler_params=params(24),
         cost_estimate=pl.CostEstimate(flops=300_000_000, bytes_accessed=5_000_000, transcendentals=0),
         name="project",
-    )(mine, theirs, this_half, other_half)
+    )(mine, theirs, this_half, pair_message)
 
 
 def finish_kernel(terms_ref, residual_ref, gate_ref, out_ref):
@@ -421,13 +449,14 @@
     my_weight, to_send = split_weight(out_weight)
     this_half = swap_far(to_send)
     mix, stats = attend_own(packed, pair_asks, block)
-    for_pair = attend_pair(pair_asks, first, second, mix, stats)
+    here = all_here(first, second, middle_asks)
+    for_pair = attend_pair(pair_asks, first, second, mix, stats, this_half, here)
     for_middle = attend_middle(middle_asks, block, first, second, for_pair)
-    other_half = swap_pair(this_half)
-    mix, stats = attend_last(packed, first, second, mix, stats, swap_pair(for_pair), other_half)
+    from_pair = swap_pair(for_pair)
+    mix, stats = attend_last(packed, first, second, mix, stats, from_pair)
     attention = merge(mix, stats, swap_middle(for_middle))
     mine = project_mine(attention, my_weight)
-    terms = project(mine, swap_far(attention), this_half, other_half)
+    terms = project(mine, swap_far(attention), this_half, from_pair)
     terms = lax.all_to_all(terms, "group", 0, 0)
     return finish(terms, residual, gate_scale)
 

time: 70.7 us -> 69.7 us (0.986)
  the two profiles are of different devices: /device:TPU:286 before, /device:TPU:1 now
where the time goes in v17:
time: 69.7 us; the launch traced here: 69.3 us
  starting transfers between devices  36.3 us (52%)
  waiting for transfers between devices  19.7 us (28%)
  Pallas kernels  11.4 us (16%)
  local copies, waits for them, and re-layouts  1.68 us (2%)
    ppermute x2, starting transfers between devices, swap_times(): return lax.ppermute(block, 'tile', route)  10.5 us
    ppermute x2, starting transfers between devices, swap_far(): return lax.ppermute(block, 'far', [(0, 1), (1, 0)])  9.43 us
    all_to_all x1, waiting for transfers between devices, shards(): terms = lax.all_to_all(terms, 'group', 0, 0)  8.64 us
    ppermute x2, waiting for transfers between devices, swap_middle(): return lax.ppermute(block, 'tile', route)  8.45 us
    ppermute x2, starting transfers between devices, swap_pair(): lax.ppermute(block, 'tile', [(tile, tile ^ 1) for tile, *_ in places()])  6.65 us
    ppermute x2, starting transfers between devices, swap_middle(): return lax.ppermute(block, 'tile', route)  5.3 us
    all_to_all x1, starting transfers between devices, shards(): terms = lax.all_to_all(terms, 'group', 0, 0)  4.43 us
    ppermute x2, waiting for transfers between devices, swap_far(): return lax.ppermute(block, 'far', [(0, 1), (1, 0)])  2.63 us
  transfers between devices with their start and end apart: 9, of which 4 were waited for; matrix products, arithmetic and copies ran while one was open for 0% of the time, Pallas kernels for 8%

profile of v17, /device:TPU:1, one launch (start us, length us, event | category | flops | bytes accessed | tf_op | source)
XLA Modules:
  0.0 69.3 jit_solution(10318121980208083241)
XLA Ops:
  0.0 2.0 %pack.1 = (bf16[272,384]{1,0:T(8,128)(2,1)}, bf16[512,384]{1,0:T(8,128)(2,1)}) custom-call(s32[1,3]{1,0:T(1,128)} %windows_ref.1, bf16[256,384]{1,0:T(8,128)(2,1)} %q_ref.1, bf16[256,384]{1,0:T(8,128)(2,1)} %k_ref.1, bf16[256,384]{1,0:T(8,128)(2,1)} %v_ref.1), custom_call_target="tpu_custom_call" | custom-call | tf_op jit(solution)/shard_map/pack/pallas_call | solution.py:95
  2.0 0.7 collective-permute-start
  2.7 9.8 %collective-permute-start.1 = (bf16[512,384]{1,0:T(8,128)(2,1)}, bf16[512,384]{1,0:T(8,128)(2,1)S(1)}, u32[]{:S(2)}, u32[]{:S(2)}) collective-permute-start(bf16[512,384]{1,0:T(8,128)(2,1)} %get-tuple-element.14.block_ref.own_ref), channel_id=1, source_target_pairs={{0,32},{8,40},{16,48},{24,56},{32,0},{40,8},{48,16},{56,24},{64,96... | collective-permute-start | bytes 1179656 | tf_op jit(solution)/shard_map/ppermute | solution.py:40
  12.5 0.0 copy-start
  12.5 1.7 %copy-done = bf16[384,3072]{1,0:T(8,128)(2,1)S(1)} copy-done((bf16[384,3072]{1,0:T(8,128)(2,1)S(1)}, bf16[384,3072]{1,0:T(8,128)(2,1)}, u32[]{:S(2)}) %copy-start) | copy-done | bytes 2359320
  14.1 0.1 split_weight.1
  14.3 4.8 %collective-permute-start.3 = (bf16[384,768]{1,0:T(8,128)(2,1)S(1)}, bf16[384,768]{1,0:T(8,128)(2,1)S(1)}, u32[]{:S(2)}, u32[]{:S(2)}) collective-permute-start(bf16[384,768]{1,0:T(8,128)(2,1)S(1)} %get-tuple-element.17), channel_id=1, source_target_pairs={{0,4},{4,0},{1,5},{5,1},{2,6},{6,2},{3,7},{7,3},{8,12},{12,8},{9,1... | collective-permute-start | bytes 1769480 | tf_op jit(solution)/shard_map/ppermute | solution.py:53
  19.1 3.4 %collective-permute-start.2 = (bf16[272,384]{1,0:T(8,128)(2,1)S(1)}, bf16[272,384]{1,0:T(8,128)(2,1)S(1)}, u32[]{:S(2)}, u32[]{:S(2)}) collective-permute-start(bf16[272,384]{1,0:T(8,128)(2,1)S(1)} %copy-done.2), channel_id=1, source_target_pairs={{0,8},{8,0},{16,24},{24,16},{32,40},{40,32},{48,56},{56,48},{64,72... | collective-permute-start | bytes 626696 | tf_op jit(solution)/shard_map/ppermute | solution.py:44
  22.5 2.2 %collective-permute-start.4 = (bf16[272,384]{1,0:T(8,128)(2,1)S(1)}, bf16[272,384]{1,0:T(8,128)(2,1)S(1)}, u32[]{:S(2)}, u32[]{:S(2)}) collective-permute-start(bf16[272,384]{1,0:T(8,128)(2,1)S(1)} %copy-done.2), channel_id=1, source_target_pairs={{8,16},{16,8},{40,48},{48,40},{72,80},{80,72},{104,112},{112,104},... | collective-permute-start | bytes 626696 | tf_op jit(solution)/shard_map/ppermute | solution.py:49
  24.7 0.0 collective-permute-done.2.pair_ref.query_ref
  24.7 1.0 %attend_own.1 = (f32[6,256,128]{2,1,0:T(8,128)S(1)}, f32[12,256,128]{2,1,0:T(8,128)S(1)}) custom-call(bf16[272,384]{1,0:T(8,128)(2,1)S(1)} %copy-done.2, bf16[272,384]{1,0:T(8,128)(2,1)S(1)} %collective-permute-done.2.pair_ref.query_ref, bf16[512,384]{1,0:T(8,128)(2,1)S(1)} %copy-done.1), custom_call_target="tpu_custom_call" | custom-call | tf_op jit(solution)/shard_map/attend_own/pallas_call | solution.py:205
  25.7 6.5 %collective-permute-done.4.refs_2_.query_ref = bf16[272,384]{1,0:T(8,128)(2,1)S(1)} collective-permute-done((bf16[272,384]{1,0:T(8,128)(2,1)S(1)}, bf16[272,384]{1,0:T(8,128)(2,1)S(1)}, u32[]{:S(2)}, u32[]{:S(2)}) %collective-permute-start.4) | collective-permute-done | bytes 208928 | tf_op jit(solution)/shard_map/ppermute | solution.py:49
  32.2 0.0 collective-permute-done.refs_0_.first_ref
  32.2 0.0 collective-permute-done.1.refs_1_.second_ref
  32.2 0.0 collective-permute-done.3.weight_ref.this_ref
  32.2 1.4 %attend_pair.1.after_ref = bf16[1040,384]{1,0:T(8,128)(2,1)S(1)} custom-call(bf16[272,384]{1,0:T(8,128)(2,1)S(1)} %collective-permute-done.2.pair_ref.query_ref, bf16[512,384]{1,0:T(8,128)(2,1)S(1)} %collective-permute-done.refs_0_.first_ref, bf16[512,384]{1,0:T(8,128)(2,1)S(1)} %collective-permute-done.1.refs_1_.second_ref, ...), custom_call_target="tpu_custom_call" | custom-call | flops 400000000 | bytes 2000000 | tf_op jit(solution)/shard_map/attend_pair/pallas_call | solution.py:259
  33.6 3.2 %collective-permute-start.5 = (bf16[1040,384]{1,0:T(8,128)(2,1)S(1)}, bf16[1040,384]{1,0:T(8,128)(2,1)S(1)}, u32[]{:S(2)}, u32[]{:S(2)}) collective-permute-start(bf16[1040,384]{1,0:T(8,128)(2,1)S(1)} %attend_pair.1.after_ref), channel_id=1, source_target_pairs={{0,8},{8,0},{16,24},{24,16},{32,40},{40,32},{48,56},{56,48},{64,72... | collective-permute-start | bytes 2396168 | tf_op jit(solution)/shard_map/ppermute | solution.py:44
  36.8 1.6 %attend_middle.1 = bf16[272,384]{1,0:T(8,128)(2,1)S(1)} custom-call(bf16[272,384]{1,0:T(8,128)(2,1)S(1)} %collective-permute-done.4.refs_2_.query_ref, bf16[512,384]{1,0:T(8,128)(2,1)S(1)} %copy-done.1, bf16[512,384]{1,0:T(8,128)(2,1)S(1)} %collective-permute-done.refs_0_.first_ref, bf16[512,384]{1,0:T(8,128)(2,1)S(1)} %collective-permute-done.1.refs_1_.second_ref, ...), custom_call_target="tpu_custom_call" | custom-call | flops 600000000 | bytes 2000000 | tf_op jit(solution)/shard_map/attend_middle/pallas_call | solution.py:291
  38.4 3.1 %collective-permute-start.6 = (bf16[272,384]{1,0:T(8,128)(2,1)S(1)}, bf16[272,384]{1,0:T(8,128)(2,1)S(1)}, u32[]{:S(2)}, u32[]{:S(2)}) collective-permute-start(bf16[272,384]{1,0:T(8,128)(2,1)S(1)} %attend_middle.1), channel_id=1, source_target_pairs={{8,16},{16,8},{40,48},{48,40},{72,80},{80,72},{104,112},{112,104},... | collective-permute-start | bytes 626696 | tf_op jit(solution)/shard_map/ppermute | solution.py:49
  41.5 0.0 collective-permute-done.5.message_ref.other_ref
  41.5 2.0 %attend_last.1 = (f32[256,384]{1,0:T(8,128)S(1)}, f32[3,8,256]{2,1,0:T(8,128)S(1)}) custom-call(bf16[272,384]{1,0:T(8,128)(2,1)S(1)} %copy-done.2, bf16[512,384]{1,0:T(8,128)(2,1)S(1)} %collective-permute-done.refs_0_.first_ref, bf16[512,384]{1,0:T(8,128)(2,1)S(1)} %collective-permute-done.1.refs_1_.second_ref, ...), custom_call_target="tpu_custom_call" | custom-call | flops 400000000 | bytes 2000000 | tf_op jit(solution)/shard_map/attend_last/pallas_call | solution.py:322
  43.6 2.0 %collective-permute-done.6.middle_ref = bf16[272,384]{1,0:T(8,128)(2,1)S(1)} collective-permute-done((bf16[272,384]{1,0:T(8,128)(2,1)S(1)}, bf16[272,384]{1,0:T(8,128)(2,1)S(1)}, u32[]{:S(2)}, u32[]{:S(2)}) %collective-permute-start.6) | collective-permute-done | bytes 208928 | tf_op jit(solution)/shard_map/ppermute | solution.py:49
  45.5 0.5 merge.1.mine_ref
  46.0 4.6 %collective-permute-start.7 = (bf16[256,384]{1,0:T(8,128)(2,1)S(1)}, bf16[256,384]{1,0:T(8,128)(2,1)S(1)}, u32[]{:S(2)}, u32[]{:S(2)}) collective-permute-start(bf16[256,384]{1,0:T(8,128)(2,1)S(1)} %merge.1.mine_ref), channel_id=1, source_target_pairs={{0,4},{4,0},{1,5},{5,1},{2,6},{6,2},{3,7},{7,3},{8,12},{12,8},{9,1... | collective-permute-start | bytes 589832 | tf_op jit(solution)/shard_map/ppermute | solution.py:53
  50.7 0.6 project_mine.1.mine_ref
  51.3 2.6 %collective-permute-done.7.theirs_ref = bf16[256,384]{1,0:T(8,128)(2,1)S(1)} collective-permute-done((bf16[256,384]{1,0:T(8,128)(2,1)S(1)}, bf16[256,384]{1,0:T(8,128)(2,1)S(1)}, u32[]{:S(2)}, u32[]{:S(2)}) %collective-permute-start.7) | collective-permute-done | bytes 196640 | tf_op jit(solution)/shard_map/ppermute | solution.py:53
  53.9 1.4 %project.1 = bf16[4,256,384]{2,1,0:T(8,128)(2,1)} custom-call(f32[4,256,384]{2,1,0:T(8,128)S(1)} %project_mine.1.mine_ref, bf16[256,384]{1,0:T(8,128)(2,1)S(1)} %collective-permute-done.7.theirs_ref, bf16[384,768]{1,0:T(8,128)(2,1)S(1)} %collective-permute-done.3.weight_ref.this_ref, bf16[1040,384]{1,0:T(8,128)(2,1)S(1)} %collective-permute-done.5.message_ref.other_ref), custom_call_target="tpu_custom_call" | custom-call | flops 300000000 | bytes 5000000 | tf_op jit(solution)/shard_map/project/pallas_call | solution.py:415
  55.4 0.0 copy-start.4
  55.4 0.0 copy-start.3
  55.4 4.4 %all-to-all-start = ((bf16[4,256,384]{2,1,0:T(8,128)(2,1)}), bf16[4,256,384]{2,1,0:T(8,128)(2,1)S(1)}, u32[]{:S(2)}, u32[]{:S(2)}) async-start(bf16[4,256,384]{2,1,0:T(8,128)(2,1)} %project.1), calls=%async_computation | async-start | bytes 1572864 | tf_op jit(solution)/shard_map/all_to_all | solution.py:460
  59.8 8.6 %all-to-all-done.terms_ref = bf16[4,256,384]{2,1,0:T(8,128)(2,1)S(1)} async-done(((bf16[4,256,384]{2,1,0:T(8,128)(2,1)}), bf16[4,256,384]{2,1,0:T(8,128)(2,1)S(1)}, u32[]{:S(2)}, u32[]{:S(2)}) %all-to-all-start) | async-done | bytes 786464 | tf_op jit(solution)/shard_map/all_to_all | solution.py:460
  68.5 0.8 %finish.1 = bf16[256,384]{1,0:T(8,128)(2,1)} custom-call(bf16[4,256,384]{2,1,0:T(8,128)(2,1)S(1)} %all-to-all-done.terms_ref, bf16[256,384]{1,0:T(8,128)(2,1)S(1)} %copy-done.3, f32[1,384]{1,0:T(1,128)S(1)} %reshape.3.gate_ref), custom_call_target="tpu_custom_call" | custom-call | flops 3932160 | bytes 2000000 | tf_op jit(solution)/shard_map/finish/pallas_call | solution.py:434
  (8 shorter events, 0.0 us)
Async XLA Ops:
  2.0 30.2 %collective-permute-start = (bf16[512,384]{1,0:T(8,128)(2,1)}, bf16[512,384]{1,0:T(8,128)(2,1)S(1)}, u32[]{:S(2)}, u32[]{:S(2)}) collective-permute-start(bf16[512,384]{1,0:T(8,128)(2,1)} %get-tuple-element.14.block_ref.own_ref), channel_id=1, source_target_pairs={{32,64},{40,72},{48,80},{56,88},{64,32},{72,40},{80,48},{88,56},{9... | collective-permute-start | bytes 1179656 | tf_op jit(solution)/shard_map/ppermute | solution.py:40
  2.7 29.5 %collective-permute-start.1 = (bf16[512,384]{1,0:T(8,128)(2,1)}, bf16[512,384]{1,0:T(8,128)(2,1)S(1)}, u32[]{:S(2)}, u32[]{:S(2)}) collective-permute-start(bf16[512,384]{1,0:T(8,128)(2,1)} %get-tuple-element.14.block_ref.own_ref), channel_id=1, source_target_pairs={{0,32},{8,40},{16,48},{24,56},{32,0},{40,8},{48,16},{56,24},{64,96... | collective-permute-start | bytes 1179656 | tf_op jit(solution)/shard_map/ppermute | solution.py:40
  12.5 1.7 %copy-start = (bf16[384,3072]{1,0:T(8,128)(2,1)S(1)}, bf16[384,3072]{1,0:T(8,128)(2,1)}, u32[]{:S(2)}) copy-start(bf16[384,3072]{1,0:T(8,128)(2,1)} %weight_ref.1) | copy-start | bytes 7077892
  14.1 4.9 %copy-start.2 = (bf16[272,384]{1,0:T(8,128)(2,1)S(1)}, bf16[272,384]{1,0:T(8,128)(2,1)}, u32[]{:S(2)}) copy-start(bf16[272,384]{1,0:T(8,128)(2,1)} %get-tuple-element.13.query_ref) | copy-start | bytes 626692
  14.1 10.6 %copy-start.1 = (bf16[512,384]{1,0:T(8,128)(2,1)S(1)}, bf16[512,384]{1,0:T(8,128)(2,1)}, u32[]{:S(2)}) copy-start(bf16[512,384]{1,0:T(8,128)(2,1)} %get-tuple-element.14.block_ref.own_ref) | copy-start | bytes 1179652
  14.3 18.0 %collective-permute-start.3 = (bf16[384,768]{1,0:T(8,128)(2,1)S(1)}, bf16[384,768]{1,0:T(8,128)(2,1)S(1)}, u32[]{:S(2)}, u32[]{:S(2)}) collective-permute-start(bf16[384,768]{1,0:T(8,128)(2,1)S(1)} %get-tuple-element.17), channel_id=1, source_target_pairs={{0,4},{4,0},{1,5},{5,1},{2,6},{6,2},{3,7},{7,3},{8,12},{12,8},{9,1... | collective-permute-start | bytes 1769480 | tf_op jit(solution)/shard_map/ppermute | solution.py:53
  19.1 5.6 %collective-permute-start.2 = (bf16[272,384]{1,0:T(8,128)(2,1)S(1)}, bf16[272,384]{1,0:T(8,128)(2,1)S(1)}, u32[]{:S(2)}, u32[]{:S(2)}) collective-permute-start(bf16[272,384]{1,0:T(8,128)(2,1)S(1)} %copy-done.2), channel_id=1, source_target_pairs={{0,8},{8,0},{16,24},{24,16},{32,40},{40,32},{48,56},{56,48},{64,72... | collective-permute-start | bytes 626696 | tf_op jit(solution)/shard_map/ppermute | solution.py:44
  22.5 9.7 %collective-permute-start.4 = (bf16[272,384]{1,0:T(8,128)(2,1)S(1)}, bf16[272,384]{1,0:T(8,128)(2,1)S(1)}, u32[]{:S(2)}, u32[]{:S(2)}) collective-permute-start(bf16[272,384]{1,0:T(8,128)(2,1)S(1)} %copy-done.2), channel_id=1, source_target_pairs={{8,16},{16,8},{40,48},{48,40},{72,80},{80,72},{104,112},{112,104},... | collective-permute-start | bytes 626696 | tf_op jit(solution)/shard_map/ppermute | solution.py:49
  33.6 7.9 %collective-permute-start.5 = (bf16[1040,384]{1,0:T(8,128)(2,1)S(1)}, bf16[1040,384]{1,0:T(8,128)(2,1)S(1)}, u32[]{:S(2)}, u32[]{:S(2)}) collective-permute-start(bf16[1040,384]{1,0:T(8,128)(2,1)S(1)} %attend_pair.1.after_ref), channel_id=1, source_target_pairs={{0,8},{8,0},{16,24},{24,16},{32,40},{40,32},{48,56},{56,48},{64,72... | collective-permute-start | bytes 2396168 | tf_op jit(solution)/shard_map/ppermute | solution.py:44
  38.4 7.1 %collective-permute-start.6 = (bf16[272,384]{1,0:T(8,128)(2,1)S(1)}, bf16[272,384]{1,0:T(8,128)(2,1)S(1)}, u32[]{:S(2)}, u32[]{:S(2)}) collective-permute-start(bf16[272,384]{1,0:T(8,128)(2,1)S(1)} %attend_middle.1), channel_id=1, source_target_pairs={{8,16},{16,8},{40,48},{48,40},{72,80},{80,72},{104,112},{112,104},... | collective-permute-start | bytes 626696 | tf_op jit(solution)/shard_map/ppermute | solution.py:49
  46.0 7.9 %collective-permute-start.7 = (bf16[256,384]{1,0:T(8,128)(2,1)S(1)}, bf16[256,384]{1,0:T(8,128)(2,1)S(1)}, u32[]{:S(2)}, u32[]{:S(2)}) collective-permute-start(bf16[256,384]{1,0:T(8,128)(2,1)S(1)} %merge.1.mine_ref), channel_id=1, source_target_pairs={{0,4},{4,0},{1,5},{5,1},{2,6},{6,2},{3,7},{7,3},{8,12},{12,8},{9,1... | collective-permute-start | bytes 589832 | tf_op jit(solution)/shard_map/ppermute | solution.py:53
  55.4 4.5 %copy-start.4 = (f32[384]{0:T(512)S(1)}, f32[384]{0:T(512)}, u32[]{:S(2)}) copy-start(f32[384]{0:T(512)} %param.13) | copy-start | bytes 4612
  55.4 13.1 %copy-start.3 = (bf16[256,384]{1,0:T(8,128)(2,1)S(1)}, bf16[256,384]{1,0:T(8,128)(2,1)}, u32[]{:S(2)}) copy-start(bf16[256,384]{1,0:T(8,128)(2,1)} %residual_ref.1) | copy-start | bytes 589828
  55.4 13.1 %all-to-all-start = ((bf16[4,256,384]{2,1,0:T(8,128)(2,1)}), bf16[4,256,384]{2,1,0:T(8,128)(2,1)S(1)}, u32[]{:S(2)}, u32[]{:S(2)}) async-start(bf16[4,256,384]{2,1,0:T(8,128)(2,1)} %project.1), calls=%async_computation | async-start | bytes 1572864 | tf_op jit(solution)/shard_map/all_to_all | solution.py:460

commit v18 on v17

--- a/solution.py
+++ b/solution.py
@@ -53,29 +53,30 @@
     return lax.ppermute(block, "far", [(0, 1), (1, 0)])
 
 
-def split_weight_kernel(weight_ref, mine_ref, theirs_ref):
-    width, half = mine_ref.shape[1], theirs_ref.shape[1]
-    far = lax.axis_index("far")
+def copy_columns(weight_ref, start, out_ref, sem):
+    return pltpu.make_async_copy(weight_ref.at[:, pl.ds(pl.multiple_of(start, HD), out_ref.shape[1])], out_ref, sem)
+
+
+def split_weight_kernel(weight_ref, theirs_ref, sem):
+    half = theirs_ref.shape[1]
     core = lax.rem(lax.axis_index("tile"), 2)
-    mine_ref[...] = weight_ref[:, pl.ds(pl.multiple_of(far * width, HD), width)]
-    theirs_ref[...] = weight_ref[:, pl.ds(pl.multiple_of((1 - far) * width + core * half, HD), half)]
+    copy = copy_columns(weight_ref, ((1 - lax.axis_index("far")) * 2 + core) * half, theirs_ref, sem)
+    copy.start()
+    copy.wait()
 
 
 def split_weight(out_weight):
     rows, features = out_weight.shape
-    whole = pl.BlockSpec(memory_space=VMEM)
     return pl.pallas_call(
         split_weight_kernel,
-        out_shape=(
-            jax.ShapeDtypeStruct((rows, features // 2), out_weight.dtype),
-            jax.ShapeDtypeStruct((rows, features // 4), out_weight.dtype),
-        ),
-        in_specs=[whole],
-        out_specs=(whole,) * 2,
+        out_shape=jax.ShapeDtypeStruct((rows, features // 4), out_weight.dtype),
+        in_specs=[pl.BlockSpec(memory_space=pl.ANY)],
+        out_specs=pl.BlockSpec(memory_space=VMEM),
+        scratch_shapes=[pltpu.SemaphoreType.DMA],
         compiler_params=params(24),
         cost_estimate=pl.CostEstimate(flops=0, bytes_accessed=0, transcendentals=0),
         name="split_weight",
-    )(out_weight)
+    )(pltpu.with_memory_space_constraint(out_weight, pltpu.HBM))
 
 
 def pack_kernel(windows_ref, q_ref, k_ref, v_ref, packed_ref, block_ref):
@@ -189,16 +190,19 @@
     return [block_bias(wide, stage) for stage in (1, 2)]
 
 
-def own_kernel(query_ref, pair_ref, block_ref, mix_ref, stats_ref):
+def own_kernel(query_ref, pair_ref, block_ref, weight_ref, mix_ref, stats_ref, mine_ref, sem):
+    copy = copy_columns(weight_ref, lax.axis_index("far") * mine_ref.shape[1], mine_ref, sem)
+    copy.start()
     rows, width = block_ref.shape[0] // 2, block_ref.shape[1]
     for place, ref in enumerate((query_ref, pair_ref)):
         for head in range(width // HD):
             low, index = head * HD, 2 * head + place
             largest, total, mix = attend(ref[:rows, low : low + HD], [block_ref], [0.0], low)
             mix_ref[index], stats_ref[2 * index], stats_ref[2 * index + 1] = mix, largest, total
-
-
-def attend_own(queries, pair, block):
+    copy.wait()
+
+
+def attend_own(queries, pair, block, out_weight):
     rows, width = block.shape[0] // 2, block.shape[1]
     heads = width // HD
     whole = pl.BlockSpec(memory_space=VMEM)
@@ -207,13 +211,15 @@
         out_shape=(
             jax.ShapeDtypeStruct((2 * heads, rows, HD), jnp.float32),
             jax.ShapeDtypeStruct((4 * heads, rows, HD), jnp.float32),
+            jax.ShapeDtypeStruct((out_weight.shape[0], out_weight.shape[1] // 2), out_weight.dtype),
         ),
-        in_specs=[whole] * 3,
-        out_specs=(whole,) * 2,
+        in_specs=[whole] * 3 + [pl.BlockSpec(memory_space=pl.ANY)],
+        out_specs=(whole,) * 3,
+        scratch_shapes=[pltpu.SemaphoreType.DMA],
         compiler_params=params(24),
         cost_estimate=pl.CostEstimate(flops=0, bytes_accessed=0, transcendentals=0),
         name="attend_own",
-    )(queries, pair, block)
+    )(queries, pair, block, pltpu.with_memory_space_constraint(out_weight, pltpu.HBM))
 
 
 def old_parts(mix_ref, stats_ref, head, place):
@@ -446,9 +452,8 @@
     packed, block = pack(windows, queries, key_rows, value_rows)
     first, second = swap_times(block, False), swap_times(block, True)
     pair_asks, middle_asks = swap_pair(packed), swap_middle(packed)
-    my_weight, to_send = split_weight(out_weight)
-    this_half = swap_far(to_send)
-    mix, stats = attend_own(packed, pair_asks, block)
+    this_half = swap_far(split_weight(out_weight))
+    mix, stats, my_weight = attend_own(packed, pair_asks, block, out_weight)
     here = all_here(first, second, middle_asks)
     for_pair = attend_pair(pair_asks, first, second, mix, stats, this_half, here)
     for_middle = attend_middle(middle_asks, block, first, second, for_pair)

time: 69.7 us -> 69.2 us (level)
  local copies, waits for them, and re-layouts: 1.68 us -> 0.02 us
  Pallas kernels: 11.4 us -> 12.7 us
    unnamed x10 -> x8, local copies, waits for them, and re-layouts: 1.68 us -> 0.02 us
    pallas_call x1, Pallas kernels: 0.12 us -> 1.09 us  [split_weight(): pl.pallas_call(split_weight_kernel, out_shape=jax.ShapeDtypeStruct((rows,...]
    ppermute x2, starting transfers between devices: 5.3 us -> 6.13 us  [swap_middle(): return lax.ppermute(block, 'tile', route)]
    ppermute x2, starting transfers between devices: 6.65 us -> 5.81 us  [swap_pair(): lax.ppermute(block, 'tile', [(tile, tile ^ 1) for tile, *_ in places()])]
  transfers between devices with their start and end apart: 9 -> 9, of which waited for: 4 -> 4; matrix products, arithmetic and copies ran while one was open for 0% -> 0% of each run, Pallas kernels for 8% -> 10%
where the time goes in v18:
time: 69.2 us; the launch traced here: 68.6 us
  starting transfers between devices  36.3 us (52%)
  waiting for transfers between devices  19.4 us (28%)
  Pallas kernels  12.7 us (18%)
    ppermute x2, starting transfers between devices, swap_times(): return lax.ppermute(block, 'tile', route)  10.6 us
    ppermute x2, starting transfers between devices, swap_far(): return lax.ppermute(block, 'far', [(0, 1), (1, 0)])  9.3 us
    ppermute x2, waiting for transfers between devices, swap_middle(): return lax.ppermute(block, 'tile', route)  8.41 us
    all_to_all x1, waiting for transfers between devices, shards(): terms = lax.all_to_all(terms, 'group', 0, 0)  8.37 us
    ppermute x2, starting transfers between devices, swap_middle(): return lax.ppermute(block, 'tile', route)  6.13 us
    ppermute x2, starting transfers between devices, swap_pair(): lax.ppermute(block, 'tile', [(tile, tile ^ 1) for tile, *_ in places()])  5.81 us
    all_to_all x1, starting transfers between devices, shards(): terms = lax.all_to_all(terms, 'group', 0, 0)  4.43 us
    ppermute x2, waiting for transfers between devices, swap_far(): return lax.ppermute(block, 'far', [(0, 1), (1, 0)])  2.63 us
  transfers between devices with their start and end apart: 9, of which 4 were waited for; matrix products, arithmetic and copies ran while one was open for 0% of the time, Pallas kernels for 10%

profile of v18, /device:TPU:1, one launch (start us, length us, event | category | flops | bytes accessed | tf_op | source)
XLA Modules:
  0.0 68.6 jit_solution(13250810531982370529)
XLA Ops:
  0.0 2.0 %pack.1 = (bf16[272,384]{1,0:T(8,128)(2,1)}, bf16[512,384]{1,0:T(8,128)(2,1)}) custom-call(s32[1,3]{1,0:T(1,128)} %windows_ref.1, bf16[256,384]{1,0:T(8,128)(2,1)} %q_ref.1, bf16[256,384]{1,0:T(8,128)(2,1)} %k_ref.1, bf16[256,384]{1,0:T(8,128)(2,1)} %v_ref.1), custom_call_target="tpu_custom_call" | custom-call | tf_op jit(solution)/shard_map/pack/pallas_call | solution.py:96
  2.0 0.8 %collective-permute-start = (bf16[512,384]{1,0:T(8,128)(2,1)}, bf16[512,384]{1,0:T(8,128)(2,1)S(1)}, u32[]{:S(2)}, u32[]{:S(2)}) collective-permute-start(bf16[512,384]{1,0:T(8,128)(2,1)} %get-tuple-element.13.block_ref.own_ref), channel_id=1, source_target_pairs={{32,64},{40,72},{48,80},{56,88},{64,32},{72,40},{80,48},{88,56},{9... | collective-permute-start | bytes 1179656 | tf_op jit(solution)/shard_map/ppermute | solution.py:40
  2.8 9.8 %collective-permute-start.1 = (bf16[512,384]{1,0:T(8,128)(2,1)}, bf16[512,384]{1,0:T(8,128)(2,1)S(1)}, u32[]{:S(2)}, u32[]{:S(2)}) collective-permute-start(bf16[512,384]{1,0:T(8,128)(2,1)} %get-tuple-element.13.block_ref.own_ref), channel_id=1, source_target_pairs={{0,32},{8,40},{16,48},{24,56},{32,0},{40,8},{48,16},{56,24},{64,96... | collective-permute-start | bytes 1179656 | tf_op jit(solution)/shard_map/ppermute | solution.py:40
  12.6 1.1 %split_weight.1 = bf16[384,768]{1,0:T(8,128)(2,1)S(1)} custom-call(bf16[384,3072]{1,0:T(8,128)(2,1)} %weight_ref.3), custom_call_target="tpu_custom_call" | custom-call | tf_op jit(solution)/shard_map/split_weight/pallas_call | solution.py:70
  13.7 4.7 %collective-permute-start.3 = (bf16[384,768]{1,0:T(8,128)(2,1)S(1)}, bf16[384,768]{1,0:T(8,128)(2,1)S(1)}, u32[]{:S(2)}, u32[]{:S(2)}) collective-permute-start(bf16[384,768]{1,0:T(8,128)(2,1)S(1)} %split_weight.1), channel_id=1, source_target_pairs={{0,4},{4,0},{1,5},{5,1},{2,6},{6,2},{3,7},{7,3},{8,12},{12,8},{9,1... | collective-permute-start | bytes 1769480 | tf_op jit(solution)/shard_map/ppermute | solution.py:53
  18.4 0.0 copy-done.1
  18.4 3.4 %collective-permute-start.2 = (bf16[272,384]{1,0:T(8,128)(2,1)S(1)}, bf16[272,384]{1,0:T(8,128)(2,1)S(1)}, u32[]{:S(2)}, u32[]{:S(2)}) collective-permute-start(bf16[272,384]{1,0:T(8,128)(2,1)S(1)} %copy-done.1), channel_id=1, source_target_pairs={{0,8},{8,0},{16,24},{24,16},{32,40},{40,32},{48,56},{56,48},{64,72... | collective-permute-start | bytes 626696 | tf_op jit(solution)/shard_map/ppermute | solution.py:44
  21.8 2.2 %collective-permute-start.4 = (bf16[272,384]{1,0:T(8,128)(2,1)S(1)}, bf16[272,384]{1,0:T(8,128)(2,1)S(1)}, u32[]{:S(2)}, u32[]{:S(2)}) collective-permute-start(bf16[272,384]{1,0:T(8,128)(2,1)S(1)} %copy-done.1), channel_id=1, source_target_pairs={{8,16},{16,8},{40,48},{48,40},{72,80},{80,72},{104,112},{112,104},... | collective-permute-start | bytes 626696 | tf_op jit(solution)/shard_map/ppermute | solution.py:49
  24.0 0.0 collective-permute-done.2.pair_ref.query_ref
  24.0 0.0 copy-done
  24.0 1.3 %attend_own.1 = (f32[6,256,128]{2,1,0:T(8,128)S(1)}, f32[12,256,128]{2,1,0:T(8,128)S(1)}, bf16[384,1536]{1,0:T(8,128)(2,1)S(1)}) custom-call(bf16[272,384]{1,0:T(8,128)(2,1)S(1)} %copy-done.1, bf16[272,384]{1,0:T(8,128)(2,1)S(1)} %collective-permute-done.2.pair_ref.query_ref, bf16[512,384]{1,0:T(8,128)(2,1)S(1)} %copy-done, bf16[384,3072]{1,0:T(8,128)(2,1)} %weight_ref.3), custom_call_target="tpu_custom_call" | custom-call | tf_op jit(solution)/shard_map/attend_own/pallas_call | solution.py:209
  25.3 7.0 %collective-permute-done.4.refs_2_.query_ref = bf16[272,384]{1,0:T(8,128)(2,1)S(1)} collective-permute-done((bf16[272,384]{1,0:T(8,128)(2,1)S(1)}, bf16[272,384]{1,0:T(8,128)(2,1)S(1)}, u32[]{:S(2)}, u32[]{:S(2)}) %collective-permute-start.4) | collective-permute-done | bytes 208928 | tf_op jit(solution)/shard_map/ppermute | solution.py:49
  32.3 0.0 collective-permute-done.refs_0_.first_ref
  32.3 0.0 collective-permute-done.1.refs_1_.second_ref
  32.4 0.0 collective-permute-done.3.weight_ref.this_ref
  32.4 1.4 %attend_pair.1.after_ref = bf16[1040,384]{1,0:T(8,128)(2,1)S(1)} custom-call(bf16[272,384]{1,0:T(8,128)(2,1)S(1)} %collective-permute-done.2.pair_ref.query_ref, bf16[512,384]{1,0:T(8,128)(2,1)S(1)} %collective-permute-done.refs_0_.first_ref, bf16[512,384]{1,0:T(8,128)(2,1)S(1)} %collective-permute-done.1.refs_1_.second_ref, ...), custom_call_target="tpu_custom_call" | custom-call | flops 400000000 | bytes 2000000 | tf_op jit(solution)/shard_map/attend_pair/pallas_call | solution.py:265
  33.8 2.4 %collective-permute-start.5 = (bf16[1040,384]{1,0:T(8,128)(2,1)S(1)}, bf16[1040,384]{1,0:T(8,128)(2,1)S(1)}, u32[]{:S(2)}, u32[]{:S(2)}) collective-permute-start(bf16[1040,384]{1,0:T(8,128)(2,1)S(1)} %attend_pair.1.after_ref), channel_id=1, source_target_pairs={{0,8},{8,0},{16,24},{24,16},{32,40},{40,32},{48,56},{56,48},{64,72... | collective-permute-start | bytes 2396168 | tf_op jit(solution)/shard_map/ppermute | solution.py:44
  36.2 1.6 %attend_middle.1 = bf16[272,384]{1,0:T(8,128)(2,1)S(1)} custom-call(bf16[272,384]{1,0:T(8,128)(2,1)S(1)} %collective-permute-done.4.refs_2_.query_ref, bf16[512,384]{1,0:T(8,128)(2,1)S(1)} %copy-done, bf16[512,384]{1,0:T(8,128)(2,1)S(1)} %collective-permute-done.refs_0_.first_ref, bf16[512,384]{1,0:T(8,128)(2,1)S(1)} %collective-permute-done.1.refs_1_.second_ref, ...), custom_call_target="tpu_custom_call" | custom-call | flops 600000000 | bytes 2000000 | tf_op jit(solution)/shard_map/attend_middle/pallas_call | solution.py:297
  37.7 3.9 %collective-permute-start.6 = (bf16[272,384]{1,0:T(8,128)(2,1)S(1)}, bf16[272,384]{1,0:T(8,128)(2,1)S(1)}, u32[]{:S(2)}, u32[]{:S(2)}) collective-permute-start(bf16[272,384]{1,0:T(8,128)(2,1)S(1)} %attend_middle.1), channel_id=1, source_target_pairs={{8,16},{16,8},{40,48},{48,40},{72,80},{80,72},{104,112},{112,104},... | collective-permute-start | bytes 626696 | tf_op jit(solution)/shard_map/ppermute | solution.py:49
  41.7 0.0 collective-permute-done.5.message_ref.other_ref
  41.7 2.1 %attend_last.1 = (f32[256,384]{1,0:T(8,128)S(1)}, f32[3,8,256]{2,1,0:T(8,128)S(1)}) custom-call(bf16[272,384]{1,0:T(8,128)(2,1)S(1)} %copy-done.1, bf16[512,384]{1,0:T(8,128)(2,1)S(1)} %collective-permute-done.refs_0_.first_ref, bf16[512,384]{1,0:T(8,128)(2,1)S(1)} %collective-permute-done.1.refs_1_.second_ref, ...), custom_call_target="tpu_custom_call" | custom-call | flops 400000000 | bytes 2000000 | tf_op jit(solution)/shard_map/attend_last/pallas_call | solution.py:328
  43.7 1.4 %collective-permute-done.6.middle_ref = bf16[272,384]{1,0:T(8,128)(2,1)S(1)} collective-permute-done((bf16[272,384]{1,0:T(8,128)(2,1)S(1)}, bf16[272,384]{1,0:T(8,128)(2,1)S(1)}, u32[]{:S(2)}, u32[]{:S(2)}) %collective-permute-start.6) | collective-permute-done | bytes 208928 | tf_op jit(solution)/shard_map/ppermute | solution.py:49
  45.1 0.5 merge.1.mine_ref
  45.6 4.6 %collective-permute-start.7 = (bf16[256,384]{1,0:T(8,128)(2,1)S(1)}, bf16[256,384]{1,0:T(8,128)(2,1)S(1)}, u32[]{:S(2)}, u32[]{:S(2)}) collective-permute-start(bf16[256,384]{1,0:T(8,128)(2,1)S(1)} %merge.1.mine_ref), channel_id=1, source_target_pairs={{0,4},{4,0},{1,5},{5,1},{2,6},{6,2},{3,7},{7,3},{8,12},{12,8},{9,1... | collective-permute-start | bytes 589832 | tf_op jit(solution)/shard_map/ppermute | solution.py:53
  50.3 0.6 project_mine.1.mine_ref
  50.9 2.6 %collective-permute-done.7.theirs_ref = bf16[256,384]{1,0:T(8,128)(2,1)S(1)} collective-permute-done((bf16[256,384]{1,0:T(8,128)(2,1)S(1)}, bf16[256,384]{1,0:T(8,128)(2,1)S(1)}, u32[]{:S(2)}, u32[]{:S(2)}) %collective-permute-start.7) | collective-permute-done | bytes 196640 | tf_op jit(solution)/shard_map/ppermute | solution.py:53
  53.5 1.4 %project.1 = bf16[4,256,384]{2,1,0:T(8,128)(2,1)} custom-call(f32[4,256,384]{2,1,0:T(8,128)S(1)} %project_mine.1.mine_ref, bf16[256,384]{1,0:T(8,128)(2,1)S(1)} %collective-permute-done.7.theirs_ref, bf16[384,768]{1,0:T(8,128)(2,1)S(1)} %collective-permute-done.3.weight_ref.this_ref, bf16[1040,384]{1,0:T(8,128)(2,1)S(1)} %collective-permute-done.5.message_ref.other_ref), custom_call_target="tpu_custom_call" | custom-call | flops 300000000 | bytes 5000000 | tf_op jit(solution)/shard_map/project/pallas_call | solution.py:421
  55.0 0.0 copy-start.3
  55.0 0.0 copy-start.2
  55.0 4.4 %all-to-all-start = ((bf16[4,256,384]{2,1,0:T(8,128)(2,1)}), bf16[4,256,384]{2,1,0:T(8,128)(2,1)S(1)}, u32[]{:S(2)}, u32[]{:S(2)}) async-start(bf16[4,256,384]{2,1,0:T(8,128)(2,1)} %project.1), calls=%async_computation | async-start | bytes 1572864 | tf_op jit(solution)/shard_map/all_to_all | solution.py:465
  59.4 8.4 %all-to-all-done.terms_ref = bf16[4,256,384]{2,1,0:T(8,128)(2,1)S(1)} async-done(((bf16[4,256,384]{2,1,0:T(8,128)(2,1)}), bf16[4,256,384]{2,1,0:T(8,128)(2,1)S(1)}, u32[]{:S(2)}, u32[]{:S(2)}) %all-to-all-start) | async-done | bytes 786464 | tf_op jit(solution)/shard_map/all_to_all | solution.py:465
  67.8 0.8 %finish.1 = bf16[256,384]{1,0:T(8,128)(2,1)} custom-call(bf16[4,256,384]{2,1,0:T(8,128)(2,1)S(1)} %all-to-all-done.terms_ref, bf16[256,384]{1,0:T(8,128)(2,1)S(1)} %copy-done.2, f32[1,384]{1,0:T(1,128)S(1)} %reshape.3.gate_ref), custom_call_target="tpu_custom_call" | custom-call | flops 3932160 | bytes 2000000 | tf_op jit(solution)/shard_map/finish/pallas_call | solution.py:440
  (6 shorter events, 0.0 us)
Async XLA Ops:
  2.0 16.4 %copy-start.1 = (bf16[272,384]{1,0:T(8,128)(2,1)S(1)}, bf16[272,384]{1,0:T(8,128)(2,1)}, u32[]{:S(2)}) copy-start(bf16[272,384]{1,0:T(8,128)(2,1)} %get-tuple-element.12.query_ref) | copy-start | bytes 626692
  2.0 22.0 %copy-start = (bf16[512,384]{1,0:T(8,128)(2,1)S(1)}, bf16[512,384]{1,0:T(8,128)(2,1)}, u32[]{:S(2)}) copy-start(bf16[512,384]{1,0:T(8,128)(2,1)} %get-tuple-element.13.block_ref.own_ref) | copy-start | bytes 1179652
  2.0 30.3 %collective-permute-start = (bf16[512,384]{1,0:T(8,128)(2,1)}, bf16[512,384]{1,0:T(8,128)(2,1)S(1)}, u32[]{:S(2)}, u32[]{:S(2)}) collective-permute-start(bf16[512,384]{1,0:T(8,128)(2,1)} %get-tuple-element.13.block_ref.own_ref), channel_id=1, source_target_pairs={{32,64},{40,72},{48,80},{56,88},{64,32},{72,40},{80,48},{88,56},{9... | collective-permute-start | bytes 1179656 | tf_op jit(solution)/shard_map/ppermute | solution.py:40
  2.8 29.5 %collective-permute-start.1 = (bf16[512,384]{1,0:T(8,128)(2,1)}, bf16[512,384]{1,0:T(8,128)(2,1)S(1)}, u32[]{:S(2)}, u32[]{:S(2)}) collective-permute-start(bf16[512,384]{1,0:T(8,128)(2,1)} %get-tuple-element.13.block_ref.own_ref), channel_id=1, source_target_pairs={{0,32},{8,40},{16,48},{24,56},{32,0},{40,8},{48,16},{56,24},{64,96... | collective-permute-start | bytes 1179656 | tf_op jit(solution)/shard_map/ppermute | solution.py:40
  13.7 18.7 %collective-permute-start.3 = (bf16[384,768]{1,0:T(8,128)(2,1)S(1)}, bf16[384,768]{1,0:T(8,128)(2,1)S(1)}, u32[]{:S(2)}, u32[]{:S(2)}) collective-permute-start(bf16[384,768]{1,0:T(8,128)(2,1)S(1)} %split_weight.1), channel_id=1, source_target_pairs={{0,4},{4,0},{1,5},{5,1},{2,6},{6,2},{3,7},{7,3},{8,12},{12,8},{9,1... | collective-permute-start | bytes 1769480 | tf_op jit(solution)/shard_map/ppermute | solution.py:53
  18.4 5.6 %collective-permute-start.2 = (bf16[272,384]{1,0:T(8,128)(2,1)S(1)}, bf16[272,384]{1,0:T(8,128)(2,1)S(1)}, u32[]{:S(2)}, u32[]{:S(2)}) collective-permute-start(bf16[272,384]{1,0:T(8,128)(2,1)S(1)} %copy-done.1), channel_id=1, source_target_pairs={{0,8},{8,0},{16,24},{24,16},{32,40},{40,32},{48,56},{56,48},{64,72... | collective-permute-start | bytes 626696 | tf_op jit(solution)/shard_map/ppermute | solution.py:44
  21.8 10.5 %collective-permute-start.4 = (bf16[272,384]{1,0:T(8,128)(2,1)S(1)}, bf16[272,384]{1,0:T(8,128)(2,1)S(1)}, u32[]{:S(2)}, u32[]{:S(2)}) collective-permute-start(bf16[272,384]{1,0:T(8,128)(2,1)S(1)} %copy-done.1), channel_id=1, source_target_pairs={{8,16},{16,8},{40,48},{48,40},{72,80},{80,72},{104,112},{112,104},... | collective-permute-start | bytes 626696 | tf_op jit(solution)/shard_map/ppermute | solution.py:49
  33.8 7.9 %collective-permute-start.5 = (bf16[1040,384]{1,0:T(8,128)(2,1)S(1)}, bf16[1040,384]{1,0:T(8,128)(2,1)S(1)}, u32[]{:S(2)}, u32[]{:S(2)}) collective-permute-start(bf16[1040,384]{1,0:T(8,128)(2,1)S(1)} %attend_pair.1.after_ref), channel_id=1, source_target_pairs={{0,8},{8,0},{16,24},{24,16},{32,40},{40,32},{48,56},{56,48},{64,72... | collective-permute-start | bytes 2396168 | tf_op jit(solution)/shard_map/ppermute | solution.py:44
  37.7 7.4 %collective-permute-start.6 = (bf16[272,384]{1,0:T(8,128)(2,1)S(1)}, bf16[272,384]{1,0:T(8,128)(2,1)S(1)}, u32[]{:S(2)}, u32[]{:S(2)}) collective-permute-start(bf16[272,384]{1,0:T(8,128)(2,1)S(1)} %attend_middle.1), channel_id=1, source_target_pairs={{8,16},{16,8},{40,48},{48,40},{72,80},{80,72},{104,112},{112,104},... | collective-permute-start | bytes 626696 | tf_op jit(solution)/shard_map/ppermute | solution.py:49
  45.6 7.9 %collective-permute-start.7 = (bf16[256,384]{1,0:T(8,128)(2,1)S(1)}, bf16[256,384]{1,0:T(8,128)(2,1)S(1)}, u32[]{:S(2)}, u32[]{:S(2)}) collective-permute-start(bf16[256,384]{1,0:T(8,128)(2,1)S(1)} %merge.1.mine_ref), channel_id=1, source_target_pairs={{0,4},{4,0},{1,5},{5,1},{2,6},{6,2},{3,7},{7,3},{8,12},{12,8},{9,1... | collective-permute-start | bytes 589832 | tf_op jit(solution)/shard_map/ppermute | solution.py:53
  55.0 4.5 %copy-start.3 = (f32[384]{0:T(512)S(1)}, f32[384]{0:T(512)}, u32[]{:S(2)}) copy-start(f32[384]{0:T(512)} %param.13) | copy-start | bytes 4612
  55.0 12.8 %copy-start.2 = (bf16[256,384]{1,0:T(8,128)(2,1)S(1)}, bf16[256,384]{1,0:T(8,128)(2,1)}, u32[]{:S(2)}) copy-start(bf16[256,384]{1,0:T(8,128)(2,1)} %residual_ref.1) | copy-start | bytes 589828
  55.0 12.8 %all-to-all-start = ((bf16[4,256,384]{2,1,0:T(8,128)(2,1)}), bf16[4,256,384]{2,1,0:T(8,128)(2,1)S(1)}, u32[]{:S(2)}, u32[]{:S(2)}) async-start(bf16[4,256,384]{2,1,0:T(8,128)(2,1)} %project.1), calls=%async_computation | async-start | bytes 1572864 | tf_op jit(solution)/shard_map/all_to_all | solution.py:465

commit v19 on v18

--- a/solution.py
+++ b/solution.py
@@ -190,41 +190,35 @@
     return [block_bias(wide, stage) for stage in (1, 2)]
 
 
-def own_kernel(query_ref, pair_ref, block_ref, weight_ref, mix_ref, stats_ref, mine_ref, sem):
+def own_kernel(query_ref, block_ref, weight_ref, mix_ref, stats_ref, mine_ref, sem):
     copy = copy_columns(weight_ref, lax.axis_index("far") * mine_ref.shape[1], mine_ref, sem)
     copy.start()
     rows, width = block_ref.shape[0] // 2, block_ref.shape[1]
-    for place, ref in enumerate((query_ref, pair_ref)):
-        for head in range(width // HD):
-            low, index = head * HD, 2 * head + place
-            largest, total, mix = attend(ref[:rows, low : low + HD], [block_ref], [0.0], low)
-            mix_ref[index], stats_ref[2 * index], stats_ref[2 * index + 1] = mix, largest, total
+    for head in range(width // HD):
+        low = head * HD
+        largest, total, mix = attend(query_ref[:rows, low : low + HD], [block_ref], [0.0], low)
+        mix_ref[head], stats_ref[2 * head], stats_ref[2 * head + 1] = mix, largest, total
     copy.wait()
 
 
-def attend_own(queries, pair, block, out_weight):
+def attend_own(queries, block, out_weight):
     rows, width = block.shape[0] // 2, block.shape[1]
     heads = width // HD
     whole = pl.BlockSpec(memory_space=VMEM)
     return pl.pallas_call(
         own_kernel,
         out_shape=(
+            jax.ShapeDtypeStruct((heads, rows, HD), jnp.float32),
             jax.ShapeDtypeStruct((2 * heads, rows, HD), jnp.float32),
-            jax.ShapeDtypeStruct((4 * heads, rows, HD), jnp.float32),
             jax.ShapeDtypeStruct((out_weight.shape[0], out_weight.shape[1] // 2), out_weight.dtype),
         ),
-        in_specs=[whole] * 3 + [pl.BlockSpec(memory_space=pl.ANY)],
+        in_specs=[whole] * 2 + [pl.BlockSpec(memory_space=pl.ANY)],
         out_specs=(whole,) * 3,
         scratch_shapes=[pltpu.SemaphoreType.DMA],
         compiler_params=params(24),
         cost_estimate=pl.CostEstimate(flops=0, bytes_accessed=0, transcendentals=0),
         name="attend_own",
-    )(queries, pair, block, pltpu.with_memory_space_constraint(out_weight, pltpu.HBM))
-
-
-def old_parts(mix_ref, stats_ref, head, place):
-    index = 2 * head + place
-    return stats_ref[2 * index], stats_ref[2 * index + 1], mix_ref[index]
+    )(queries, block, pltpu.with_memory_space_constraint(out_weight, pltpu.HBM))
 
 
 def here_kernel(*refs):
@@ -247,30 +241,30 @@
     return [rows + SIDE + part * weight_shape[0] for part in range(weight_shape[1] // width)]
 
 
-def pair_kernel(query_ref, first_ref, second_ref, mix_ref, stats_ref, weight_ref, after_ref, out_ref):
+def pair_kernel(query_ref, own_ref, first_ref, second_ref, weight_ref, after_ref, out_ref):
     rows, width = first_ref.shape[0] // 2, first_ref.shape[1]
     for part, start in enumerate(half_rows(weight_ref.shape, rows, width)):
         out_ref[start : start + weight_ref.shape[0]] = weight_ref[:, part * width : (part + 1) * width]
-    biases = block_biases(query_ref, rows)
+    biases = [0.0] + block_biases(query_ref, rows)
+    blocks = [own_ref, first_ref, second_ref]
     for head in range(width // HD):
         low = head * HD
-        old = old_parts(mix_ref, stats_ref, head, 1)
-        largest, total, mix = attend(query_ref[:rows, low : low + HD], [first_ref, second_ref], biases, low, old)
+        largest, total, mix = attend(query_ref[:rows, low : low + HD], blocks, biases, low)
         put_message(out_ref, head, mix, row_stats(largest, total), 0)
 
 
-def attend_pair(query, first, second, mix, stats, weight, after):
+def attend_pair(query, own, first, second, weight, after):
     rows, width = query.shape
     whole = pl.BlockSpec(memory_space=VMEM)
     return pl.pallas_call(
         pair_kernel,
         out_shape=jax.ShapeDtypeStruct((rows + weight.size // width, width), jnp.bfloat16),
-        in_specs=[whole] * 6 + [pl.BlockSpec(memory_space=pl.ANY)],
+        in_specs=[whole] * 5 + [pl.BlockSpec(memory_space=pl.ANY)],
         out_specs=whole,
         compiler_params=params(24),
         cost_estimate=pl.CostEstimate(flops=PAIR_FLOPS, bytes_accessed=2_000_000, transcendentals=0),
         name="attend_pair",
-    )(query, first, second, mix, stats, weight, after)
+    )(query, own, first, second, weight, after)
 
 
 def middle_kernel(query_ref, own_ref, first_ref, second_ref, after_ref, out_ref):
@@ -311,7 +305,7 @@
     biases = block_biases(query_ref, rows)
     for head in range(width // HD):
         low = head * HD
-        old = old_parts(old_mix_ref, old_stats_ref, head, 0)
+        old = (old_stats_ref[2 * head], old_stats_ref[2 * head + 1], old_mix_ref[head])
         largest, total, mix = attend(query_ref[:rows, low : low + HD], [first_ref, second_ref], biases, low, old)
         their_largest, their_total = message_columns(message_ref, head, rows)
         peak = jnp.maximum(largest, jnp.where(wide, their_largest, MASKED))
@@ -453,9 +447,9 @@
     first, second = swap_times(block, False), swap_times(block, True)
     pair_asks, middle_asks = swap_pair(packed), swap_middle(packed)
     this_half = swap_far(split_weight(out_weight))
-    mix, stats, my_weight = attend_own(packed, pair_asks, block, out_weight)
-    here = all_here(first, second, middle_asks)
-    for_pair = attend_pair(pair_asks, first, second, mix, stats, this_half, here)
+    mix, stats, my_weight = attend_own(packed, block, out_weight)
+    here = all_here(first, second, middle_asks, stats)
+    for_pair = attend_pair(pair_asks, block, first, second, this_half, here)
     for_middle = attend_middle(middle_asks, block, first, second, for_pair)
     from_pair = swap_pair(for_pair)
     mix, stats = attend_last(packed, first, second, mix, stats, from_pair)

time: 69.2 us -> 69.4 us (level)
  Pallas kernels: 12.7 us -> 13.4 us
    ppermute x2, starting transfers between devices: 6.13 us -> 7.64 us  [swap_middle(): return lax.ppermute(block, 'tile', route)]
    ppermute x2, starting transfers between devices: 5.81 us -> 4.3 us  [swap_pair(): lax.ppermute(block, 'tile', [(tile, tile ^ 1) for tile, *_ in places()])]
where the time goes in v19:
time: 69.4 us; the launch traced here: 68.8 us
  starting transfers between devices  36.3 us (52%)
  waiting for transfers between devices  18.9 us (27%)
  Pallas kernels  13.4 us (19%)
    ppermute x2, starting transfers between devices, swap_times(): return lax.ppermute(block, 'tile', route)  10.6 us
    ppermute x2, starting transfers between devices, swap_far(): return lax.ppermute(block, 'far', [(0, 1), (1, 0)])  9.3 us
    all_to_all x1, waiting for transfers between devices, shards(): terms = lax.all_to_all(terms, 'group', 0, 0)  8.37 us
    ppermute x2, waiting for transfers between devices, swap_middle(): return lax.ppermute(block, 'tile', route)  7.93 us
    ppermute x2, starting transfers between devices, swap_middle(): return lax.ppermute(block, 'tile', route)  7.64 us
    all_to_all x1, starting transfers between devices, shards(): terms = lax.all_to_all(terms, 'group', 0, 0)  4.43 us
    ppermute x2, starting transfers between devices, swap_pair(): lax.ppermute(block, 'tile', [(tile, tile ^ 1) for tile, *_ in places()])  4.3 us
    ppermute x2, waiting for transfers between devices, swap_far(): return lax.ppermute(block, 'far', [(0, 1), (1, 0)])  2.63 us
  transfers between devices with their start and end apart: 9, of which 4 were waited for; matrix products, arithmetic and copies ran while one was open for 0% of the time, Pallas kernels for 10%

profile of v19, /device:TPU:1, one launch (start us, length us, event | category | flops | bytes accessed | tf_op | source)
XLA Modules:
  0.0 68.8 jit_solution(14839770921881922259)
XLA Ops:
  0.0 2.0 %pack.1 = (bf16[272,384]{1,0:T(8,128)(2,1)}, bf16[512,384]{1,0:T(8,128)(2,1)}) custom-call(s32[1,3]{1,0:T(1,128)} %windows_ref.1, bf16[256,384]{1,0:T(8,128)(2,1)} %q_ref.1, bf16[256,384]{1,0:T(8,128)(2,1)} %k_ref.1, bf16[256,384]{1,0:T(8,128)(2,1)} %v_ref.1), custom_call_target="tpu_custom_call" | custom-call | tf_op jit(solution)/shard_map/pack/pallas_call | solution.py:96
  2.0 0.8 %collective-permute-start = (bf16[512,384]{1,0:T(8,128)(2,1)}, bf16[512,384]{1,0:T(8,128)(2,1)S(1)}, u32[]{:S(2)}, u32[]{:S(2)}) collective-permute-start(bf16[512,384]{1,0:T(8,128)(2,1)} %get-tuple-element.13.block_ref.own_ref), channel_id=1, source_target_pairs={{32,64},{40,72},{48,80},{56,88},{64,32},{72,40},{80,48},{88,56},{9... | collective-permute-start | bytes 1179656 | tf_op jit(solution)/shard_map/ppermute | solution.py:40
  2.8 9.8 %collective-permute-start.1 = (bf16[512,384]{1,0:T(8,128)(2,1)}, bf16[512,384]{1,0:T(8,128)(2,1)S(1)}, u32[]{:S(2)}, u32[]{:S(2)}) collective-permute-start(bf16[512,384]{1,0:T(8,128)(2,1)} %get-tuple-element.13.block_ref.own_ref), channel_id=1, source_target_pairs={{0,32},{8,40},{16,48},{24,56},{32,0},{40,8},{48,16},{56,24},{64,96... | collective-permute-start | bytes 1179656 | tf_op jit(solution)/shard_map/ppermute | solution.py:40
  12.6 1.1 %split_weight.1 = bf16[384,768]{1,0:T(8,128)(2,1)S(1)} custom-call(bf16[384,3072]{1,0:T(8,128)(2,1)} %weight_ref.3), custom_call_target="tpu_custom_call" | custom-call | tf_op jit(solution)/shard_map/split_weight/pallas_call | solution.py:70
  13.7 4.7 %collective-permute-start.3 = (bf16[384,768]{1,0:T(8,128)(2,1)S(1)}, bf16[384,768]{1,0:T(8,128)(2,1)S(1)}, u32[]{:S(2)}, u32[]{:S(2)}) collective-permute-start(bf16[384,768]{1,0:T(8,128)(2,1)S(1)} %split_weight.1), channel_id=1, source_target_pairs={{0,4},{4,0},{1,5},{5,1},{2,6},{6,2},{3,7},{7,3},{8,12},{12,8},{9,1... | collective-permute-start | bytes 1769480 | tf_op jit(solution)/shard_map/ppermute | solution.py:53
  18.4 0.0 copy-done.1
  18.4 3.7 %collective-permute-start.4 = (bf16[272,384]{1,0:T(8,128)(2,1)S(1)}, bf16[272,384]{1,0:T(8,128)(2,1)S(1)}, u32[]{:S(2)}, u32[]{:S(2)}) collective-permute-start(bf16[272,384]{1,0:T(8,128)(2,1)S(1)} %copy-done.1), channel_id=1, source_target_pairs={{8,16},{16,8},{40,48},{48,40},{72,80},{80,72},{104,112},{112,104},... | collective-permute-start | bytes 626696 | tf_op jit(solution)/shard_map/ppermute | solution.py:49
  22.1 1.9 %collective-permute-start.2 = (bf16[272,384]{1,0:T(8,128)(2,1)S(1)}, bf16[272,384]{1,0:T(8,128)(2,1)S(1)}, u32[]{:S(2)}, u32[]{:S(2)}) collective-permute-start(bf16[272,384]{1,0:T(8,128)(2,1)S(1)} %copy-done.1), channel_id=1, source_target_pairs={{0,8},{8,0},{16,24},{24,16},{32,40},{40,32},{48,56},{56,48},{64,72... | collective-permute-start | bytes 626696 | tf_op jit(solution)/shard_map/ppermute | solution.py:44
  24.0 0.0 copy-done
  24.0 1.8 %attend_own.1 = (f32[3,256,128]{2,1,0:T(8,128)S(1)}, f32[6,256,128]{2,1,0:T(8,128)S(1)}, bf16[384,1536]{1,0:T(8,128)(2,1)S(1)}) custom-call(bf16[272,384]{1,0:T(8,128)(2,1)S(1)} %copy-done.1, bf16[512,384]{1,0:T(8,128)(2,1)S(1)} %copy-done, bf16[384,3072]{1,0:T(8,128)(2,1)} %weight_ref.3), custom_call_target="tpu_custom_call" | custom-call | tf_op jit(solution)/shard_map/attend_own/pallas_call | solution.py:208
  25.8 6.5 %collective-permute-done.4.refs_2_.query_ref = bf16[272,384]{1,0:T(8,128)(2,1)S(1)} collective-permute-done((bf16[272,384]{1,0:T(8,128)(2,1)S(1)}, bf16[272,384]{1,0:T(8,128)(2,1)S(1)}, u32[]{:S(2)}, u32[]{:S(2)}) %collective-permute-start.4) | collective-permute-done | bytes 208928 | tf_op jit(solution)/shard_map/ppermute | solution.py:49
  32.3 0.0 collective-permute-done.refs_0_.first_ref
  32.3 0.0 collective-permute-done.1.refs_1_.second_ref
  32.4 0.0 collective-permute-done.2.query_ref
  32.4 0.0 collective-permute-done.3.weight_ref.this_ref
  32.4 1.6 %attend_pair.1.after_ref = bf16[1040,384]{1,0:T(8,128)(2,1)S(1)} custom-call(bf16[272,384]{1,0:T(8,128)(2,1)S(1)} %collective-permute-done.2.query_ref, bf16[512,384]{1,0:T(8,128)(2,1)S(1)} %copy-done, bf16[512,384]{1,0:T(8,128)(2,1)S(1)} %collective-permute-done.refs_0_.first_ref, bf16[512,384]{1,0:T(8,128)(2,1)S(1)} %collective-permute-done.1.refs_1_.second_ref, ...), custom_call_target="tpu_custom_call" | custom-call | flops 400000000 | bytes 2000000 | tf_op jit(solution)/shard_map/attend_pair/pallas_call | solution.py:259
  34.0 2.4 %collective-permute-start.5 = (bf16[1040,384]{1,0:T(8,128)(2,1)S(1)}, bf16[1040,384]{1,0:T(8,128)(2,1)S(1)}, u32[]{:S(2)}, u32[]{:S(2)}) collective-permute-start(bf16[1040,384]{1,0:T(8,128)(2,1)S(1)} %attend_pair.1.after_ref), channel_id=1, source_target_pairs={{0,8},{8,0},{16,24},{24,16},{32,40},{40,32},{48,56},{56,48},{64,72... | collective-permute-start | bytes 2396168 | tf_op jit(solution)/shard_map/ppermute | solution.py:44
  36.4 1.5 %attend_middle.1 = bf16[272,384]{1,0:T(8,128)(2,1)S(1)} custom-call(bf16[272,384]{1,0:T(8,128)(2,1)S(1)} %collective-permute-done.4.refs_2_.query_ref, bf16[512,384]{1,0:T(8,128)(2,1)S(1)} %copy-done, bf16[512,384]{1,0:T(8,128)(2,1)S(1)} %collective-permute-done.refs_0_.first_ref, bf16[512,384]{1,0:T(8,128)(2,1)S(1)} %collective-permute-done.1.refs_1_.second_ref, ...), custom_call_target="tpu_custom_call" | custom-call | flops 600000000 | bytes 2000000 | tf_op jit(solution)/shard_map/attend_middle/pallas_call | solution.py:291
  37.9 3.9 %collective-permute-start.6 = (bf16[272,384]{1,0:T(8,128)(2,1)S(1)}, bf16[272,384]{1,0:T(8,128)(2,1)S(1)}, u32[]{:S(2)}, u32[]{:S(2)}) collective-permute-start(bf16[272,384]{1,0:T(8,128)(2,1)S(1)} %attend_middle.1), channel_id=1, source_target_pairs={{8,16},{16,8},{40,48},{48,40},{72,80},{80,72},{104,112},{112,104},... | collective-permute-start | bytes 626696 | tf_op jit(solution)/shard_map/ppermute | solution.py:49
  41.9 0.0 collective-permute-done.5.message_ref.other_ref
  41.9 2.0 %attend_last.1 = (f32[256,384]{1,0:T(8,128)S(1)}, f32[3,8,256]{2,1,0:T(8,128)S(1)}) custom-call(bf16[272,384]{1,0:T(8,128)(2,1)S(1)} %copy-done.1, bf16[512,384]{1,0:T(8,128)(2,1)S(1)} %collective-permute-done.refs_0_.first_ref, bf16[512,384]{1,0:T(8,128)(2,1)S(1)} %collective-permute-done.1.refs_1_.second_ref, ...), custom_call_target="tpu_custom_call" | custom-call | flops 400000000 | bytes 2000000 | tf_op jit(solution)/shard_map/attend_last/pallas_call | solution.py:322
  43.9 1.4 %collective-permute-done.6.middle_ref = bf16[272,384]{1,0:T(8,128)(2,1)S(1)} collective-permute-done((bf16[272,384]{1,0:T(8,128)(2,1)S(1)}, bf16[272,384]{1,0:T(8,128)(2,1)S(1)}, u32[]{:S(2)}, u32[]{:S(2)}) %collective-permute-start.6) | collective-permute-done | bytes 208928 | tf_op jit(solution)/shard_map/ppermute | solution.py:49
  45.3 0.5 merge.1.mine_ref
  45.8 4.6 %collective-permute-start.7 = (bf16[256,384]{1,0:T(8,128)(2,1)S(1)}, bf16[256,384]{1,0:T(8,128)(2,1)S(1)}, u32[]{:S(2)}, u32[]{:S(2)}) collective-permute-start(bf16[256,384]{1,0:T(8,128)(2,1)S(1)} %merge.1.mine_ref), channel_id=1, source_target_pairs={{0,4},{4,0},{1,5},{5,1},{2,6},{6,2},{3,7},{7,3},{8,12},{12,8},{9,1... | collective-permute-start | bytes 589832 | tf_op jit(solution)/shard_map/ppermute | solution.py:53
  50.5 0.6 project_mine.1.mine_ref
  51.1 2.6 %collective-permute-done.7.theirs_ref = bf16[256,384]{1,0:T(8,128)(2,1)S(1)} collective-permute-done((bf16[256,384]{1,0:T(8,128)(2,1)S(1)}, bf16[256,384]{1,0:T(8,128)(2,1)S(1)}, u32[]{:S(2)}, u32[]{:S(2)}) %collective-permute-start.7) | collective-permute-done | bytes 196640 | tf_op jit(solution)/shard_map/ppermute | solution.py:53
  53.7 1.4 %project.1 = bf16[4,256,384]{2,1,0:T(8,128)(2,1)} custom-call(f32[4,256,384]{2,1,0:T(8,128)S(1)} %project_mine.1.mine_ref, bf16[256,384]{1,0:T(8,128)(2,1)S(1)} %collective-permute-done.7.theirs_ref, bf16[384,768]{1,0:T(8,128)(2,1)S(1)} %collective-permute-done.3.weight_ref.this_ref, bf16[1040,384]{1,0:T(8,128)(2,1)S(1)} %collective-permute-done.5.message_ref.other_ref), custom_call_target="tpu_custom_call" | custom-call | flops 300000000 | bytes 5000000 | tf_op jit(solution)/shard_map/project/pallas_call | solution.py:415
  55.2 0.0 copy-start.3
  55.2 0.0 copy-start.2
  55.2 4.4 %all-to-all-start = ((bf16[4,256,384]{2,1,0:T(8,128)(2,1)}), bf16[4,256,384]{2,1,0:T(8,128)(2,1)S(1)}, u32[]{:S(2)}, u32[]{:S(2)}) async-start(bf16[4,256,384]{2,1,0:T(8,128)(2,1)} %project.1), calls=%async_computation | async-start | bytes 1572864 | tf_op jit(solution)/shard_map/all_to_all | solution.py:459
  59.6 8.4 %all-to-all-done.terms_ref = bf16[4,256,384]{2,1,0:T(8,128)(2,1)S(1)} async-done(((bf16[4,256,384]{2,1,0:T(8,128)(2,1)}), bf16[4,256,384]{2,1,0:T(8,128)(2,1)S(1)}, u32[]{:S(2)}, u32[]{:S(2)}) %all-to-all-start) | async-done | bytes 786464 | tf_op jit(solution)/shard_map/all_to_all | solution.py:459
  68.0 0.8 %finish.1 = bf16[256,384]{1,0:T(8,128)(2,1)} custom-call(bf16[4,256,384]{2,1,0:T(8,128)(2,1)S(1)} %all-to-all-done.terms_ref, bf16[256,384]{1,0:T(8,128)(2,1)S(1)} %copy-done.2, f32[1,384]{1,0:T(1,128)S(1)} %reshape.3.gate_ref), custom_call_target="tpu_custom_call" | custom-call | flops 3932160 | bytes 2000000 | tf_op jit(solution)/shard_map/finish/pallas_call | solution.py:434
  (6 shorter events, 0.0 us)
Async XLA Ops:
  2.0 16.4 %copy-start.1 = (bf16[272,384]{1,0:T(8,128)(2,1)S(1)}, bf16[272,384]{1,0:T(8,128)(2,1)}, u32[]{:S(2)}) copy-start(bf16[272,384]{1,0:T(8,128)(2,1)} %get-tuple-element.12.query_ref) | copy-start | bytes 626692
  2.0 22.0 %copy-start = (bf16[512,384]{1,0:T(8,128)(2,1)S(1)}, bf16[512,384]{1,0:T(8,128)(2,1)}, u32[]{:S(2)}) copy-start(bf16[512,384]{1,0:T(8,128)(2,1)} %get-tuple-element.13.block_ref.own_ref) | copy-start | bytes 1179652
  2.0 30.3 %collective-permute-start = (bf16[512,384]{1,0:T(8,128)(2,1)}, bf16[512,384]{1,0:T(8,128)(2,1)S(1)}, u32[]{:S(2)}, u32[]{:S(2)}) collective-permute-start(bf16[512,384]{1,0:T(8,128)(2,1)} %get-tuple-element.13.block_ref.own_ref), channel_id=1, source_target_pairs={{32,64},{40,72},{48,80},{56,88},{64,32},{72,40},{80,48},{88,56},{9... | collective-permute-start | bytes 1179656 | tf_op jit(solution)/shard_map/ppermute | solution.py:40
  2.8 29.5 %collective-permute-start.1 = (bf16[512,384]{1,0:T(8,128)(2,1)}, bf16[512,384]{1,0:T(8,128)(2,1)S(1)}, u32[]{:S(2)}, u32[]{:S(2)}) collective-permute-start(bf16[512,384]{1,0:T(8,128)(2,1)} %get-tuple-element.13.block_ref.own_ref), channel_id=1, source_target_pairs={{0,32},{8,40},{16,48},{24,56},{32,0},{40,8},{48,16},{56,24},{64,96... | collective-permute-start | bytes 1179656 | tf_op jit(solution)/shard_map/ppermute | solution.py:40
  13.7 18.7 %collective-permute-start.3 = (bf16[384,768]{1,0:T(8,128)(2,1)S(1)}, bf16[384,768]{1,0:T(8,128)(2,1)S(1)}, u32[]{:S(2)}, u32[]{:S(2)}) collective-permute-start(bf16[384,768]{1,0:T(8,128)(2,1)S(1)} %split_weight.1), channel_id=1, source_target_pairs={{0,4},{4,0},{1,5},{5,1},{2,6},{6,2},{3,7},{7,3},{8,12},{12,8},{9,1... | collective-permute-start | bytes 1769480 | tf_op jit(solution)/shard_map/ppermute | solution.py:53
  18.4 14.0 %collective-permute-start.4 = (bf16[272,384]{1,0:T(8,128)(2,1)S(1)}, bf16[272,384]{1,0:T(8,128)(2,1)S(1)}, u32[]{:S(2)}, u32[]{:S(2)}) collective-permute-start(bf16[272,384]{1,0:T(8,128)(2,1)S(1)} %copy-done.1), channel_id=1, source_target_pairs={{8,16},{16,8},{40,48},{48,40},{72,80},{80,72},{104,112},{112,104},... | collective-permute-start | bytes 626696 | tf_op jit(solution)/shard_map/ppermute | solution.py:49
  22.1 10.3 %collective-permute-start.2 = (bf16[272,384]{1,0:T(8,128)(2,1)S(1)}, bf16[272,384]{1,0:T(8,128)(2,1)S(1)}, u32[]{:S(2)}, u32[]{:S(2)}) collective-permute-start(bf16[272,384]{1,0:T(8,128)(2,1)S(1)} %copy-done.1), channel_id=1, source_target_pairs={{0,8},{8,0},{16,24},{24,16},{32,40},{40,32},{48,56},{56,48},{64,72... | collective-permute-start | bytes 626696 | tf_op jit(solution)/shard_map/ppermute | solution.py:44
  34.0 7.9 %collective-permute-start.5 = (bf16[1040,384]{1,0:T(8,128)(2,1)S(1)}, bf16[1040,384]{1,0:T(8,128)(2,1)S(1)}, u32[]{:S(2)}, u32[]{:S(2)}) collective-permute-start(bf16[1040,384]{1,0:T(8,128)(2,1)S(1)} %attend_pair.1.after_ref), channel_id=1, source_target_pairs={{0,8},{8,0},{16,24},{24,16},{32,40},{40,32},{48,56},{56,48},{64,72... | collective-permute-start | bytes 2396168 | tf_op jit(solution)/shard_map/ppermute | solution.py:44
  37.9 7.4 %collective-permute-start.6 = (bf16[272,384]{1,0:T(8,128)(2,1)S(1)}, bf16[272,384]{1,0:T(8,128)(2,1)S(1)}, u32[]{:S(2)}, u32[]{:S(2)}) collective-permute-start(bf16[272,384]{1,0:T(8,128)(2,1)S(1)} %attend_middle.1), channel_id=1, source_target_pairs={{8,16},{16,8},{40,48},{48,40},{72,80},{80,72},{104,112},{112,104},... | collective-permute-start | bytes 626696 | tf_op jit(solution)/shard_map/ppermute | solution.py:49
  45.8 7.9 %collective-permute-start.7 = (bf16[256,384]{1,0:T(8,128)(2,1)S(1)}, bf16[256,384]{1,0:T(8,128)(2,1)S(1)}, u32[]{:S(2)}, u32[]{:S(2)}) collective-permute-start(bf16[256,384]{1,0:T(8,128)(2,1)S(1)} %merge.1.mine_ref), channel_id=1, source_target_pairs={{0,4},{4,0},{1,5},{5,1},{2,6},{6,2},{3,7},{7,3},{8,12},{12,8},{9,1... | collective-permute-start | bytes 589832 | tf_op jit(solution)/shard_map/ppermute | solution.py:53
  55.2 4.5 %copy-start.3 = (f32[384]{0:T(512)S(1)}, f32[384]{0:T(512)}, u32[]{:S(2)}) copy-start(f32[384]{0:T(512)} %param.13) | copy-start | bytes 4612
  55.2 12.8 %copy-start.2 = (bf16[256,384]{1,0:T(8,128)(2,1)S(1)}, bf16[256,384]{1,0:T(8,128)(2,1)}, u32[]{:S(2)}) copy-start(bf16[256,384]{1,0:T(8,128)(2,1)} %residual_ref.1) | copy-start | bytes 589828
  55.2 12.8 %all-to-all-start = ((bf16[4,256,384]{2,1,0:T(8,128)(2,1)}), bf16[4,256,384]{2,1,0:T(8,128)(2,1)S(1)}, u32[]{:S(2)}, u32[]{:S(2)}) async-start(bf16[4,256,384]{2,1,0:T(8,128)(2,1)} %project.1), calls=%async_computation | async-start | bytes 1572864 | tf_op jit(solution)/shard_map/all_to_all | solution.py:459

commit v20 on v19

--- a/solution.py
+++ b/solution.py
@@ -16,7 +16,7 @@
 LAST_FLOPS = 400_000_000
 MIDDLE_FLOPS = 600_000_000
 PAIR_FLOPS = 400_000_000
-HERE_FLOPS = 3_000_000_000
+HERE_FLOPS = 5_000_000_000
 MESH_AXES = ("tile", "head")
 VMEM = pltpu.VMEM
 SMEM = pltpu.SMEM

time: 69.4 us -> 71.1 us (1.024)
  waiting for transfers between devices: 18.9 us -> 23.2 us
  starting transfers between devices: 36.3 us -> 33.8 us
    ppermute x2, waiting for transfers between devices: 2.63 us -> 4.69 us  [swap_far(): return lax.ppermute(block, 'far', [(0, 1), (1, 0)])]
    ppermute x2, starting transfers between devices: 7.64 us -> 5.67 us  [swap_middle(): return lax.ppermute(block, 'tile', route)]
    ppermute x2, waiting for transfers between devices: 7.93 us -> 9.72 us  [swap_middle(): return lax.ppermute(block, 'tile', route)]
  transfers between devices with their start and end apart: 9 -> 9, of which waited for: 4 -> 5; matrix products, arithmetic and copies ran while one was open for 0% -> 0% of each run, Pallas kernels for 10% -> 10%
where the time goes in v20:
time: 71.1 us; the launch traced here: 70.6 us
  starting transfers between devices  33.8 us (48%)
  waiting for transfers between devices  23.2 us (33%)
  Pallas kernels  13.4 us (19%)
    ppermute x2, starting transfers between devices, swap_times(): return lax.ppermute(block, 'tile', route)  10.6 us
    ppermute x2, waiting for transfers between devices, swap_middle(): return lax.ppermute(block, 'tile', route)  9.72 us
    ppermute x2, starting transfers between devices, swap_far(): return lax.ppermute(block, 'far', [(0, 1), (1, 0)])  9.31 us
    all_to_all x1, waiting for transfers between devices, shards(): terms = lax.all_to_all(terms, 'group', 0, 0)  8.78 us
    ppermute x2, starting transfers between devices, swap_middle(): return lax.ppermute(block, 'tile', route)  5.67 us
    ppermute x2, waiting for transfers between devices, swap_far(): return lax.ppermute(block, 'far', [(0, 1), (1, 0)])  4.69 us
    all_to_all x1, starting transfers between devices, shards(): terms = lax.all_to_all(terms, 'group', 0, 0)  4.43 us
    ppermute x2, starting transfers between devices, swap_pair(): lax.ppermute(block, 'tile', [(tile, tile ^ 1) for tile, *_ in places()])  3.84 us
  transfers between devices with their start and end apart: 9, of which 5 were waited for; matrix products, arithmetic and copies ran while one was open for 0% of the time, Pallas kernels for 10%

profile of v20, /device:TPU:1, one launch (start us, length us, event | category | flops | bytes accessed | tf_op | source)
XLA Modules:
  0.0 70.6 jit_solution(15110542889898761781)
XLA Ops:
  0.0 2.0 %pack.1 = (bf16[272,384]{1,0:T(8,128)(2,1)}, bf16[512,384]{1,0:T(8,128)(2,1)}) custom-call(s32[1,3]{1,0:T(1,128)} %windows_ref.1, bf16[256,384]{1,0:T(8,128)(2,1)} %q_ref.1, bf16[256,384]{1,0:T(8,128)(2,1)} %k_ref.1, bf16[256,384]{1,0:T(8,128)(2,1)} %v_ref.1), custom_call_target="tpu_custom_call" | custom-call | tf_op jit(solution)/shard_map/pack/pallas_call | solution.py:96
  2.0 0.8 %collective-permute-start = (bf16[512,384]{1,0:T(8,128)(2,1)}, bf16[512,384]{1,0:T(8,128)(2,1)S(1)}, u32[]{:S(2)}, u32[]{:S(2)}) collective-permute-start(bf16[512,384]{1,0:T(8,128)(2,1)} %get-tuple-element.13.block_ref.own_ref), channel_id=1, source_target_pairs={{32,64},{40,72},{48,80},{56,88},{64,32},{72,40},{80,48},{88,56},{9... | collective-permute-start | bytes 1179656 | tf_op jit(solution)/shard_map/ppermute | solution.py:40
  2.8 9.8 %collective-permute-start.1 = (bf16[512,384]{1,0:T(8,128)(2,1)}, bf16[512,384]{1,0:T(8,128)(2,1)S(1)}, u32[]{:S(2)}, u32[]{:S(2)}) collective-permute-start(bf16[512,384]{1,0:T(8,128)(2,1)} %get-tuple-element.13.block_ref.own_ref), channel_id=1, source_target_pairs={{0,32},{8,40},{16,48},{24,56},{32,0},{40,8},{48,16},{56,24},{64,96... | collective-permute-start | bytes 1179656 | tf_op jit(solution)/shard_map/ppermute | solution.py:40
  12.6 3.4 %collective-permute-start.4 = (bf16[272,384]{1,0:T(8,128)(2,1)}, bf16[272,384]{1,0:T(8,128)(2,1)S(1)}, u32[]{:S(2)}, u32[]{:S(2)}) collective-permute-start(bf16[272,384]{1,0:T(8,128)(2,1)} %get-tuple-element.12.query_ref), channel_id=1, source_target_pairs={{8,16},{16,8},{40,48},{48,40},{72,80},{80,72},{104,112},{112,104},... | collective-permute-start | bytes 626696 | tf_op jit(solution)/shard_map/ppermute | solution.py:49
  16.0 1.1 %split_weight.1 = bf16[384,768]{1,0:T(8,128)(2,1)S(1)} custom-call(bf16[384,3072]{1,0:T(8,128)(2,1)} %weight_ref.3), custom_call_target="tpu_custom_call" | custom-call | tf_op jit(solution)/shard_map/split_weight/pallas_call | solution.py:70
  17.1 4.7 %collective-permute-start.3 = (bf16[384,768]{1,0:T(8,128)(2,1)S(1)}, bf16[384,768]{1,0:T(8,128)(2,1)S(1)}, u32[]{:S(2)}, u32[]{:S(2)}) collective-permute-start(bf16[384,768]{1,0:T(8,128)(2,1)S(1)} %split_weight.1), channel_id=1, source_target_pairs={{0,4},{4,0},{1,5},{5,1},{2,6},{6,2},{3,7},{7,3},{8,12},{12,8},{9,1... | collective-permute-start | bytes 1769480 | tf_op jit(solution)/shard_map/ppermute | solution.py:53
  21.8 0.0 copy-done.1
  21.8 1.9 %collective-permute-start.2 = (bf16[272,384]{1,0:T(8,128)(2,1)S(1)}, bf16[272,384]{1,0:T(8,128)(2,1)S(1)}, u32[]{:S(2)}, u32[]{:S(2)}) collective-permute-start(bf16[272,384]{1,0:T(8,128)(2,1)S(1)} %copy-done.1), channel_id=1, source_target_pairs={{0,8},{8,0},{16,24},{24,16},{32,40},{40,32},{48,56},{56,48},{64,72... | collective-permute-start | bytes 626696 | tf_op jit(solution)/shard_map/ppermute | solution.py:44
  23.7 0.0 copy-done
  23.7 1.8 %attend_own.1 = (f32[3,256,128]{2,1,0:T(8,128)S(1)}, f32[6,256,128]{2,1,0:T(8,128)S(1)}, bf16[384,1536]{1,0:T(8,128)(2,1)S(1)}) custom-call(bf16[272,384]{1,0:T(8,128)(2,1)S(1)} %copy-done.1, bf16[512,384]{1,0:T(8,128)(2,1)S(1)} %copy-done, bf16[384,3072]{1,0:T(8,128)(2,1)} %weight_ref.3), custom_call_target="tpu_custom_call" | custom-call | tf_op jit(solution)/shard_map/attend_own/pallas_call | solution.py:208
  25.5 6.9 %collective-permute-done.4.refs_2_.query_ref = bf16[272,384]{1,0:T(8,128)(2,1)S(1)} collective-permute-done((bf16[272,384]{1,0:T(8,128)(2,1)}, bf16[272,384]{1,0:T(8,128)(2,1)S(1)}, u32[]{:S(2)}, u32[]{:S(2)}) %collective-permute-start.4) | collective-permute-done | bytes 208928 | tf_op jit(solution)/shard_map/ppermute | solution.py:49
  32.4 0.0 collective-permute-done.refs_0_.first_ref
  32.5 0.0 collective-permute-done.1.refs_1_.second_ref
  32.5 0.0 collective-permute-done.2.query_ref
  32.5 2.1 %collective-permute-done.3.weight_ref.this_ref = bf16[384,768]{1,0:T(8,128)(2,1)S(1)} collective-permute-done((bf16[384,768]{1,0:T(8,128)(2,1)S(1)}, bf16[384,768]{1,0:T(8,128)(2,1)S(1)}, u32[]{:S(2)}, u32[]{:S(2)}) %collective-permute-start.3) | collective-permute-done | bytes 589856 | tf_op jit(solution)/shard_map/ppermute | solution.py:53
  34.5 1.6 %attend_pair.1.after_ref = bf16[1040,384]{1,0:T(8,128)(2,1)S(1)} custom-call(bf16[272,384]{1,0:T(8,128)(2,1)S(1)} %collective-permute-done.2.query_ref, bf16[512,384]{1,0:T(8,128)(2,1)S(1)} %copy-done, bf16[512,384]{1,0:T(8,128)(2,1)S(1)} %collective-permute-done.refs_0_.first_ref, bf16[512,384]{1,0:T(8,128)(2,1)S(1)} %collective-permute-done.1.refs_1_.second_ref, ...), custom_call_target="tpu_custom_call" | custom-call | flops 400000000 | bytes 2000000 | tf_op jit(solution)/shard_map/attend_pair/pallas_call | solution.py:259
  36.1 1.9 %collective-permute-start.5 = (bf16[1040,384]{1,0:T(8,128)(2,1)S(1)}, bf16[1040,384]{1,0:T(8,128)(2,1)S(1)}, u32[]{:S(2)}, u32[]{:S(2)}) collective-permute-start(bf16[1040,384]{1,0:T(8,128)(2,1)S(1)} %attend_pair.1.after_ref), channel_id=1, source_target_pairs={{0,8},{8,0},{16,24},{24,16},{32,40},{40,32},{48,56},{56,48},{64,72... | collective-permute-start | bytes 2396168 | tf_op jit(solution)/shard_map/ppermute | solution.py:44
  38.1 1.5 %attend_middle.1 = bf16[272,384]{1,0:T(8,128)(2,1)S(1)} custom-call(bf16[272,384]{1,0:T(8,128)(2,1)S(1)} %collective-permute-done.4.refs_2_.query_ref, bf16[512,384]{1,0:T(8,128)(2,1)S(1)} %copy-done, bf16[512,384]{1,0:T(8,128)(2,1)S(1)} %collective-permute-done.refs_0_.first_ref, bf16[512,384]{1,0:T(8,128)(2,1)S(1)} %collective-permute-done.1.refs_1_.second_ref, ...), custom_call_target="tpu_custom_call" | custom-call | flops 600000000 | bytes 2000000 | tf_op jit(solution)/shard_map/attend_middle/pallas_call | solution.py:291
  39.6 2.2 %collective-permute-start.6 = (bf16[272,384]{1,0:T(8,128)(2,1)S(1)}, bf16[272,384]{1,0:T(8,128)(2,1)S(1)}, u32[]{:S(2)}, u32[]{:S(2)}) collective-permute-start(bf16[272,384]{1,0:T(8,128)(2,1)S(1)} %attend_middle.1), channel_id=1, source_target_pairs={{8,16},{16,8},{40,48},{48,40},{72,80},{80,72},{104,112},{112,104},... | collective-permute-start | bytes 626696 | tf_op jit(solution)/shard_map/ppermute | solution.py:49
  41.9 0.0 collective-permute-done.5.message_ref.other_ref
  41.9 2.0 %attend_last.1 = (f32[256,384]{1,0:T(8,128)S(1)}, f32[3,8,256]{2,1,0:T(8,128)S(1)}) custom-call(bf16[272,384]{1,0:T(8,128)(2,1)S(1)} %copy-done.1, bf16[512,384]{1,0:T(8,128)(2,1)S(1)} %collective-permute-done.refs_0_.first_ref, bf16[512,384]{1,0:T(8,128)(2,1)S(1)} %collective-permute-done.1.refs_1_.second_ref, ...), custom_call_target="tpu_custom_call" | custom-call | flops 400000000 | bytes 2000000 | tf_op jit(solution)/shard_map/attend_last/pallas_call | solution.py:322
  43.9 2.8 %collective-permute-done.6.middle_ref = bf16[272,384]{1,0:T(8,128)(2,1)S(1)} collective-permute-done((bf16[272,384]{1,0:T(8,128)(2,1)S(1)}, bf16[272,384]{1,0:T(8,128)(2,1)S(1)}, u32[]{:S(2)}, u32[]{:S(2)}) %collective-permute-start.6) | collective-permute-done | bytes 208928 | tf_op jit(solution)/shard_map/ppermute | solution.py:49
  46.7 0.5 merge.1.mine_ref
  47.2 4.7 %collective-permute-start.7 = (bf16[256,384]{1,0:T(8,128)(2,1)S(1)}, bf16[256,384]{1,0:T(8,128)(2,1)S(1)}, u32[]{:S(2)}, u32[]{:S(2)}) collective-permute-start(bf16[256,384]{1,0:T(8,128)(2,1)S(1)} %merge.1.mine_ref), channel_id=1, source_target_pairs={{0,4},{4,0},{1,5},{5,1},{2,6},{6,2},{3,7},{7,3},{8,12},{12,8},{9,1... | collective-permute-start | bytes 589832 | tf_op jit(solution)/shard_map/ppermute | solution.py:53
  51.9 0.6 project_mine.1.mine_ref
  52.5 2.6 %collective-permute-done.7.theirs_ref = bf16[256,384]{1,0:T(8,128)(2,1)S(1)} collective-permute-done((bf16[256,384]{1,0:T(8,128)(2,1)S(1)}, bf16[256,384]{1,0:T(8,128)(2,1)S(1)}, u32[]{:S(2)}, u32[]{:S(2)}) %collective-permute-start.7) | collective-permute-done | bytes 196640 | tf_op jit(solution)/shard_map/ppermute | solution.py:53
  55.1 1.4 %project.1 = bf16[4,256,384]{2,1,0:T(8,128)(2,1)} custom-call(f32[4,256,384]{2,1,0:T(8,128)S(1)} %project_mine.1.mine_ref, bf16[256,384]{1,0:T(8,128)(2,1)S(1)} %collective-permute-done.7.theirs_ref, bf16[384,768]{1,0:T(8,128)(2,1)S(1)} %collective-permute-done.3.weight_ref.this_ref, bf16[1040,384]{1,0:T(8,128)(2,1)S(1)} %collective-permute-done.5.message_ref.other_ref), custom_call_target="tpu_custom_call" | custom-call | flops 300000000 | bytes 5000000 | tf_op jit(solution)/shard_map/project/pallas_call | solution.py:415
  56.6 0.0 copy-start.3
  56.6 0.0 copy-start.2
  56.6 4.4 %all-to-all-start = ((bf16[4,256,384]{2,1,0:T(8,128)(2,1)}), bf16[4,256,384]{2,1,0:T(8,128)(2,1)S(1)}, u32[]{:S(2)}, u32[]{:S(2)}) async-start(bf16[4,256,384]{2,1,0:T(8,128)(2,1)} %project.1), calls=%async_computation | async-start | bytes 1572864 | tf_op jit(solution)/shard_map/all_to_all | solution.py:459
  61.0 8.8 %all-to-all-done.terms_ref = bf16[4,256,384]{2,1,0:T(8,128)(2,1)S(1)} async-done(((bf16[4,256,384]{2,1,0:T(8,128)(2,1)}), bf16[4,256,384]{2,1,0:T(8,128)(2,1)S(1)}, u32[]{:S(2)}, u32[]{:S(2)}) %all-to-all-start) | async-done | bytes 786464 | tf_op jit(solution)/shard_map/all_to_all | solution.py:459
  69.8 0.8 %finish.1 = bf16[256,384]{1,0:T(8,128)(2,1)} custom-call(bf16[4,256,384]{2,1,0:T(8,128)(2,1)S(1)} %all-to-all-done.terms_ref, bf16[256,384]{1,0:T(8,128)(2,1)S(1)} %copy-done.2, f32[1,384]{1,0:T(1,128)S(1)} %reshape.3.gate_ref), custom_call_target="tpu_custom_call" | custom-call | flops 3932160 | bytes 2000000 | tf_op jit(solution)/shard_map/finish/pallas_call | solution.py:434
  (6 shorter events, 0.0 us)
Async XLA Ops:
  2.0 19.8 %copy-start.1 = (bf16[272,384]{1,0:T(8,128)(2,1)S(1)}, bf16[272,384]{1,0:T(8,128)(2,1)}, u32[]{:S(2)}) copy-start(bf16[272,384]{1,0:T(8,128)(2,1)} %get-tuple-element.12.query_ref) | copy-start | bytes 626692
  2.0 21.7 %copy-start = (bf16[512,384]{1,0:T(8,128)(2,1)S(1)}, bf16[512,384]{1,0:T(8,128)(2,1)}, u32[]{:S(2)}) copy-start(bf16[512,384]{1,0:T(8,128)(2,1)} %get-tuple-element.13.block_ref.own_ref) | copy-start | bytes 1179652
  2.0 30.5 %collective-permute-start = (bf16[512,384]{1,0:T(8,128)(2,1)}, bf16[512,384]{1,0:T(8,128)(2,1)S(1)}, u32[]{:S(2)}, u32[]{:S(2)}) collective-permute-start(bf16[512,384]{1,0:T(8,128)(2,1)} %get-tuple-element.13.block_ref.own_ref), channel_id=1, source_target_pairs={{32,64},{40,72},{48,80},{56,88},{64,32},{72,40},{80,48},{88,56},{9... | collective-permute-start | bytes 1179656 | tf_op jit(solution)/shard_map/ppermute | solution.py:40
  2.8 29.6 %collective-permute-start.1 = (bf16[512,384]{1,0:T(8,128)(2,1)}, bf16[512,384]{1,0:T(8,128)(2,1)S(1)}, u32[]{:S(2)}, u32[]{:S(2)}) collective-permute-start(bf16[512,384]{1,0:T(8,128)(2,1)} %get-tuple-element.13.block_ref.own_ref), channel_id=1, source_target_pairs={{0,32},{8,40},{16,48},{24,56},{32,0},{40,8},{48,16},{56,24},{64,96... | collective-permute-start | bytes 1179656 | tf_op jit(solution)/shard_map/ppermute | solution.py:40
  12.6 19.8 %collective-permute-start.4 = (bf16[272,384]{1,0:T(8,128)(2,1)}, bf16[272,384]{1,0:T(8,128)(2,1)S(1)}, u32[]{:S(2)}, u32[]{:S(2)}) collective-permute-start(bf16[272,384]{1,0:T(8,128)(2,1)} %get-tuple-element.12.query_ref), channel_id=1, source_target_pairs={{8,16},{16,8},{40,48},{48,40},{72,80},{80,72},{104,112},{112,104},... | collective-permute-start | bytes 626696 | tf_op jit(solution)/shard_map/ppermute | solution.py:49
  17.1 17.4 %collective-permute-start.3 = (bf16[384,768]{1,0:T(8,128)(2,1)S(1)}, bf16[384,768]{1,0:T(8,128)(2,1)S(1)}, u32[]{:S(2)}, u32[]{:S(2)}) collective-permute-start(bf16[384,768]{1,0:T(8,128)(2,1)S(1)} %split_weight.1), channel_id=1, source_target_pairs={{0,4},{4,0},{1,5},{5,1},{2,6},{6,2},{3,7},{7,3},{8,12},{12,8},{9,1... | collective-permute-start | bytes 1769480 | tf_op jit(solution)/shard_map/ppermute | solution.py:53
  21.8 10.7 %collective-permute-start.2 = (bf16[272,384]{1,0:T(8,128)(2,1)S(1)}, bf16[272,384]{1,0:T(8,128)(2,1)S(1)}, u32[]{:S(2)}, u32[]{:S(2)}) collective-permute-start(bf16[272,384]{1,0:T(8,128)(2,1)S(1)} %copy-done.1), channel_id=1, source_target_pairs={{0,8},{8,0},{16,24},{24,16},{32,40},{40,32},{48,56},{56,48},{64,72... | collective-permute-start | bytes 626696 | tf_op jit(solution)/shard_map/ppermute | solution.py:44
  36.1 5.7 %collective-permute-start.5 = (bf16[1040,384]{1,0:T(8,128)(2,1)S(1)}, bf16[1040,384]{1,0:T(8,128)(2,1)S(1)}, u32[]{:S(2)}, u32[]{:S(2)}) collective-permute-start(bf16[1040,384]{1,0:T(8,128)(2,1)S(1)} %attend_pair.1.after_ref), channel_id=1, source_target_pairs={{0,8},{8,0},{16,24},{24,16},{32,40},{40,32},{48,56},{56,48},{64,72... | collective-permute-start | bytes 2396168 | tf_op jit(solution)/shard_map/ppermute | solution.py:44
  39.6 7.1 %collective-permute-start.6 = (bf16[272,384]{1,0:T(8,128)(2,1)S(1)}, bf16[272,384]{1,0:T(8,128)(2,1)S(1)}, u32[]{:S(2)}, u32[]{:S(2)}) collective-permute-start(bf16[272,384]{1,0:T(8,128)(2,1)S(1)} %attend_middle.1), channel_id=1, source_target_pairs={{8,16},{16,8},{40,48},{48,40},{72,80},{80,72},{104,112},{112,104},... | collective-permute-start | bytes 626696 | tf_op jit(solution)/shard_map/ppermute | solution.py:49
  47.2 7.9 %collective-permute-start.7 = (bf16[256,384]{1,0:T(8,128)(2,1)S(1)}, bf16[256,384]{1,0:T(8,128)(2,1)S(1)}, u32[]{:S(2)}, u32[]{:S(2)}) collective-permute-start(bf16[256,384]{1,0:T(8,128)(2,1)S(1)} %merge.1.mine_ref), channel_id=1, source_target_pairs={{0,4},{4,0},{1,5},{5,1},{2,6},{6,2},{3,7},{7,3},{8,12},{12,8},{9,1... | collective-permute-start | bytes 589832 | tf_op jit(solution)/shard_map/ppermute | solution.py:53
  56.6 4.5 %copy-start.3 = (f32[384]{0:T(512)S(1)}, f32[384]{0:T(512)}, u32[]{:S(2)}) copy-start(f32[384]{0:T(512)} %param.13) | copy-start | bytes 4612
  56.6 13.2 %copy-start.2 = (bf16[256,384]{1,0:T(8,128)(2,1)S(1)}, bf16[256,384]{1,0:T(8,128)(2,1)}, u32[]{:S(2)}) copy-start(bf16[256,384]{1,0:T(8,128)(2,1)} %residual_ref.1) | copy-start | bytes 589828
  56.6 13.2 %all-to-all-start = ((bf16[4,256,384]{2,1,0:T(8,128)(2,1)}), bf16[4,256,384]{2,1,0:T(8,128)(2,1)S(1)}, u32[]{:S(2)}, u32[]{:S(2)}) async-start(bf16[4,256,384]{2,1,0:T(8,128)(2,1)} %project.1), calls=%async_computation | async-start | bytes 1572864 | tf_op jit(solution)/shard_map/all_to_all | solution.py:459
